TPU v7x, 32 devices: a whole 2x2x4 slice. The times are simulated.
32 devices in a mesh: parts: 2 (over y), row: 4 (over z), col: 4 (over x, core).
Axes of the slice: x: 2, y: 2, z: 4, core: 2. Of those that a mesh axis runs over, the one named last changes fastest.
Arguments:
- charges: bfloat16 [32, 32, 1024], P(('parts', 'row')), parts along dimension 0, may hold values from -6 to 6
- near_blocks: bfloat16 [32, 1024, 1024], P(('parts', 'row', 'col')), parts along dimension 0, may hold values from -0.09375 to 0.09375
- near_rows: int32 [32], P(('parts', 'row', 'col')), parts along dimension 0, may hold values from 0 to 15, as said below
- near_cols: int32 [32], P(('parts', 'row', 'col')), parts along dimension 0, may hold values from 0 to 15, as said below
- far_u: bfloat16 [768, 16, 1024], P(('parts', 'row', 'col')), parts along dimension 0, may hold values from -0.3125 to 0.3125
- far_v: bfloat16 [768, 16, 1024], P(('parts', 'row', 'col')), parts along dimension 0, may hold values from -0.1875 to 0.1875
- far_rows: int32 [768], P(('parts', 'row', 'col')), parts along dimension 0, may hold values from 0 to 15, as said below
- far_cols: int32 [768], P(('parts', 'row', 'col')), parts along dimension 0, may hold values from 0 to 15, as said below
Outputs:
- potential: float32 [32, 32, 1024], P(('parts', 'row'), None, 'col'), parts along dimension 0
There are 2 independent parts, one for each index of `parts`. A program takes and returns all parts, laid end to end along the dimension named above; each array names one. Nothing has to cross between parts.
Inputs may be any that keep to these rules, and one draw needn't show every extreme that they name: `near_rows`: entry e lies in row group g = e // 4: its cluster is one of g * 4 to (g + 1) * 4 - 1. `near_cols`: entry e lies in row group g = e // 4: its cluster is one of g * 4 to (g + 1) * 4 - 1. `far_rows`: entry e has its row cluster in row group g = e // 96, that is one of g * 4 to (g + 1) * 4 - 1. `far_cols`: a column cluster never lies in its entry's own row group; of the 24 entries of one device at most 8 have column clusters in one row group, and some device reaches 8; a pair of clusters may occur in several entries, whose terms add.
All inputs are finite; a program needn't handle non-finite values.
Results may differ from a plain program's by a relative error of at most 0.0026.
Values may be sent and summed in bfloat16 or wider, within the bound.
No kernel may reach another device: no remote copies, remote signals or barrier semaphores. Data moves between devices by JAX's collectives and lax.ppermute only.
A program may use at most 128 MiB of HBM per device.

v0:
```python
import jax
import jax.numpy as jnp
from jax import lax
from jax.sharding import PartitionSpec as P


def body(charges, near_blocks, near_rows, near_cols, far_u, far_v, far_rows, far_cols):
    cluster_count = charges.shape[0]
    excitations = charges.shape[1]
    panels = charges.shape[2]
    far_count = far_u.shape[0]
    row_count = lax.axis_size("row")
    slot_cap = max(2, (far_count + row_count - 2) // (row_count - 1))
    first_cluster = lax.axis_index("row") * cluster_count
    near_row_local = near_rows - first_cluster
    near_col_local = near_cols - first_cluster
    near_weight = jnp.where(near_row_local == near_col_local, 0.5, 1.0).astype(jnp.float32)[
        :, None, None
    ]
    near_forward = jnp.einsum(
        "beq,bpq->bep", charges[near_col_local], near_blocks, preferred_element_type=jnp.float32
    )
    near_mirror = jnp.einsum(
        "bep,bpq->beq", charges[near_row_local], near_blocks, preferred_element_type=jnp.float32
    )
    partial_sum = jnp.zeros((cluster_count, excitations, panels), jnp.float32)
    partial_sum = partial_sum.at[near_row_local].add(near_weight * near_forward)
    partial_sum = partial_sum.at[near_col_local].add(near_weight * near_mirror)
    far_row_local = far_rows - first_cluster
    owners = far_cols // cluster_count
    col_within = far_cols % cluster_count
    entry_order = jnp.arange(far_count)
    earlier_same = (owners[:, None] == owners[None, :]) & (
        entry_order[None, :] < entry_order[:, None]
    )
    slot_number = jnp.sum(earlier_same.astype(jnp.int32), axis=1)
    slot_index = owners * slot_cap + slot_number
    request = (
        jnp.zeros((row_count * slot_cap,), jnp.int32)
        .at[slot_index]
        .set(col_within)
        .reshape(row_count, slot_cap)
    )
    coef_t = jnp.einsum(
        "bes,bks->bek", charges[far_row_local], far_u, preferred_element_type=jnp.float32
    ).astype(jnp.bfloat16)
    asked_ids = lax.all_to_all(request, "row", split_axis=0, concat_axis=0, tiled=True)
    served, asked_ids = (charges[asked_ids], asked_ids)
    fetched = lax.all_to_all(served, "row", split_axis=0, concat_axis=0, tiled=True)
    far_x = fetched.reshape(row_count * slot_cap, excitations, panels)[slot_index]
    coef = jnp.einsum("bes,bks->bek", far_x, far_v, preferred_element_type=jnp.float32).astype(
        jnp.bfloat16
    )
    far_forward = jnp.einsum("bek,bks->bes", coef, far_u, preferred_element_type=jnp.float32)
    partial_sum = partial_sum.at[far_row_local].add(far_forward)
    far_mirror = jnp.einsum("bek,bks->bes", coef_t, far_v, preferred_element_type=jnp.float32)
    outbox = (
        jnp.zeros((row_count * slot_cap, excitations, panels), jnp.float32)
        .at[slot_index]
        .add(far_mirror)
    )
    inbox = lax.all_to_all(
        outbox.reshape(row_count, slot_cap, excitations, panels),
        "row",
        split_axis=0,
        concat_axis=0,
        tiled=True,
    )
    partial_sum = partial_sum.at[asked_ids.reshape(-1)].add(inbox.reshape(-1, excitations, panels))
    return lax.psum_scatter(partial_sum, "col", scatter_dimension=2, tiled=True)


def solution(mesh):
    placed = (
        P(("parts", "row"), None, None),
        P(("parts", "row", "col"), None, None),
        P(("parts", "row", "col")),
        P(("parts", "row", "col")),
        P(("parts", "row", "col"), None, None),
        P(("parts", "row", "col"), None, None),
        P(("parts", "row", "col")),
        P(("parts", "row", "col")),
    )
    return jax.shard_map(
        body,
        mesh=mesh,
        in_specs=placed,
        out_specs=P(("parts", "row"), None, "col"),
        check_vma=False,
    )
```

profile of v0, /device:TPU:0, one launch (start us, length us, event | category | flops | bytes accessed | tf_op | source)
XLA Modules:
  0.0 207.4 jit_solution(13132240910520899113)
XLA Ops:
  6.5 0.8 and_select_fusion
  7.4 0.2 convert_reduce_fusion
  7.5 0.6 scatter_custom_fusion
  8.3 11.7 %all_to_all.22 = s32[4,1,8]{2,1,0:T(1,128)S(1)} all-to-all(s32[4,1,8]{2,1,0:T(1,128)S(1)} %bitcast.65), channel_id=1, replica_groups=mesh['parts'=2,'row'=4,'col'=4] {'row'}, dimensions={0} | all-to-all | bytes 256 | tf_op jit(solution)/shard_map/all_to_all | solution.py:47
  20.0 2.9 %gather_fusion = bf16[32,32,1024]{2,1,0:T(8,128)(2,1)} fusion(bf16[4,32,1024]{2,1,0:T(8,128)(2,1)} %param.12, s32[1024]{0:T(1024)S(1)} %pad_clamp_fusion.2), kind=kCustom, calls=%fused_computation | custom fusion | bytes 4194432 | tf_op jit(solution)/shard_map/gather | solution.py:48
  23.0 4.6 %all-to-all-start.1 = ((bf16[4,8,32,1024]{3,2,1,0:T(8,128)(2,1)}), bf16[4,8,32,1024]{3,2,1,0:T(8,128)(2,1)}, u32[]{:S(2)}, u32[]{:S(2)}) async-start(bf16[4,8,32,1024]{3,2,1,0:T(8,128)(2,1)} %bitcast.63), calls=%async_computation.1 | async-start | bytes 4194304 | tf_op jit(solution)/shard_map/all_to_all | solution.py:49
  27.7 1.8 gather_fusion.2
  29.5 4.2 %fusion.32 = f32[24,32,1024]{2,1,0:T(8,128)} fusion(bf16[24,16,1024]{2,1,0:T(8,128)(2,1)} %param.17, bf16[24,32,1024]{2,1,0:T(8,128)(2,1)} %gather_fusion.2, bf16[24,16,1024]{2,1,0:T(8,128)(2,1)S(1)} %copy-done.3), kind=kOutput, calls=%fused_computation.23 | convolution fusion | flops 50343936 | bytes 6291456 | tf_op jit(solution)/shard_map/bek,bks->bes/dot_general | solution.py:56
  33.7 2.5 %broadcast_in_dim.21 = f32[32,32,1024]{2,1,0:T(8,128)} broadcast(f32[]{:T(128)} %constant.81.clone.1), dimensions={} | broadcast | bytes 4194308 | tf_op jit(solution)/shard_map/broadcast_in_dim | solution.py:58
  36.2 9.5 %scatter_fusion.1 = f32[32,32,1024]{2,1,0:T(8,128)} fusion(f32[32,32,1024]{2,1,0:T(8,128)} %broadcast_in_dim.21, s32[24]{0:T(128)S(1)} %compare_select_fusion.2, f32[24,32,1024]{2,1,0:T(8,128)} %fusion.32), kind=kCustom, calls=%fused_computation.5 | custom fusion | flops 786432 | bytes 9437280 | tf_op jit(solution)/shard_map/scatter-add | solution.py:60
  45.7 29.0 %all-to-all-done.1 = bf16[4,8,32,1024]{3,2,1,0:T(8,128)(2,1)} async-done(((bf16[4,8,32,1024]{3,2,1,0:T(8,128)(2,1)}), bf16[4,8,32,1024]{3,2,1,0:T(8,128)(2,1)}, u32[]{:S(2)}, u32[]{:S(2)}) %all-to-all-start.1) | async-done | bytes 2097184 | tf_op jit(solution)/shard_map/all_to_all | solution.py:49
  74.7 5.0 %all-to-all-start.2 = ((f32[4,8,32,1024]{3,2,1,0:T(8,128)}), f32[4,8,32,1024]{3,2,1,0:T(8,128)}, u32[]{:S(2)}, u32[]{:S(2)}) async-start(f32[4,8,32,1024]{3,2,1,0:T(8,128)} %bitcast.62), calls=%async_computation.2 | async-start | bytes 8388608 | tf_op jit(solution)/shard_map/all_to_all | solution.py:62
  81.1 0.8 and_reduce_fusion
  81.9 1.3 fusion.13
  83.3 1.1 fusion.28
  84.4 0.5 broadcast.185
  84.9 0.7 reduce.19
  85.7 3.5 %gather_fusion.1 = bf16[24,32,1024]{2,1,0:T(8,128)(2,1)} fusion(bf16[32,32,1024]{2,1,0:T(8,128)(2,1)} %bitcast.12, s32[1024]{0:T(1024)S(1)} %pad_clamp_fusion.1), kind=kCustom, calls=%fused_computation.1 | custom fusion | bytes 3145824 | tf_op jit(solution)/shard_map/gather | solution.py:50
  89.2 4.5 %fusion.31 = f32[24,32,1024]{2,1,0:T(8,128)} fusion(bf16[24,16,1024]{2,1,0:T(8,128)(2,1)} %param.16, bf16[24,32,1024]{2,1,0:T(8,128)(2,1)} %gather_fusion.1, bf16[24,16,1024]{2,1,0:T(8,128)(2,1)} %param.17), kind=kOutput, calls=%fused_computation.22 | convolution fusion | flops 50343936 | bytes 6291456 | tf_op jit(solution)/shard_map/bek,bks->bes/dot_general | solution.py:54
  93.7 6.1 %scatter_fusion = f32[4,32,1024]{2,1,0:T(8,128)S(1)} fusion(f32[4,32,1024]{2,1,0:T(8,128)S(1)} %fusion.28, s32[24]{0:T(128)S(1)} %compare_select_fusion.3, f32[24,32,1024]{2,1,0:T(8,128)} %fusion.31), kind=kCustom, calls=%fused_computation.4 | custom fusion | flops 786432 | bytes 9437280 | tf_op jit(solution)/shard_map/scatter-add | solution.py:55
  99.8 72.6 %all-to-all-done.2 = f32[4,8,32,1024]{3,2,1,0:T(8,128)} async-done(((f32[4,8,32,1024]{3,2,1,0:T(8,128)}), f32[4,8,32,1024]{3,2,1,0:T(8,128)}, u32[]{:S(2)}, u32[]{:S(2)}) %all-to-all-start.2) | async-done | bytes 4194336 | tf_op jit(solution)/shard_map/all_to_all | solution.py:62
  172.4 6.4 %scatter_fusion.2 = f32[4,32,1024]{2,1,0:T(8,128)S(1)} fusion(f32[4,32,1024]{2,1,0:T(8,128)S(1)} %scatter_fusion, s32[32]{0:T(128)S(1)} %fusion.40, f32[32,32,1024]{2,1,0:T(8,128)} %bitcast.15), kind=kCustom, calls=%fused_computation.6 | custom fusion | flops 1048576 | bytes 12583040 | tf_op jit(solution)/shard_map/scatter-add | solution.py:69
  178.8 0.8 copy-done.1
  179.6 20.9 %reduce-scatter.2.cloned.1.call-done = f32[4,32,256]{2,1,0:T(8,128)} async-done(((f32[4,32,1024]{2,1,0:T(8,128)}), f32[4,32,256]{2,1,0:T(8,128)}) %reduce-scatter.2.cloned.1.call-update) | async-done | bytes 131088 | tf_op jit(solution)/shard_map/reduce_scatter | solution.py:70
  (24 shorter events, 0.4 us)
Async XLA Ops:
  6.5 75.4 %copy-start = (bf16[1,1024,1024]{2,1,0:T(8,128)(2,1)S(1)}, bf16[1,1024,1024]{2,1,0:T(8,128)(2,1)}, u32[]{:S(2)}) copy-start(bf16[1,1024,1024]{2,1,0:T(8,128)(2,1)} %param.13) | copy-start | bytes 6291460
  23.0 4.7 %copy-start.5 = (s32[24]{0:T(128)S(1)}, s32[24]{0:T(128)}, u32[]{:S(2)}) copy-start(s32[24]{0:T(128)} %param.18) | copy-start | bytes 292
  23.0 4.7 %copy-start.2 = (bf16[4,32,1024]{2,1,0:T(8,128)(2,1)S(1)}, bf16[4,32,1024]{2,1,0:T(8,128)(2,1)}, u32[]{:S(2)}) copy-start(bf16[4,32,1024]{2,1,0:T(8,128)(2,1)} %param.12) | copy-start | bytes 786436
  23.0 51.7 %all-to-all-start.1 = ((bf16[4,8,32,1024]{3,2,1,0:T(8,128)(2,1)}), bf16[4,8,32,1024]{3,2,1,0:T(8,128)(2,1)}, u32[]{:S(2)}, u32[]{:S(2)}) async-start(bf16[4,8,32,1024]{3,2,1,0:T(8,128)(2,1)} %bitcast.63), calls=%async_computation.1 | async-start | bytes 4194304 | tf_op jit(solution)/shard_map/all_to_all | solution.py:49
  27.6 1.9 copy-start.3
  74.7 6.4 %copy-start.4 = (s32[3]{0:T(128)S(1)}, s32[3]{0:T(128)}, u32[]{:S(2)}) copy-start(s32[3]{0:T(128)} %constant.88.clone.1) | copy-start | bytes 40
  74.7 97.7 %all-to-all-start.2 = ((f32[4,8,32,1024]{3,2,1,0:T(8,128)}), f32[4,8,32,1024]{3,2,1,0:T(8,128)}, u32[]{:S(2)}, u32[]{:S(2)}) async-start(f32[4,8,32,1024]{3,2,1,0:T(8,128)} %bitcast.62), calls=%async_computation.2 | async-start | bytes 8388608 | tf_op jit(solution)/shard_map/all_to_all | solution.py:62
  79.7 120.8 %reduce-scatter.2.cloned.1.call-start = ((), (), s32[]{:S(2)}) async-start(), calls=%async_computation.4 | async-start | bytes 655360 | tf_op jit(solution)/shard_map/reduce_scatter | solution.py:70
  178.8 0.8 copy-start.1
Sparse Core Ops, SparseCore 0:
  179.8 20.7 reduce-scatter.1
where the time goes:
time: 208 us; the launch traced here: 207 us
  waiting for transfers between devices  123 us (59%)
  other arithmetic  24.4 us (12%)
  between operations  14.9 us (7%)
  local copies, waits for them, and re-layouts  13 us (6%)
  blocking collectives  11.7 us (6%)
  matrix products  11.2 us (5%)
  starting transfers between devices  9.66 us (5%)
    all_to_all x1, waiting for transfers between devices, body(): lax.all_to_all(outbox.reshape(row_count, slot_cap, excitations, panels),...  72.6 us
    all_to_all x1, waiting for transfers between devices, body(): lax.all_to_all(served, 'row', split_axis=0, concat_axis=0, tiled=True)  29 us
    reduce_scatter x1, waiting for transfers between devices, body(): return lax.psum_scatter(partial_sum, 'col', scatter_dimension=2, tiled=True)  20.9 us
    all_to_all x1, blocking collectives, body(): lax.all_to_all(request, 'row', split_axis=0, concat_axis=0, tiled=True)  11.7 us
    scatter-add x1, other arithmetic, body(): outbox = jnp.zeros((row_count * slot_cap, excitations, panels), jnp.float...  9.48 us
    scatter-add x1, other arithmetic, body(): partial_sum.at[asked_ids.reshape(-1)]  6.42 us
    scatter-add x1, other arithmetic, body(): partial_sum = partial_sum.at[far_row_local].add(far_forward)  6.05 us
    all_to_all x1, starting transfers between devices, body(): lax.all_to_all(outbox.reshape(row_count, slot_cap, excitations, panels),...  4.99 us
  transfers between devices with their start and end apart: 3, of which 3 were waited for; matrix products, arithmetic and copies ran while one was open for 18% of the time, Pallas kernels for 0%

commit v1 on v0

v1 whole, which is shorter than its diff:
```python
import jax
import jax.numpy as jnp
from jax import lax
from jax.experimental import pallas as pl
from jax.experimental.pallas import tpu as pltpu
from jax.sharding import PartitionSpec as P

F32 = jnp.float32
BF16 = jnp.bfloat16
SMEM = pl.BlockSpec(memory_space=pltpu.SMEM)
VMEM = pl.BlockSpec(memory_space=pltpu.VMEM)


def dot(a, b):
    return jnp.dot(a, b, preferred_element_type=F32)


def dot_t(a, b):
    return lax.dot_general(a, b, (((1,), (1,)), ((), ())), preferred_element_type=F32)


def params():
    return pltpu.CompilerParams(vmem_limit_bytes=48 * 1024 * 1024)


def each(count, step):
    if count <= 4:
        for i in range(count):
            step(i)
    else:
        lax.fori_loop(0, count, lambda i, c: (step(i), c)[1], 0)


def lane_ids(ids_ref, rank):
    count = ids_ref.shape[0]
    lane = lax.broadcasted_iota(jnp.int32, (1, count * rank), 1) // rank
    out = jnp.full((1, count * rank), -1, jnp.int32)
    for b in range(count):
        out = jnp.where(lane == b, ids_ref[b], out)
    return out


def mirror_kernel(clusters, exc, rank, others, at_ref, rows_ref, cols_ref, x_ref, u_ref, v_ref, send_ref, keep_ref, mask_ref):
    group = at_ref[0]
    place = at_ref[1]
    half = lax.rem(place, 2)
    width = keep_ref.shape[2]
    row_lane = lane_ids(rows_ref, rank)
    col_lane = lane_ids(cols_ref, rank)
    every = dot_t(x_ref[...], u_ref[...])
    coef = jnp.zeros((exc, every.shape[1]), F32)
    for c in range(clusters):
        coef += jnp.where(row_lane == group * clusters + c, every[c * exc : (c + 1) * exc], 0.0)
    coef = coef.astype(BF16).astype(F32)
    span = clusters * exc

    def one(i):
        other = group ^ (i + 1)
        for c in range(clusters):
            mask_ref[c * exc : (c + 1) * exc, :] = jnp.where(
                col_lane == other * clusters + c, coef, 0.0
            ).astype(BF16)
        rows = pl.ds(i * span if isinstance(i, int) else pl.multiple_of(i * span, span), span)
        for q in range(keep_ref.shape[0]):
            for side in range(2):
                at = (2 * q + side) * width
                part = dot(mask_ref[...], v_ref[:, at : at + width])

                @pl.when(half == side)
                def _():
                    keep_ref[q, rows, :] = part

                @pl.when(half != side)
                def _():
                    send_ref[q, rows, :] = part.astype(BF16)

    each(others, one)


def near_kernel(clusters, exc, at_ref, rows_ref, cols_ref, x_ref, n_ref, out_ref):
    first = at_ref[0] * clusters
    out_ref[...] = jnp.zeros_like(out_ref)
    for b in range(n_ref.shape[0]):
        row = rows_ref[b] - first
        col = cols_ref[b] - first
        weight = jnp.where(row == col, 0.5, 1.0).astype(F32)
        out_ref[row] += weight * dot_t(x_ref[col], n_ref[b])
        out_ref[col] += weight * dot(x_ref[row], n_ref[b])


def forward_kernel(clusters, exc, rank, others, at_ref, rows_ref, cols_ref, u_ref, v_ref, near_ref, *refs):
    pieces = refs[: 2 * others]
    own_ref = refs[2 * others]
    sends = refs[2 * others + 1 : -1]
    part_ref = refs[-1]
    group = at_ref[0]
    place = at_ref[1]
    half = lax.rem(place, 2)
    width = own_ref.shape[1]
    row_lane = lane_ids(rows_ref, rank)
    col_lane = lane_ids(cols_ref, rank)
    some = clusters // 2
    coef = jnp.zeros((exc, u_ref.shape[0]), F32)
    for i in range(others):
        other = group ^ (i + 1)
        for side in range(2):
            every = dot_t(pieces[2 * i + side][...], v_ref[...])
            first = other * clusters + jnp.where(half == side, 0, 1) * some
            for c in range(some):
                coef += jnp.where(col_lane == first + c, every[c * exc : (c + 1) * exc], 0.0)
    coef = coef.astype(BF16).astype(F32)
    masked = jnp.concatenate(
        [jnp.where(row_lane == group * clusters + c, coef, 0.0) for c in range(clusters)], axis=0
    ).astype(BF16)
    for q in range(len(sends) + 1):
        cols = slice(q * width, (q + 1) * width)
        part_ref[q] = dot(masked, u_ref[:, cols]) + near_ref[:, cols]
    own_ref[...] = part_ref[place]
    for m in range(1, len(sends) + 1):
        sends[m - 1][...] = part_ref[place ^ m].astype(BF16)


def swap(value, axis, size, step):
    return lax.ppermute(value, axis, [(i, i ^ step) for i in range(size)])


def body(charges, near_blocks, near_rows, near_cols, far_u, far_v, far_rows, far_cols):
    clusters, exc, panels = charges.shape
    entries, rank, _ = far_u.shape
    row_count = lax.axis_size("row")
    col_count = lax.axis_size("col")
    others = row_count - 1
    pairs = col_count // 2
    width = panels // col_count
    span = clusters * exc
    some = span // 2
    place = lax.axis_index("col")
    at = jnp.stack([lax.axis_index("row"), place])
    x = charges.reshape(span, panels)
    u = far_u.reshape(entries * rank, panels)
    v = far_v.reshape(entries * rank, panels)

    mine = lax.dynamic_slice_in_dim(x, lax.rem(place, 2) * some, some, 0)
    got = [swap(mine, "row", row_count, d) for d in range(1, row_count)]

    send, keep = pl.pallas_call(
        lambda *refs: mirror_kernel(clusters, exc, rank, others, *refs),
        in_specs=[SMEM, SMEM, SMEM, VMEM, VMEM, VMEM],
        out_specs=[VMEM, VMEM],
        out_shape=[
            jax.ShapeDtypeStruct((pairs, others * span, width), BF16),
            jax.ShapeDtypeStruct((pairs, others * span, width), F32),
        ],
        scratch_shapes=[pltpu.VMEM((span, entries * rank), BF16)],
        compiler_params=params(),
        name="mirror",
    )(at, far_rows, far_cols, x, u, v)
    from_core = swap(send, "col", col_count, 1)

    near = pl.pallas_call(
        lambda *refs: near_kernel(clusters, exc, *refs),
        in_specs=[SMEM, SMEM, SMEM, VMEM, VMEM],
        out_specs=VMEM,
        out_shape=jax.ShapeDtypeStruct((clusters, exc, panels), F32),
        compiler_params=params(),
        name="near",
    )(at, near_rows, near_cols, charges, near_blocks).reshape(span, panels)

    other_half = [swap(piece, "col", col_count, 1) for piece in got]

    pair_sum = keep + from_core.astype(F32)
    my_pair = place // 2

    def chunk(q):
        return lax.dynamic_index_in_dim(pair_sum, q, 0, keepdims=False)

    mirror = chunk(my_pair)
    for m in range(1, pairs):
        mirror = mirror + swap(chunk(my_pair ^ m).astype(BF16), "col", col_count, 2 * m).astype(F32)
    mirror = mirror.astype(BF16)
    from_rows = [
        swap(mirror[(d - 1) * span : d * span], "row", row_count, d) for d in range(1, row_count)
    ]

    pieces = []
    for a, b in zip(got, other_half):
        pieces += [a, b]
    own, *sends = pl.pallas_call(
        lambda *refs: forward_kernel(clusters, exc, rank, others, *refs),
        in_specs=[SMEM, SMEM, SMEM] + [VMEM] * (3 + 2 * others),
        out_specs=[VMEM] * col_count,
        out_shape=[jax.ShapeDtypeStruct((span, width), F32)]
        + [jax.ShapeDtypeStruct((span, width), BF16)] * (col_count - 1),
        scratch_shapes=[pltpu.VMEM((col_count, span, width), F32)],
        compiler_params=params(),
        name="forward",
    )(at, far_rows, far_cols, u, v, near, *pieces)
    total = own
    for m in range(1, col_count):
        total = total + swap(sends[m - 1], "col", col_count, m).astype(F32)
    for term in from_rows:
        total = total + term.astype(F32)
    return total.reshape(clusters, exc, width)


def solution(mesh):
    placed = (
        P(("parts", "row"), None, None),
        P(("parts", "row", "col"), None, None),
        P(("parts", "row", "col")),
        P(("parts", "row", "col")),
        P(("parts", "row", "col"), None, None),
        P(("parts", "row", "col"), None, None),
        P(("parts", "row", "col")),
        P(("parts", "row", "col")),
    )
    return jax.shard_map(
        body,
        mesh=mesh,
        in_specs=placed,
        out_specs=P(("parts", "row"), None, "col"),
        check_vma=False,
    )
```

time: 208 us -> 47.1 us (0.23)
  waiting for transfers between devices: 123 us -> 13.7 us
  other arithmetic: 24.4 us -> 1.84 us
  between operations: 14.9 us -> 1.46 us
  blocking collectives: 11.7 us -> 0 us
  matrix products: 11.2 us -> 0 us
  Pallas kernels: 0 us -> 7.6 us
  local copies, waits for them, and re-layouts: 13 us -> 7.77 us
  starting transfers between devices: 9.66 us -> 14.4 us
    all_to_all x2 -> x0, waiting for transfers between devices: 102 us -> none  [the longest x1 72.6 us: body(): lax.all_to_all(outbox.reshape(row_count, slot_cap, excitations, panels),...]
    scatter-add x3 -> x0, other arithmetic: 22 us -> none  [the longest x1 9.48 us: body(): outbox = jnp.zeros((row_count * slot_cap, excitations, panels), jnp.float...]
    reduce_scatter x1 -> x0, waiting for transfers between devices: 20.9 us -> none  [body(): return lax.psum_scatter(partial_sum, 'col', scatter_dimension=2, tiled=True)]
    ppermute x0 -> x14, starting transfers between devices: none -> 14.4 us  [swap(): return lax.ppermute(value, axis, [(i, i ^ step) for i in range(size)])]
    ppermute x0 -> x14, waiting for transfers between devices: none -> 13.7 us  [swap(): return lax.ppermute(value, axis, [(i, i ^ step) for i in range(size)])]
    all_to_all x1 -> x0, blocking collectives: 11.7 us -> none  [body(): lax.all_to_all(request, 'row', split_axis=0, concat_axis=0, tiled=True)]
    dot_general x4 -> x0, matrix products: 11.2 us -> none  [the longest x1 4.54 us: body(): jnp.einsum('bek,bks->bes', coef, far_u, preferred_element_type=jnp.float32)]
    all_to_all x2 -> x0, starting transfers between devices: 9.62 us -> none  [the longest x1 4.99 us: body(): lax.all_to_all(outbox.reshape(row_count, slot_cap, excitations, panels),...]
  transfers between devices with their start and end apart: 3 -> 14, of which waited for: 3 -> 4; matrix products, arithmetic and copies ran while one was open for 18% -> 6% of each run, Pallas kernels for 0% -> 9%
where the time goes in v1:
time: 47.1 us; the launch traced here: 46.7 us
  starting transfers between devices  14.4 us (31%)
  waiting for transfers between devices  13.7 us (29%)
  local copies, waits for them, and re-layouts  7.77 us (16%)
  Pallas kernels  7.6 us (16%)
  other arithmetic  1.84 us (4%)
  between operations  1.46 us (3%)
    ppermute x14, starting transfers between devices, swap(): return lax.ppermute(value, axis, [(i, i ^ step) for i in range(size)])  14.4 us
    ppermute x14, waiting for transfers between devices, swap(): return lax.ppermute(value, axis, [(i, i ^ step) for i in range(size)])  13.7 us
    unnamed x22, local copies, waits for them, and re-layouts  6.14 us
    pallas_call x1, Pallas kernels, body(): pl.pallas_call(lambda *refs: mirror_kernel(clusters, exc, rank, others, *...  3.58 us
    pallas_call x1, Pallas kernels, body(): pl.pallas_call(lambda *refs: forward_kernel(clusters, exc, rank, others,...  2.4 us
    pallas_call x1, Pallas kernels, body(): pl.pallas_call(lambda *refs: near_kernel(clusters, exc, *refs), in_specs=...  1.62 us
    convert_element_type x1, other arithmetic, body(): mirror = mirror.astype(BF16)  0.98 us
  transfers between devices with their start and end apart: 14, of which 4 were waited for; matrix products, arithmetic and copies ran while one was open for 6% of the time, Pallas kernels for 9%

profile of v1, /device:TPU:0, one launch (start us, length us, event | category | flops | bytes accessed | tf_op | source)
XLA Modules:
  0.0 46.7 jit_solution(9903955129562379207)
XLA Ops:
  0.1 1.1 %copy-done = bf16[24,16,1024]{2,1,0:T(8,128)(2,1)S(1)} copy-done((bf16[24,16,1024]{2,1,0:T(8,128)(2,1)S(1)}, bf16[24,16,1024]{2,1,0:T(8,128)(2,1)}, u32[]{:S(2)}) %copy-start) | copy-done | bytes 786456
  1.2 1.1 %copy-done.2 = bf16[24,16,1024]{2,1,0:T(8,128)(2,1)S(1)} copy-done((bf16[24,16,1024]{2,1,0:T(8,128)(2,1)S(1)}, bf16[24,16,1024]{2,1,0:T(8,128)(2,1)}, u32[]{:S(2)}) %copy-start.2) | copy-done | bytes 786456
  2.3 0.9 %copy-done.5 = bf16[4,32,1024]{2,1,0:T(8,128)(2,1)S(1)} copy-done((bf16[4,32,1024]{2,1,0:T(8,128)(2,1)S(1)}, bf16[4,32,1024]{2,1,0:T(8,128)(2,1)}, u32[]{:S(2)}) %copy-start.5) | copy-done | bytes 262168
  3.3 0.7 %copy-done.7 = s32[24]{0:T(128)S(1)} copy-done((s32[24]{0:T(128)S(1)}, s32[24]{0:T(128)}, u32[]{:S(2)}) %copy-start.7) | copy-done | bytes 120
  4.0 0.7 %copy-done.9 = s32[24]{0:T(128)S(1)} copy-done((s32[24]{0:T(128)S(1)}, s32[24]{0:T(128)}, u32[]{:S(2)}) %copy-start.9) | copy-done | bytes 120
  4.6 3.6 %mirror.1 = (bf16[2,384,256]{2,1,0:T(8,128)(2,1)S(1)}, f32[2,384,256]{2,1,0:T(8,128)S(1)}) custom-call(s32[2]{0:T(128)S(1)} %pad_add_fusion.refs_0_, s32[24]{0:T(128)S(1)} %copy-done.7, s32[24]{0:T(128)S(1)} %copy-done.9, bf16[128,1024]{1,0:T(8,128)(2,1)S(1)} %bitcast.19, bf16[384,1024]{1,0:T(8,128)(2,1)S(1)} %bitcast.13, bf16[384,1024]{1,0:T(8,128)(2,1)S(1)} %bitcast.15), custom_call_target="tpu_custom_call" | custom-call | tf_op jit(solution)/shard_map/mirror/pallas_call | solution.py:146
  8.7 0.9 %constant_dynamic-slice_fusion = bf16[64,1024]{1,0:T(8,128)(2,1)S(1)} fusion(bf16[128,1024]{1,0:T(8,128)(2,1)} %bitcast.18, s32[]{:T(128)S(6)} %select_n.15), kind=kLoop, calls=%fused_computation.6 | loop fusion | bytes 262148 | tf_op jit(solution)/shard_map/dynamic_slice | solution.py:143
  9.6 2.7 %collective-permute-start = (bf16[64,1024]{1,0:T(8,128)(2,1)S(1)}, bf16[64,1024]{1,0:T(8,128)(2,1)S(1)}, u32[]{:S(2)}, u32[]{:S(2)}) collective-permute-start(bf16[64,1024]{1,0:T(8,128)(2,1)S(1)} %constant_dynamic-slice_fusion), channel_id=1, source_target_pairs={{0,4},{4,0},{8,12},{12,8},{1,5},{5,1},{9,13},{13,9},{2,6},{6,2},{1... | collective-permute-start | bytes 393224 | tf_op jit(solution)/shard_map/ppermute | solution.py:124
  12.3 2.6 %collective-permute-start.2 = (bf16[64,1024]{1,0:T(8,128)(2,1)S(1)}, bf16[64,1024]{1,0:T(8,128)(2,1)S(1)}, u32[]{:S(2)}, u32[]{:S(2)}) collective-permute-start(bf16[64,1024]{1,0:T(8,128)(2,1)S(1)} %constant_dynamic-slice_fusion), channel_id=1, source_target_pairs={{0,8},{4,12},{8,0},{12,4},{1,9},{5,13},{9,1},{13,5},{2,10},{6,14},... | collective-permute-start | bytes 393224 | tf_op jit(solution)/shard_map/ppermute | solution.py:124
  15.0 0.7 %fusion.1 = bf16[384,256]{1,0:T(8,128)(2,1)} fusion(f32[2,384,256]{2,1,0:T(8,128)S(1)} %convert_add_fusion, s32[]{:T(128)S(6)} %select_n.18), kind=kLoop, calls=%fused_computation.4 | loop fusion | bytes 393220 | tf_op jit(solution)/shard_map/convert_element_type | solution.py:179
  15.7 1.7 %collective-permute-start.10 = (bf16[384,256]{1,0:T(8,128)(2,1)}, bf16[384,256]{1,0:T(8,128)(2,1)}, u32[]{:S(2)}, u32[]{:S(2)}) collective-permute-start(bf16[384,256]{1,0:T(8,128)(2,1)} %fusion.1), channel_id=1, source_target_pairs={{0,2},{1,3},{2,0},{3,1},{4,6},{5,7},{6,4},{7,5},{8,10},{9,11},{10,... | collective-permute-start | bytes 589832 | tf_op jit(solution)/shard_map/ppermute | solution.py:124
  17.4 1.3 %collective-permute-done.refs_6_ = bf16[64,1024]{1,0:T(8,128)(2,1)S(1)} collective-permute-done((bf16[64,1024]{1,0:T(8,128)(2,1)S(1)}, bf16[64,1024]{1,0:T(8,128)(2,1)S(1)}, u32[]{:S(2)}, u32[]{:S(2)}) %collective-permute-start) | collective-permute-done | bytes 131104 | tf_op jit(solution)/shard_map/ppermute | solution.py:124
  18.7 6.5 %collective-permute-done.2.refs_8_ = bf16[64,1024]{1,0:T(8,128)(2,1)S(1)} collective-permute-done((bf16[64,1024]{1,0:T(8,128)(2,1)S(1)}, bf16[64,1024]{1,0:T(8,128)(2,1)S(1)}, u32[]{:S(2)}, u32[]{:S(2)}) %collective-permute-start.2) | collective-permute-done | bytes 131104 | tf_op jit(solution)/shard_map/ppermute | solution.py:124
  27.0 1.6 %copy-done.4 = bf16[1,1024,1024]{2,1,0:T(8,128)(2,1)S(1)} copy-done((bf16[1,1024,1024]{2,1,0:T(8,128)(2,1)S(1)}, bf16[1,1024,1024]{2,1,0:T(8,128)(2,1)}, u32[]{:S(2)}) %copy-start.4) | copy-done | bytes 2097176
  28.6 1.6 %near.1 = f32[4,32,1024]{2,1,0:T(8,128)S(1)} custom-call(s32[2]{0:T(128)S(1)} %pad_add_fusion.refs_0_, s32[1]{0:T(128)S(6)} %copy.9.refs_1_, s32[1]{0:T(128)S(6)} %copy.10.refs_2_, bf16[4,32,1024]{2,1,0:T(8,128)(2,1)S(1)} %copy-done.6, bf16[1,1024,1024]{2,1,0:T(8,128)(2,1)S(1)} %copy-done.4), custom_call_target="tpu_custom_call" | custom-call | tf_op jit(solution)/shard_map/near/pallas_call | solution.py:160
  30.3 2.4 %forward.1 = (f32[128,256]{1,0:T(8,128)S(1)}, bf16[128,256]{1,0:T(8,128)(2,1)S(1)}, bf16[128,256]{1,0:T(8,128)(2,1)S(1)}, bf16[128,256]{1,0:T(8,128)(2,1)S(1)}) custom-call(s32[2]{0:T(128)S(1)} %pad_add_fusion.refs_0_, s32[24]{0:T(128)S(1)} %copy-done.8, s32[24]{0:T(128)S(1)} %copy-done.10, bf16[384,1024]{1,0:T(8,128)(2,1)S(1)} %bitcast.14, ...), custom_call_target="tpu_custom_call" | custom-call | tf_op jit(solution)/shard_map/forward/pallas_call | solution.py:188
  32.7 1.2 %collective-permute-start.8 = (bf16[128,256]{1,0:T(8,128)(2,1)S(1)}, bf16[128,256]{1,0:T(8,128)(2,1)S(1)}, u32[]{:S(2)}, u32[]{:S(2)}) collective-permute-start(bf16[128,256]{1,0:T(8,128)(2,1)S(1)} %get-tuple-element.14), channel_id=1, source_target_pairs={{0,3},{1,2},{2,1},{3,0},{4,7},{5,6},{6,5},{7,4},{8,11},{9,10},{10,... | collective-permute-start | bytes 196616 | tf_op jit(solution)/shard_map/ppermute | solution.py:124
  33.9 0.5 %collective-permute-start.7 = (bf16[128,256]{1,0:T(8,128)(2,1)S(1)}, bf16[128,256]{1,0:T(8,128)(2,1)S(1)}, u32[]{:S(2)}, u32[]{:S(2)}) collective-permute-start(bf16[128,256]{1,0:T(8,128)(2,1)S(1)} %get-tuple-element.13), channel_id=1, source_target_pairs={{0,2},{1,3},{2,0},{3,1},{4,6},{5,7},{6,4},{7,5},{8,10},{9,11},{10,... | collective-permute-start | bytes 196616 | tf_op jit(solution)/shard_map/ppermute | solution.py:124
  34.6 1.0 %fusion = bf16[384,256]{1,0:T(8,128)(2,1)S(1)} fusion(bf16[384,256]{1,0:T(8,128)(2,1)} %collective-permute-done.10, f32[2,384,256]{2,1,0:T(8,128)S(1)} %convert_add_fusion, s32[]{:T(128)S(6)} %select_n.17), kind=kLoop, calls=%fused_computation.2 | loop fusion | flops 294912 | bytes 786436 | tf_op jit(solution)/shard_map/convert_element_type | solution.py:180
  35.6 2.5 %collective-permute-start.13 = (bf16[128,256]{1,0:T(8,128)(2,1)S(1)}, bf16[128,256]{1,0:T(8,128)(2,1)S(1)}, u32[]{:S(2)}, u32[]{:S(2)}) collective-permute-start(bf16[128,256]{1,0:T(8,128)(2,1)S(1)} %get-tuple-element.18), channel_id=1, source_target_pairs={{0,12},{4,8},{8,4},{12,0},{1,13},{5,9},{9,5},{13,1},{2,14},{6,10},... | collective-permute-start | bytes 196616 | tf_op jit(solution)/shard_map/ppermute | solution.py:124
  38.2 1.4 %collective-permute-start.12 = (bf16[128,256]{1,0:T(8,128)(2,1)S(1)}, bf16[128,256]{1,0:T(8,128)(2,1)S(1)}, u32[]{:S(2)}, u32[]{:S(2)}) collective-permute-start(bf16[128,256]{1,0:T(8,128)(2,1)S(1)} %get-tuple-element.19), channel_id=1, source_target_pairs={{0,8},{4,12},{8,0},{12,4},{1,9},{5,13},{9,1},{13,5},{2,10},{6,14},... | collective-permute-start | bytes 196616 | tf_op jit(solution)/shard_map/ppermute | solution.py:124
  40.1 1.8 %collective-permute-done.13 = bf16[128,256]{1,0:T(8,128)(2,1)S(1)} collective-permute-done((bf16[128,256]{1,0:T(8,128)(2,1)S(1)}, bf16[128,256]{1,0:T(8,128)(2,1)S(1)}, u32[]{:S(2)}, u32[]{:S(2)}) %collective-permute-start.13) | collective-permute-done | bytes 65568 | tf_op jit(solution)/shard_map/ppermute | solution.py:124
  41.9 4.1 %collective-permute-done.12 = bf16[128,256]{1,0:T(8,128)(2,1)S(1)} collective-permute-done((bf16[128,256]{1,0:T(8,128)(2,1)S(1)}, bf16[128,256]{1,0:T(8,128)(2,1)S(1)}, u32[]{:S(2)}, u32[]{:S(2)}) %collective-permute-start.12) | collective-permute-done | bytes 65568 | tf_op jit(solution)/shard_map/ppermute | solution.py:124
  46.0 0.7 %convert_add_fusion.1 = f32[128,256]{1,0:T(8,128)} fusion(bf16[128,256]{1,0:T(8,128)(2,1)S(1)} %collective-permute-done.13, bf16[128,256]{1,0:T(8,128)(2,1)S(1)} %collective-permute-done.12, bf16[128,256]{1,0:T(8,128)(2,1)S(1)} %collective-permute-done.11, bf16[128,256]{1,0:T(8,128)(2,1)S(1)} %collective-permute-done.8, ...), kind=kLoop, calls=%fused_computation.5 | loop fusion | flops 393216 | bytes 655360 | tf_op jit(solution)/shard_map/add | solution.py:202
  (36 shorter events, 2.0 us)
Async XLA Ops:
  0.1 1.1 %copy-start = (bf16[24,16,1024]{2,1,0:T(8,128)(2,1)S(1)}, bf16[24,16,1024]{2,1,0:T(8,128)(2,1)}, u32[]{:S(2)}) copy-start(bf16[24,16,1024]{2,1,0:T(8,128)(2,1)} %param.12) | copy-start | bytes 2359300
  1.2 1.1 %copy-start.2 = (bf16[24,16,1024]{2,1,0:T(8,128)(2,1)S(1)}, bf16[24,16,1024]{2,1,0:T(8,128)(2,1)}, u32[]{:S(2)}) copy-start(bf16[24,16,1024]{2,1,0:T(8,128)(2,1)} %param.13) | copy-start | bytes 2359300
  2.3 0.9 %copy-start.5 = (bf16[4,32,1024]{2,1,0:T(8,128)(2,1)S(1)}, bf16[4,32,1024]{2,1,0:T(8,128)(2,1)}, u32[]{:S(2)}) copy-start(bf16[4,32,1024]{2,1,0:T(8,128)(2,1)} %refs_3_.1) | copy-start | bytes 786436
  3.3 0.7 %copy-start.7 = (s32[24]{0:T(128)S(1)}, s32[24]{0:T(128)}, u32[]{:S(2)}) copy-start(s32[24]{0:T(128)} %refs_1_.4) | copy-start | bytes 292
  4.6 22.4 %copy-start.6 = (bf16[4,32,1024]{2,1,0:T(8,128)(2,1)S(1)}, bf16[4,32,1024]{2,1,0:T(8,128)(2,1)}, u32[]{:S(2)}) copy-start(bf16[4,32,1024]{2,1,0:T(8,128)(2,1)} %refs_3_.1) | copy-start | bytes 786436
  8.2 6.7 %collective-permute-start.9 = (bf16[2,384,256]{2,1,0:T(8,128)(2,1)S(1)}, bf16[2,384,256]{2,1,0:T(8,128)(2,1)S(1)}, u32[]{:S(2)}, u32[]{:S(2)}) collective-permute-start(bf16[2,384,256]{2,1,0:T(8,128)(2,1)S(1)} %get-tuple-element.16), channel_id=1, source_target_pairs={{0,1},{1,0},{2,3},{3,2},{4,5},{5,4},{6,7},{7,6},{8,9},{9,8},{10,11... | collective-permute-start | bytes 1179656 | tf_op jit(solution)/shard_map/ppermute | solution.py:124
  9.6 9.1 %collective-permute-start = (bf16[64,1024]{1,0:T(8,128)(2,1)S(1)}, bf16[64,1024]{1,0:T(8,128)(2,1)S(1)}, u32[]{:S(2)}, u32[]{:S(2)}) collective-permute-start(bf16[64,1024]{1,0:T(8,128)(2,1)S(1)} %constant_dynamic-slice_fusion), channel_id=1, source_target_pairs={{0,4},{4,0},{8,12},{12,8},{1,5},{5,1},{9,13},{13,9},{2,6},{6,2},{1... | collective-permute-start | bytes 393224 | tf_op jit(solution)/shard_map/ppermute | solution.py:124
  12.3 12.9 %collective-permute-start.2 = (bf16[64,1024]{1,0:T(8,128)(2,1)S(1)}, bf16[64,1024]{1,0:T(8,128)(2,1)S(1)}, u32[]{:S(2)}, u32[]{:S(2)}) collective-permute-start(bf16[64,1024]{1,0:T(8,128)(2,1)S(1)} %constant_dynamic-slice_fusion), channel_id=1, source_target_pairs={{0,8},{4,12},{8,0},{12,4},{1,9},{5,13},{9,1},{13,5},{2,10},{6,14},... | collective-permute-start | bytes 393224 | tf_op jit(solution)/shard_map/ppermute | solution.py:124
  14.9 10.3 %collective-permute-start.4 = (bf16[64,1024]{1,0:T(8,128)(2,1)S(1)}, bf16[64,1024]{1,0:T(8,128)(2,1)S(1)}, u32[]{:S(2)}, u32[]{:S(2)}) collective-permute-start(bf16[64,1024]{1,0:T(8,128)(2,1)S(1)} %constant_dynamic-slice_fusion), channel_id=1, source_target_pairs={{0,12},{4,8},{8,4},{12,0},{1,13},{5,9},{9,5},{13,1},{2,14},{6,10},... | collective-permute-start | bytes 393224 | tf_op jit(solution)/shard_map/ppermute | solution.py:124
  14.9 15.4 %copy-start.8 = (s32[24]{0:T(128)S(1)}, s32[24]{0:T(128)}, u32[]{:S(2)}) copy-start(s32[24]{0:T(128)} %refs_1_.4) | copy-start | bytes 292
  14.9 15.4 %copy-start.10 = (s32[24]{0:T(128)S(1)}, s32[24]{0:T(128)}, u32[]{:S(2)}) copy-start(s32[24]{0:T(128)} %refs_2_.4) | copy-start | bytes 292
  15.0 15.3 %copy-start.1 = (bf16[24,16,1024]{2,1,0:T(8,128)(2,1)S(1)}, bf16[24,16,1024]{2,1,0:T(8,128)(2,1)}, u32[]{:S(2)}) copy-start(bf16[24,16,1024]{2,1,0:T(8,128)(2,1)} %param.12) | copy-start | bytes 2359300
  15.0 15.3 %copy-start.3 = (bf16[24,16,1024]{2,1,0:T(8,128)(2,1)S(1)}, bf16[24,16,1024]{2,1,0:T(8,128)(2,1)}, u32[]{:S(2)}) copy-start(bf16[24,16,1024]{2,1,0:T(8,128)(2,1)} %param.13) | copy-start | bytes 2359300
  15.7 18.9 %collective-permute-start.10 = (bf16[384,256]{1,0:T(8,128)(2,1)}, bf16[384,256]{1,0:T(8,128)(2,1)}, u32[]{:S(2)}, u32[]{:S(2)}) collective-permute-start(bf16[384,256]{1,0:T(8,128)(2,1)} %fusion.1), channel_id=1, source_target_pairs={{0,2},{1,3},{2,0},{3,1},{4,6},{5,7},{6,4},{7,5},{8,10},{9,11},{10,... | collective-permute-start | bytes 589832 | tf_op jit(solution)/shard_map/ppermute | solution.py:124
  18.7 11.6 %collective-permute-start.1 = (bf16[64,1024]{1,0:T(8,128)(2,1)S(1)}, bf16[64,1024]{1,0:T(8,128)(2,1)S(1)}, u32[]{:S(2)}, u32[]{:S(2)}) collective-permute-start(bf16[64,1024]{1,0:T(8,128)(2,1)S(1)} %collective-permute-done.refs_6_), channel_id=1, source_target_pairs={{0,1},{1,0},{2,3},{3,2},{4,5},{5,4},{6,7},{7,6},{8,9},{9,8},{10,11... | collective-permute-start | bytes 393224 | tf_op jit(solution)/shard_map/ppermute | solution.py:124
  25.2 5.1 %collective-permute-start.3 = (bf16[64,1024]{1,0:T(8,128)(2,1)S(1)}, bf16[64,1024]{1,0:T(8,128)(2,1)S(1)}, u32[]{:S(2)}, u32[]{:S(2)}) collective-permute-start(bf16[64,1024]{1,0:T(8,128)(2,1)S(1)} %collective-permute-done.2.refs_8_), channel_id=1, source_target_pairs={{0,1},{1,0},{2,3},{3,2},{4,5},{5,4},{6,7},{7,6},{8,9},{9,8},{10,11... | collective-permute-start | bytes 393224 | tf_op jit(solution)/shard_map/ppermute | solution.py:124
  25.2 5.1 %collective-permute-start.5 = (bf16[64,1024]{1,0:T(8,128)(2,1)S(1)}, bf16[64,1024]{1,0:T(8,128)(2,1)S(1)}, u32[]{:S(2)}, u32[]{:S(2)}) collective-permute-start(bf16[64,1024]{1,0:T(8,128)(2,1)S(1)} %collective-permute-done.4.refs_10_), channel_id=1, source_target_pairs={{0,1},{1,0},{2,3},{3,2},{4,5},{5,4},{6,7},{7,6},{8,9},{9,8},{10,11... | collective-permute-start | bytes 393224 | tf_op jit(solution)/shard_map/ppermute | solution.py:124
  27.0 1.6 %copy-start.4 = (bf16[1,1024,1024]{2,1,0:T(8,128)(2,1)S(1)}, bf16[1,1024,1024]{2,1,0:T(8,128)(2,1)}, u32[]{:S(2)}) copy-start(bf16[1,1024,1024]{2,1,0:T(8,128)(2,1)} %refs_4_.1) | copy-start | bytes 6291460
  32.7 6.9 %collective-permute-start.8 = (bf16[128,256]{1,0:T(8,128)(2,1)S(1)}, bf16[128,256]{1,0:T(8,128)(2,1)S(1)}, u32[]{:S(2)}, u32[]{:S(2)}) collective-permute-start(bf16[128,256]{1,0:T(8,128)(2,1)S(1)} %get-tuple-element.14), channel_id=1, source_target_pairs={{0,3},{1,2},{2,1},{3,0},{4,7},{5,6},{6,5},{7,4},{8,11},{9,10},{10,... | collective-permute-start | bytes 196616 | tf_op jit(solution)/shard_map/ppermute | solution.py:124
  33.9 6.2 %collective-permute-start.7 = (bf16[128,256]{1,0:T(8,128)(2,1)S(1)}, bf16[128,256]{1,0:T(8,128)(2,1)S(1)}, u32[]{:S(2)}, u32[]{:S(2)}) collective-permute-start(bf16[128,256]{1,0:T(8,128)(2,1)S(1)} %get-tuple-element.13), channel_id=1, source_target_pairs={{0,2},{1,3},{2,0},{3,1},{4,6},{5,7},{6,4},{7,5},{8,10},{9,11},{10,... | collective-permute-start | bytes 196616 | tf_op jit(solution)/shard_map/ppermute | solution.py:124
  34.4 5.7 %collective-permute-start.6 = (bf16[128,256]{1,0:T(8,128)(2,1)S(1)}, bf16[128,256]{1,0:T(8,128)(2,1)S(1)}, u32[]{:S(2)}, u32[]{:S(2)}) collective-permute-start(bf16[128,256]{1,0:T(8,128)(2,1)S(1)} %get-tuple-element.12), channel_id=1, source_target_pairs={{0,1},{1,0},{2,3},{3,2},{4,5},{5,4},{6,7},{7,6},{8,9},{9,8},{10,11... | collective-permute-start | bytes 196616 | tf_op jit(solution)/shard_map/ppermute | solution.py:124
  35.6 6.2 %collective-permute-start.13 = (bf16[128,256]{1,0:T(8,128)(2,1)S(1)}, bf16[128,256]{1,0:T(8,128)(2,1)S(1)}, u32[]{:S(2)}, u32[]{:S(2)}) collective-permute-start(bf16[128,256]{1,0:T(8,128)(2,1)S(1)} %get-tuple-element.18), channel_id=1, source_target_pairs={{0,12},{4,8},{8,4},{12,0},{1,13},{5,9},{9,5},{13,1},{2,14},{6,10},... | collective-permute-start | bytes 196616 | tf_op jit(solution)/shard_map/ppermute | solution.py:124
  38.2 7.8 %collective-permute-start.12 = (bf16[128,256]{1,0:T(8,128)(2,1)S(1)}, bf16[128,256]{1,0:T(8,128)(2,1)S(1)}, u32[]{:S(2)}, u32[]{:S(2)}) collective-permute-start(bf16[128,256]{1,0:T(8,128)(2,1)S(1)} %get-tuple-element.19), channel_id=1, source_target_pairs={{0,8},{4,12},{8,0},{12,4},{1,9},{5,13},{9,1},{13,5},{2,10},{6,14},... | collective-permute-start | bytes 196616 | tf_op jit(solution)/shard_map/ppermute | solution.py:124
  39.6 6.4 %collective-permute-start.11 = (bf16[128,256]{1,0:T(8,128)(2,1)S(1)}, bf16[128,256]{1,0:T(8,128)(2,1)S(1)}, u32[]{:S(2)}, u32[]{:S(2)}) collective-permute-start(bf16[128,256]{1,0:T(8,128)(2,1)S(1)} %get-tuple-element.17), channel_id=1, source_target_pairs={{0,4},{4,0},{8,12},{12,8},{1,5},{5,1},{9,13},{13,9},{2,6},{6,2},{1... | collective-permute-start | bytes 196616 | tf_op jit(solution)/shard_map/ppermute | solution.py:124
  (1 other events, 0.7 us)

commit v2 on v1

v2 whole, which is shorter than its diff:
```python
import jax
import jax.numpy as jnp
from jax import lax
from jax.experimental import pallas as pl
from jax.experimental.pallas import tpu as pltpu
from jax.sharding import PartitionSpec as P

F32 = jnp.float32
BF16 = jnp.bfloat16
SMEM = pl.BlockSpec(memory_space=pltpu.SMEM)
ANY = pl.BlockSpec(memory_space=pltpu.HBM)
VMEM = pl.BlockSpec(memory_space=pltpu.VMEM)


def dot(a, b):
    return jnp.dot(a, b, preferred_element_type=F32)


def dot_t(a, b):
    return lax.dot_general(a, b, (((1,), (1,)), ((), ())), preferred_element_type=F32)


def params():
    return pltpu.CompilerParams(vmem_limit_bytes=48 * 1024 * 1024)


def each(count, step):
    if count <= 4:
        for i in range(count):
            step(i)
    else:
        lax.fori_loop(0, count, lambda i, c: (step(i), c)[1], 0)


def lane_ids(ids_ref, rank):
    count = ids_ref.shape[0]
    lane = lax.broadcasted_iota(jnp.int32, (1, count * rank), 1) // rank
    out = jnp.full((1, count * rank), -1, jnp.int32)
    for b in range(count):
        out = jnp.where(lane == b, ids_ref[b], out)
    return out


def mirror_kernel(
    clusters, exc, rank, others, rows_hbm, cols_hbm, x_hbm, u_hbm, v_hbm, send_ref, keep_ref, lanes_ref,
    rows_ref, cols_ref, x_ref, u_ref, v_ref, mask_ref, sems,
):
    copies = [
        pltpu.make_async_copy(src, dst, sems.at[i])
        for i, (src, dst) in enumerate(
            [(rows_hbm, rows_ref), (cols_hbm, cols_ref), (x_hbm, x_ref), (u_hbm, u_ref), (v_hbm, v_ref)]
        )
    ]
    for copy in copies:
        copy.start()
    group = lax.axis_index("row")
    half = lax.rem(lax.axis_index("col"), 2)
    width = keep_ref.shape[2]
    copies[0].wait()
    copies[1].wait()
    row_lane = lane_ids(rows_ref, rank)
    col_lane = lane_ids(cols_ref, rank)
    lanes_ref[0:1, :] = row_lane
    lanes_ref[1:2, :] = col_lane
    copies[2].wait()
    copies[3].wait()
    every = dot_t(x_ref[...], u_ref[...])
    coef = jnp.zeros((exc, every.shape[1]), F32)
    for c in range(clusters):
        coef += jnp.where(row_lane == group * clusters + c, every[c * exc : (c + 1) * exc], 0.0)
    coef = coef.astype(BF16).astype(F32)
    span = clusters * exc
    copies[4].wait()

    def one(i):
        other = group ^ (i + 1)
        for c in range(clusters):
            mask_ref[c * exc : (c + 1) * exc, :] = jnp.where(
                col_lane == other * clusters + c, coef, 0.0
            ).astype(BF16)
        rows = pl.ds(i * span if isinstance(i, int) else pl.multiple_of(i * span, span), span)
        for q in range(keep_ref.shape[0]):
            for side in range(2):
                at = (2 * q + side) * width
                part = dot(mask_ref[...], v_ref[:, at : at + width])

                @pl.when(half == side)
                def _():
                    keep_ref[q, rows, :] = part

                @pl.when(half != side)
                def _():
                    send_ref[q, rows, :] = part.astype(BF16)

    each(others, one)


def near_kernel(clusters, exc, rows_ref, cols_ref, x_ref, n_ref, out_ref):
    first = lax.axis_index("row") * clusters
    out_ref[...] = jnp.zeros_like(out_ref)
    for b in range(n_ref.shape[0]):
        row = rows_ref[b] - first
        col = cols_ref[b] - first
        weight = jnp.where(row == col, 0.5, 1.0).astype(F32)
        out_ref[row] += weight * dot_t(x_ref[col], n_ref[b])
        out_ref[col] += weight * dot(x_ref[row], n_ref[b])


def forward_kernel(clusters, exc, others, lanes_ref, u_ref, v_ref, near_ref, *refs):
    count = 2 * others - 1
    pieces = refs[:count]
    own_ref = refs[count]
    sends = refs[count + 1 : -1]
    part_ref = refs[-1]
    group = lax.axis_index("row")
    place = lax.axis_index("col")
    half = lax.rem(place, 2)
    width = own_ref.shape[1]
    row_lane = lanes_ref[0:1, :]
    col_lane = lanes_ref[1:2, :]
    some = clusters // 2
    coef = jnp.zeros((exc, u_ref.shape[0]), F32)
    for n, piece in enumerate(pieces):
        every = dot_t(piece[...], v_ref[...])
        if n == 0:
            first = (group ^ 1) * clusters
        else:
            first = (group ^ (2 + (n - 1) // 2)) * clusters + (half if n % 2 == 1 else 1 - half) * some
        for c in range(piece.shape[0] // exc):
            coef += jnp.where(col_lane == first + c, every[c * exc : (c + 1) * exc], 0.0)
    coef = coef.astype(BF16).astype(F32)
    masked = jnp.concatenate(
        [jnp.where(row_lane == group * clusters + c, coef, 0.0) for c in range(clusters)], axis=0
    ).astype(BF16)
    for q in range(len(sends) + 1):
        cols = slice(q * width, (q + 1) * width)
        part_ref[q] = dot(masked, u_ref[:, cols]) + near_ref[:, cols]
    own_ref[...] = part_ref[place]
    for m in range(1, len(sends) + 1):
        sends[m - 1][...] = part_ref[place ^ m].astype(BF16)


def swap(value, axis, size, step):
    return lax.ppermute(value, axis, [(i, i ^ step) for i in range(size)])


def stage(work):
    shapes = jax.eval_shape(work)
    inside = lax.axis_index("row") < lax.axis_size("row")
    return lax.cond(inside, work, lambda: jax.tree.map(lambda a: jnp.zeros(a.shape, a.dtype), shapes))


def body(charges, near_blocks, near_rows, near_cols, far_u, far_v, far_rows, far_cols):
    clusters, exc, panels = charges.shape
    entries, rank, _ = far_u.shape
    row_count = lax.axis_size("row")
    col_count = lax.axis_size("col")
    others = row_count - 1
    pairs = col_count // 2
    width = panels // col_count
    span = clusters * exc
    some = span // 2
    place = lax.axis_index("col")
    x = charges.reshape(span, panels)
    u = far_u.reshape(entries * rank, panels)
    v = far_v.reshape(entries * rank, panels)

    whole = swap(x, "row", row_count, 1)
    mine = lax.dynamic_slice_in_dim(x, lax.rem(place, 2) * some, some, 0)
    got = [swap(mine, "row", row_count, d) for d in range(2, row_count)]

    def local():
        send, keep, lanes = pl.pallas_call(
            lambda *refs: mirror_kernel(clusters, exc, rank, others, *refs),
            in_specs=[ANY] * 5,
            out_specs=[VMEM] * 3,
            out_shape=[
                jax.ShapeDtypeStruct((pairs, others * span, width), BF16),
                jax.ShapeDtypeStruct((pairs, others * span, width), F32),
                jax.ShapeDtypeStruct((8, entries * rank), jnp.int32),
            ],
            scratch_shapes=[
                pltpu.SMEM(far_rows.shape, jnp.int32),
                pltpu.SMEM(far_cols.shape, jnp.int32),
                pltpu.VMEM(x.shape, BF16),
                pltpu.VMEM(u.shape, BF16),
                pltpu.VMEM(v.shape, BF16),
                pltpu.VMEM((span, entries * rank), BF16),
                pltpu.SemaphoreType.DMA((5,)),
            ],
            compiler_params=params(),
            name="mirror",
        )(far_rows, far_cols, x, u, v)
        from_core = swap(send, "col", col_count, 1)
        pair_sum = keep + from_core.astype(F32)

        def chunk(m):
            return lax.dynamic_index_in_dim(pair_sum, place // 2 ^ m, 0, keepdims=False)

        leaving = [chunk(m).astype(BF16) for m in range(1, pairs)]
        *leaving, x_near = lax.optimization_barrier((*leaving, charges))
        near = pl.pallas_call(
            lambda *refs: near_kernel(clusters, exc, *refs),
            in_specs=[SMEM, SMEM, VMEM, VMEM],
            out_specs=VMEM,
            out_shape=jax.ShapeDtypeStruct((clusters, exc, panels), F32),
            compiler_params=params(),
            name="near",
        )(near_rows, near_cols, x_near, near_blocks).reshape(span, panels)
        mirror = chunk(0)
        for m, part in enumerate(leaving):
            mirror = mirror + swap(part, "col", col_count, 2 * m + 2).astype(F32)
        mirror = mirror.astype(BF16)
        return [mirror[i * span : (i + 1) * span] for i in range(others)], near, lanes

    mirror, near, lanes = stage(local)
    whole, *got, lanes = lax.optimization_barrier((whole, *got, lanes))
    other_half = [swap(piece, "col", col_count, 1) for piece in got]
    from_rows = [swap(part, "row", row_count, i + 1) for i, part in enumerate(mirror)]

    pieces = [whole]
    for a, b in zip(got, other_half):
        pieces += [a, b]

    def forward():
        own, *sends = pl.pallas_call(
            lambda *refs: forward_kernel(clusters, exc, others, *refs),
            in_specs=[VMEM] * (4 + len(pieces)),
            out_specs=[VMEM] * col_count,
            out_shape=[jax.ShapeDtypeStruct((span, width), F32)]
            + [jax.ShapeDtypeStruct((span, width), BF16)] * (col_count - 1),
            scratch_shapes=[pltpu.VMEM((col_count, span, width), F32)],
            compiler_params=params(),
            name="forward",
        )(lanes, u, v, near, *pieces)
        for m in range(1, col_count):
            own = own + swap(sends[m - 1], "col", col_count, m).astype(F32)
        return own

    total = stage(forward)
    for term in from_rows:
        total = total + term.astype(F32)
    return total.reshape(clusters, exc, width)


def solution(mesh):
    placed = (
        P(("parts", "row"), None, None),
        P(("parts", "row", "col"), None, None),
        P(("parts", "row", "col")),
        P(("parts", "row", "col")),
        P(("parts", "row", "col"), None, None),
        P(("parts", "row", "col"), None, None),
        P(("parts", "row", "col")),
        P(("parts", "row", "col")),
    )
    return jax.shard_map(
        body,
        mesh=mesh,
        in_specs=placed,
        out_specs=P(("parts", "row"), None, "col"),
        check_vma=False,
    )
```

time: 47.1 us -> 38.7 us (0.82)
  local copies, waits for them, and re-layouts: 7.77 us -> 1 us
  Pallas kernels: 7.6 us -> 11.4 us
  waiting for transfers between devices: 13.7 us -> 10.7 us
  between operations: 1.46 us -> 0.06 us
  other arithmetic: 1.84 us -> 0.85 us
    unnamed x22 -> x0, local copies, waits for them, and re-layouts: 6.14 us -> none
    pallas_call x3, Pallas kernels: 7.6 us -> 11.4 us  [the longest x1 4.37 us: local(): pl.pallas_call(lambda *refs: mirror_kernel(clusters, exc, rank, others, *...]
    ppermute x14 -> x13, waiting for transfers between devices: 13.7 us -> 10.7 us  [swap(): return lax.ppermute(value, axis, [(i, i ^ step) for i in range(size)])]
    convert_element_type x1, other arithmetic: 0.98 us -> 0.05 us  [local(): mirror = mirror.astype(BF16)]
    convert_element_type x1, local copies, waits for them, and re-layouts: 0.7 us -> 0.03 us  [local(): leaving = [chunk(m).astype(BF16) for m in range(1, pairs)]]
    ppermute x14 -> x13, starting transfers between devices: 14.4 us -> 14.5 us  [swap(): return lax.ppermute(value, axis, [(i, i ^ step) for i in range(size)])]
  transfers between devices with their start and end apart: 14 -> 13, of which waited for: 4 -> 5; matrix products, arithmetic and copies ran while one was open for 6% -> 3% of each run, Pallas kernels for 9% -> 30%
where the time goes in v2:
time: 38.7 us; the launch traced here: 38.5 us
  starting transfers between devices  14.5 us (37%)
  Pallas kernels  11.4 us (29%)
  waiting for transfers between devices  10.7 us (28%)
  local copies, waits for them, and re-layouts  1 us (3%)
  other arithmetic  0.85 us (2%)
    ppermute x13, starting transfers between devices, swap(): return lax.ppermute(value, axis, [(i, i ^ step) for i in range(size)])  14.5 us
    ppermute x13, waiting for transfers between devices, swap(): return lax.ppermute(value, axis, [(i, i ^ step) for i in range(size)])  10.7 us
    pallas_call x1, Pallas kernels, local(): pl.pallas_call(lambda *refs: mirror_kernel(clusters, exc, rank, others, *...  4.37 us
    pallas_call x1, Pallas kernels, local(): pl.pallas_call(lambda *refs: near_kernel(clusters, exc, *refs), in_specs=...  3.89 us
    pallas_call x1, Pallas kernels, forward(): pl.pallas_call(lambda *refs: forward_kernel(clusters, exc, others, *refs)...  3.11 us
    dynamic_slice x1, local copies, waits for them, and re-layouts, body(): mine = lax.dynamic_slice_in_dim(x, lax.rem(place, 2) * some, some, 0)  0.95 us
  transfers between devices with their start and end apart: 13, of which 5 were waited for; matrix products, arithmetic and copies ran while one was open for 3% of the time, Pallas kernels for 30%

profile of v2, /device:TPU:0, one launch (start us, length us, event | category | flops | bytes accessed | tf_op | source)
XLA Modules:
  0.0 38.5 jit_solution(16770684037556134878)
XLA Ops:
  0.0 3.0 %collective-permute-start.5 = (bf16[128,1024]{1,0:T(8,128)(2,1)}, bf16[128,1024]{1,0:T(8,128)(2,1)S(1)}, u32[]{:S(2)}, u32[]{:S(2)}) collective-permute-start(bf16[128,1024]{1,0:T(8,128)(2,1)} %bitcast.16), channel_id=1, source_target_pairs={{0,4},{4,0},{8,12},{12,8},{1,5},{5,1},{9,13},{13,9},{2,6},{6,2},{1... | collective-permute-start | bytes 786440 | tf_op jit(solution)/shard_map/ppermute | solution.py:144
  3.0 0.9 %constant_dynamic-slice_fusion = bf16[64,1024]{1,0:T(8,128)(2,1)S(1)} fusion(bf16[128,1024]{1,0:T(8,128)(2,1)} %bitcast.17, s32[]{:T(128)S(6)} %select_n.16), kind=kLoop, calls=%fused_computation.7 | loop fusion | bytes 262148 | tf_op jit(solution)/shard_map/dynamic_slice | solution.py:169
  4.0 2.7 %collective-permute-start.6 = (bf16[64,1024]{1,0:T(8,128)(2,1)S(1)}, bf16[64,1024]{1,0:T(8,128)(2,1)S(1)}, u32[]{:S(2)}, u32[]{:S(2)}) collective-permute-start(bf16[64,1024]{1,0:T(8,128)(2,1)S(1)} %constant_dynamic-slice_fusion), channel_id=1, source_target_pairs={{0,8},{4,12},{8,0},{12,4},{1,9},{5,13},{9,1},{13,5},{2,10},{6,14},... | collective-permute-start | bytes 393224 | tf_op jit(solution)/shard_map/ppermute | solution.py:144
  6.6 13.4 %conditional.2 = (bf16[128,256]{1,0:T(8,128)(2,1)S(1)}, bf16[128,256]{1,0:T(8,128)(2,1)S(1)}, bf16[128,256]{1,0:T(8,128)(2,1)S(1)}, f32[128,1024]{1,0:T(8,128)S(1)}, s32[8,384]{1,0:T(8,128)S(1)}) conditional(s32[]{:T(128)} %convert_element_type.37, () %tuple.22, (s32[24]{0:T(128)}, s32[24]{0:T(128)}, bf16[128,1024]{1,0:T(8,128)(2,1)}, ...), branch_computations={%region_0.0_spmd, %region_1.2_spmd} | conditional | flops 688150 | bytes 6947202 | solution.py:150
  6.6 4.4 %mirror.1 = (bf16[2,384,256]{2,1,0:T(8,128)(2,1)S(1)}, f32[2,384,256]{2,1,0:T(8,128)S(1)}, s32[8,384]{1,0:T(8,128)S(1)}) custom-call(s32[24]{0:T(128)} %get-tuple-element.97.refs_0_, s32[24]{0:T(128)} %get-tuple-element.98.refs_1_, bf16[128,1024]{1,0:T(8,128)(2,1)} %bitcast.19, bf16[384,1024]{1,0:T(8,128)(2,1)} %get-tuple-element.49.refs_3_, ...), custom_call_target="tpu_custom_call" | custom-call | tf_op jit(solution)/shard_map/cond/branch_1_fun/mirror/pallas_call | solution.py:173
  11.0 0.1 collective-permute-start.3
  11.1 1.7 %collective-permute-done.3 = bf16[2,384,256]{2,1,0:T(8,128)(2,1)S(1)} collective-permute-done((bf16[2,384,256]{2,1,0:T(8,128)(2,1)S(1)}, bf16[2,384,256]{2,1,0:T(8,128)(2,1)S(1)}, u32[]{:S(2)}, u32[]{:S(2)}) %collective-permute-start.3) | collective-permute-done | bytes 393248 | tf_op jit(solution)/shard_map/cond/branch_1_fun/ppermute | solution.py:144
  12.8 0.1 convert_add_fusion
  12.9 1.8 %collective-permute-start.4 = (bf16[384,256]{1,0:T(8,128)(2,1)S(1)}, bf16[384,256]{1,0:T(8,128)(2,1)S(1)}, u32[]{:S(2)}, u32[]{:S(2)}) collective-permute-start(bf16[384,256]{1,0:T(8,128)(2,1)S(1)} %fusion.1), channel_id=1, source_target_pairs={{0,2},{1,3},{2,0},{3,1},{4,6},{5,7},{6,4},{7,5},{8,10},{9,11},{10,... | collective-permute-start | bytes 589832 | tf_op jit(solution)/shard_map/cond/branch_1_fun/ppermute | solution.py:144
  14.7 3.9 %near.1 = f32[4,32,1024]{2,1,0:T(8,128)S(1)} custom-call(s32[1]{0:T(128)} %get-tuple-element.99.refs_0_, s32[1]{0:T(128)} %get-tuple-element.100.refs_1_, bf16[4,32,1024]{2,1,0:T(8,128)(2,1)S(1)} %copy-done, bf16[1,1024,1024]{2,1,0:T(8,128)(2,1)} %get-tuple-element.101.refs_3_), custom_call_target="tpu_custom_call" | custom-call | tf_op jit(solution)/shard_map/cond/branch_1_fun/near/pallas_call | solution.py:202
  18.6 1.3 %collective-permute-done.4 = bf16[384,256]{1,0:T(8,128)(2,1)S(1)} collective-permute-done((bf16[384,256]{1,0:T(8,128)(2,1)S(1)}, bf16[384,256]{1,0:T(8,128)(2,1)S(1)}, u32[]{:S(2)}, u32[]{:S(2)}) %collective-permute-start.4) | collective-permute-done | bytes 196640 | tf_op jit(solution)/shard_map/cond/branch_1_fun/ppermute | solution.py:144
  20.0 0.1 collective-permute-start.8
  20.1 0.5 %collective-permute-start.9 = (bf16[64,1024]{1,0:T(8,128)(2,1)S(1)}, bf16[64,1024]{1,0:T(8,128)(2,1)S(1)}, u32[]{:S(2)}, u32[]{:S(2)}) collective-permute-start(bf16[64,1024]{1,0:T(8,128)(2,1)S(1)} %collective-permute-done.7), channel_id=1, source_target_pairs={{0,1},{1,0},{2,3},{3,2},{4,5},{5,4},{6,7},{7,6},{8,9},{9,8},{10,11... | collective-permute-start | bytes 393224 | tf_op jit(solution)/shard_map/ppermute | solution.py:144
  20.6 3.8 %collective-permute-start.12 = (bf16[128,256]{1,0:T(8,128)(2,1)S(1)}, bf16[128,256]{1,0:T(8,128)(2,1)S(1)}, u32[]{:S(2)}, u32[]{:S(2)}) collective-permute-start(bf16[128,256]{1,0:T(8,128)(2,1)S(1)} %get-tuple-element.91), channel_id=1, source_target_pairs={{0,12},{4,8},{8,4},{12,0},{1,13},{5,9},{9,5},{13,1},{2,14},{6,10},... | collective-permute-start | bytes 196616 | tf_op jit(solution)/shard_map/ppermute | solution.py:144
  24.4 9.0 %conditional.3 = (f32[128,256]{1,0:T(8,128)S(1)}) conditional(s32[]{:T(128)} %convert_element_type.37, () %tuple.21, (s32[8,384]{1,0:T(8,128)S(1)}, bf16[384,1024]{1,0:T(8,128)(2,1)}, bf16[384,1024]{1,0:T(8,128)(2,1)}, f32[128,1024]{1,0:T(8,128)S(1)}, bf16[128,1024]{1,0:T(8,128)(2,1)S(1)}, /*index=5*/bf16[64,1024]{1,0:T(8,128)(2,1)S(1)}, ...), branch_computations={%region_2.3_spmd, %region_3.4_spmd} | conditional | flops 196608 | bytes 1245312 | solution.py:150
  24.5 3.1 %forward.1 = (f32[128,256]{1,0:T(8,128)S(1)}, bf16[128,256]{1,0:T(8,128)(2,1)S(1)}, bf16[128,256]{1,0:T(8,128)(2,1)S(1)}, bf16[128,256]{1,0:T(8,128)(2,1)S(1)}) custom-call(s32[8,384]{1,0:T(8,128)S(1)} %get-tuple-element.61.refs_0_, bf16[384,1024]{1,0:T(8,128)(2,1)} %get-tuple-element.62.refs_1_, bf16[384,1024]{1,0:T(8,128)(2,1)} %get-tuple-element.63.refs_2_, ...), custom_call_target="tpu_custom_call" | custom-call | tf_op jit(solution)/shard_map/cond/branch_1_fun/forward/pallas_call | solution.py:226
  27.6 1.0 %collective-permute-start.2 = (bf16[128,256]{1,0:T(8,128)(2,1)S(1)}, bf16[128,256]{1,0:T(8,128)(2,1)S(1)}, u32[]{:S(2)}, u32[]{:S(2)}) collective-permute-start(bf16[128,256]{1,0:T(8,128)(2,1)S(1)} %get-tuple-element.73), channel_id=1, source_target_pairs={{0,3},{1,2},{2,1},{3,0},{4,7},{5,6},{6,5},{7,4},{8,11},{9,10},{10,... | collective-permute-start | bytes 196616 | tf_op jit(solution)/shard_map/cond/branch_1_fun/ppermute | solution.py:144
  28.6 0.7 %collective-permute-start.1 = (bf16[128,256]{1,0:T(8,128)(2,1)S(1)}, bf16[128,256]{1,0:T(8,128)(2,1)S(1)}, u32[]{:S(2)}, u32[]{:S(2)}) collective-permute-start(bf16[128,256]{1,0:T(8,128)(2,1)S(1)} %get-tuple-element.72), channel_id=1, source_target_pairs={{0,2},{1,3},{2,0},{3,1},{4,6},{5,7},{6,4},{7,5},{8,10},{9,11},{10,... | collective-permute-start | bytes 196616 | tf_op jit(solution)/shard_map/cond/branch_1_fun/ppermute | solution.py:144
  29.2 0.3 collective-permute-start
  29.5 2.5 %collective-permute-done.2 = bf16[128,256]{1,0:T(8,128)(2,1)S(1)} collective-permute-done((bf16[128,256]{1,0:T(8,128)(2,1)S(1)}, bf16[128,256]{1,0:T(8,128)(2,1)S(1)}, u32[]{:S(2)}, u32[]{:S(2)}) %collective-permute-start.2) | collective-permute-done | bytes 65568 | tf_op jit(solution)/shard_map/cond/branch_1_fun/ppermute | solution.py:144
  32.0 1.4 %collective-permute-done.1 = bf16[128,256]{1,0:T(8,128)(2,1)S(1)} collective-permute-done((bf16[128,256]{1,0:T(8,128)(2,1)S(1)}, bf16[128,256]{1,0:T(8,128)(2,1)S(1)}, u32[]{:S(2)}, u32[]{:S(2)}) %collective-permute-start.1) | collective-permute-done | bytes 65568 | tf_op jit(solution)/shard_map/cond/branch_1_fun/ppermute | solution.py:144
  33.5 0.6 %collective-permute-start.10 = (bf16[128,256]{1,0:T(8,128)(2,1)S(1)}, bf16[128,256]{1,0:T(8,128)(2,1)S(1)}, u32[]{:S(2)}, u32[]{:S(2)}) collective-permute-start(bf16[128,256]{1,0:T(8,128)(2,1)S(1)} %get-tuple-element.89), channel_id=1, source_target_pairs={{0,4},{4,0},{8,12},{12,8},{1,5},{5,1},{9,13},{13,9},{2,6},{6,2},{1... | collective-permute-start | bytes 196616 | tf_op jit(solution)/shard_map/ppermute | solution.py:144
  34.1 3.7 %collective-permute-done.10 = bf16[128,256]{1,0:T(8,128)(2,1)S(1)} collective-permute-done((bf16[128,256]{1,0:T(8,128)(2,1)S(1)}, bf16[128,256]{1,0:T(8,128)(2,1)S(1)}, u32[]{:S(2)}, u32[]{:S(2)}) %collective-permute-start.10) | collective-permute-done | bytes 65568 | tf_op jit(solution)/shard_map/ppermute | solution.py:144
  37.8 0.7 %convert_add_fusion.2 = f32[128,256]{1,0:T(8,128)} fusion(bf16[128,256]{1,0:T(8,128)(2,1)S(1)} %collective-permute-done.12, bf16[128,256]{1,0:T(8,128)(2,1)S(1)} %collective-permute-done.11, f32[128,256]{1,0:T(8,128)S(1)} %get-tuple-element.115, bf16[128,256]{1,0:T(8,128)(2,1)S(1)} %collective-permute-done.10), kind=kLoop, calls=%fused_computation.6 | loop fusion | flops 196608 | bytes 458752 | tf_op jit(solution)/shard_map/add | solution.py:242
  (16 shorter events, 0.2 us)
Async XLA Ops:
  0.0 20.0 %collective-permute-start.5 = (bf16[128,1024]{1,0:T(8,128)(2,1)}, bf16[128,1024]{1,0:T(8,128)(2,1)S(1)}, u32[]{:S(2)}, u32[]{:S(2)}) collective-permute-start(bf16[128,1024]{1,0:T(8,128)(2,1)} %bitcast.16), channel_id=1, source_target_pairs={{0,4},{4,0},{8,12},{12,8},{1,5},{5,1},{9,13},{13,9},{2,6},{6,2},{1... | collective-permute-start | bytes 786440 | tf_op jit(solution)/shard_map/ppermute | solution.py:144
  4.0 16.0 %collective-permute-start.6 = (bf16[64,1024]{1,0:T(8,128)(2,1)S(1)}, bf16[64,1024]{1,0:T(8,128)(2,1)S(1)}, u32[]{:S(2)}, u32[]{:S(2)}) collective-permute-start(bf16[64,1024]{1,0:T(8,128)(2,1)S(1)} %constant_dynamic-slice_fusion), channel_id=1, source_target_pairs={{0,8},{4,12},{8,0},{12,4},{1,9},{5,13},{9,1},{13,5},{2,10},{6,14},... | collective-permute-start | bytes 393224 | tf_op jit(solution)/shard_map/ppermute | solution.py:144
  6.6 13.4 %collective-permute-start.7 = (bf16[64,1024]{1,0:T(8,128)(2,1)S(1)}, bf16[64,1024]{1,0:T(8,128)(2,1)S(1)}, u32[]{:S(2)}, u32[]{:S(2)}) collective-permute-start(bf16[64,1024]{1,0:T(8,128)(2,1)S(1)} %constant_dynamic-slice_fusion), channel_id=1, source_target_pairs={{0,12},{4,8},{8,4},{12,0},{1,13},{5,9},{9,5},{13,1},{2,14},{6,10},... | collective-permute-start | bytes 393224 | tf_op jit(solution)/shard_map/ppermute | solution.py:144
  6.6 8.1 %copy-start = (bf16[4,32,1024]{2,1,0:T(8,128)(2,1)S(1)}, bf16[4,32,1024]{2,1,0:T(8,128)(2,1)}, u32[]{:S(2)}) copy-start(bf16[4,32,1024]{2,1,0:T(8,128)(2,1)} %get-tuple-element.58.refs_2_) | copy-start | bytes 786436 | tf_op jit(solution)/shard_map/cond
  11.0 1.8 %collective-permute-start.3 = (bf16[2,384,256]{2,1,0:T(8,128)(2,1)S(1)}, bf16[2,384,256]{2,1,0:T(8,128)(2,1)S(1)}, u32[]{:S(2)}, u32[]{:S(2)}) collective-permute-start(bf16[2,384,256]{2,1,0:T(8,128)(2,1)S(1)} %get-tuple-element.52), channel_id=1, source_target_pairs={{0,1},{1,0},{2,3},{3,2},{4,5},{5,4},{6,7},{7,6},{8,9},{9,8},{10,11... | collective-permute-start | bytes 1179656 | tf_op jit(solution)/shard_map/cond/branch_1_fun/ppermute | solution.py:144
  12.9 7.0 %collective-permute-start.4 = (bf16[384,256]{1,0:T(8,128)(2,1)S(1)}, bf16[384,256]{1,0:T(8,128)(2,1)S(1)}, u32[]{:S(2)}, u32[]{:S(2)}) collective-permute-start(bf16[384,256]{1,0:T(8,128)(2,1)S(1)} %fusion.1), channel_id=1, source_target_pairs={{0,2},{1,3},{2,0},{3,1},{4,6},{5,7},{6,4},{7,5},{8,10},{9,11},{10,... | collective-permute-start | bytes 589832 | tf_op jit(solution)/shard_map/cond/branch_1_fun/ppermute | solution.py:144
  20.0 4.4 %collective-permute-start.8 = (bf16[64,1024]{1,0:T(8,128)(2,1)S(1)}, bf16[64,1024]{1,0:T(8,128)(2,1)S(1)}, u32[]{:S(2)}, u32[]{:S(2)}) collective-permute-start(bf16[64,1024]{1,0:T(8,128)(2,1)S(1)} %collective-permute-done.6), channel_id=1, source_target_pairs={{0,1},{1,0},{2,3},{3,2},{4,5},{5,4},{6,7},{7,6},{8,9},{9,8},{10,11... | collective-permute-start | bytes 393224 | tf_op jit(solution)/shard_map/ppermute | solution.py:144
  20.1 4.3 %collective-permute-start.9 = (bf16[64,1024]{1,0:T(8,128)(2,1)S(1)}, bf16[64,1024]{1,0:T(8,128)(2,1)S(1)}, u32[]{:S(2)}, u32[]{:S(2)}) collective-permute-start(bf16[64,1024]{1,0:T(8,128)(2,1)S(1)} %collective-permute-done.7), channel_id=1, source_target_pairs={{0,1},{1,0},{2,3},{3,2},{4,5},{5,4},{6,7},{7,6},{8,9},{9,8},{10,11... | collective-permute-start | bytes 393224 | tf_op jit(solution)/shard_map/ppermute | solution.py:144
  20.6 13.5 %collective-permute-start.12 = (bf16[128,256]{1,0:T(8,128)(2,1)S(1)}, bf16[128,256]{1,0:T(8,128)(2,1)S(1)}, u32[]{:S(2)}, u32[]{:S(2)}) collective-permute-start(bf16[128,256]{1,0:T(8,128)(2,1)S(1)} %get-tuple-element.91), channel_id=1, source_target_pairs={{0,12},{4,8},{8,4},{12,0},{1,13},{5,9},{9,5},{13,1},{2,14},{6,10},... | collective-permute-start | bytes 196616 | tf_op jit(solution)/shard_map/ppermute | solution.py:144
  24.4 9.7 %collective-permute-start.11 = (bf16[128,256]{1,0:T(8,128)(2,1)S(1)}, bf16[128,256]{1,0:T(8,128)(2,1)S(1)}, u32[]{:S(2)}, u32[]{:S(2)}) collective-permute-start(bf16[128,256]{1,0:T(8,128)(2,1)S(1)} %get-tuple-element.90), channel_id=1, source_target_pairs={{0,8},{4,12},{8,0},{12,4},{1,9},{5,13},{9,1},{13,5},{2,10},{6,14},... | collective-permute-start | bytes 196616 | tf_op jit(solution)/shard_map/ppermute | solution.py:144
  27.6 4.4 %collective-permute-start.2 = (bf16[128,256]{1,0:T(8,128)(2,1)S(1)}, bf16[128,256]{1,0:T(8,128)(2,1)S(1)}, u32[]{:S(2)}, u32[]{:S(2)}) collective-permute-start(bf16[128,256]{1,0:T(8,128)(2,1)S(1)} %get-tuple-element.73), channel_id=1, source_target_pairs={{0,3},{1,2},{2,1},{3,0},{4,7},{5,6},{6,5},{7,4},{8,11},{9,10},{10,... | collective-permute-start | bytes 196616 | tf_op jit(solution)/shard_map/cond/branch_1_fun/ppermute | solution.py:144
  28.6 4.9 %collective-permute-start.1 = (bf16[128,256]{1,0:T(8,128)(2,1)S(1)}, bf16[128,256]{1,0:T(8,128)(2,1)S(1)}, u32[]{:S(2)}, u32[]{:S(2)}) collective-permute-start(bf16[128,256]{1,0:T(8,128)(2,1)S(1)} %get-tuple-element.72), channel_id=1, source_target_pairs={{0,2},{1,3},{2,0},{3,1},{4,6},{5,7},{6,4},{7,5},{8,10},{9,11},{10,... | collective-permute-start | bytes 196616 | tf_op jit(solution)/shard_map/cond/branch_1_fun/ppermute | solution.py:144
  29.2 4.2 %collective-permute-start = (bf16[128,256]{1,0:T(8,128)(2,1)S(1)}, bf16[128,256]{1,0:T(8,128)(2,1)S(1)}, u32[]{:S(2)}, u32[]{:S(2)}) collective-permute-start(bf16[128,256]{1,0:T(8,128)(2,1)S(1)} %get-tuple-element.71), channel_id=1, source_target_pairs={{0,1},{1,0},{2,3},{3,2},{4,5},{5,4},{6,7},{7,6},{8,9},{9,8},{10,11... | collective-permute-start | bytes 196616 | tf_op jit(solution)/shard_map/cond/branch_1_fun/ppermute | solution.py:144
  33.5 4.3 %collective-permute-start.10 = (bf16[128,256]{1,0:T(8,128)(2,1)S(1)}, bf16[128,256]{1,0:T(8,128)(2,1)S(1)}, u32[]{:S(2)}, u32[]{:S(2)}) collective-permute-start(bf16[128,256]{1,0:T(8,128)(2,1)S(1)} %get-tuple-element.89), channel_id=1, source_target_pairs={{0,4},{4,0},{8,12},{12,8},{1,5},{5,1},{9,13},{13,9},{2,6},{6,2},{1... | collective-permute-start | bytes 196616 | tf_op jit(solution)/shard_map/ppermute | solution.py:144

commit v3 on v2

v3 whole, which is shorter than its diff:
```python
import jax
import jax.numpy as jnp
from jax import lax
from jax.experimental import pallas as pl
from jax.experimental.pallas import tpu as pltpu
from jax.sharding import PartitionSpec as P

F32 = jnp.float32
BF16 = jnp.bfloat16
SMEM = pl.BlockSpec(memory_space=pltpu.SMEM)
ANY = pl.BlockSpec(memory_space=pltpu.HBM)
VMEM = pl.BlockSpec(memory_space=pltpu.VMEM)


def dot(a, b):
    return jnp.dot(a, b, preferred_element_type=F32)


def dot_t(a, b):
    return lax.dot_general(a, b, (((1,), (1,)), ((), ())), preferred_element_type=F32)


def params():
    return pltpu.CompilerParams(vmem_limit_bytes=48 * 1024 * 1024)


def each(count, step):
    if count <= 4:
        for i in range(count):
            step(i)
    else:
        lax.fori_loop(0, count, lambda i, c: (step(i), c)[1], 0)


def lane_ids(ids_ref, rank):
    count = ids_ref.shape[0]
    lane = lax.broadcasted_iota(jnp.int32, (1, count * rank), 1) // rank
    out = jnp.full((1, count * rank), -1, jnp.int32)
    for b in range(count):
        out = jnp.where(lane == b, ids_ref[b], out)
    return out


def split_columns(half, keep_ref, send_ref, rows, product):
    width = keep_ref.shape[2]
    for q in range(keep_ref.shape[0]):
        for side in range(2):
            at = (2 * q + side) * width
            part = product(slice(at, at + width))

            @pl.when(half == side)
            def _():
                keep_ref[q, rows, :] = part

            @pl.when(half != side)
            def _():
                send_ref[q, rows, :] = part.astype(BF16)


def mirror_kernel(
    clusters, exc, rank, others, rows_hbm, cols_hbm, x_hbm, u_hbm, v_hbm,
    send_ref, keep_ref, lanes_ref, u_ref, v_ref,
    rows_ref, cols_ref, x_ref, mask_ref, sems,
):
    copies = [
        pltpu.make_async_copy(src, dst, sems.at[i])
        for i, (src, dst) in enumerate(
            [(rows_hbm, rows_ref), (cols_hbm, cols_ref), (x_hbm, x_ref), (u_hbm, u_ref), (v_hbm, v_ref)]
        )
    ]
    for copy in copies:
        copy.start()
    group = lax.axis_index("row")
    half = lax.rem(lax.axis_index("col"), 2)
    copies[0].wait()
    copies[1].wait()
    row_lane = lane_ids(rows_ref, rank)
    col_lane = lane_ids(cols_ref, rank)
    lanes_ref[0:1, :] = row_lane
    lanes_ref[1:2, :] = col_lane
    copies[2].wait()
    copies[3].wait()
    every = dot_t(x_ref[...], u_ref[...])
    coef = jnp.zeros((exc, every.shape[1]), F32)
    for c in range(clusters):
        coef += jnp.where(row_lane == group * clusters + c, every[c * exc : (c + 1) * exc], 0.0)
    coef = coef.astype(BF16).astype(F32)
    span = clusters * exc
    copies[4].wait()
    batch = mask_ref.shape[0] // span

    def one(step):
        for i in range(batch):
            other = group ^ (step * batch + i + 1)
            for c in range(clusters):
                at = (i * clusters + c) * exc
                mask_ref[at : at + exc, :] = jnp.where(
                    col_lane == other * clusters + c, coef, 0.0
                ).astype(BF16)
        size = batch * span
        rows = pl.ds(step * size if isinstance(step, int) else pl.multiple_of(step * size, size), size)
        split_columns(half, keep_ref, send_ref, rows, lambda cols: dot(mask_ref[...], v_ref[:, cols]))

    each(others // batch, one)


def near_kernel(clusters, exc, rows_ref, cols_ref, x_ref, n_ref, out_ref):
    first = lax.axis_index("row") * clusters
    out_ref[...] = jnp.zeros_like(out_ref)
    for b in range(n_ref.shape[0]):
        row = rows_ref[b] - first
        col = cols_ref[b] - first
        weight = jnp.where(row == col, 0.5, 1.0).astype(F32)
        out_ref[row] += weight * dot_t(x_ref[col], n_ref[b])
        out_ref[col] += weight * dot(x_ref[row], n_ref[b])


def forward_kernel(clusters, exc, others, lanes_ref, u_ref, v_ref, near_ref, *refs):
    pieces = refs[:others]
    send_ref, keep_ref = refs[others:]
    group = lax.axis_index("row")
    half = lax.rem(lax.axis_index("col"), 2)
    row_lane = lanes_ref[0:1, :]
    col_lane = lanes_ref[1:2, :]
    coef = jnp.zeros((exc, u_ref.shape[0]), F32)
    batch = others if others <= 4 else 1
    for n in range(0, others, batch):
        every = dot_t(jnp.concatenate([p[...] for p in pieces[n : n + batch]], axis=0), v_ref[...])
        for i in range(batch):
            away = n + i + 1
            if away > 1:
                away = away + half if away % 2 == 0 else away - half
            first = (group ^ away) * clusters
            for c in range(clusters):
                at = (i * clusters + c) * exc
                coef += jnp.where(col_lane == first + c, every[at : at + exc], 0.0)
    coef = coef.astype(BF16).astype(F32)
    masked = jnp.concatenate(
        [jnp.where(row_lane == group * clusters + c, coef, 0.0) for c in range(clusters)], axis=0
    ).astype(BF16)
    rows = slice(None)
    split_columns(
        half, keep_ref, send_ref, rows, lambda cols: dot(masked, u_ref[:, cols]) + near_ref[:, cols]
    )


def swap(value, axis, size, step):
    return lax.ppermute(value, axis, [(i, i ^ step) for i in range(size)])


def stage(work):
    shapes = jax.eval_shape(work)
    inside = lax.axis_index("row") < lax.axis_size("row")
    return lax.cond(inside, work, lambda: jax.tree.map(lambda a: jnp.zeros(a.shape, a.dtype), shapes))


def body(charges, near_blocks, near_rows, near_cols, far_u, far_v, far_rows, far_cols):
    clusters, exc, panels = charges.shape
    entries, rank, _ = far_u.shape
    row_count = lax.axis_size("row")
    col_count = lax.axis_size("col")
    others = row_count - 1
    pairs = col_count // 2
    width = panels // col_count
    span = clusters * exc
    batch = others if others <= 4 else 1
    place = lax.axis_index("col")
    x = charges.reshape(span, panels)
    u = far_u.reshape(entries * rank, panels)
    v = far_v.reshape(entries * rank, panels)

    def shares(count):
        return [
            jax.ShapeDtypeStruct((pairs, count * span, width), BF16),
            jax.ShapeDtypeStruct((pairs, count * span, width), F32),
        ]

    def pair_sum(send, keep):
        total = keep + swap(send, "col", col_count, 1).astype(F32)

        def chunk(m):
            return lax.dynamic_index_in_dim(total, place // 2 ^ m, 0, keepdims=False)

        return chunk(0), [chunk(m).astype(BF16) for m in range(1, pairs)]

    def col_sum(total, leaving):
        for m, part in enumerate(leaving):
            total = total + swap(part, "col", col_count, 2 * m + 2).astype(F32)
        return total

    whole = swap(x, "row", row_count, 1)
    got = []
    for d in range(2, row_count, 2):
        perm = [
            (r * col_count + c, (r ^ (d + c % 2)) * col_count + c)
            for r in range(row_count)
            for c in range(col_count)
        ]
        got.append(lax.ppermute(x, ("row", "col"), perm))

    def local():
        send, keep, lanes, u_held, v_held = pl.pallas_call(
            lambda *refs: mirror_kernel(clusters, exc, rank, others, *refs),
            in_specs=[ANY] * 5,
            out_specs=[VMEM] * 5,
            out_shape=shares(others)
            + [
                jax.ShapeDtypeStruct((8, entries * rank), jnp.int32),
                jax.ShapeDtypeStruct(u.shape, BF16),
                jax.ShapeDtypeStruct(v.shape, BF16),
            ],
            scratch_shapes=[
                pltpu.SMEM(far_rows.shape, jnp.int32),
                pltpu.SMEM(far_cols.shape, jnp.int32),
                pltpu.VMEM(x.shape, BF16),
                pltpu.VMEM((batch * span, entries * rank), BF16),
                pltpu.SemaphoreType.DMA((5,)),
            ],
            compiler_params=params(),
            cost_estimate=pl.CostEstimate(flops=1024, bytes_accessed=1024, transcendentals=0),
            name="mirror",
        )(far_rows, far_cols, x, u, v)
        mirror, leaving = pair_sum(send, keep)
        *leaving, x_near = lax.optimization_barrier((*leaving, charges))
        near = pl.pallas_call(
            lambda *refs: near_kernel(clusters, exc, *refs),
            in_specs=[SMEM, SMEM, VMEM, VMEM],
            out_specs=VMEM,
            out_shape=jax.ShapeDtypeStruct((clusters, exc, panels), F32),
            compiler_params=params(),
            cost_estimate=pl.CostEstimate(flops=1024, bytes_accessed=1024, transcendentals=0),
            name="near",
        )(near_rows, near_cols, x_near, near_blocks).reshape(span, panels)
        mirror = col_sum(mirror, leaving).astype(BF16)
        return [mirror[i * span : (i + 1) * span] for i in range(others)], near, lanes, u_held, v_held

    mirror, near, lanes, u_held, v_held = stage(local)
    whole, *got, lanes = lax.optimization_barrier((whole, *got, lanes))
    pieces = [whole]
    for piece in got:
        pieces += [piece, swap(piece, "col", col_count, 1)]
    from_rows = [swap(part, "row", row_count, i + 1) for i, part in enumerate(mirror)]

    def forward():
        send, keep = pl.pallas_call(
            lambda *refs: forward_kernel(clusters, exc, others, *refs),
            in_specs=[VMEM] * (4 + others),
            out_specs=[VMEM] * 2,
            out_shape=shares(1),
            compiler_params=params(),
            cost_estimate=pl.CostEstimate(flops=1024, bytes_accessed=1024, transcendentals=0),
            name="forward",
        )(lanes, u_held, v_held, near, *pieces)
        return col_sum(*pair_sum(send, keep))

    total = stage(forward)
    for term in from_rows:
        total = total + term.astype(F32)
    return total.reshape(clusters, exc, width)


def solution(mesh):
    placed = (
        P(("parts", "row"), None, None),
        P(("parts", "row", "col"), None, None),
        P(("parts", "row", "col")),
        P(("parts", "row", "col")),
        P(("parts", "row", "col"), None, None),
        P(("parts", "row", "col"), None, None),
        P(("parts", "row", "col")),
        P(("parts", "row", "col")),
    )
    return jax.shard_map(
        body,
        mesh=mesh,
        in_specs=placed,
        out_specs=P(("parts", "row"), None, "col"),
        check_vma=False,
    )
```

time: 38.7 us -> 34 us (0.88)
  waiting for transfers between devices: 10.7 us -> 6.47 us
  starting transfers between devices: 14.5 us -> 13.3 us
  other arithmetic: 0.85 us -> 1.85 us
  Pallas kernels: 11.4 us -> 10.5 us
  local copies, waits for them, and re-layouts: 1 us -> 1.45 us
    ppermute x13 -> x9, waiting for transfers between devices: 10.7 us -> 6.47 us  [swap(): return lax.ppermute(value, axis, [(i, i ^ step) for i in range(size)])]
    ppermute x13 -> x9, starting transfers between devices: 14.5 us -> 10.7 us  [swap(): return lax.ppermute(value, axis, [(i, i ^ step) for i in range(size)])]
    ppermute x0 -> x1, starting transfers between devices: none -> 2.59 us  [body(): got.append(lax.ppermute(x, ('row', 'col'), perm))]
    pallas_call x1, Pallas kernels: 4.37 us -> 3.14 us  [local(): pl.pallas_call(lambda *refs: mirror_kernel(clusters, exc, rank, others, *...]
    add x2 -> x3, other arithmetic: 0.11 us -> 1.11 us  [the longest x2 1.1 us: pair_sum(): total = keep + swap(send, 'col', col_count, 1).astype(F32)]
    dynamic_slice x1 -> x0, local copies, waits for them, and re-layouts: 0.95 us -> none  [body(): mine = lax.dynamic_slice_in_dim(x, lax.rem(place, 2) * some, some, 0)]
    pallas_call x1, Pallas kernels: 3.89 us -> 4.77 us  [local(): pl.pallas_call(lambda *refs: near_kernel(clusters, exc, *refs), in_specs=...]
    cond x2 -> x4, local copies, waits for them, and re-layouts: 0.01 us -> 0.76 us
  transfers between devices with their start and end apart: 13 -> 10, of which waited for: 5 -> 4; matrix products, arithmetic and copies ran while one was open for 3% -> 5% of each run, Pallas kernels for 30% -> 31%
where the time goes in v3:
time: 34 us; the launch traced here: 33.8 us
  starting transfers between devices  13.3 us (39%)
  Pallas kernels  10.5 us (31%)
  waiting for transfers between devices  6.47 us (19%)
  other arithmetic  1.85 us (5%)
  local copies, waits for them, and re-layouts  1.45 us (4%)
    ppermute x9, starting transfers between devices, swap(): return lax.ppermute(value, axis, [(i, i ^ step) for i in range(size)])  10.7 us
    ppermute x9, waiting for transfers between devices, swap(): return lax.ppermute(value, axis, [(i, i ^ step) for i in range(size)])  6.47 us
    pallas_call x1, Pallas kernels, local(): pl.pallas_call(lambda *refs: near_kernel(clusters, exc, *refs), in_specs=...  4.77 us
    pallas_call x1, Pallas kernels, local(): pl.pallas_call(lambda *refs: mirror_kernel(clusters, exc, rank, others, *...  3.14 us
    pallas_call x1, Pallas kernels, forward(): pl.pallas_call(lambda *refs: forward_kernel(clusters, exc, others, *refs)...  2.61 us
    ppermute x1, starting transfers between devices, body(): got.append(lax.ppermute(x, ('row', 'col'), perm))  2.59 us
    add x2, other arithmetic, pair_sum(): total = keep + swap(send, 'col', col_count, 1).astype(F32)  1.1 us
    cond x4, local copies, waits for them, and re-layouts  0.76 us
  transfers between devices with their start and end apart: 10, of which 4 were waited for; matrix products, arithmetic and copies ran while one was open for 5% of the time, Pallas kernels for 31%

profile of v3, /device:TPU:0, one launch (start us, length us, event | category | flops | bytes accessed | tf_op | source)
XLA Modules:
  0.0 33.8 jit_solution(15003687709283736088)
XLA Ops:
  0.0 3.0 %collective-permute-start.4 = (bf16[128,1024]{1,0:T(8,128)(2,1)}, bf16[128,1024]{1,0:T(8,128)(2,1)}, u32[]{:S(2)}, u32[]{:S(2)}) collective-permute-start(bf16[128,1024]{1,0:T(8,128)(2,1)} %bitcast.15), channel_id=1, source_target_pairs={{0,4},{4,0},{8,12},{12,8},{1,5},{5,1},{9,13},{13,9},{2,6},{6,2},{1... | collective-permute-start | bytes 786440 | tf_op jit(solution)/shard_map/ppermute | solution.py:148
  3.0 2.6 %collective-permute-start.5 = (bf16[128,1024]{1,0:T(8,128)(2,1)}, bf16[128,1024]{1,0:T(8,128)(2,1)}, u32[]{:S(2)}, u32[]{:S(2)}) collective-permute-start(bf16[128,1024]{1,0:T(8,128)(2,1)} %bitcast.16), channel_id=1, source_target_pairs={{0,8},{1,13},{2,10},{3,15},{4,12},{5,9},{6,14},{7,11},{8,0},{9,5},... | collective-permute-start | bytes 786440 | tf_op jit(solution)/shard_map/ppermute | solution.py:199
  5.6 14.5 %conditional.2 = (bf16[128,256]{1,0:T(8,128)(2,1)S(1)}, bf16[128,256]{1,0:T(8,128)(2,1)S(1)}, bf16[128,256]{1,0:T(8,128)(2,1)}, f32[128,1024]{1,0:T(8,128)}, s32...) conditional(s32[]{:T(128)} %convert_element_type.40, () %tuple.22, ...), branch_computations={%region_0.0_spmd, %region_1.2_spmd} | conditional | flops 690198 | bytes 8522158 | solution.py:154
  5.6 3.1 %mirror.1 = (bf16[2,384,256]{2,1,0:T(8,128)(2,1)S(1)}, f32[2,384,256]{2,1,0:T(8,128)S(1)}, s32[8,384]{1,0:T(8,128)S(1)}, bf16[384,1024]{1,0:T(8,128)(2,1)S(1)}, bf16[384,1024]{1,0:T(8,128)(2,1)S(1)}) custom-call(s32[24]{0:T(128)} %get-tuple-element.98.refs_0_, s32[24]{0:T(128)} %get-tuple-element.99.refs_1_, bf16[128,1024]{1,0:T(8,128)(2,1)} %bitcast.18, ...), custom_call_target="tpu_custom_call" | custom-call | flops 1024 | bytes 1024 | tf_op jit(solution)/shard_map/cond/branch_1_fun/mirror/pallas_call | solution.py:202
  8.8 0.1 collective-permute-start.2
  8.9 1.7 %collective-permute-done.2 = bf16[2,384,256]{2,1,0:T(8,128)(2,1)S(1)} collective-permute-done((bf16[2,384,256]{2,1,0:T(8,128)(2,1)S(1)}, bf16[2,384,256]{2,1,0:T(8,128)(2,1)S(1)}, u32[]{:S(2)}, u32[]{:S(2)}) %collective-permute-start.2) | collective-permute-done | bytes 393248 | tf_op jit(solution)/shard_map/cond/branch_1_fun/ppermute | solution.py:148
  10.6 0.8 %copy-done.1 = bf16[2,384,256]{2,1,0:T(8,128)(2,1)} copy-done((bf16[2,384,256]{2,1,0:T(8,128)(2,1)}, bf16[2,384,256]{2,1,0:T(8,128)(2,1)S(1)}, u32[]{:S(2)}) %copy-start.1) | copy-done | bytes 393240 | tf_op jit(solution)/shard_map/cond
  11.3 1.1 %convert_add_fusion = f32[2,384,256]{2,1,0:T(8,128)S(1)} fusion(f32[2,384,256]{2,1,0:T(8,128)S(1)} %get-tuple-element.49, bf16[2,384,256]{2,1,0:T(8,128)(2,1)} %copy-done.1), kind=kLoop, calls=%fused_computation | loop fusion | flops 393216 | bytes 1966080 | tf_op jit(solution)/shard_map/cond/branch_1_fun/add | solution.py:179
  12.4 1.6 %collective-permute-start.3 = (bf16[384,256]{1,0:T(8,128)(2,1)S(1)}, bf16[384,256]{1,0:T(8,128)(2,1)S(1)}, u32[]{:S(2)}, u32[]{:S(2)}) collective-permute-start(bf16[384,256]{1,0:T(8,128)(2,1)S(1)} %fusion.1), channel_id=1, source_target_pairs={{0,2},{1,3},{2,0},{3,1},{4,6},{5,7},{6,4},{7,5},{8,10},{9,11},{10,... | collective-permute-start | bytes 589832 | tf_op jit(solution)/shard_map/cond/branch_1_fun/ppermute | solution.py:148
  14.0 4.8 %near.1 = f32[4,32,1024]{2,1,0:T(8,128)} custom-call(s32[1]{0:T(128)} %get-tuple-element.102.refs_0_, s32[1]{0:T(128)} %get-tuple-element.103.refs_1_, bf16[4,32,1024]{2,1,0:T(8,128)(2,1)S(1)} %copy-done, bf16[1,1024,1024]{2,1,0:T(8,128)(2,1)} %get-tuple-element.104.refs_3_), custom_call_target="tpu_custom_call" | custom-call | flops 1024 | bytes 1024 | tf_op jit(solution)/shard_map/cond/branch_1_fun/near/pallas_call | solution.py:225
  18.8 0.7 %collective-permute-done.3 = bf16[384,256]{1,0:T(8,128)(2,1)S(1)} collective-permute-done((bf16[384,256]{1,0:T(8,128)(2,1)S(1)}, bf16[384,256]{1,0:T(8,128)(2,1)S(1)}, u32[]{:S(2)}, u32[]{:S(2)}) %collective-permute-start.3) | collective-permute-done | bytes 196640 | tf_op jit(solution)/shard_map/cond/branch_1_fun/ppermute | solution.py:148
  19.4 0.1 fusion
  19.5 0.6 %fusion.3 = (bf16[128,256]{1,0:T(8,128)(2,1)}, bf16[128,256]{1,0:T(8,128)(2,1)S(1)}, bf16[128,256]{1,0:T(8,128)(2,1)S(1)}) fusion(bf16[384,256]{1,0:T(8,128)(2,1)S(1)} %fusion), kind=kLoop, calls=%fused_computation.10 | loop fusion | bytes 393216 | tf_op jit(solution)/shard_map/cond/branch_1_fun/slice | solution.py:235
  20.1 0.5 %collective-permute-start.7 = (bf16[128,256]{1,0:T(8,128)(2,1)S(1)}, bf16[128,256]{1,0:T(8,128)(2,1)S(1)}, u32[]{:S(2)}, u32[]{:S(2)}) collective-permute-start(bf16[128,256]{1,0:T(8,128)(2,1)S(1)} %get-tuple-element.88), channel_id=1, source_target_pairs={{0,4},{4,0},{8,12},{12,8},{1,5},{5,1},{9,13},{13,9},{2,6},{6,2},{1... | collective-permute-start | bytes 196616 | tf_op jit(solution)/shard_map/ppermute | solution.py:148
  20.7 0.5 %collective-permute-start.8 = (bf16[128,256]{1,0:T(8,128)(2,1)S(1)}, bf16[128,256]{1,0:T(8,128)(2,1)S(1)}, u32[]{:S(2)}, u32[]{:S(2)}) collective-permute-start(bf16[128,256]{1,0:T(8,128)(2,1)S(1)} %get-tuple-element.89), channel_id=1, source_target_pairs={{0,8},{4,12},{8,0},{12,4},{1,9},{5,13},{9,1},{13,5},{2,10},{6,14},... | collective-permute-start | bytes 196616 | tf_op jit(solution)/shard_map/ppermute | solution.py:148
  21.1 3.5 %collective-permute-start.9 = (bf16[128,256]{1,0:T(8,128)(2,1)}, bf16[128,256]{1,0:T(8,128)(2,1)S(1)}, u32[]{:S(2)}, u32[]{:S(2)}) collective-permute-start(bf16[128,256]{1,0:T(8,128)(2,1)} %get-tuple-element.90), channel_id=1, source_target_pairs={{0,12},{4,8},{8,4},{12,0},{1,13},{5,9},{9,5},{13,1},{2,14},{6,10},... | collective-permute-start | bytes 196616 | tf_op jit(solution)/shard_map/ppermute | solution.py:148
  24.6 8.4 %conditional.3 = (f32[128,256]{1,0:T(8,128)S(1)}) conditional(s32[]{:T(128)} %convert_element_type.40, () %tuple.21, (s32[8,384]{1,0:T(8,128)S(1)}, bf16[384,1024]{1,0:T(8,128)(2,1)S(1)}, bf16[384,1024]{1,0:T(8,128)(2,1)S(1)}, f32[128,1024]{1,0:T(8,128)}, bf16[128,1024]{1,0:T(8,128)(2,1)}, /*index=5*/bf16[128,1024]{1,0:T(8,128)(2,1)}, ...), branch_computations={%region_2.3_spmd, %region_3.4_spmd} | conditional | flops 197654 | bytes 1901894 | solution.py:154
  24.6 2.6 %forward.1 = (bf16[2,128,256]{2,1,0:T(8,128)(2,1)S(1)}, f32[2,128,256]{2,1,0:T(8,128)S(1)}) custom-call(s32[8,384]{1,0:T(8,128)S(1)} %get-tuple-element.61.refs_0_, bf16[384,1024]{1,0:T(8,128)(2,1)S(1)} %get-tuple-element.62.refs_1_, bf16[384,1024]{1,0:T(8,128)(2,1)S(1)} %get-tuple-element.63.refs_2_, f32[128,1024]{1,0:T(8,128)} %get-tuple-element.64.refs_3_, ...), custom_call_target="tpu_custom_call" | custom-call | flops 1024 | bytes 1024 | tf_op jit(solution)/shard_map/cond/branch_1_fun/forward/pallas_call | solution.py:245
  27.2 0.1 collective-permute-start
  27.3 1.3 %collective-permute-done = bf16[2,128,256]{2,1,0:T(8,128)(2,1)S(1)} collective-permute-done((bf16[2,128,256]{2,1,0:T(8,128)(2,1)S(1)}, bf16[2,128,256]{2,1,0:T(8,128)(2,1)S(1)}, u32[]{:S(2)}, u32[]{:S(2)}) %collective-permute-start) | collective-permute-done | bytes 131104 | tf_op jit(solution)/shard_map/cond/branch_1_fun/ppermute | solution.py:148
  28.7 1.6 %collective-permute-start.1 = (bf16[128,256]{1,0:T(8,128)(2,1)S(1)}, bf16[128,256]{1,0:T(8,128)(2,1)S(1)}, u32[]{:S(2)}, u32[]{:S(2)}) collective-permute-start(bf16[128,256]{1,0:T(8,128)(2,1)S(1)} %fusion.2), channel_id=1, source_target_pairs={{0,2},{1,3},{2,0},{3,1},{4,6},{5,7},{6,4},{7,5},{8,10},{9,11},{10,... | collective-permute-start | bytes 196616 | tf_op jit(solution)/shard_map/cond/branch_1_fun/ppermute | solution.py:148
  30.2 2.8 %collective-permute-done.1 = bf16[128,256]{1,0:T(8,128)(2,1)S(1)} collective-permute-done((bf16[128,256]{1,0:T(8,128)(2,1)S(1)}, bf16[128,256]{1,0:T(8,128)(2,1)S(1)}, u32[]{:S(2)}, u32[]{:S(2)}) %collective-permute-start.1) | collective-permute-done | bytes 65568 | tf_op jit(solution)/shard_map/cond/branch_1_fun/ppermute | solution.py:148
  33.0 0.0 collective-permute-done.7
  33.1 0.7 %convert_add_fusion.2 = f32[128,256]{1,0:T(8,128)} fusion(bf16[128,256]{1,0:T(8,128)(2,1)S(1)} %collective-permute-done.9, bf16[128,256]{1,0:T(8,128)(2,1)S(1)} %collective-permute-done.8, f32[128,256]{1,0:T(8,128)S(1)} %get-tuple-element.124, bf16[128,256]{1,0:T(8,128)(2,1)S(1)} %collective-permute-done.7), kind=kLoop, calls=%fused_computation.9 | loop fusion | flops 196608 | bytes 458752 | tf_op jit(solution)/shard_map/add | solution.py:258
  (13 shorter events, 0.1 us)
Async XLA Ops:
  0.0 20.1 %collective-permute-start.4 = (bf16[128,1024]{1,0:T(8,128)(2,1)}, bf16[128,1024]{1,0:T(8,128)(2,1)}, u32[]{:S(2)}, u32[]{:S(2)}) collective-permute-start(bf16[128,1024]{1,0:T(8,128)(2,1)} %bitcast.15), channel_id=1, source_target_pairs={{0,4},{4,0},{8,12},{12,8},{1,5},{5,1},{9,13},{13,9},{2,6},{6,2},{1... | collective-permute-start | bytes 786440 | tf_op jit(solution)/shard_map/ppermute | solution.py:148
  3.0 17.1 %collective-permute-start.5 = (bf16[128,1024]{1,0:T(8,128)(2,1)}, bf16[128,1024]{1,0:T(8,128)(2,1)}, u32[]{:S(2)}, u32[]{:S(2)}) collective-permute-start(bf16[128,1024]{1,0:T(8,128)(2,1)} %bitcast.16), channel_id=1, source_target_pairs={{0,8},{1,13},{2,10},{3,15},{4,12},{5,9},{6,14},{7,11},{8,0},{9,5},... | collective-permute-start | bytes 786440 | tf_op jit(solution)/shard_map/ppermute | solution.py:199
  5.6 8.4 %copy-start = (bf16[4,32,1024]{2,1,0:T(8,128)(2,1)S(1)}, bf16[4,32,1024]{2,1,0:T(8,128)(2,1)}, u32[]{:S(2)}) copy-start(bf16[4,32,1024]{2,1,0:T(8,128)(2,1)} %get-tuple-element.56.refs_2_) | copy-start | bytes 786436 | tf_op jit(solution)/shard_map/cond
  8.8 1.8 %collective-permute-start.2 = (bf16[2,384,256]{2,1,0:T(8,128)(2,1)S(1)}, bf16[2,384,256]{2,1,0:T(8,128)(2,1)S(1)}, u32[]{:S(2)}, u32[]{:S(2)}) collective-permute-start(bf16[2,384,256]{2,1,0:T(8,128)(2,1)S(1)} %get-tuple-element.50), channel_id=1, source_target_pairs={{0,1},{1,0},{2,3},{3,2},{4,5},{5,4},{6,7},{7,6},{8,9},{9,8},{10,11... | collective-permute-start | bytes 1179656 | tf_op jit(solution)/shard_map/cond/branch_1_fun/ppermute | solution.py:148
  10.6 0.8 %copy-start.1 = (bf16[2,384,256]{2,1,0:T(8,128)(2,1)}, bf16[2,384,256]{2,1,0:T(8,128)(2,1)S(1)}, u32[]{:S(2)}) copy-start(bf16[2,384,256]{2,1,0:T(8,128)(2,1)S(1)} %collective-permute-done.2) | copy-start | bytes 1179652 | tf_op jit(solution)/shard_map/cond
  12.4 7.0 %collective-permute-start.3 = (bf16[384,256]{1,0:T(8,128)(2,1)S(1)}, bf16[384,256]{1,0:T(8,128)(2,1)S(1)}, u32[]{:S(2)}, u32[]{:S(2)}) collective-permute-start(bf16[384,256]{1,0:T(8,128)(2,1)S(1)} %fusion.1), channel_id=1, source_target_pairs={{0,2},{1,3},{2,0},{3,1},{4,6},{5,7},{6,4},{7,5},{8,10},{9,11},{10,... | collective-permute-start | bytes 589832 | tf_op jit(solution)/shard_map/cond/branch_1_fun/ppermute | solution.py:148
  20.1 4.5 %collective-permute-start.6 = (bf16[128,1024]{1,0:T(8,128)(2,1)}, bf16[128,1024]{1,0:T(8,128)(2,1)S(1)}, u32[]{:S(2)}, u32[]{:S(2)}) collective-permute-start(bf16[128,1024]{1,0:T(8,128)(2,1)} %collective-permute-done.5), channel_id=1, source_target_pairs={{0,1},{1,0},{2,3},{3,2},{4,5},{5,4},{6,7},{7,6},{8,9},{9,8},{10,11... | collective-permute-start | bytes 786440 | tf_op jit(solution)/shard_map/ppermute | solution.py:148
  20.1 12.9 %collective-permute-start.7 = (bf16[128,256]{1,0:T(8,128)(2,1)S(1)}, bf16[128,256]{1,0:T(8,128)(2,1)S(1)}, u32[]{:S(2)}, u32[]{:S(2)}) collective-permute-start(bf16[128,256]{1,0:T(8,128)(2,1)S(1)} %get-tuple-element.88), channel_id=1, source_target_pairs={{0,4},{4,0},{8,12},{12,8},{1,5},{5,1},{9,13},{13,9},{2,6},{6,2},{1... | collective-permute-start | bytes 196616 | tf_op jit(solution)/shard_map/ppermute | solution.py:148
  20.7 12.4 %collective-permute-start.8 = (bf16[128,256]{1,0:T(8,128)(2,1)S(1)}, bf16[128,256]{1,0:T(8,128)(2,1)S(1)}, u32[]{:S(2)}, u32[]{:S(2)}) collective-permute-start(bf16[128,256]{1,0:T(8,128)(2,1)S(1)} %get-tuple-element.89), channel_id=1, source_target_pairs={{0,8},{4,12},{8,0},{12,4},{1,9},{5,13},{9,1},{13,5},{2,10},{6,14},... | collective-permute-start | bytes 196616 | tf_op jit(solution)/shard_map/ppermute | solution.py:148
  21.1 11.9 %collective-permute-start.9 = (bf16[128,256]{1,0:T(8,128)(2,1)}, bf16[128,256]{1,0:T(8,128)(2,1)S(1)}, u32[]{:S(2)}, u32[]{:S(2)}) collective-permute-start(bf16[128,256]{1,0:T(8,128)(2,1)} %get-tuple-element.90), channel_id=1, source_target_pairs={{0,12},{4,8},{8,4},{12,0},{1,13},{5,9},{9,5},{13,1},{2,14},{6,10},... | collective-permute-start | bytes 196616 | tf_op jit(solution)/shard_map/ppermute | solution.py:148
  27.2 1.4 %collective-permute-start = (bf16[2,128,256]{2,1,0:T(8,128)(2,1)S(1)}, bf16[2,128,256]{2,1,0:T(8,128)(2,1)S(1)}, u32[]{:S(2)}, u32[]{:S(2)}) collective-permute-start(bf16[2,128,256]{2,1,0:T(8,128)(2,1)S(1)} %get-tuple-element.69), channel_id=1, source_target_pairs={{0,1},{1,0},{2,3},{3,2},{4,5},{5,4},{6,7},{7,6},{8,9},{9,8},{10,11... | collective-permute-start | bytes 393224 | tf_op jit(solution)/shard_map/cond/branch_1_fun/ppermute | solution.py:148
  28.7 4.3 %collective-permute-start.1 = (bf16[128,256]{1,0:T(8,128)(2,1)S(1)}, bf16[128,256]{1,0:T(8,128)(2,1)S(1)}, u32[]{:S(2)}, u32[]{:S(2)}) collective-permute-start(bf16[128,256]{1,0:T(8,128)(2,1)S(1)} %fusion.2), channel_id=1, source_target_pairs={{0,2},{1,3},{2,0},{3,1},{4,6},{5,7},{6,4},{7,5},{8,10},{9,11},{10,... | collective-permute-start | bytes 196616 | tf_op jit(solution)/shard_map/cond/branch_1_fun/ppermute | solution.py:148

commit v4 on v3

--- a/solution.py
+++ b/solution.py
@@ -20,8 +20,8 @@
     return lax.dot_general(a, b, (((1,), (1,)), ((), ())), preferred_element_type=F32)
 
 
-def params():
-    return pltpu.CompilerParams(vmem_limit_bytes=48 * 1024 * 1024)
+def params(others):
+    return pltpu.CompilerParams(vmem_limit_bytes=(12 if others <= 4 else 48) * 1024 * 1024)
 
 
 def each(count, step):
@@ -115,26 +115,37 @@
         out_ref[col] += weight * dot(x_ref[row], n_ref[b])
 
 
-def forward_kernel(clusters, exc, others, lanes_ref, u_ref, v_ref, near_ref, *refs):
-    pieces = refs[:others]
-    send_ref, keep_ref = refs[others:]
+def coef_of(clusters, exc, aways, lanes_ref, v_ref, pieces):
     group = lax.axis_index("row")
-    half = lax.rem(lax.axis_index("col"), 2)
-    row_lane = lanes_ref[0:1, :]
     col_lane = lanes_ref[1:2, :]
-    coef = jnp.zeros((exc, u_ref.shape[0]), F32)
-    batch = others if others <= 4 else 1
-    for n in range(0, others, batch):
+    coef = jnp.zeros((exc, v_ref.shape[0]), F32)
+    batch = len(pieces) if len(pieces) <= 4 else 1
+    for n in range(0, len(pieces), batch):
         every = dot_t(jnp.concatenate([p[...] for p in pieces[n : n + batch]], axis=0), v_ref[...])
         for i in range(batch):
-            away = n + i + 1
-            if away > 1:
-                away = away + half if away % 2 == 0 else away - half
-            first = (group ^ away) * clusters
+            first = (group ^ aways[n + i]) * clusters
             for c in range(clusters):
                 at = (i * clusters + c) * exc
                 coef += jnp.where(col_lane == first + c, every[at : at + exc], 0.0)
+    return coef
+
+
+def early_kernel(clusters, exc, lanes_ref, v_ref, *refs):
+    half = lax.rem(lax.axis_index("col"), 2)
+    pieces = refs[:-1]
+    aways = [1] + [2 * t + half for t in range(1, len(pieces))]
+    refs[-1][...] = coef_of(clusters, exc, aways, lanes_ref, v_ref, pieces)
+
+
+def forward_kernel(clusters, exc, lanes_ref, u_ref, v_ref, near_ref, early_ref, *refs):
+    pieces = refs[:-2]
+    send_ref, keep_ref = refs[-2:]
+    group = lax.axis_index("row")
+    half = lax.rem(lax.axis_index("col"), 2)
+    aways = [2 * t + 3 - half for t in range(len(pieces))]
+    coef = early_ref[...] + coef_of(clusters, exc, aways, lanes_ref, v_ref, pieces)
     coef = coef.astype(BF16).astype(F32)
+    row_lane = lanes_ref[0:1, :]
     masked = jnp.concatenate(
         [jnp.where(row_lane == group * clusters + c, coef, 0.0) for c in range(clusters)], axis=0
     ).astype(BF16)
@@ -216,7 +227,7 @@
                 pltpu.VMEM((batch * span, entries * rank), BF16),
                 pltpu.SemaphoreType.DMA((5,)),
             ],
-            compiler_params=params(),
+            compiler_params=params(others),
             cost_estimate=pl.CostEstimate(flops=1024, bytes_accessed=1024, transcendentals=0),
             name="mirror",
         )(far_rows, far_cols, x, u, v)
@@ -227,7 +238,7 @@
             in_specs=[SMEM, SMEM, VMEM, VMEM],
             out_specs=VMEM,
             out_shape=jax.ShapeDtypeStruct((clusters, exc, panels), F32),
-            compiler_params=params(),
+            compiler_params=params(others),
             cost_estimate=pl.CostEstimate(flops=1024, bytes_accessed=1024, transcendentals=0),
             name="near",
         )(near_rows, near_cols, x_near, near_blocks).reshape(span, panels)
@@ -236,21 +247,27 @@
 
     mirror, near, lanes, u_held, v_held = stage(local)
     whole, *got, lanes = lax.optimization_barrier((whole, *got, lanes))
-    pieces = [whole]
-    for piece in got:
-        pieces += [piece, swap(piece, "col", col_count, 1)]
     from_rows = [swap(part, "row", row_count, i + 1) for i, part in enumerate(mirror)]
 
     def forward():
+        early = pl.pallas_call(
+            lambda *refs: early_kernel(clusters, exc, *refs),
+            in_specs=[VMEM] * (3 + len(got)),
+            out_specs=VMEM,
+            out_shape=jax.ShapeDtypeStruct((exc, entries * rank), F32),
+            compiler_params=params(others),
+            cost_estimate=pl.CostEstimate(flops=1024, bytes_accessed=1024, transcendentals=0),
+            name="early",
+        )(lanes, v_held, whole, *got)
         send, keep = pl.pallas_call(
-            lambda *refs: forward_kernel(clusters, exc, others, *refs),
-            in_specs=[VMEM] * (4 + others),
+            lambda *refs: forward_kernel(clusters, exc, *refs),
+            in_specs=[VMEM] * (5 + len(got)),
             out_specs=[VMEM] * 2,
             out_shape=shares(1),
-            compiler_params=params(),
+            compiler_params=params(others),
             cost_estimate=pl.CostEstimate(flops=1024, bytes_accessed=1024, transcendentals=0),
             name="forward",
-        )(lanes, u_held, v_held, near, *pieces)
+        )(lanes, u_held, v_held, near, early, *[swap(piece, "col", col_count, 1) for piece in got])
         return col_sum(*pair_sum(send, keep))
 
     total = stage(forward)

time: 34 us -> 35.4 us (1.041)
  Pallas kernels: 10.5 us -> 11.7 us
    pallas_call x1 -> x2, Pallas kernels: 2.61 us -> 3.8 us  [the longest x1 2.31 us: forward(): pl.pallas_call(lambda *refs: forward_kernel(clusters, exc, *refs), in_spe...]
  transfers between devices with their start and end apart: 10 -> 10, of which waited for: 4 -> 5; matrix products, arithmetic and copies ran while one was open for 5% -> 5% of each run, Pallas kernels for 31% -> 33%
where the time goes in v4:
time: 35.4 us; the launch traced here: 35.1 us
  starting transfers between devices  13.5 us (38%)
  Pallas kernels  11.7 us (33%)
  waiting for transfers between devices  6.48 us (18%)
  other arithmetic  1.85 us (5%)
  local copies, waits for them, and re-layouts  1.45 us (4%)
    ppermute x9, starting transfers between devices, swap(): return lax.ppermute(value, axis, [(i, i ^ step) for i in range(size)])  10.9 us
    ppermute x9, waiting for transfers between devices, swap(): return lax.ppermute(value, axis, [(i, i ^ step) for i in range(size)])  6.47 us
    pallas_call x1, Pallas kernels, local(): pl.pallas_call(lambda *refs: near_kernel(clusters, exc, *refs), in_specs=...  4.77 us
    pallas_call x1, Pallas kernels, local(): pl.pallas_call(lambda *refs: mirror_kernel(clusters, exc, rank, others, *...  3.14 us
    ppermute x1, starting transfers between devices, body(): got.append(lax.ppermute(x, ('row', 'col'), perm))  2.59 us
    pallas_call x1, Pallas kernels, forward(): pl.pallas_call(lambda *refs: forward_kernel(clusters, exc, *refs), in_spe...  2.31 us
    pallas_call x1, Pallas kernels, forward(): pl.pallas_call(lambda *refs: early_kernel(clusters, exc, *refs), in_specs...  1.49 us
    add x2, other arithmetic, pair_sum(): total = keep + swap(send, 'col', col_count, 1).astype(F32)  1.1 us
  transfers between devices with their start and end apart: 10, of which 5 were waited for; matrix products, arithmetic and copies ran while one was open for 5% of the time, Pallas kernels for 33%

profile of v4, /device:TPU:0, one launch (start us, length us, event | category | flops | bytes accessed | tf_op | source)
XLA Modules:
  0.0 35.1 jit_solution(12879221335158363589)
XLA Ops:
  0.0 3.0 %collective-permute-start.5 = (bf16[128,1024]{1,0:T(8,128)(2,1)}, bf16[128,1024]{1,0:T(8,128)(2,1)}, u32[]{:S(2)}, u32[]{:S(2)}) collective-permute-start(bf16[128,1024]{1,0:T(8,128)(2,1)} %bitcast.15), channel_id=1, source_target_pairs={{0,4},{4,0},{8,12},{12,8},{1,5},{5,1},{9,13},{13,9},{2,6},{6,2},{1... | collective-permute-start | bytes 786440 | tf_op jit(solution)/shard_map/ppermute | solution.py:159
  3.0 2.6 %collective-permute-start.6 = (bf16[128,1024]{1,0:T(8,128)(2,1)}, bf16[128,1024]{1,0:T(8,128)(2,1)}, u32[]{:S(2)}, u32[]{:S(2)}) collective-permute-start(bf16[128,1024]{1,0:T(8,128)(2,1)} %bitcast.16), channel_id=1, source_target_pairs={{0,8},{1,13},{2,10},{3,15},{4,12},{5,9},{6,14},{7,11},{8,0},{9,5},... | collective-permute-start | bytes 786440 | tf_op jit(solution)/shard_map/ppermute | solution.py:210
  5.6 14.5 %conditional.2 = (bf16[128,256]{1,0:T(8,128)(2,1)S(1)}, bf16[128,256]{1,0:T(8,128)(2,1)S(1)}, bf16[128,256]{1,0:T(8,128)(2,1)}, f32[128,1024]{1,0:T(8,128)}, s32...) conditional(s32[]{:T(128)} %convert_element_type.40, () %tuple.22, ...), branch_computations={%region_0.0_spmd, %region_1.2_spmd} | conditional | flops 690198 | bytes 8522158 | solution.py:165
  5.6 3.1 %mirror.1 = (bf16[2,384,256]{2,1,0:T(8,128)(2,1)S(1)}, f32[2,384,256]{2,1,0:T(8,128)S(1)}, s32[8,384]{1,0:T(8,128)S(1)}, bf16[384,1024]{1,0:T(8,128)(2,1)S(1)}, bf16[384,1024]{1,0:T(8,128)(2,1)S(1)}) custom-call(s32[24]{0:T(128)} %get-tuple-element.95.refs_0_, s32[24]{0:T(128)} %get-tuple-element.96.refs_1_, bf16[128,1024]{1,0:T(8,128)(2,1)} %bitcast.18, ...), custom_call_target="tpu_custom_call" | custom-call | flops 1024 | bytes 1024 | tf_op jit(solution)/shard_map/cond/branch_1_fun/mirror/pallas_call | solution.py:213
  8.8 0.1 collective-permute-start.3
  8.9 1.7 %collective-permute-done.3 = bf16[2,384,256]{2,1,0:T(8,128)(2,1)S(1)} collective-permute-done((bf16[2,384,256]{2,1,0:T(8,128)(2,1)S(1)}, bf16[2,384,256]{2,1,0:T(8,128)(2,1)S(1)}, u32[]{:S(2)}, u32[]{:S(2)}) %collective-permute-start.3) | collective-permute-done | bytes 393248 | tf_op jit(solution)/shard_map/cond/branch_1_fun/ppermute | solution.py:159
  10.6 0.8 %copy-done.1 = bf16[2,384,256]{2,1,0:T(8,128)(2,1)} copy-done((bf16[2,384,256]{2,1,0:T(8,128)(2,1)}, bf16[2,384,256]{2,1,0:T(8,128)(2,1)S(1)}, u32[]{:S(2)}) %copy-start.1) | copy-done | bytes 393240 | tf_op jit(solution)/shard_map/cond
  11.3 1.1 %convert_add_fusion = f32[2,384,256]{2,1,0:T(8,128)S(1)} fusion(f32[2,384,256]{2,1,0:T(8,128)S(1)} %get-tuple-element.47, bf16[2,384,256]{2,1,0:T(8,128)(2,1)} %copy-done.1), kind=kLoop, calls=%fused_computation | loop fusion | flops 393216 | bytes 1966080 | tf_op jit(solution)/shard_map/cond/branch_1_fun/add | solution.py:190
  12.4 1.6 %collective-permute-start.4 = (bf16[384,256]{1,0:T(8,128)(2,1)S(1)}, bf16[384,256]{1,0:T(8,128)(2,1)S(1)}, u32[]{:S(2)}, u32[]{:S(2)}) collective-permute-start(bf16[384,256]{1,0:T(8,128)(2,1)S(1)} %fusion.1), channel_id=1, source_target_pairs={{0,2},{1,3},{2,0},{3,1},{4,6},{5,7},{6,4},{7,5},{8,10},{9,11},{10,... | collective-permute-start | bytes 589832 | tf_op jit(solution)/shard_map/cond/branch_1_fun/ppermute | solution.py:159
  14.0 4.8 %near.1 = f32[4,32,1024]{2,1,0:T(8,128)} custom-call(s32[1]{0:T(128)} %get-tuple-element.99.refs_0_, s32[1]{0:T(128)} %get-tuple-element.100.refs_1_, bf16[4,32,1024]{2,1,0:T(8,128)(2,1)S(1)} %copy-done, bf16[1,1024,1024]{2,1,0:T(8,128)(2,1)} %get-tuple-element.101.refs_3_), custom_call_target="tpu_custom_call" | custom-call | flops 1024 | bytes 1024 | tf_op jit(solution)/shard_map/cond/branch_1_fun/near/pallas_call | solution.py:236
  18.8 0.7 %collective-permute-done.4 = bf16[384,256]{1,0:T(8,128)(2,1)S(1)} collective-permute-done((bf16[384,256]{1,0:T(8,128)(2,1)S(1)}, bf16[384,256]{1,0:T(8,128)(2,1)S(1)}, u32[]{:S(2)}, u32[]{:S(2)}) %collective-permute-start.4) | collective-permute-done | bytes 196640 | tf_op jit(solution)/shard_map/cond/branch_1_fun/ppermute | solution.py:159
  19.5 0.6 %fusion.3 = (bf16[128,256]{1,0:T(8,128)(2,1)}, bf16[128,256]{1,0:T(8,128)(2,1)S(1)}, bf16[128,256]{1,0:T(8,128)(2,1)S(1)}) fusion(bf16[384,256]{1,0:T(8,128)(2,1)S(1)} %fusion), kind=kLoop, calls=%fused_computation.10 | loop fusion | bytes 393216 | tf_op jit(solution)/shard_map/cond/branch_1_fun/slice | solution.py:246
  20.1 0.5 %collective-permute-start.7 = (bf16[128,256]{1,0:T(8,128)(2,1)S(1)}, bf16[128,256]{1,0:T(8,128)(2,1)S(1)}, u32[]{:S(2)}, u32[]{:S(2)}) collective-permute-start(bf16[128,256]{1,0:T(8,128)(2,1)S(1)} %get-tuple-element.85), channel_id=1, source_target_pairs={{0,4},{4,0},{8,12},{12,8},{1,5},{5,1},{9,13},{13,9},{2,6},{6,2},{1... | collective-permute-start | bytes 196616 | tf_op jit(solution)/shard_map/ppermute | solution.py:159
  20.6 0.5 %collective-permute-start.8 = (bf16[128,256]{1,0:T(8,128)(2,1)S(1)}, bf16[128,256]{1,0:T(8,128)(2,1)S(1)}, u32[]{:S(2)}, u32[]{:S(2)}) collective-permute-start(bf16[128,256]{1,0:T(8,128)(2,1)S(1)} %get-tuple-element.86), channel_id=1, source_target_pairs={{0,8},{4,12},{8,0},{12,4},{1,9},{5,13},{9,1},{13,5},{2,10},{6,14},... | collective-permute-start | bytes 196616 | tf_op jit(solution)/shard_map/ppermute | solution.py:159
  21.1 3.5 %collective-permute-start.9 = (bf16[128,256]{1,0:T(8,128)(2,1)}, bf16[128,256]{1,0:T(8,128)(2,1)S(1)}, u32[]{:S(2)}, u32[]{:S(2)}) collective-permute-start(bf16[128,256]{1,0:T(8,128)(2,1)} %get-tuple-element.87), channel_id=1, source_target_pairs={{0,12},{4,8},{8,4},{12,0},{1,13},{5,9},{9,5},{13,1},{2,14},{6,10},... | collective-permute-start | bytes 196616 | tf_op jit(solution)/shard_map/ppermute | solution.py:159
  24.5 9.9 %conditional.3 = (f32[128,256]{1,0:T(8,128)S(1)}) conditional(s32[]{:T(128)} %convert_element_type.40, () %tuple.21, (s32[8,384]{1,0:T(8,128)S(1)}, bf16[384,1024]{1,0:T(8,128)(2,1)S(1)}, bf16[128,1024]{1,0:T(8,128)(2,1)}, bf16[128,1024]{1,0:T(8,128)(2,1)}, bf16[384,1024]{1,0:T(8,128)(2,1)S(1)}, /*index=5*/f32[128,1024]{1,0:T(8,128)}, s32[]{:T(128)}) %tuple.25), branch_computations={%region_2.3_spmd, %region_3.4_spmd} | conditional | flops 198678 | bytes 2951534 | solution.py:165
  24.5 1.5 %early.1.refs_4_ = f32[32,384]{1,0:T(8,128)S(1)} custom-call(s32[8,384]{1,0:T(8,128)S(1)} %get-tuple-element.59.refs_0_, bf16[384,1024]{1,0:T(8,128)(2,1)S(1)} %get-tuple-element.61.refs_1_.refs_2_, bf16[128,1024]{1,0:T(8,128)(2,1)} %get-tuple-element.63.refs_2_, bf16[128,1024]{1,0:T(8,128)(2,1)} %get-tuple-element.64.refs_3_), custom_call_target="tpu_custom_call" | custom-call | flops 1024 | bytes 1024 | tf_op jit(solution)/shard_map/cond/branch_1_fun/early/pallas_call | solution.py:253
  26.0 0.2 collective-permute-done.refs_5_
  26.3 2.3 %forward.1 = (bf16[2,128,256]{2,1,0:T(8,128)(2,1)S(1)}, f32[2,128,256]{2,1,0:T(8,128)S(1)}) custom-call(s32[8,384]{1,0:T(8,128)S(1)} %get-tuple-element.59.refs_0_, bf16[384,1024]{1,0:T(8,128)(2,1)S(1)} %get-tuple-element.60.refs_1_, bf16[384,1024]{1,0:T(8,128)(2,1)S(1)} %get-tuple-element.61.refs_1_.refs_2_, f32[128,1024]{1,0:T(8,128)} %get-tuple-element.62.refs_3_, ...), custom_call_target="tpu_custom_call" | custom-call | flops 1024 | bytes 1024 | tf_op jit(solution)/shard_map/cond/branch_1_fun/forward/pallas_call | solution.py:262
  28.6 0.3 collective-permute-start.1
  28.9 1.1 %collective-permute-done.1 = bf16[2,128,256]{2,1,0:T(8,128)(2,1)S(1)} collective-permute-done((bf16[2,128,256]{2,1,0:T(8,128)(2,1)S(1)}, bf16[2,128,256]{2,1,0:T(8,128)(2,1)S(1)}, u32[]{:S(2)}, u32[]{:S(2)}) %collective-permute-start.1) | collective-permute-done | bytes 131104 | tf_op jit(solution)/shard_map/cond/branch_1_fun/ppermute | solution.py:159
  30.1 1.6 %collective-permute-start.2 = (bf16[128,256]{1,0:T(8,128)(2,1)S(1)}, bf16[128,256]{1,0:T(8,128)(2,1)S(1)}, u32[]{:S(2)}, u32[]{:S(2)}) collective-permute-start(bf16[128,256]{1,0:T(8,128)(2,1)S(1)} %fusion.2), channel_id=1, source_target_pairs={{0,2},{1,3},{2,0},{3,1},{4,6},{5,7},{6,4},{7,5},{8,10},{9,11},{10,... | collective-permute-start | bytes 196616 | tf_op jit(solution)/shard_map/cond/branch_1_fun/ppermute | solution.py:159
  31.6 2.8 %collective-permute-done.2 = bf16[128,256]{1,0:T(8,128)(2,1)S(1)} collective-permute-done((bf16[128,256]{1,0:T(8,128)(2,1)S(1)}, bf16[128,256]{1,0:T(8,128)(2,1)S(1)}, u32[]{:S(2)}, u32[]{:S(2)}) %collective-permute-start.2) | collective-permute-done | bytes 65568 | tf_op jit(solution)/shard_map/cond/branch_1_fun/ppermute | solution.py:159
  34.4 0.7 %convert_add_fusion.2 = f32[128,256]{1,0:T(8,128)} fusion(bf16[128,256]{1,0:T(8,128)(2,1)S(1)} %collective-permute-done.9, bf16[128,256]{1,0:T(8,128)(2,1)S(1)} %collective-permute-done.8, f32[128,256]{1,0:T(8,128)S(1)} %get-tuple-element.121, bf16[128,256]{1,0:T(8,128)(2,1)S(1)} %collective-permute-done.7), kind=kLoop, calls=%fused_computation.9 | loop fusion | flops 196608 | bytes 458752 | tf_op jit(solution)/shard_map/add | solution.py:275
  (14 shorter events, 0.2 us)
Async XLA Ops:
  0.0 24.5 %collective-permute-start.5 = (bf16[128,1024]{1,0:T(8,128)(2,1)}, bf16[128,1024]{1,0:T(8,128)(2,1)}, u32[]{:S(2)}, u32[]{:S(2)}) collective-permute-start(bf16[128,1024]{1,0:T(8,128)(2,1)} %bitcast.15), channel_id=1, source_target_pairs={{0,4},{4,0},{8,12},{12,8},{1,5},{5,1},{9,13},{13,9},{2,6},{6,2},{1... | collective-permute-start | bytes 786440 | tf_op jit(solution)/shard_map/ppermute | solution.py:159
  3.0 21.5 %collective-permute-start.6 = (bf16[128,1024]{1,0:T(8,128)(2,1)}, bf16[128,1024]{1,0:T(8,128)(2,1)}, u32[]{:S(2)}, u32[]{:S(2)}) collective-permute-start(bf16[128,1024]{1,0:T(8,128)(2,1)} %bitcast.16), channel_id=1, source_target_pairs={{0,8},{1,13},{2,10},{3,15},{4,12},{5,9},{6,14},{7,11},{8,0},{9,5},... | collective-permute-start | bytes 786440 | tf_op jit(solution)/shard_map/ppermute | solution.py:210
  5.6 8.4 %copy-start = (bf16[4,32,1024]{2,1,0:T(8,128)(2,1)S(1)}, bf16[4,32,1024]{2,1,0:T(8,128)(2,1)}, u32[]{:S(2)}) copy-start(bf16[4,32,1024]{2,1,0:T(8,128)(2,1)} %get-tuple-element.54.refs_2_) | copy-start | bytes 786436 | tf_op jit(solution)/shard_map/cond
  8.8 1.8 %collective-permute-start.3 = (bf16[2,384,256]{2,1,0:T(8,128)(2,1)S(1)}, bf16[2,384,256]{2,1,0:T(8,128)(2,1)S(1)}, u32[]{:S(2)}, u32[]{:S(2)}) collective-permute-start(bf16[2,384,256]{2,1,0:T(8,128)(2,1)S(1)} %get-tuple-element.48), channel_id=1, source_target_pairs={{0,1},{1,0},{2,3},{3,2},{4,5},{5,4},{6,7},{7,6},{8,9},{9,8},{10,11... | collective-permute-start | bytes 1179656 | tf_op jit(solution)/shard_map/cond/branch_1_fun/ppermute | solution.py:159
  10.6 0.8 %copy-start.1 = (bf16[2,384,256]{2,1,0:T(8,128)(2,1)}, bf16[2,384,256]{2,1,0:T(8,128)(2,1)S(1)}, u32[]{:S(2)}) copy-start(bf16[2,384,256]{2,1,0:T(8,128)(2,1)S(1)} %collective-permute-done.3) | copy-start | bytes 1179652 | tf_op jit(solution)/shard_map/cond
  12.4 7.0 %collective-permute-start.4 = (bf16[384,256]{1,0:T(8,128)(2,1)S(1)}, bf16[384,256]{1,0:T(8,128)(2,1)S(1)}, u32[]{:S(2)}, u32[]{:S(2)}) collective-permute-start(bf16[384,256]{1,0:T(8,128)(2,1)S(1)} %fusion.1), channel_id=1, source_target_pairs={{0,2},{1,3},{2,0},{3,1},{4,6},{5,7},{6,4},{7,5},{8,10},{9,11},{10,... | collective-permute-start | bytes 589832 | tf_op jit(solution)/shard_map/cond/branch_1_fun/ppermute | solution.py:159
  20.1 14.3 %collective-permute-start.7 = (bf16[128,256]{1,0:T(8,128)(2,1)S(1)}, bf16[128,256]{1,0:T(8,128)(2,1)S(1)}, u32[]{:S(2)}, u32[]{:S(2)}) collective-permute-start(bf16[128,256]{1,0:T(8,128)(2,1)S(1)} %get-tuple-element.85), channel_id=1, source_target_pairs={{0,4},{4,0},{8,12},{12,8},{1,5},{5,1},{9,13},{13,9},{2,6},{6,2},{1... | collective-permute-start | bytes 196616 | tf_op jit(solution)/shard_map/ppermute | solution.py:159
  20.6 13.8 %collective-permute-start.8 = (bf16[128,256]{1,0:T(8,128)(2,1)S(1)}, bf16[128,256]{1,0:T(8,128)(2,1)S(1)}, u32[]{:S(2)}, u32[]{:S(2)}) collective-permute-start(bf16[128,256]{1,0:T(8,128)(2,1)S(1)} %get-tuple-element.86), channel_id=1, source_target_pairs={{0,8},{4,12},{8,0},{12,4},{1,9},{5,13},{9,1},{13,5},{2,10},{6,14},... | collective-permute-start | bytes 196616 | tf_op jit(solution)/shard_map/ppermute | solution.py:159
  21.1 13.4 %collective-permute-start.9 = (bf16[128,256]{1,0:T(8,128)(2,1)}, bf16[128,256]{1,0:T(8,128)(2,1)S(1)}, u32[]{:S(2)}, u32[]{:S(2)}) collective-permute-start(bf16[128,256]{1,0:T(8,128)(2,1)} %get-tuple-element.87), channel_id=1, source_target_pairs={{0,12},{4,8},{8,4},{12,0},{1,13},{5,9},{9,5},{13,1},{2,14},{6,10},... | collective-permute-start | bytes 196616 | tf_op jit(solution)/shard_map/ppermute | solution.py:159
  24.5 1.7 %collective-permute-start = (bf16[128,1024]{1,0:T(8,128)(2,1)}, bf16[128,1024]{1,0:T(8,128)(2,1)S(1)}, u32[]{:S(2)}, u32[]{:S(2)}) collective-permute-start(bf16[128,1024]{1,0:T(8,128)(2,1)} %get-tuple-element.64.refs_3_), channel_id=1, source_target_pairs={{0,1},{1,0},{2,3},{3,2},{4,5},{5,4},{6,7},{7,6},{8,9},{9,8},{10,11... | collective-permute-start | bytes 786440 | tf_op jit(solution)/shard_map/cond/branch_1_fun/ppermute | solution.py:159
  28.6 1.4 %collective-permute-start.1 = (bf16[2,128,256]{2,1,0:T(8,128)(2,1)S(1)}, bf16[2,128,256]{2,1,0:T(8,128)(2,1)S(1)}, u32[]{:S(2)}, u32[]{:S(2)}) collective-permute-start(bf16[2,128,256]{2,1,0:T(8,128)(2,1)S(1)} %get-tuple-element.66), channel_id=1, source_target_pairs={{0,1},{1,0},{2,3},{3,2},{4,5},{5,4},{6,7},{7,6},{8,9},{9,8},{10,11... | collective-permute-start | bytes 393224 | tf_op jit(solution)/shard_map/cond/branch_1_fun/ppermute | solution.py:159
  30.1 4.3 %collective-permute-start.2 = (bf16[128,256]{1,0:T(8,128)(2,1)S(1)}, bf16[128,256]{1,0:T(8,128)(2,1)S(1)}, u32[]{:S(2)}, u32[]{:S(2)}) collective-permute-start(bf16[128,256]{1,0:T(8,128)(2,1)S(1)} %fusion.2), channel_id=1, source_target_pairs={{0,2},{1,3},{2,0},{3,1},{4,6},{5,7},{6,4},{7,5},{8,10},{9,11},{10,... | collective-permute-start | bytes 196616 | tf_op jit(solution)/shard_map/cond/branch_1_fun/ppermute | solution.py:159

commit v5 on v3

--- a/solution.py
+++ b/solution.py
@@ -20,8 +20,8 @@
     return lax.dot_general(a, b, (((1,), (1,)), ((), ())), preferred_element_type=F32)
 
 
-def params():
-    return pltpu.CompilerParams(vmem_limit_bytes=48 * 1024 * 1024)
+def params(others):
+    return pltpu.CompilerParams(vmem_limit_bytes=(12 if others <= 4 else 48) * 1024 * 1024)
 
 
 def each(count, step):
@@ -59,8 +59,8 @@
 
 def mirror_kernel(
     clusters, exc, rank, others, rows_hbm, cols_hbm, x_hbm, u_hbm, v_hbm,
-    send_ref, keep_ref, lanes_ref, u_ref, v_ref,
-    rows_ref, cols_ref, x_ref, mask_ref, sems,
+    send_ref, keep_ref, lanes_ref,
+    rows_ref, cols_ref, x_ref, u_ref, v_ref, mask_ref, sems,
 ):
     copies = [
         pltpu.make_async_copy(src, dst, sems.at[i])
@@ -115,17 +115,26 @@
         out_ref[col] += weight * dot(x_ref[row], n_ref[b])
 
 
-def forward_kernel(clusters, exc, others, lanes_ref, u_ref, v_ref, near_ref, *refs):
-    pieces = refs[:others]
-    send_ref, keep_ref = refs[others:]
+def forward_kernel(clusters, exc, others, lanes_ref, u_hbm, v_hbm, near_hbm, *refs):
+    sources = refs[:others]
+    send_ref, keep_ref, u_ref, v_ref, near_ref, pieces_ref, sems = refs[others:]
+    span = clusters * exc
+    moves = [(v_hbm, v_ref)]
+    moves += [(piece, pieces_ref.at[i * span : (i + 1) * span]) for i, piece in enumerate(sources)]
+    moves += [(u_hbm, u_ref), (near_hbm, near_ref)]
+    copies = [pltpu.make_async_copy(src, dst, sems.at[i]) for i, (src, dst) in enumerate(moves)]
+    for copy in copies:
+        copy.start()
     group = lax.axis_index("row")
     half = lax.rem(lax.axis_index("col"), 2)
     row_lane = lanes_ref[0:1, :]
     col_lane = lanes_ref[1:2, :]
     coef = jnp.zeros((exc, u_ref.shape[0]), F32)
     batch = others if others <= 4 else 1
+    for copy in copies[:-2]:
+        copy.wait()
     for n in range(0, others, batch):
-        every = dot_t(jnp.concatenate([p[...] for p in pieces[n : n + batch]], axis=0), v_ref[...])
+        every = dot_t(pieces_ref[n * span : (n + batch) * span], v_ref[...])
         for i in range(batch):
             away = n + i + 1
             if away > 1:
@@ -138,6 +147,8 @@
     masked = jnp.concatenate(
         [jnp.where(row_lane == group * clusters + c, coef, 0.0) for c in range(clusters)], axis=0
     ).astype(BF16)
+    copies[-2].wait()
+    copies[-1].wait()
     rows = slice(None)
     split_columns(
         half, keep_ref, send_ref, rows, lambda cols: dot(masked, u_ref[:, cols]) + near_ref[:, cols]
@@ -199,24 +210,21 @@
         got.append(lax.ppermute(x, ("row", "col"), perm))
 
     def local():
-        send, keep, lanes, u_held, v_held = pl.pallas_call(
+        send, keep, lanes = pl.pallas_call(
             lambda *refs: mirror_kernel(clusters, exc, rank, others, *refs),
             in_specs=[ANY] * 5,
-            out_specs=[VMEM] * 5,
-            out_shape=shares(others)
-            + [
-                jax.ShapeDtypeStruct((8, entries * rank), jnp.int32),
-                jax.ShapeDtypeStruct(u.shape, BF16),
-                jax.ShapeDtypeStruct(v.shape, BF16),
-            ],
+            out_specs=[VMEM] * 3,
+            out_shape=shares(others) + [jax.ShapeDtypeStruct((8, entries * rank), jnp.int32)],
             scratch_shapes=[
                 pltpu.SMEM(far_rows.shape, jnp.int32),
                 pltpu.SMEM(far_cols.shape, jnp.int32),
                 pltpu.VMEM(x.shape, BF16),
+                pltpu.VMEM(u.shape, BF16),
+                pltpu.VMEM(v.shape, BF16),
                 pltpu.VMEM((batch * span, entries * rank), BF16),
                 pltpu.SemaphoreType.DMA((5,)),
             ],
-            compiler_params=params(),
+            compiler_params=params(others),
             cost_estimate=pl.CostEstimate(flops=1024, bytes_accessed=1024, transcendentals=0),
             name="mirror",
         )(far_rows, far_cols, x, u, v)
@@ -227,31 +235,39 @@
             in_specs=[SMEM, SMEM, VMEM, VMEM],
             out_specs=VMEM,
             out_shape=jax.ShapeDtypeStruct((clusters, exc, panels), F32),
-            compiler_params=params(),
+            compiler_params=params(others),
             cost_estimate=pl.CostEstimate(flops=1024, bytes_accessed=1024, transcendentals=0),
             name="near",
         )(near_rows, near_cols, x_near, near_blocks).reshape(span, panels)
         mirror = col_sum(mirror, leaving).astype(BF16)
-        return [mirror[i * span : (i + 1) * span] for i in range(others)], near, lanes, u_held, v_held
-
-    mirror, near, lanes, u_held, v_held = stage(local)
+        return [mirror[i * span : (i + 1) * span] for i in range(others)], near, lanes
+
+    mirror, near, lanes = stage(local)
     whole, *got, lanes = lax.optimization_barrier((whole, *got, lanes))
     pieces = [whole]
     for piece in got:
         pieces += [piece, swap(piece, "col", col_count, 1)]
-    from_rows = [swap(part, "row", row_count, i + 1) for i, part in enumerate(mirror)]
+    from_rows = [swap(mirror[d - 1], "row", row_count, d) for d in range(2, row_count)]
 
     def forward():
         send, keep = pl.pallas_call(
             lambda *refs: forward_kernel(clusters, exc, others, *refs),
-            in_specs=[VMEM] * (4 + others),
+            in_specs=[VMEM] + [ANY] * (3 + others),
             out_specs=[VMEM] * 2,
             out_shape=shares(1),
-            compiler_params=params(),
+            scratch_shapes=[
+                pltpu.VMEM(u.shape, BF16),
+                pltpu.VMEM(v.shape, BF16),
+                pltpu.VMEM(near.shape, F32),
+                pltpu.VMEM((others * span, panels), BF16),
+                pltpu.SemaphoreType.DMA((3 + others,)),
+            ],
+            compiler_params=params(others),
             cost_estimate=pl.CostEstimate(flops=1024, bytes_accessed=1024, transcendentals=0),
             name="forward",
-        )(lanes, u_held, v_held, near, *pieces)
-        return col_sum(*pair_sum(send, keep))
+        )(lanes, u, v, near, *pieces)
+        own, leaving = pair_sum(send, keep)
+        return col_sum(own, leaving) + swap(mirror[0], "row", row_count, 1).astype(F32)
 
     total = stage(forward)
     for term in from_rows:

time: 34 us -> 30.1 us (0.89)
  local copies, waits for them, and re-layouts: 1.45 us -> 0.07 us
  other arithmetic: 1.85 us -> 0.85 us
  Pallas kernels: 10.5 us -> 9.69 us
  starting transfers between devices: 13.3 us -> 12.6 us
    add x2, other arithmetic: 1.1 us -> 0.1 us  [pair_sum(): total = keep + swap(send, 'col', col_count, 1).astype(F32)]
    pallas_call x1, Pallas kernels: 4.77 us -> 3.89 us  [local(): pl.pallas_call(lambda *refs: near_kernel(clusters, exc, *refs), in_specs=...]
    ppermute x9, starting transfers between devices: 10.7 us -> 9.97 us  [swap(): return lax.ppermute(value, axis, [(i, i ^ step) for i in range(size)])]
    cond x4 -> x2, local copies, waits for them, and re-layouts: 0.76 us -> 0.01 us
    slice x1, local copies, waits for them, and re-layouts: 0.64 us -> 0.02 us  [local(): mirror[i * span:(i + 1) * span]]
  transfers between devices with their start and end apart: 10 -> 10, of which waited for: 4 -> 5; matrix products, arithmetic and copies ran while one was open for 5% -> 1% of each run, Pallas kernels for 31% -> 32%
where the time goes in v5:
time: 30.1 us; the launch traced here: 29.9 us
  starting transfers between devices  12.6 us (42%)
  Pallas kernels  9.69 us (32%)
  waiting for transfers between devices  6.62 us (22%)
  other arithmetic  0.85 us (3%)
    ppermute x9, starting transfers between devices, swap(): return lax.ppermute(value, axis, [(i, i ^ step) for i in range(size)])  9.97 us
    ppermute x9, waiting for transfers between devices, swap(): return lax.ppermute(value, axis, [(i, i ^ step) for i in range(size)])  6.62 us
    pallas_call x1, Pallas kernels, local(): pl.pallas_call(lambda *refs: near_kernel(clusters, exc, *refs), in_specs=...  3.89 us
    pallas_call x1, Pallas kernels, local(): pl.pallas_call(lambda *refs: mirror_kernel(clusters, exc, rank, others, *...  3.14 us
    pallas_call x1, Pallas kernels, forward(): pl.pallas_call(lambda *refs: forward_kernel(clusters, exc, others, *refs)...  2.66 us
    ppermute x1, starting transfers between devices, body(): got.append(lax.ppermute(x, ('row', 'col'), perm))  2.59 us
    add x1, other arithmetic, body(): total = total + term.astype(F32)  0.68 us
  transfers between devices with their start and end apart: 10, of which 5 were waited for; matrix products, arithmetic and copies ran while one was open for 1% of the time, Pallas kernels for 32%

profile of v5, /device:TPU:0, one launch (start us, length us, event | category | flops | bytes accessed | tf_op | source)
XLA Modules:
  0.0 29.9 jit_solution(4577535064697804762)
XLA Ops:
  0.0 3.0 %collective-permute-start.5 = (bf16[128,1024]{1,0:T(8,128)(2,1)}, bf16[128,1024]{1,0:T(8,128)(2,1)S(1)}, u32[]{:S(2)}, u32[]{:S(2)}) collective-permute-start(bf16[128,1024]{1,0:T(8,128)(2,1)} %bitcast.22), channel_id=1, source_target_pairs={{0,4},{4,0},{8,12},{12,8},{1,5},{5,1},{9,13},{13,9},{2,6},{6,2},{1... | collective-permute-start | bytes 786440 | tf_op jit(solution)/shard_map/ppermute | solution.py:159
  3.0 2.6 %collective-permute-start.6 = (bf16[128,1024]{1,0:T(8,128)(2,1)}, bf16[128,1024]{1,0:T(8,128)(2,1)S(1)}, u32[]{:S(2)}, u32[]{:S(2)}) collective-permute-start(bf16[128,1024]{1,0:T(8,128)(2,1)} %bitcast.23), channel_id=1, source_target_pairs={{0,8},{1,13},{2,10},{3,15},{4,12},{5,9},{6,14},{7,11},{8,0},{9,5},... | collective-permute-start | bytes 786440 | tf_op jit(solution)/shard_map/ppermute | solution.py:210
  5.6 12.1 %conditional.2 = (bf16[128,256]{1,0:T(8,128)(2,1)S(1)}, bf16[128,256]{1,0:T(8,128)(2,1)S(1)}, bf16[128,256]{1,0:T(8,128)(2,1)S(1)}, f32[128,1024]{1,0:T(8,128)S(1)}, s32[8,384]{1,0:T(8,128)S(1)}) conditional(s32[]{:T(128)} %convert_element_type.40, () %tuple.22, (s32[24]{0:T(128)}, s32[24]{0:T(128)}, bf16[128,1024]{1,0:T(8,128)(2,1)}, ...), branch_computations={%region_0.0_spmd, %region_1.2_spmd} | conditional | flops 690198 | bytes 6949250 | solution.py:165
  5.6 3.1 %mirror.1 = (bf16[2,384,256]{2,1,0:T(8,128)(2,1)S(1)}, f32[2,384,256]{2,1,0:T(8,128)S(1)}, s32[8,384]{1,0:T(8,128)S(1)}) custom-call(s32[24]{0:T(128)} %get-tuple-element.93.refs_0_, s32[24]{0:T(128)} %get-tuple-element.94.refs_1_, bf16[128,1024]{1,0:T(8,128)(2,1)} %bitcast.25, bf16[384,1024]{1,0:T(8,128)(2,1)} %get-tuple-element.49.refs_3_, ...), custom_call_target="tpu_custom_call" | custom-call | flops 1024 | bytes 1024 | tf_op jit(solution)/shard_map/cond/branch_1_fun/mirror/pallas_call | solution.py:213
  8.8 0.1 collective-permute-start.3
  8.9 1.7 %collective-permute-done.3 = bf16[2,384,256]{2,1,0:T(8,128)(2,1)S(1)} collective-permute-done((bf16[2,384,256]{2,1,0:T(8,128)(2,1)S(1)}, bf16[2,384,256]{2,1,0:T(8,128)(2,1)S(1)}, u32[]{:S(2)}, u32[]{:S(2)}) %collective-permute-start.3) | collective-permute-done | bytes 393248 | tf_op jit(solution)/shard_map/cond/branch_1_fun/ppermute | solution.py:159
  10.6 0.1 convert_add_fusion
  10.7 1.6 %collective-permute-start.4 = (bf16[384,256]{1,0:T(8,128)(2,1)S(1)}, bf16[384,256]{1,0:T(8,128)(2,1)S(1)}, u32[]{:S(2)}, u32[]{:S(2)}) collective-permute-start(bf16[384,256]{1,0:T(8,128)(2,1)S(1)} %fusion.1), channel_id=1, source_target_pairs={{0,2},{1,3},{2,0},{3,1},{4,6},{5,7},{6,4},{7,5},{8,10},{9,11},{10,... | collective-permute-start | bytes 589832 | tf_op jit(solution)/shard_map/cond/branch_1_fun/ppermute | solution.py:159
  12.2 3.9 %near.1 = f32[4,32,1024]{2,1,0:T(8,128)S(1)} custom-call(s32[1]{0:T(128)} %get-tuple-element.95.refs_0_, s32[1]{0:T(128)} %get-tuple-element.96.refs_1_, bf16[4,32,1024]{2,1,0:T(8,128)(2,1)S(1)} %copy-done, bf16[1,1024,1024]{2,1,0:T(8,128)(2,1)} %get-tuple-element.97.refs_3_), custom_call_target="tpu_custom_call" | custom-call | flops 1024 | bytes 1024 | tf_op jit(solution)/shard_map/cond/branch_1_fun/near/pallas_call | solution.py:233
  16.1 1.5 %collective-permute-done.4 = bf16[384,256]{1,0:T(8,128)(2,1)S(1)} collective-permute-done((bf16[384,256]{1,0:T(8,128)(2,1)S(1)}, bf16[384,256]{1,0:T(8,128)(2,1)S(1)}, u32[]{:S(2)}, u32[]{:S(2)}) %collective-permute-start.4) | collective-permute-done | bytes 196640 | tf_op jit(solution)/shard_map/cond/branch_1_fun/ppermute | solution.py:159
  17.7 0.1 fusion
  17.8 0.0 collective-permute-done.5
  17.8 0.1 collective-permute-start.7
  17.9 0.4 %collective-permute-start.8 = (bf16[128,256]{1,0:T(8,128)(2,1)S(1)}, bf16[128,256]{1,0:T(8,128)(2,1)S(1)}, u32[]{:S(2)}, u32[]{:S(2)}) collective-permute-start(bf16[128,256]{1,0:T(8,128)(2,1)S(1)} %get-tuple-element.86), channel_id=1, source_target_pairs={{0,8},{4,12},{8,0},{12,4},{1,9},{5,13},{9,1},{13,5},{2,10},{6,14},... | collective-permute-start | bytes 196616 | tf_op jit(solution)/shard_map/ppermute | solution.py:159
  18.3 2.5 %collective-permute-start.9 = (bf16[128,256]{1,0:T(8,128)(2,1)S(1)}, bf16[128,256]{1,0:T(8,128)(2,1)S(1)}, u32[]{:S(2)}, u32[]{:S(2)}) collective-permute-start(bf16[128,256]{1,0:T(8,128)(2,1)S(1)} %get-tuple-element.87), channel_id=1, source_target_pairs={{0,12},{4,8},{8,4},{12,0},{1,13},{5,9},{9,5},{13,1},{2,14},{6,10},... | collective-permute-start | bytes 196616 | tf_op jit(solution)/shard_map/ppermute | solution.py:159
  20.7 8.5 %conditional.3 = (f32[128,256]{1,0:T(8,128)S(1)}) conditional(s32[]{:T(128)} %convert_element_type.40, () %tuple.21, (s32[8,384]{1,0:T(8,128)S(1)}, bf16[384,1024]{1,0:T(8,128)(2,1)}, bf16[384,1024]{1,0:T(8,128)(2,1)}, f32[128,1024]{1,0:T(8,128)S(1)}, bf16[128,1024]{1,0:T(8,128)(2,1)S(1)}, /*index=5*/bf16[128,1024]{1,0:T(8,128)(2,1)S(1)}, ...), branch_computations={%region_2.3_spmd, %region_3.4_spmd} | conditional | flops 263190 | bytes 2229614 | solution.py:165
  20.7 2.7 %forward.1 = (bf16[2,128,256]{2,1,0:T(8,128)(2,1)S(1)}, f32[2,128,256]{2,1,0:T(8,128)S(1)}) custom-call(s32[8,384]{1,0:T(8,128)S(1)} %get-tuple-element.61.refs_0_, bf16[384,1024]{1,0:T(8,128)(2,1)} %get-tuple-element.62.refs_1_, bf16[384,1024]{1,0:T(8,128)(2,1)} %get-tuple-element.63.refs_2_, f32[128,1024]{1,0:T(8,128)S(1)} %get-tuple-element.64.refs_3_, ...), custom_call_target="tpu_custom_call" | custom-call | flops 1024 | bytes 1024 | tf_op jit(solution)/shard_map/cond/branch_1_fun/forward/pallas_call | solution.py:253
  23.4 0.1 collective-permute-start
  23.5 0.7 %collective-permute-start.2 = (bf16[128,256]{1,0:T(8,128)(2,1)S(1)}, bf16[128,256]{1,0:T(8,128)(2,1)S(1)}, u32[]{:S(2)}, u32[]{:S(2)}) collective-permute-start(bf16[128,256]{1,0:T(8,128)(2,1)S(1)} %get-tuple-element.71), channel_id=1, source_target_pairs={{0,4},{4,0},{8,12},{12,8},{1,5},{5,1},{9,13},{13,9},{2,6},{6,2},{1... | collective-permute-start | bytes 196616 | tf_op jit(solution)/shard_map/cond/branch_1_fun/ppermute | solution.py:159
  24.2 0.6 %collective-permute-done = bf16[2,128,256]{2,1,0:T(8,128)(2,1)S(1)} collective-permute-done((bf16[2,128,256]{2,1,0:T(8,128)(2,1)S(1)}, bf16[2,128,256]{2,1,0:T(8,128)(2,1)S(1)}, u32[]{:S(2)}, u32[]{:S(2)}) %collective-permute-start) | collective-permute-done | bytes 131104 | tf_op jit(solution)/shard_map/cond/branch_1_fun/ppermute | solution.py:159
  24.9 1.6 %collective-permute-start.1 = (bf16[128,256]{1,0:T(8,128)(2,1)S(1)}, bf16[128,256]{1,0:T(8,128)(2,1)S(1)}, u32[]{:S(2)}, u32[]{:S(2)}) collective-permute-start(bf16[128,256]{1,0:T(8,128)(2,1)S(1)} %fusion.3), channel_id=1, source_target_pairs={{0,2},{1,3},{2,0},{3,1},{4,6},{5,7},{6,4},{7,5},{8,10},{9,11},{10,... | collective-permute-start | bytes 196616 | tf_op jit(solution)/shard_map/cond/branch_1_fun/ppermute | solution.py:159
  26.4 1.6 %collective-permute-done.2 = bf16[128,256]{1,0:T(8,128)(2,1)S(1)} collective-permute-done((bf16[128,256]{1,0:T(8,128)(2,1)S(1)}, bf16[128,256]{1,0:T(8,128)(2,1)S(1)}, u32[]{:S(2)}, u32[]{:S(2)}) %collective-permute-start.2) | collective-permute-done | bytes 65568 | tf_op jit(solution)/shard_map/cond/branch_1_fun/ppermute | solution.py:159
  28.0 1.2 %collective-permute-done.1 = bf16[128,256]{1,0:T(8,128)(2,1)S(1)} collective-permute-done((bf16[128,256]{1,0:T(8,128)(2,1)S(1)}, bf16[128,256]{1,0:T(8,128)(2,1)S(1)}, u32[]{:S(2)}, u32[]{:S(2)}) %collective-permute-start.1) | collective-permute-done | bytes 65568 | tf_op jit(solution)/shard_map/cond/branch_1_fun/ppermute | solution.py:159
  29.3 0.7 %convert_add_fusion.2 = f32[128,256]{1,0:T(8,128)} fusion(bf16[128,256]{1,0:T(8,128)(2,1)S(1)} %collective-permute-done.9, f32[128,256]{1,0:T(8,128)S(1)} %get-tuple-element.111, bf16[128,256]{1,0:T(8,128)(2,1)S(1)} %collective-permute-done.8), kind=kLoop, calls=%fused_computation.10 | loop fusion | flops 131072 | bytes 393216 | tf_op jit(solution)/shard_map/add | solution.py:274
  (11 shorter events, 0.1 us)
Async XLA Ops:
  0.0 17.8 %collective-permute-start.5 = (bf16[128,1024]{1,0:T(8,128)(2,1)}, bf16[128,1024]{1,0:T(8,128)(2,1)S(1)}, u32[]{:S(2)}, u32[]{:S(2)}) collective-permute-start(bf16[128,1024]{1,0:T(8,128)(2,1)} %bitcast.22), channel_id=1, source_target_pairs={{0,4},{4,0},{8,12},{12,8},{1,5},{5,1},{9,13},{13,9},{2,6},{6,2},{1... | collective-permute-start | bytes 786440 | tf_op jit(solution)/shard_map/ppermute | solution.py:159
  3.0 14.8 %collective-permute-start.6 = (bf16[128,1024]{1,0:T(8,128)(2,1)}, bf16[128,1024]{1,0:T(8,128)(2,1)S(1)}, u32[]{:S(2)}, u32[]{:S(2)}) collective-permute-start(bf16[128,1024]{1,0:T(8,128)(2,1)} %bitcast.23), channel_id=1, source_target_pairs={{0,8},{1,13},{2,10},{3,15},{4,12},{5,9},{6,14},{7,11},{8,0},{9,5},... | collective-permute-start | bytes 786440 | tf_op jit(solution)/shard_map/ppermute | solution.py:210
  5.6 6.6 %copy-start = (bf16[4,32,1024]{2,1,0:T(8,128)(2,1)S(1)}, bf16[4,32,1024]{2,1,0:T(8,128)(2,1)}, u32[]{:S(2)}) copy-start(bf16[4,32,1024]{2,1,0:T(8,128)(2,1)} %get-tuple-element.58.refs_2_) | copy-start | bytes 786436 | tf_op jit(solution)/shard_map/cond
  8.8 1.8 %collective-permute-start.3 = (bf16[2,384,256]{2,1,0:T(8,128)(2,1)S(1)}, bf16[2,384,256]{2,1,0:T(8,128)(2,1)S(1)}, u32[]{:S(2)}, u32[]{:S(2)}) collective-permute-start(bf16[2,384,256]{2,1,0:T(8,128)(2,1)S(1)} %get-tuple-element.52), channel_id=1, source_target_pairs={{0,1},{1,0},{2,3},{3,2},{4,5},{5,4},{6,7},{7,6},{8,9},{9,8},{10,11... | collective-permute-start | bytes 1179656 | tf_op jit(solution)/shard_map/cond/branch_1_fun/ppermute | solution.py:159
  10.7 7.0 %collective-permute-start.4 = (bf16[384,256]{1,0:T(8,128)(2,1)S(1)}, bf16[384,256]{1,0:T(8,128)(2,1)S(1)}, u32[]{:S(2)}, u32[]{:S(2)}) collective-permute-start(bf16[384,256]{1,0:T(8,128)(2,1)S(1)} %fusion.1), channel_id=1, source_target_pairs={{0,2},{1,3},{2,0},{3,1},{4,6},{5,7},{6,4},{7,5},{8,10},{9,11},{10,... | collective-permute-start | bytes 589832 | tf_op jit(solution)/shard_map/cond/branch_1_fun/ppermute | solution.py:159
  17.8 3.0 %collective-permute-start.7 = (bf16[128,1024]{1,0:T(8,128)(2,1)S(1)}, bf16[128,1024]{1,0:T(8,128)(2,1)S(1)}, u32[]{:S(2)}, u32[]{:S(2)}) collective-permute-start(bf16[128,1024]{1,0:T(8,128)(2,1)S(1)} %collective-permute-done.6), channel_id=1, source_target_pairs={{0,1},{1,0},{2,3},{3,2},{4,5},{5,4},{6,7},{7,6},{8,9},{9,8},{10,11... | collective-permute-start | bytes 786440 | tf_op jit(solution)/shard_map/ppermute | solution.py:159
  17.9 11.4 %collective-permute-start.8 = (bf16[128,256]{1,0:T(8,128)(2,1)S(1)}, bf16[128,256]{1,0:T(8,128)(2,1)S(1)}, u32[]{:S(2)}, u32[]{:S(2)}) collective-permute-start(bf16[128,256]{1,0:T(8,128)(2,1)S(1)} %get-tuple-element.86), channel_id=1, source_target_pairs={{0,8},{4,12},{8,0},{12,4},{1,9},{5,13},{9,1},{13,5},{2,10},{6,14},... | collective-permute-start | bytes 196616 | tf_op jit(solution)/shard_map/ppermute | solution.py:159
  18.3 11.0 %collective-permute-start.9 = (bf16[128,256]{1,0:T(8,128)(2,1)S(1)}, bf16[128,256]{1,0:T(8,128)(2,1)S(1)}, u32[]{:S(2)}, u32[]{:S(2)}) collective-permute-start(bf16[128,256]{1,0:T(8,128)(2,1)S(1)} %get-tuple-element.87), channel_id=1, source_target_pairs={{0,12},{4,8},{8,4},{12,0},{1,13},{5,9},{9,5},{13,1},{2,14},{6,10},... | collective-permute-start | bytes 196616 | tf_op jit(solution)/shard_map/ppermute | solution.py:159
  23.4 1.4 %collective-permute-start = (bf16[2,128,256]{2,1,0:T(8,128)(2,1)S(1)}, bf16[2,128,256]{2,1,0:T(8,128)(2,1)S(1)}, u32[]{:S(2)}, u32[]{:S(2)}) collective-permute-start(bf16[2,128,256]{2,1,0:T(8,128)(2,1)S(1)} %get-tuple-element.69), channel_id=1, source_target_pairs={{0,1},{1,0},{2,3},{3,2},{4,5},{5,4},{6,7},{7,6},{8,9},{9,8},{10,11... | collective-permute-start | bytes 393224 | tf_op jit(solution)/shard_map/cond/branch_1_fun/ppermute | solution.py:159
  23.5 4.5 %collective-permute-start.2 = (bf16[128,256]{1,0:T(8,128)(2,1)S(1)}, bf16[128,256]{1,0:T(8,128)(2,1)S(1)}, u32[]{:S(2)}, u32[]{:S(2)}) collective-permute-start(bf16[128,256]{1,0:T(8,128)(2,1)S(1)} %get-tuple-element.71), channel_id=1, source_target_pairs={{0,4},{4,0},{8,12},{12,8},{1,5},{5,1},{9,13},{13,9},{2,6},{6,2},{1... | collective-permute-start | bytes 196616 | tf_op jit(solution)/shard_map/cond/branch_1_fun/ppermute | solution.py:159
  24.9 4.3 %collective-permute-start.1 = (bf16[128,256]{1,0:T(8,128)(2,1)S(1)}, bf16[128,256]{1,0:T(8,128)(2,1)S(1)}, u32[]{:S(2)}, u32[]{:S(2)}) collective-permute-start(bf16[128,256]{1,0:T(8,128)(2,1)S(1)} %fusion.3), channel_id=1, source_target_pairs={{0,2},{1,3},{2,0},{3,1},{4,6},{5,7},{6,4},{7,5},{8,10},{9,11},{10,... | collective-permute-start | bytes 196616 | tf_op jit(solution)/shard_map/cond/branch_1_fun/ppermute | solution.py:159

commit v6 on v4

--- a/solution.py
+++ b/solution.py
@@ -59,8 +59,8 @@
 
 def mirror_kernel(
     clusters, exc, rank, others, rows_hbm, cols_hbm, x_hbm, u_hbm, v_hbm,
-    send_ref, keep_ref, lanes_ref, u_ref, v_ref,
-    rows_ref, cols_ref, x_ref, mask_ref, sems,
+    send_ref, keep_ref, lanes_ref,
+    rows_ref, cols_ref, x_ref, u_ref, v_ref, mask_ref, sems,
 ):
     copies = [
         pltpu.make_async_copy(src, dst, sems.at[i])
@@ -121,7 +121,7 @@
     coef = jnp.zeros((exc, v_ref.shape[0]), F32)
     batch = len(pieces) if len(pieces) <= 4 else 1
     for n in range(0, len(pieces), batch):
-        every = dot_t(jnp.concatenate([p[...] for p in pieces[n : n + batch]], axis=0), v_ref[...])
+        every = dot_t(jnp.concatenate(pieces[n : n + batch], axis=0), v_ref[...])
         for i in range(batch):
             first = (group ^ aways[n + i]) * clusters
             for c in range(clusters):
@@ -130,19 +130,32 @@
     return coef
 
 
-def early_kernel(clusters, exc, lanes_ref, v_ref, *refs):
+def early_kernel(clusters, exc, count, lanes_ref, *refs):
+    sources, (coef_ref, *targets) = refs[: 4 + count], refs[4 + count : 9 + count]
+    got_ref, sems = refs[9 + count :]
+    span = clusters * exc
+    moves = [(sources[0], targets[0])]
+    moves += [(src, got_ref.at[i * span : (i + 1) * span]) for i, src in enumerate(sources[4:])]
+    moves += list(zip(sources[1:4], targets[1:]))
+    copies = [pltpu.make_async_copy(src, dst, sems.at[i]) for i, (src, dst) in enumerate(moves)]
+    for copy in copies:
+        copy.start()
     half = lax.rem(lax.axis_index("col"), 2)
-    pieces = refs[:-1]
-    aways = [1] + [2 * t + half for t in range(1, len(pieces))]
-    refs[-1][...] = coef_of(clusters, exc, aways, lanes_ref, v_ref, pieces)
-
-
-def forward_kernel(clusters, exc, lanes_ref, u_ref, v_ref, near_ref, early_ref, *refs):
-    pieces = refs[:-2]
+    for copy in copies[: 1 + count]:
+        copy.wait()
+    pieces = [got_ref[i * span : (i + 1) * span] for i in range(count)]
+    aways = [2 * t + half for t in range(1, count + 1)]
+    coef_ref[...] = coef_of(clusters, exc, aways, lanes_ref, targets[0], pieces)
+    for copy in copies[1 + count :]:
+        copy.wait()
+
+
+def forward_kernel(clusters, exc, lanes_ref, early_ref, v_ref, u_ref, near_ref, whole_ref, handed_ref, *refs):
     send_ref, keep_ref = refs[-2:]
     group = lax.axis_index("row")
     half = lax.rem(lax.axis_index("col"), 2)
-    aways = [2 * t + 3 - half for t in range(len(pieces))]
+    pieces = [jnp.where(half == 0, whole_ref[...], handed_ref[...])] + [ref[...] for ref in refs[:-2]]
+    aways = [1] + [2 * t + 1 - half for t in range(1, len(pieces))]
     coef = early_ref[...] + coef_of(clusters, exc, aways, lanes_ref, v_ref, pieces)
     coef = coef.astype(BF16).astype(F32)
     row_lane = lanes_ref[0:1, :]
@@ -187,53 +200,27 @@
         ]
 
     def pair_sum(send, keep):
-        total = keep + swap(send, "col", col_count, 1).astype(F32)
-
+        return keep + swap(send, "col", col_count, 1).astype(F32)
+
+    def col_sum(total, between=lambda leaving: leaving):
         def chunk(m):
             return lax.dynamic_index_in_dim(total, place // 2 ^ m, 0, keepdims=False)
 
-        return chunk(0), [chunk(m).astype(BF16) for m in range(1, pairs)]
-
-    def col_sum(total, leaving):
+        leaving = between([chunk(m).astype(BF16) for m in range(1, pairs)])
+        out = chunk(0)
         for m, part in enumerate(leaving):
-            total = total + swap(part, "col", col_count, 2 * m + 2).astype(F32)
-        return total
-
-    whole = swap(x, "row", row_count, 1)
-    got = []
-    for d in range(2, row_count, 2):
-        perm = [
-            (r * col_count + c, (r ^ (d + c % 2)) * col_count + c)
+            out = out + swap(part, "col", col_count, 2 * m + 2).astype(F32)
+        return out
+
+    def rows_perm(distance, cores):
+        return [
+            (r * col_count + c, (r ^ (distance + c % cores)) * col_count + c)
             for r in range(row_count)
-            for c in range(col_count)
+            for c in range(0, col_count, 3 - cores)
         ]
-        got.append(lax.ppermute(x, ("row", "col"), perm))
-
-    def local():
-        send, keep, lanes, u_held, v_held = pl.pallas_call(
-            lambda *refs: mirror_kernel(clusters, exc, rank, others, *refs),
-            in_specs=[ANY] * 5,
-            out_specs=[VMEM] * 5,
-            out_shape=shares(others)
-            + [
-                jax.ShapeDtypeStruct((8, entries * rank), jnp.int32),
-                jax.ShapeDtypeStruct(u.shape, BF16),
-                jax.ShapeDtypeStruct(v.shape, BF16),
-            ],
-            scratch_shapes=[
-                pltpu.SMEM(far_rows.shape, jnp.int32),
-                pltpu.SMEM(far_cols.shape, jnp.int32),
-                pltpu.VMEM(x.shape, BF16),
-                pltpu.VMEM((batch * span, entries * rank), BF16),
-                pltpu.SemaphoreType.DMA((5,)),
-            ],
-            compiler_params=params(others),
-            cost_estimate=pl.CostEstimate(flops=1024, bytes_accessed=1024, transcendentals=0),
-            name="mirror",
-        )(far_rows, far_cols, x, u, v)
-        mirror, leaving = pair_sum(send, keep)
-        *leaving, x_near = lax.optimization_barrier((*leaving, charges))
-        near = pl.pallas_call(
+
+    def near_of(x_near):
+        return pl.pallas_call(
             lambda *refs: near_kernel(clusters, exc, *refs),
             in_specs=[SMEM, SMEM, VMEM, VMEM],
             out_specs=VMEM,
@@ -242,33 +229,77 @@
             cost_estimate=pl.CostEstimate(flops=1024, bytes_accessed=1024, transcendentals=0),
             name="near",
         )(near_rows, near_cols, x_near, near_blocks).reshape(span, panels)
-        mirror = col_sum(mirror, leaving).astype(BF16)
-        return [mirror[i * span : (i + 1) * span] for i in range(others)], near, lanes, u_held, v_held
-
-    mirror, near, lanes, u_held, v_held = stage(local)
+
+    whole = lax.ppermute(x, ("row", "col"), rows_perm(1, 1))
+    got = [lax.ppermute(x, ("row", "col"), rows_perm(d, 2)) for d in range(2, row_count, 2)]
+
+    def local():
+        send, keep, lanes = pl.pallas_call(
+            lambda *refs: mirror_kernel(clusters, exc, rank, others, *refs),
+            in_specs=[ANY] * 5,
+            out_specs=[VMEM] * 3,
+            out_shape=shares(others) + [jax.ShapeDtypeStruct((8, entries * rank), jnp.int32)],
+            scratch_shapes=[
+                pltpu.SMEM(far_rows.shape, jnp.int32),
+                pltpu.SMEM(far_cols.shape, jnp.int32),
+                pltpu.VMEM(x.shape, BF16),
+                pltpu.VMEM(u.shape, BF16),
+                pltpu.VMEM(v.shape, BF16),
+                pltpu.VMEM((batch * span, entries * rank), BF16),
+                pltpu.SemaphoreType.DMA((5,)),
+            ],
+            compiler_params=params(others),
+            cost_estimate=pl.CostEstimate(flops=1024, bytes_accessed=1024, transcendentals=0),
+            name="mirror",
+        )(far_rows, far_cols, x, u, v)
+        total = pair_sum(send, keep)
+        beside = swap(total[:, :span].astype(BF16), "row", row_count, 1)
+        held = []
+
+        def with_near(leaving):
+            *leaving, x_near = lax.optimization_barrier((*leaving, charges))
+            held.append(near_of(x_near))
+            return leaving
+
+        mirror = col_sum(total[:, span:], with_near).astype(BF16)
+        return [mirror[i * span : (i + 1) * span] for i in range(others - 1)], beside, held[0], lanes
+
+    mirror, beside, near, lanes = stage(local)
+    from_rows = [swap(part, "row", row_count, i + 2) for i, part in enumerate(mirror)]
     whole, *got, lanes = lax.optimization_barrier((whole, *got, lanes))
-    from_rows = [swap(part, "row", row_count, i + 1) for i, part in enumerate(mirror)]
 
     def forward():
-        early = pl.pallas_call(
-            lambda *refs: early_kernel(clusters, exc, *refs),
-            in_specs=[VMEM] * (3 + len(got)),
-            out_specs=VMEM,
-            out_shape=jax.ShapeDtypeStruct((exc, entries * rank), F32),
+        handed = lax.ppermute(whole, "col", [(c, c + 1) for c in range(0, col_count, 2)])
+        other = [swap(piece, "col", col_count, 1) for piece in got]
+        early, *fetched = pl.pallas_call(
+            lambda *refs: early_kernel(clusters, exc, len(got), *refs),
+            in_specs=[VMEM] + [ANY] * (4 + len(got)),
+            out_specs=[VMEM] * 5,
+            out_shape=[
+                jax.ShapeDtypeStruct((exc, entries * rank), F32),
+                jax.ShapeDtypeStruct(v.shape, BF16),
+                jax.ShapeDtypeStruct(u.shape, BF16),
+                jax.ShapeDtypeStruct(near.shape, F32),
+                jax.ShapeDtypeStruct(x.shape, BF16),
+            ],
+            scratch_shapes=[
+                pltpu.VMEM((len(got) * span, panels), BF16),
+                pltpu.SemaphoreType.DMA((4 + len(got),)),
+            ],
             compiler_params=params(others),
             cost_estimate=pl.CostEstimate(flops=1024, bytes_accessed=1024, transcendentals=0),
             name="early",
-        )(lanes, v_held, whole, *got)
+        )(lanes, v, u, near, whole, *got)
         send, keep = pl.pallas_call(
             lambda *refs: forward_kernel(clusters, exc, *refs),
-            in_specs=[VMEM] * (5 + len(got)),
+            in_specs=[VMEM] * (7 + len(other)),
             out_specs=[VMEM] * 2,
             out_shape=shares(1),
             compiler_params=params(others),
             cost_estimate=pl.CostEstimate(flops=1024, bytes_accessed=1024, transcendentals=0),
             name="forward",
-        )(lanes, u_held, v_held, near, early, *[swap(piece, "col", col_count, 1) for piece in got])
-        return col_sum(*pair_sum(send, keep))
+        )(lanes, early, *fetched, handed, *other)
+        return col_sum(pair_sum(send, keep + beside.astype(F32)))
 
     total = stage(forward)
     for term in from_rows:

time: 35.4 us -> 34 us (0.960)
  Pallas kernels: 11.7 us -> 9.84 us
  starting transfers between devices: 13.5 us -> 14.9 us
  local copies, waits for them, and re-layouts: 1.45 us -> 0.11 us
  waiting for transfers between devices: 6.48 us -> 6.95 us
    ppermute x1 -> x3, starting transfers between devices: 2.59 us -> 8.87 us  [the longest x1 4.92 us: body(): whole = lax.ppermute(x, ('row', 'col'), rows_perm(1, 1))]
    ppermute x9 -> x8, starting transfers between devices: 10.9 us -> 6.06 us  [swap(): return lax.ppermute(value, axis, [(i, i ^ step) for i in range(size)])]
    pallas_call x1, Pallas kernels: 2.31 us -> 1.29 us  [forward(): pl.pallas_call(lambda *refs: forward_kernel(clusters, exc, *refs), in_spe...]
    pallas_call x2, Pallas kernels: 6.26 us -> 5.45 us  [the longest x1 3.89 us: near_of(): pl.pallas_call(lambda *refs: near_kernel(clusters, exc, *refs), in_specs=...]
    cond x4 -> x2, local copies, waits for them, and re-layouts: 0.76 us -> 0.01 us
    slice x1, local copies, waits for them, and re-layouts: 0.64 us -> 0.01 us  [local(): mirror[i * span:(i + 1) * span]]
    ppermute x9 -> x8, waiting for transfers between devices: 6.47 us -> 6.94 us  [swap(): return lax.ppermute(value, axis, [(i, i ^ step) for i in range(size)])]
  transfers between devices with their start and end apart: 10 -> 11, of which waited for: 5 -> 4; matrix products, arithmetic and copies ran while one was open for 5% -> 3% of each run, Pallas kernels for 33% -> 29%
where the time goes in v6:
time: 34 us; the launch traced here: 33.8 us
  starting transfers between devices  14.9 us (44%)
  Pallas kernels  9.84 us (29%)
  waiting for transfers between devices  6.95 us (20%)
  other arithmetic  1.74 us (5%)
    ppermute x8, waiting for transfers between devices, swap(): return lax.ppermute(value, axis, [(i, i ^ step) for i in range(size)])  6.94 us
    ppermute x8, starting transfers between devices, swap(): return lax.ppermute(value, axis, [(i, i ^ step) for i in range(size)])  6.06 us
    ppermute x1, starting transfers between devices, body(): whole = lax.ppermute(x, ('row', 'col'), rows_perm(1, 1))  4.92 us
    pallas_call x1, Pallas kernels, near_of(): pl.pallas_call(lambda *refs: near_kernel(clusters, exc, *refs), in_specs=...  3.89 us
    pallas_call x1, Pallas kernels, local(): pl.pallas_call(lambda *refs: mirror_kernel(clusters, exc, rank, others, *...  3.1 us
    ppermute x1, starting transfers between devices, body(): lax.ppermute(x, ('row', 'col'), rows_perm(d, 2))  2.65 us
    pallas_call x1, Pallas kernels, forward(): pl.pallas_call(lambda *refs: early_kernel(clusters, exc, len(got), *refs)...  1.56 us
    ppermute x1, starting transfers between devices, forward(): lax.ppermute(whole, 'col', [(c, c + 1) for c in range(0, col_count, 2)])  1.3 us
  transfers between devices with their start and end apart: 11, of which 4 were waited for; matrix products, arithmetic and copies ran while one was open for 3% of the time, Pallas kernels for 29%

profile of v6, /device:TPU:0, one launch (start us, length us, event | category | flops | bytes accessed | tf_op | source)
XLA Modules:
  0.0 33.8 jit_solution(3785162571338425468)
XLA Ops:
  0.0 4.9 %collective-permute-start.7 = (bf16[128,1024]{1,0:T(8,128)(2,1)}, bf16[128,1024]{1,0:T(8,128)(2,1)S(1)}, u32[]{:S(2)}, u32[]{:S(2)}) collective-permute-start(bf16[128,1024]{1,0:T(8,128)(2,1)} %bitcast.20), channel_id=1, source_target_pairs={{0,4},{2,6},{4,0},{6,2},{8,12},{10,14},{12,8},{14,10},{16,20},{18,... | collective-permute-start | bytes 786440 | tf_op jit(solution)/shard_map/ppermute | solution.py:233
  4.9 2.7 %collective-permute-start.8 = (bf16[128,1024]{1,0:T(8,128)(2,1)}, bf16[128,1024]{1,0:T(8,128)(2,1)S(1)}, u32[]{:S(2)}, u32[]{:S(2)}) collective-permute-start(bf16[128,1024]{1,0:T(8,128)(2,1)} %bitcast.21), channel_id=1, source_target_pairs={{0,8},{1,13},{2,10},{3,15},{4,12},{5,9},{6,14},{7,11},{8,0},{9,5},... | collective-permute-start | bytes 786440 | tf_op jit(solution)/shard_map/ppermute | solution.py:234
  7.6 12.4 %conditional.2 = (bf16[128,256]{1,0:T(8,128)(2,1)S(1)}, bf16[128,256]{1,0:T(8,128)(2,1)S(1)}, bf16[2,128,256]{2,1,0:T(8,128)(2,1)}, f32[128,1024]{1,0:T(8,128)S(1)}, s32[8,384]{1,0:T(8,128)S(1)}) conditional(s32[]{:T(128)} %convert_element_type.41, () %tuple.22, (s32[24]{0:T(128)}, s32[24]{0:T(128)}, bf16[128,1024]{1,0:T(8,128)(2,1)}, ...), branch_computations={%region_0.0_spmd, %region_1.2_spmd} | conditional | flops 591894 | bytes 7997866 | solution.py:178
  7.6 3.1 %mirror.1 = (bf16[2,384,256]{2,1,0:T(8,128)(2,1)S(1)}, f32[2,384,256]{2,1,0:T(8,128)S(1)}, s32[8,384]{1,0:T(8,128)S(1)}) custom-call(s32[24]{0:T(128)} %get-tuple-element.95.refs_0_, s32[24]{0:T(128)} %get-tuple-element.96.refs_1_, bf16[128,1024]{1,0:T(8,128)(2,1)} %bitcast.23, bf16[384,1024]{1,0:T(8,128)(2,1)} %get-tuple-element.47.refs_3_, ...), custom_call_target="tpu_custom_call" | custom-call | flops 1024 | bytes 1024 | tf_op jit(solution)/shard_map/cond/branch_1_fun/mirror/pallas_call | solution.py:237
  10.7 0.1 collective-permute-start.4
  10.8 1.7 %collective-permute-done.4 = bf16[2,384,256]{2,1,0:T(8,128)(2,1)S(1)} collective-permute-done((bf16[2,384,256]{2,1,0:T(8,128)(2,1)S(1)}, bf16[2,384,256]{2,1,0:T(8,128)(2,1)S(1)}, u32[]{:S(2)}, u32[]{:S(2)}) %collective-permute-start.4) | collective-permute-done | bytes 393248 | tf_op jit(solution)/shard_map/cond/branch_1_fun/ppermute | solution.py:172
  12.5 0.1 convert_add_fusion
  12.7 1.6 %collective-permute-start.5 = (bf16[256,256]{1,0:T(8,128)(2,1)S(1)}, bf16[256,256]{1,0:T(8,128)(2,1)S(1)}, u32[]{:S(2)}, u32[]{:S(2)}) collective-permute-start(bf16[256,256]{1,0:T(8,128)(2,1)S(1)} %fusion.1), channel_id=1, source_target_pairs={{0,2},{1,3},{2,0},{3,1},{4,6},{5,7},{6,4},{7,5},{8,10},{9,11},{10,... | collective-permute-start | bytes 393224 | tf_op jit(solution)/shard_map/cond/branch_1_fun/ppermute | solution.py:172
  14.2 0.5 %collective-permute-start.6 = (bf16[2,128,256]{2,1,0:T(8,128)(2,1)S(1)}, bf16[2,128,256]{2,1,0:T(8,128)(2,1)}, u32[]{:S(2)}, u32[]{:S(2)}) collective-permute-start(bf16[2,128,256]{2,1,0:T(8,128)(2,1)S(1)} %slice.18), channel_id=1, source_target_pairs={{0,4},{4,0},{8,12},{12,8},{1,5},{5,1},{9,13},{13,9},{2,6},{6,2},{1... | collective-permute-start | bytes 393224 | tf_op jit(solution)/shard_map/cond/branch_1_fun/ppermute | solution.py:172
  14.7 3.9 %near.1 = f32[4,32,1024]{2,1,0:T(8,128)S(1)} custom-call(s32[1]{0:T(128)} %get-tuple-element.97.refs_0_, s32[1]{0:T(128)} %get-tuple-element.98.refs_1_, bf16[4,32,1024]{2,1,0:T(8,128)(2,1)S(1)} %copy-done, bf16[1,1024,1024]{2,1,0:T(8,128)(2,1)} %get-tuple-element.99.refs_3_), custom_call_target="tpu_custom_call" | custom-call | flops 1024 | bytes 1024 | tf_op jit(solution)/shard_map/cond/branch_1_fun/near/pallas_call | solution.py:223
  18.7 1.3 %collective-permute-done.6 = bf16[2,128,256]{2,1,0:T(8,128)(2,1)} collective-permute-done((bf16[2,128,256]{2,1,0:T(8,128)(2,1)S(1)}, bf16[2,128,256]{2,1,0:T(8,128)(2,1)}, u32[]{:S(2)}, u32[]{:S(2)}) %collective-permute-start.6) | collective-permute-done | bytes 131104 | tf_op jit(solution)/shard_map/cond/branch_1_fun/ppermute | solution.py:172
  20.0 1.7 %collective-permute-start.10 = (bf16[128,256]{1,0:T(8,128)(2,1)S(1)}, bf16[128,256]{1,0:T(8,128)(2,1)S(1)}, u32[]{:S(2)}, u32[]{:S(2)}) collective-permute-start(bf16[128,256]{1,0:T(8,128)(2,1)S(1)} %get-tuple-element.89), channel_id=1, source_target_pairs={{0,12},{4,8},{8,4},{12,0},{1,13},{5,9},{9,5},{13,1},{2,14},{6,10},... | collective-permute-start | bytes 196616 | tf_op jit(solution)/shard_map/ppermute | solution.py:172
  21.7 0.1 collective-permute-start.9
  21.8 11.2 %conditional.3 = (f32[128,256]{1,0:T(8,128)S(1)}) conditional(s32[]{:T(128)} %convert_element_type.41, () %tuple.21, (s32[8,384]{1,0:T(8,128)S(1)}, bf16[384,1024]{1,0:T(8,128)(2,1)}, bf16[384,1024]{1,0:T(8,128)(2,1)}, f32[128,1024]{1,0:T(8,128)S(1)}, bf16[128,1024]{1,0:T(8,128)(2,1)S(1)}, /*index=5*/bf16[128,1024]{1,0:T(8,128)(2,1)S(1)}, ...), branch_computations={%region_2.3_spmd, %region_3.4_spmd} | conditional | flops 329750 | bytes 4131222 | solution.py:178
  21.8 1.3 %collective-permute-start = (bf16[128,1024]{1,0:T(8,128)(2,1)S(1)}, bf16[128,1024]{1,0:T(8,128)(2,1)S(1)}, u32[]{:S(2)}, u32[]{:S(2)}) collective-permute-start(bf16[128,1024]{1,0:T(8,128)(2,1)S(1)} %get-tuple-element.63.refs_4_), channel_id=1, source_target_pairs={{0,1},{2,3},{4,5},{6,7},{8,9},{10,11},{12,13},{14,15},{16,17},{18,... | collective-permute-start | bytes 786440 | tf_op jit(solution)/shard_map/cond/branch_1_fun/ppermute | solution.py:272
  23.1 0.1 collective-permute-start.1
  23.2 1.6 %early.1 = (f32[32,384]{1,0:T(8,128)S(1)}, bf16[384,1024]{1,0:T(8,128)(2,1)S(1)}, bf16[384,1024]{1,0:T(8,128)(2,1)S(1)}, f32[128,1024]{1,0:T(8,128)S(1)}, bf16[128,1024]{1,0:T(8,128)(2,1)S(1)}) custom-call(s32[8,384]{1,0:T(8,128)S(1)} %get-tuple-element.59.refs_0_, bf16[384,1024]{1,0:T(8,128)(2,1)} %get-tuple-element.60.refs_1_, ...), custom_call_target="tpu_custom_call" | custom-call | flops 1024 | bytes 1024 | tf_op jit(solution)/shard_map/cond/branch_1_fun/early/pallas_call | solution.py:274
  24.8 1.3 %forward.1 = (bf16[2,128,256]{2,1,0:T(8,128)(2,1)S(1)}, f32[2,128,256]{2,1,0:T(8,128)S(1)}) custom-call(s32[8,384]{1,0:T(8,128)S(1)} %get-tuple-element.59.refs_0_, f32[32,384]{1,0:T(8,128)S(1)} %get-tuple-element.65.refs_1_, bf16[384,1024]{1,0:T(8,128)(2,1)S(1)} %get-tuple-element.66.refs_2_, bf16[384,1024]{1,0:T(8,128)(2,1)S(1)} %get-tuple-element.67.refs_3_, ...), custom_call_target="tpu_custom_call" | custom-call | flops 1024 | bytes 1024 | tf_op jit(solution)/shard_map/cond/branch_1_fun/forward/pallas_call | solution.py:293
  26.1 0.6 %collective-permute-start.2 = (bf16[2,128,256]{2,1,0:T(8,128)(2,1)S(1)}, bf16[2,128,256]{2,1,0:T(8,128)(2,1)S(1)}, u32[]{:S(2)}, u32[]{:S(2)}) collective-permute-start(bf16[2,128,256]{2,1,0:T(8,128)(2,1)S(1)} %get-tuple-element.72), channel_id=1, source_target_pairs={{0,1},{1,0},{2,3},{3,2},{4,5},{5,4},{6,7},{7,6},{8,9},{9,8},{10,11... | collective-permute-start | bytes 393224 | tf_op jit(solution)/shard_map/cond/branch_1_fun/ppermute | solution.py:172
  26.7 1.0 %collective-permute-done.2 = bf16[2,128,256]{2,1,0:T(8,128)(2,1)S(1)} collective-permute-done((bf16[2,128,256]{2,1,0:T(8,128)(2,1)S(1)}, bf16[2,128,256]{2,1,0:T(8,128)(2,1)S(1)}, u32[]{:S(2)}, u32[]{:S(2)}) %collective-permute-start.2) | collective-permute-done | bytes 131104 | tf_op jit(solution)/shard_map/cond/branch_1_fun/ppermute | solution.py:172
  27.7 0.9 %convert_add_fusion.1 = f32[2,128,256]{2,1,0:T(8,128)S(1)} fusion(bf16[2,128,256]{2,1,0:T(8,128)(2,1)S(1)} %collective-permute-done.2, f32[2,128,256]{2,1,0:T(8,128)S(1)} %get-tuple-element.70, bf16[2,128,256]{2,1,0:T(8,128)(2,1)} %get-tuple-element.71), kind=kLoop, calls=%fused_computation.6 | loop fusion | flops 262144 | bytes 786432 | tf_op jit(solution)/shard_map/cond/branch_1_fun/add | solution.py:203
  28.6 1.5 %collective-permute-start.3 = (bf16[128,256]{1,0:T(8,128)(2,1)S(1)}, bf16[128,256]{1,0:T(8,128)(2,1)S(1)}, u32[]{:S(2)}, u32[]{:S(2)}) collective-permute-start(bf16[128,256]{1,0:T(8,128)(2,1)S(1)} %fusion.2), channel_id=1, source_target_pairs={{0,2},{1,3},{2,0},{3,1},{4,6},{5,7},{6,4},{7,5},{8,10},{9,11},{10,... | collective-permute-start | bytes 196616 | tf_op jit(solution)/shard_map/cond/branch_1_fun/ppermute | solution.py:172
  30.1 3.0 %collective-permute-done.3 = bf16[128,256]{1,0:T(8,128)(2,1)S(1)} collective-permute-done((bf16[128,256]{1,0:T(8,128)(2,1)S(1)}, bf16[128,256]{1,0:T(8,128)(2,1)S(1)}, u32[]{:S(2)}, u32[]{:S(2)}) %collective-permute-start.3) | collective-permute-done | bytes 65568 | tf_op jit(solution)/shard_map/cond/branch_1_fun/ppermute | solution.py:172
  33.1 0.7 %convert_add_fusion.2 = f32[128,256]{1,0:T(8,128)} fusion(bf16[128,256]{1,0:T(8,128)(2,1)S(1)} %collective-permute-done.10, f32[128,256]{1,0:T(8,128)S(1)} %get-tuple-element.112, bf16[128,256]{1,0:T(8,128)(2,1)S(1)} %collective-permute-done.9), kind=kLoop, calls=%fused_computation.10 | loop fusion | flops 131072 | bytes 393216 | tf_op jit(solution)/shard_map/add | solution.py:306
  (16 shorter events, 0.2 us)
Async XLA Ops:
  0.0 21.8 %collective-permute-start.7 = (bf16[128,1024]{1,0:T(8,128)(2,1)}, bf16[128,1024]{1,0:T(8,128)(2,1)S(1)}, u32[]{:S(2)}, u32[]{:S(2)}) collective-permute-start(bf16[128,1024]{1,0:T(8,128)(2,1)} %bitcast.20), channel_id=1, source_target_pairs={{0,4},{2,6},{4,0},{6,2},{8,12},{10,14},{12,8},{14,10},{16,20},{18,... | collective-permute-start | bytes 786440 | tf_op jit(solution)/shard_map/ppermute | solution.py:233
  4.9 16.9 %collective-permute-start.8 = (bf16[128,1024]{1,0:T(8,128)(2,1)}, bf16[128,1024]{1,0:T(8,128)(2,1)S(1)}, u32[]{:S(2)}, u32[]{:S(2)}) collective-permute-start(bf16[128,1024]{1,0:T(8,128)(2,1)} %bitcast.21), channel_id=1, source_target_pairs={{0,8},{1,13},{2,10},{3,15},{4,12},{5,9},{6,14},{7,11},{8,0},{9,5},... | collective-permute-start | bytes 786440 | tf_op jit(solution)/shard_map/ppermute | solution.py:234
  10.7 4.0 %copy-start = (bf16[4,32,1024]{2,1,0:T(8,128)(2,1)S(1)}, bf16[4,32,1024]{2,1,0:T(8,128)(2,1)}, u32[]{:S(2)}) copy-start(bf16[4,32,1024]{2,1,0:T(8,128)(2,1)} %get-tuple-element.56.refs_2_) | copy-start | bytes 786436 | tf_op jit(solution)/shard_map/cond
  10.7 1.8 %collective-permute-start.4 = (bf16[2,384,256]{2,1,0:T(8,128)(2,1)S(1)}, bf16[2,384,256]{2,1,0:T(8,128)(2,1)S(1)}, u32[]{:S(2)}, u32[]{:S(2)}) collective-permute-start(bf16[2,384,256]{2,1,0:T(8,128)(2,1)S(1)} %get-tuple-element.50), channel_id=1, source_target_pairs={{0,1},{1,0},{2,3},{3,2},{4,5},{5,4},{6,7},{7,6},{8,9},{9,8},{10,11... | collective-permute-start | bytes 1179656 | tf_op jit(solution)/shard_map/cond/branch_1_fun/ppermute | solution.py:172
  12.7 6.0 %collective-permute-start.5 = (bf16[256,256]{1,0:T(8,128)(2,1)S(1)}, bf16[256,256]{1,0:T(8,128)(2,1)S(1)}, u32[]{:S(2)}, u32[]{:S(2)}) collective-permute-start(bf16[256,256]{1,0:T(8,128)(2,1)S(1)} %fusion.1), channel_id=1, source_target_pairs={{0,2},{1,3},{2,0},{3,1},{4,6},{5,7},{6,4},{7,5},{8,10},{9,11},{10,... | collective-permute-start | bytes 393224 | tf_op jit(solution)/shard_map/cond/branch_1_fun/ppermute | solution.py:172
  14.2 5.8 %collective-permute-start.6 = (bf16[2,128,256]{2,1,0:T(8,128)(2,1)S(1)}, bf16[2,128,256]{2,1,0:T(8,128)(2,1)}, u32[]{:S(2)}, u32[]{:S(2)}) collective-permute-start(bf16[2,128,256]{2,1,0:T(8,128)(2,1)S(1)} %slice.18), channel_id=1, source_target_pairs={{0,4},{4,0},{8,12},{12,8},{1,5},{5,1},{9,13},{13,9},{2,6},{6,2},{1... | collective-permute-start | bytes 393224 | tf_op jit(solution)/shard_map/cond/branch_1_fun/ppermute | solution.py:172
  20.0 13.1 %collective-permute-start.10 = (bf16[128,256]{1,0:T(8,128)(2,1)S(1)}, bf16[128,256]{1,0:T(8,128)(2,1)S(1)}, u32[]{:S(2)}, u32[]{:S(2)}) collective-permute-start(bf16[128,256]{1,0:T(8,128)(2,1)S(1)} %get-tuple-element.89), channel_id=1, source_target_pairs={{0,12},{4,8},{8,4},{12,0},{1,13},{5,9},{9,5},{13,1},{2,14},{6,10},... | collective-permute-start | bytes 196616 | tf_op jit(solution)/shard_map/ppermute | solution.py:172
  21.7 11.4 %collective-permute-start.9 = (bf16[128,256]{1,0:T(8,128)(2,1)S(1)}, bf16[128,256]{1,0:T(8,128)(2,1)S(1)}, u32[]{:S(2)}, u32[]{:S(2)}) collective-permute-start(bf16[128,256]{1,0:T(8,128)(2,1)S(1)} %get-tuple-element.88), channel_id=1, source_target_pairs={{0,8},{4,12},{8,0},{12,4},{1,9},{5,13},{9,1},{13,5},{2,10},{6,14},... | collective-permute-start | bytes 196616 | tf_op jit(solution)/shard_map/ppermute | solution.py:172
  21.8 3.0 %collective-permute-start = (bf16[128,1024]{1,0:T(8,128)(2,1)S(1)}, bf16[128,1024]{1,0:T(8,128)(2,1)S(1)}, u32[]{:S(2)}, u32[]{:S(2)}) collective-permute-start(bf16[128,1024]{1,0:T(8,128)(2,1)S(1)} %get-tuple-element.63.refs_4_), channel_id=1, source_target_pairs={{0,1},{2,3},{4,5},{6,7},{8,9},{10,11},{12,13},{14,15},{16,17},{18,... | collective-permute-start | bytes 786440 | tf_op jit(solution)/shard_map/cond/branch_1_fun/ppermute | solution.py:272
  23.1 1.7 %collective-permute-start.1 = (bf16[128,1024]{1,0:T(8,128)(2,1)S(1)}, bf16[128,1024]{1,0:T(8,128)(2,1)S(1)}, u32[]{:S(2)}, u32[]{:S(2)}) collective-permute-start(bf16[128,1024]{1,0:T(8,128)(2,1)S(1)} %get-tuple-element.64.refs_5_), channel_id=1, source_target_pairs={{0,1},{1,0},{2,3},{3,2},{4,5},{5,4},{6,7},{7,6},{8,9},{9,8},{10,11... | collective-permute-start | bytes 786440 | tf_op jit(solution)/shard_map/cond/branch_1_fun/ppermute | solution.py:172
  26.1 1.5 %collective-permute-start.2 = (bf16[2,128,256]{2,1,0:T(8,128)(2,1)S(1)}, bf16[2,128,256]{2,1,0:T(8,128)(2,1)S(1)}, u32[]{:S(2)}, u32[]{:S(2)}) collective-permute-start(bf16[2,128,256]{2,1,0:T(8,128)(2,1)S(1)} %get-tuple-element.72), channel_id=1, source_target_pairs={{0,1},{1,0},{2,3},{3,2},{4,5},{5,4},{6,7},{7,6},{8,9},{9,8},{10,11... | collective-permute-start | bytes 393224 | tf_op jit(solution)/shard_map/cond/branch_1_fun/ppermute | solution.py:172
  28.6 4.4 %collective-permute-start.3 = (bf16[128,256]{1,0:T(8,128)(2,1)S(1)}, bf16[128,256]{1,0:T(8,128)(2,1)S(1)}, u32[]{:S(2)}, u32[]{:S(2)}) collective-permute-start(bf16[128,256]{1,0:T(8,128)(2,1)S(1)} %fusion.2), channel_id=1, source_target_pairs={{0,2},{1,3},{2,0},{3,1},{4,6},{5,7},{6,4},{7,5},{8,10},{9,11},{10,... | collective-permute-start | bytes 196616 | tf_op jit(solution)/shard_map/cond/branch_1_fun/ppermute | solution.py:172

commit v7 on v6

--- a/solution.py
+++ b/solution.py
@@ -131,31 +131,31 @@
 
 
 def early_kernel(clusters, exc, count, lanes_ref, *refs):
-    sources, (coef_ref, *targets) = refs[: 4 + count], refs[4 + count : 9 + count]
-    got_ref, sems = refs[9 + count :]
+    sources, (coef_ref, *targets) = refs[: 3 + count], refs[3 + count : 7 + count]
+    pieces_ref, sems = refs[7 + count :]
     span = clusters * exc
     moves = [(sources[0], targets[0])]
-    moves += [(src, got_ref.at[i * span : (i + 1) * span]) for i, src in enumerate(sources[4:])]
-    moves += list(zip(sources[1:4], targets[1:]))
+    moves += [(src, pieces_ref.at[i * span : (i + 1) * span]) for i, src in enumerate(sources[3:])]
+    moves += list(zip(sources[1:3], targets[1:]))
     copies = [pltpu.make_async_copy(src, dst, sems.at[i]) for i, (src, dst) in enumerate(moves)]
     for copy in copies:
         copy.start()
     half = lax.rem(lax.axis_index("col"), 2)
     for copy in copies[: 1 + count]:
         copy.wait()
-    pieces = [got_ref[i * span : (i + 1) * span] for i in range(count)]
-    aways = [2 * t + half for t in range(1, count + 1)]
+    pieces = [pieces_ref[i * span : (i + 1) * span] for i in range(count)]
+    aways = [1] + [2 * t + half for t in range(1, count)]
     coef_ref[...] = coef_of(clusters, exc, aways, lanes_ref, targets[0], pieces)
     for copy in copies[1 + count :]:
         copy.wait()
 
 
-def forward_kernel(clusters, exc, lanes_ref, early_ref, v_ref, u_ref, near_ref, whole_ref, handed_ref, *refs):
+def forward_kernel(clusters, exc, lanes_ref, early_ref, v_ref, u_ref, near_ref, *refs):
     send_ref, keep_ref = refs[-2:]
     group = lax.axis_index("row")
     half = lax.rem(lax.axis_index("col"), 2)
-    pieces = [jnp.where(half == 0, whole_ref[...], handed_ref[...])] + [ref[...] for ref in refs[:-2]]
-    aways = [1] + [2 * t + 1 - half for t in range(1, len(pieces))]
+    pieces = [ref[...] for ref in refs[:-2]]
+    aways = [2 * t + 3 - half for t in range(len(pieces))]
     coef = early_ref[...] + coef_of(clusters, exc, aways, lanes_ref, v_ref, pieces)
     coef = coef.astype(BF16).astype(F32)
     row_lane = lanes_ref[0:1, :]
@@ -212,13 +212,6 @@
             out = out + swap(part, "col", col_count, 2 * m + 2).astype(F32)
         return out
 
-    def rows_perm(distance, cores):
-        return [
-            (r * col_count + c, (r ^ (distance + c % cores)) * col_count + c)
-            for r in range(row_count)
-            for c in range(0, col_count, 3 - cores)
-        ]
-
     def near_of(x_near):
         return pl.pallas_call(
             lambda *refs: near_kernel(clusters, exc, *refs),
@@ -230,8 +223,15 @@
             name="near",
         )(near_rows, near_cols, x_near, near_blocks).reshape(span, panels)
 
-    whole = lax.ppermute(x, ("row", "col"), rows_perm(1, 1))
-    got = [lax.ppermute(x, ("row", "col"), rows_perm(d, 2)) for d in range(2, row_count, 2)]
+    whole = swap(x, "row", row_count, 1)
+    got = []
+    for d in range(2, row_count, 2):
+        perm = [
+            (r * col_count + c, (r ^ (d + c % 2)) * col_count + c)
+            for r in range(row_count)
+            for c in range(col_count)
+        ]
+        got.append(lax.ppermute(x, ("row", "col"), perm))
 
     def local():
         send, keep, lanes = pl.pallas_call(
@@ -253,7 +253,6 @@
             name="mirror",
         )(far_rows, far_cols, x, u, v)
         total = pair_sum(send, keep)
-        beside = swap(total[:, :span].astype(BF16), "row", row_count, 1)
         held = []
 
         def with_near(leaving):
@@ -261,29 +260,27 @@
             held.append(near_of(x_near))
             return leaving
 
-        mirror = col_sum(total[:, span:], with_near).astype(BF16)
-        return [mirror[i * span : (i + 1) * span] for i in range(others - 1)], beside, held[0], lanes
-
-    mirror, beside, near, lanes = stage(local)
-    from_rows = [swap(part, "row", row_count, i + 2) for i, part in enumerate(mirror)]
+        mirror = col_sum(total, with_near).astype(BF16)
+        return [mirror[i * span : (i + 1) * span] for i in range(others)], held[0], lanes
+
+    mirror, near, lanes = stage(local)
+    from_rows = [swap(mirror[d - 1], "row", row_count, d) for d in range(2, row_count)]
     whole, *got, lanes = lax.optimization_barrier((whole, *got, lanes))
 
     def forward():
-        handed = lax.ppermute(whole, "col", [(c, c + 1) for c in range(0, col_count, 2)])
         other = [swap(piece, "col", col_count, 1) for piece in got]
         early, *fetched = pl.pallas_call(
-            lambda *refs: early_kernel(clusters, exc, len(got), *refs),
+            lambda *refs: early_kernel(clusters, exc, 1 + len(got), *refs),
             in_specs=[VMEM] + [ANY] * (4 + len(got)),
-            out_specs=[VMEM] * 5,
+            out_specs=[VMEM] * 4,
             out_shape=[
                 jax.ShapeDtypeStruct((exc, entries * rank), F32),
                 jax.ShapeDtypeStruct(v.shape, BF16),
                 jax.ShapeDtypeStruct(u.shape, BF16),
                 jax.ShapeDtypeStruct(near.shape, F32),
-                jax.ShapeDtypeStruct(x.shape, BF16),
             ],
             scratch_shapes=[
-                pltpu.VMEM((len(got) * span, panels), BF16),
+                pltpu.VMEM(((1 + len(got)) * span, panels), BF16),
                 pltpu.SemaphoreType.DMA((4 + len(got),)),
             ],
             compiler_params=params(others),
@@ -292,14 +289,14 @@
         )(lanes, v, u, near, whole, *got)
         send, keep = pl.pallas_call(
             lambda *refs: forward_kernel(clusters, exc, *refs),
-            in_specs=[VMEM] * (7 + len(other)),
+            in_specs=[VMEM] * (5 + len(other)),
             out_specs=[VMEM] * 2,
             out_shape=shares(1),
             compiler_params=params(others),
             cost_estimate=pl.CostEstimate(flops=1024, bytes_accessed=1024, transcendentals=0),
             name="forward",
-        )(lanes, early, *fetched, handed, *other)
-        return col_sum(pair_sum(send, keep + beside.astype(F32)))
+        )(lanes, early, *fetched, *other)
+        return col_sum(pair_sum(send, keep)) + swap(mirror[0], "row", row_count, 1).astype(F32)
 
     total = stage(forward)
     for term in from_rows:

time: 34 us -> 30.6 us (0.900)
  starting transfers between devices: 14.9 us -> 12.9 us
  other arithmetic: 1.74 us -> 0.85 us
  waiting for transfers between devices: 6.95 us -> 6.42 us
    ppermute x3 -> x1, starting transfers between devices: 8.87 us -> 2.59 us  [body(): got.append(lax.ppermute(x, ('row', 'col'), perm))]
    ppermute x8 -> x9, starting transfers between devices: 6.06 us -> 10.3 us  [swap(): return lax.ppermute(value, axis, [(i, i ^ step) for i in range(size)])]
    add x2, other arithmetic: 1.02 us -> 0.1 us  [pair_sum(): return keep + swap(send, 'col', col_count, 1).astype(F32)]
    ppermute x8 -> x9, waiting for transfers between devices: 6.94 us -> 6.42 us  [swap(): return lax.ppermute(value, axis, [(i, i ^ step) for i in range(size)])]
  transfers between devices with their start and end apart: 11 -> 10, of which waited for: 4 -> 5; matrix products, arithmetic and copies ran while one was open for 3% -> 1% of each run, Pallas kernels for 29% -> 33%
where the time goes in v7:
time: 30.6 us; the launch traced here: 30.4 us
  starting transfers between devices  12.9 us (42%)
  Pallas kernels  9.95 us (33%)
  waiting for transfers between devices  6.42 us (21%)
  other arithmetic  0.85 us (3%)
    ppermute x9, starting transfers between devices, swap(): return lax.ppermute(value, axis, [(i, i ^ step) for i in range(size)])  10.3 us
    ppermute x9, waiting for transfers between devices, swap(): return lax.ppermute(value, axis, [(i, i ^ step) for i in range(size)])  6.42 us
    pallas_call x1, Pallas kernels, near_of(): pl.pallas_call(lambda *refs: near_kernel(clusters, exc, *refs), in_specs=...  3.89 us
    pallas_call x1, Pallas kernels, local(): pl.pallas_call(lambda *refs: mirror_kernel(clusters, exc, rank, others, *...  3.14 us
    ppermute x1, starting transfers between devices, body(): got.append(lax.ppermute(x, ('row', 'col'), perm))  2.59 us
    pallas_call x1, Pallas kernels, forward(): pl.pallas_call(lambda *refs: early_kernel(clusters, exc, 1 + len(got), *r...  1.65 us
    pallas_call x1, Pallas kernels, forward(): pl.pallas_call(lambda *refs: forward_kernel(clusters, exc, *refs), in_spe...  1.27 us
    add x1, other arithmetic, body(): total = total + term.astype(F32)  0.68 us
  transfers between devices with their start and end apart: 10, of which 5 were waited for; matrix products, arithmetic and copies ran while one was open for 1% of the time, Pallas kernels for 33%

profile of v7, /device:TPU:0, one launch (start us, length us, event | category | flops | bytes accessed | tf_op | source)
XLA Modules:
  0.0 30.4 jit_solution(8064240861510648361)
XLA Ops:
  0.0 3.0 %collective-permute-start.6 = (bf16[128,1024]{1,0:T(8,128)(2,1)}, bf16[128,1024]{1,0:T(8,128)(2,1)S(1)}, u32[]{:S(2)}, u32[]{:S(2)}) collective-permute-start(bf16[128,1024]{1,0:T(8,128)(2,1)} %bitcast.22), channel_id=1, source_target_pairs={{0,4},{4,0},{8,12},{12,8},{1,5},{5,1},{9,13},{13,9},{2,6},{6,2},{1... | collective-permute-start | bytes 786440 | tf_op jit(solution)/shard_map/ppermute | solution.py:172
  3.0 2.6 %collective-permute-start.7 = (bf16[128,1024]{1,0:T(8,128)(2,1)}, bf16[128,1024]{1,0:T(8,128)(2,1)S(1)}, u32[]{:S(2)}, u32[]{:S(2)}) collective-permute-start(bf16[128,1024]{1,0:T(8,128)(2,1)} %bitcast.23), channel_id=1, source_target_pairs={{0,8},{1,13},{2,10},{3,15},{4,12},{5,9},{6,14},{7,11},{8,0},{9,5},... | collective-permute-start | bytes 786440 | tf_op jit(solution)/shard_map/ppermute | solution.py:234
  5.6 12.1 %conditional.2 = (bf16[128,256]{1,0:T(8,128)(2,1)S(1)}, bf16[128,256]{1,0:T(8,128)(2,1)S(1)}, bf16[128,256]{1,0:T(8,128)(2,1)S(1)}, f32[128,1024]{1,0:T(8,128)S(1)}, s32[8,384]{1,0:T(8,128)S(1)}) conditional(s32[]{:T(128)} %convert_element_type.40, () %tuple.22, (s32[24]{0:T(128)}, s32[24]{0:T(128)}, bf16[128,1024]{1,0:T(8,128)(2,1)}, ...), branch_computations={%region_0.0_spmd, %region_1.2_spmd} | conditional | flops 690198 | bytes 6949250 | solution.py:178
  5.6 3.1 %mirror.1 = (bf16[2,384,256]{2,1,0:T(8,128)(2,1)S(1)}, f32[2,384,256]{2,1,0:T(8,128)S(1)}, s32[8,384]{1,0:T(8,128)S(1)}) custom-call(s32[24]{0:T(128)} %get-tuple-element.94.refs_0_, s32[24]{0:T(128)} %get-tuple-element.95.refs_1_, bf16[128,1024]{1,0:T(8,128)(2,1)} %bitcast.25, bf16[384,1024]{1,0:T(8,128)(2,1)} %get-tuple-element.47.refs_3_, ...), custom_call_target="tpu_custom_call" | custom-call | flops 1024 | bytes 1024 | tf_op jit(solution)/shard_map/cond/branch_1_fun/mirror/pallas_call | solution.py:237
  8.8 0.1 collective-permute-start.4
  8.9 1.7 %collective-permute-done.4 = bf16[2,384,256]{2,1,0:T(8,128)(2,1)S(1)} collective-permute-done((bf16[2,384,256]{2,1,0:T(8,128)(2,1)S(1)}, bf16[2,384,256]{2,1,0:T(8,128)(2,1)S(1)}, u32[]{:S(2)}, u32[]{:S(2)}) %collective-permute-start.4) | collective-permute-done | bytes 393248 | tf_op jit(solution)/shard_map/cond/branch_1_fun/ppermute | solution.py:172
  10.6 0.1 convert_add_fusion
  10.7 1.6 %collective-permute-start.5 = (bf16[384,256]{1,0:T(8,128)(2,1)S(1)}, bf16[384,256]{1,0:T(8,128)(2,1)S(1)}, u32[]{:S(2)}, u32[]{:S(2)}) collective-permute-start(bf16[384,256]{1,0:T(8,128)(2,1)S(1)} %fusion.1), channel_id=1, source_target_pairs={{0,2},{1,3},{2,0},{3,1},{4,6},{5,7},{6,4},{7,5},{8,10},{9,11},{10,... | collective-permute-start | bytes 589832 | tf_op jit(solution)/shard_map/cond/branch_1_fun/ppermute | solution.py:172
  12.2 3.9 %near.1 = f32[4,32,1024]{2,1,0:T(8,128)S(1)} custom-call(s32[1]{0:T(128)} %get-tuple-element.96.refs_0_, s32[1]{0:T(128)} %get-tuple-element.97.refs_1_, bf16[4,32,1024]{2,1,0:T(8,128)(2,1)S(1)} %copy-done, bf16[1,1024,1024]{2,1,0:T(8,128)(2,1)} %get-tuple-element.98.refs_3_), custom_call_target="tpu_custom_call" | custom-call | flops 1024 | bytes 1024 | tf_op jit(solution)/shard_map/cond/branch_1_fun/near/pallas_call | solution.py:216
  16.1 1.5 %collective-permute-done.5 = bf16[384,256]{1,0:T(8,128)(2,1)S(1)} collective-permute-done((bf16[384,256]{1,0:T(8,128)(2,1)S(1)}, bf16[384,256]{1,0:T(8,128)(2,1)S(1)}, u32[]{:S(2)}, u32[]{:S(2)}) %collective-permute-start.5) | collective-permute-done | bytes 196640 | tf_op jit(solution)/shard_map/cond/branch_1_fun/ppermute | solution.py:172
  17.7 0.1 fusion
  17.8 0.4 %collective-permute-start.8 = (bf16[128,256]{1,0:T(8,128)(2,1)S(1)}, bf16[128,256]{1,0:T(8,128)(2,1)S(1)}, u32[]{:S(2)}, u32[]{:S(2)}) collective-permute-start(bf16[128,256]{1,0:T(8,128)(2,1)S(1)} %get-tuple-element.87), channel_id=1, source_target_pairs={{0,8},{4,12},{8,0},{12,4},{1,9},{5,13},{9,1},{13,5},{2,10},{6,14},... | collective-permute-start | bytes 196616 | tf_op jit(solution)/shard_map/ppermute | solution.py:172
  18.2 2.5 %collective-permute-start.9 = (bf16[128,256]{1,0:T(8,128)(2,1)S(1)}, bf16[128,256]{1,0:T(8,128)(2,1)S(1)}, u32[]{:S(2)}, u32[]{:S(2)}) collective-permute-start(bf16[128,256]{1,0:T(8,128)(2,1)S(1)} %get-tuple-element.88), channel_id=1, source_target_pairs={{0,12},{4,8},{8,4},{12,0},{1,13},{5,9},{9,5},{13,1},{2,14},{6,10},... | collective-permute-start | bytes 196616 | tf_op jit(solution)/shard_map/ppermute | solution.py:172
  20.6 9.0 %conditional.3 = (f32[128,256]{1,0:T(8,128)S(1)}) conditional(s32[]{:T(128)} %convert_element_type.40, () %tuple.21, (s32[8,384]{1,0:T(8,128)S(1)}, bf16[384,1024]{1,0:T(8,128)(2,1)}, bf16[384,1024]{1,0:T(8,128)(2,1)}, f32[128,1024]{1,0:T(8,128)S(1)}, bf16[128,1024]{1,0:T(8,128)(2,1)S(1)}, /*index=5*/bf16[128,1024]{1,0:T(8,128)(2,1)S(1)}, s32[]{:T(128)}, ...), branch_computations={%region_2.3_spmd, %region_3.4_spmd} | conditional | flops 264214 | bytes 3279254 | solution.py:178
  20.7 1.7 %early.1 = (f32[32,384]{1,0:T(8,128)S(1)}, bf16[384,1024]{1,0:T(8,128)(2,1)S(1)}, bf16[384,1024]{1,0:T(8,128)(2,1)S(1)}, f32[128,1024]{1,0:T(8,128)S(1)}) custom-call(s32[8,384]{1,0:T(8,128)S(1)} %get-tuple-element.59.refs_0_, bf16[384,1024]{1,0:T(8,128)(2,1)} %get-tuple-element.60.refs_1_, bf16[384,1024]{1,0:T(8,128)(2,1)} %get-tuple-element.61.refs_2_, ...), custom_call_target="tpu_custom_call" | custom-call | flops 1024 | bytes 1024 | tf_op jit(solution)/shard_map/cond/branch_1_fun/early/pallas_call | solution.py:272
  22.3 0.0 collective-permute-done.refs_5_
  22.3 1.3 %forward.1 = (bf16[2,128,256]{2,1,0:T(8,128)(2,1)S(1)}, f32[2,128,256]{2,1,0:T(8,128)S(1)}) custom-call(s32[8,384]{1,0:T(8,128)S(1)} %get-tuple-element.59.refs_0_, f32[32,384]{1,0:T(8,128)S(1)} %get-tuple-element.65.refs_1_, bf16[384,1024]{1,0:T(8,128)(2,1)S(1)} %get-tuple-element.66.refs_2_, bf16[384,1024]{1,0:T(8,128)(2,1)S(1)} %get-tuple-element.67.refs_3_, ...), custom_call_target="tpu_custom_call" | custom-call | flops 1024 | bytes 1024 | tf_op jit(solution)/shard_map/cond/branch_1_fun/forward/pallas_call | solution.py:290
  23.6 0.6 %collective-permute-start.1 = (bf16[2,128,256]{2,1,0:T(8,128)(2,1)S(1)}, bf16[2,128,256]{2,1,0:T(8,128)(2,1)S(1)}, u32[]{:S(2)}, u32[]{:S(2)}) collective-permute-start(bf16[2,128,256]{2,1,0:T(8,128)(2,1)S(1)} %get-tuple-element.70), channel_id=1, source_target_pairs={{0,1},{1,0},{2,3},{3,2},{4,5},{5,4},{6,7},{7,6},{8,9},{9,8},{10,11... | collective-permute-start | bytes 393224 | tf_op jit(solution)/shard_map/cond/branch_1_fun/ppermute | solution.py:172
  24.2 0.7 %collective-permute-start.3 = (bf16[128,256]{1,0:T(8,128)(2,1)S(1)}, bf16[128,256]{1,0:T(8,128)(2,1)S(1)}, u32[]{:S(2)}, u32[]{:S(2)}) collective-permute-start(bf16[128,256]{1,0:T(8,128)(2,1)S(1)} %get-tuple-element.72), channel_id=1, source_target_pairs={{0,4},{4,0},{8,12},{12,8},{1,5},{5,1},{9,13},{13,9},{2,6},{6,2},{1... | collective-permute-start | bytes 196616 | tf_op jit(solution)/shard_map/cond/branch_1_fun/ppermute | solution.py:172
  24.8 0.3 %collective-permute-done.1 = bf16[2,128,256]{2,1,0:T(8,128)(2,1)S(1)} collective-permute-done((bf16[2,128,256]{2,1,0:T(8,128)(2,1)S(1)}, bf16[2,128,256]{2,1,0:T(8,128)(2,1)S(1)}, u32[]{:S(2)}, u32[]{:S(2)}) %collective-permute-start.1) | collective-permute-done | bytes 131104 | tf_op jit(solution)/shard_map/cond/branch_1_fun/ppermute | solution.py:172
  25.2 1.6 %collective-permute-start.2 = (bf16[128,256]{1,0:T(8,128)(2,1)S(1)}, bf16[128,256]{1,0:T(8,128)(2,1)S(1)}, u32[]{:S(2)}, u32[]{:S(2)}) collective-permute-start(bf16[128,256]{1,0:T(8,128)(2,1)S(1)} %fusion.3), channel_id=1, source_target_pairs={{0,2},{1,3},{2,0},{3,1},{4,6},{5,7},{6,4},{7,5},{8,10},{9,11},{10,... | collective-permute-start | bytes 196616 | tf_op jit(solution)/shard_map/cond/branch_1_fun/ppermute | solution.py:172
  26.8 1.7 %collective-permute-done.3 = bf16[128,256]{1,0:T(8,128)(2,1)S(1)} collective-permute-done((bf16[128,256]{1,0:T(8,128)(2,1)S(1)}, bf16[128,256]{1,0:T(8,128)(2,1)S(1)}, u32[]{:S(2)}, u32[]{:S(2)}) %collective-permute-start.3) | collective-permute-done | bytes 65568 | tf_op jit(solution)/shard_map/cond/branch_1_fun/ppermute | solution.py:172
  28.4 1.2 %collective-permute-done.2 = bf16[128,256]{1,0:T(8,128)(2,1)S(1)} collective-permute-done((bf16[128,256]{1,0:T(8,128)(2,1)S(1)}, bf16[128,256]{1,0:T(8,128)(2,1)S(1)}, u32[]{:S(2)}, u32[]{:S(2)}) %collective-permute-start.2) | collective-permute-done | bytes 65568 | tf_op jit(solution)/shard_map/cond/branch_1_fun/ppermute | solution.py:172
  29.7 0.7 %convert_add_fusion.2 = f32[128,256]{1,0:T(8,128)} fusion(bf16[128,256]{1,0:T(8,128)(2,1)S(1)} %collective-permute-done.9, f32[128,256]{1,0:T(8,128)S(1)} %get-tuple-element.112, bf16[128,256]{1,0:T(8,128)(2,1)S(1)} %collective-permute-done.8), kind=kLoop, calls=%fused_computation.10 | loop fusion | flops 131072 | bytes 393216 | tf_op jit(solution)/shard_map/add | solution.py:303
  (12 shorter events, 0.1 us)
Async XLA Ops:
  0.0 20.6 %collective-permute-start.6 = (bf16[128,1024]{1,0:T(8,128)(2,1)}, bf16[128,1024]{1,0:T(8,128)(2,1)S(1)}, u32[]{:S(2)}, u32[]{:S(2)}) collective-permute-start(bf16[128,1024]{1,0:T(8,128)(2,1)} %bitcast.22), channel_id=1, source_target_pairs={{0,4},{4,0},{8,12},{12,8},{1,5},{5,1},{9,13},{13,9},{2,6},{6,2},{1... | collective-permute-start | bytes 786440 | tf_op jit(solution)/shard_map/ppermute | solution.py:172
  3.0 17.6 %collective-permute-start.7 = (bf16[128,1024]{1,0:T(8,128)(2,1)}, bf16[128,1024]{1,0:T(8,128)(2,1)S(1)}, u32[]{:S(2)}, u32[]{:S(2)}) collective-permute-start(bf16[128,1024]{1,0:T(8,128)(2,1)} %bitcast.23), channel_id=1, source_target_pairs={{0,8},{1,13},{2,10},{3,15},{4,12},{5,9},{6,14},{7,11},{8,0},{9,5},... | collective-permute-start | bytes 786440 | tf_op jit(solution)/shard_map/ppermute | solution.py:234
  5.6 6.6 %copy-start = (bf16[4,32,1024]{2,1,0:T(8,128)(2,1)S(1)}, bf16[4,32,1024]{2,1,0:T(8,128)(2,1)}, u32[]{:S(2)}) copy-start(bf16[4,32,1024]{2,1,0:T(8,128)(2,1)} %get-tuple-element.56.refs_2_) | copy-start | bytes 786436 | tf_op jit(solution)/shard_map/cond
  8.8 1.8 %collective-permute-start.4 = (bf16[2,384,256]{2,1,0:T(8,128)(2,1)S(1)}, bf16[2,384,256]{2,1,0:T(8,128)(2,1)S(1)}, u32[]{:S(2)}, u32[]{:S(2)}) collective-permute-start(bf16[2,384,256]{2,1,0:T(8,128)(2,1)S(1)} %get-tuple-element.50), channel_id=1, source_target_pairs={{0,1},{1,0},{2,3},{3,2},{4,5},{5,4},{6,7},{7,6},{8,9},{9,8},{10,11... | collective-permute-start | bytes 1179656 | tf_op jit(solution)/shard_map/cond/branch_1_fun/ppermute | solution.py:172
  10.7 7.0 %collective-permute-start.5 = (bf16[384,256]{1,0:T(8,128)(2,1)S(1)}, bf16[384,256]{1,0:T(8,128)(2,1)S(1)}, u32[]{:S(2)}, u32[]{:S(2)}) collective-permute-start(bf16[384,256]{1,0:T(8,128)(2,1)S(1)} %fusion.1), channel_id=1, source_target_pairs={{0,2},{1,3},{2,0},{3,1},{4,6},{5,7},{6,4},{7,5},{8,10},{9,11},{10,... | collective-permute-start | bytes 589832 | tf_op jit(solution)/shard_map/cond/branch_1_fun/ppermute | solution.py:172
  17.8 11.9 %collective-permute-start.8 = (bf16[128,256]{1,0:T(8,128)(2,1)S(1)}, bf16[128,256]{1,0:T(8,128)(2,1)S(1)}, u32[]{:S(2)}, u32[]{:S(2)}) collective-permute-start(bf16[128,256]{1,0:T(8,128)(2,1)S(1)} %get-tuple-element.87), channel_id=1, source_target_pairs={{0,8},{4,12},{8,0},{12,4},{1,9},{5,13},{9,1},{13,5},{2,10},{6,14},... | collective-permute-start | bytes 196616 | tf_op jit(solution)/shard_map/ppermute | solution.py:172
  18.2 11.5 %collective-permute-start.9 = (bf16[128,256]{1,0:T(8,128)(2,1)S(1)}, bf16[128,256]{1,0:T(8,128)(2,1)S(1)}, u32[]{:S(2)}, u32[]{:S(2)}) collective-permute-start(bf16[128,256]{1,0:T(8,128)(2,1)S(1)} %get-tuple-element.88), channel_id=1, source_target_pairs={{0,12},{4,8},{8,4},{12,0},{1,13},{5,9},{9,5},{13,1},{2,14},{6,10},... | collective-permute-start | bytes 196616 | tf_op jit(solution)/shard_map/ppermute | solution.py:172
  20.6 1.7 %collective-permute-start = (bf16[128,1024]{1,0:T(8,128)(2,1)S(1)}, bf16[128,1024]{1,0:T(8,128)(2,1)S(1)}, u32[]{:S(2)}, u32[]{:S(2)}) collective-permute-start(bf16[128,1024]{1,0:T(8,128)(2,1)S(1)} %get-tuple-element.64.refs_5_), channel_id=1, source_target_pairs={{0,1},{1,0},{2,3},{3,2},{4,5},{5,4},{6,7},{7,6},{8,9},{9,8},{10,11... | collective-permute-start | bytes 786440 | tf_op jit(solution)/shard_map/cond/branch_1_fun/ppermute | solution.py:172
  23.6 1.6 %collective-permute-start.1 = (bf16[2,128,256]{2,1,0:T(8,128)(2,1)S(1)}, bf16[2,128,256]{2,1,0:T(8,128)(2,1)S(1)}, u32[]{:S(2)}, u32[]{:S(2)}) collective-permute-start(bf16[2,128,256]{2,1,0:T(8,128)(2,1)S(1)} %get-tuple-element.70), channel_id=1, source_target_pairs={{0,1},{1,0},{2,3},{3,2},{4,5},{5,4},{6,7},{7,6},{8,9},{9,8},{10,11... | collective-permute-start | bytes 393224 | tf_op jit(solution)/shard_map/cond/branch_1_fun/ppermute | solution.py:172
  24.2 4.3 %collective-permute-start.3 = (bf16[128,256]{1,0:T(8,128)(2,1)S(1)}, bf16[128,256]{1,0:T(8,128)(2,1)S(1)}, u32[]{:S(2)}, u32[]{:S(2)}) collective-permute-start(bf16[128,256]{1,0:T(8,128)(2,1)S(1)} %get-tuple-element.72), channel_id=1, source_target_pairs={{0,4},{4,0},{8,12},{12,8},{1,5},{5,1},{9,13},{13,9},{2,6},{6,2},{1... | collective-permute-start | bytes 196616 | tf_op jit(solution)/shard_map/cond/branch_1_fun/ppermute | solution.py:172
  25.2 4.4 %collective-permute-start.2 = (bf16[128,256]{1,0:T(8,128)(2,1)S(1)}, bf16[128,256]{1,0:T(8,128)(2,1)S(1)}, u32[]{:S(2)}, u32[]{:S(2)}) collective-permute-start(bf16[128,256]{1,0:T(8,128)(2,1)S(1)} %fusion.3), channel_id=1, source_target_pairs={{0,2},{1,3},{2,0},{3,1},{4,6},{5,7},{6,4},{7,5},{8,10},{9,11},{10,... | collective-permute-start | bytes 196616 | tf_op jit(solution)/shard_map/cond/branch_1_fun/ppermute | solution.py:172

commit v8 on v7

--- a/solution.py
+++ b/solution.py
@@ -57,10 +57,30 @@
                 send_ref[q, rows, :] = part.astype(BF16)
 
 
+def side_columns(half, out_ref, rows, product):
+    width = out_ref.shape[2]
+    for side in range(2):
+
+        @pl.when(half == side)
+        def _():
+            for q in range(out_ref.shape[0]):
+                at = (2 * q + side) * width
+                out_ref[q, rows, :] = product(slice(at, at + width)).astype(out_ref.dtype)
+
+
+def batches(count, span):
+    size = span * (count if count <= 4 else 1)
+
+    def rows_of(step):
+        return pl.ds(step * size if isinstance(step, int) else pl.multiple_of(step * size, size), size)
+
+    return size // span, count * span // size, rows_of
+
+
 def mirror_kernel(
     clusters, exc, rank, others, rows_hbm, cols_hbm, x_hbm, u_hbm, v_hbm,
-    send_ref, keep_ref, lanes_ref,
-    rows_ref, cols_ref, x_ref, u_ref, v_ref, mask_ref, sems,
+    send_ref, mask_ref, lanes_ref,
+    rows_ref, cols_ref, x_ref, u_ref, v_ref, sems,
 ):
     copies = [
         pltpu.make_async_copy(src, dst, sems.at[i])
@@ -85,23 +105,30 @@
     for c in range(clusters):
         coef += jnp.where(row_lane == group * clusters + c, every[c * exc : (c + 1) * exc], 0.0)
     coef = coef.astype(BF16).astype(F32)
-    span = clusters * exc
     copies[4].wait()
-    batch = mask_ref.shape[0] // span
+    batch, steps, rows_of = batches(others, clusters * exc)
 
     def one(step):
+        masked = []
         for i in range(batch):
-            other = group ^ (step * batch + i + 1)
-            for c in range(clusters):
-                at = (i * clusters + c) * exc
-                mask_ref[at : at + exc, :] = jnp.where(
-                    col_lane == other * clusters + c, coef, 0.0
-                ).astype(BF16)
-        size = batch * span
-        rows = pl.ds(step * size if isinstance(step, int) else pl.multiple_of(step * size, size), size)
-        split_columns(half, keep_ref, send_ref, rows, lambda cols: dot(mask_ref[...], v_ref[:, cols]))
-
-    each(others // batch, one)
+            first = (group ^ (step * batch + i + 1)) * clusters
+            masked += [jnp.where(col_lane == first + c, coef, 0.0) for c in range(clusters)]
+        rows = rows_of(step)
+        mask_ref[rows, :] = jnp.concatenate(masked, axis=0).astype(BF16)
+        side_columns(1 - half, send_ref, rows, lambda cols: dot(mask_ref[rows, :], v_ref[:, cols]))
+
+    each(steps, one)
+
+
+def kept_kernel(clusters, exc, others, mask_ref, v_ref, keep_ref):
+    half = lax.rem(lax.axis_index("col"), 2)
+    _, steps, rows_of = batches(others, clusters * exc)
+
+    def one(step):
+        rows = rows_of(step)
+        side_columns(half, keep_ref, rows, lambda cols: dot(mask_ref[rows, :], v_ref[:, cols]))
+
+    each(steps, one)
 
 
 def near_kernel(clusters, exc, rows_ref, cols_ref, x_ref, n_ref, out_ref):
@@ -144,18 +171,18 @@
     for copy in copies[: 1 + count]:
         copy.wait()
     pieces = [pieces_ref[i * span : (i + 1) * span] for i in range(count)]
-    aways = [1] + [2 * t + half for t in range(1, count)]
+    aways = [2 * t + half for t in range(1, count + 1)]
     coef_ref[...] = coef_of(clusters, exc, aways, lanes_ref, targets[0], pieces)
     for copy in copies[1 + count :]:
         copy.wait()
 
 
-def forward_kernel(clusters, exc, lanes_ref, early_ref, v_ref, u_ref, near_ref, *refs):
+def forward_kernel(clusters, exc, lanes_ref, early_ref, v_ref, u_ref, near_ref, whole_ref, handed_ref, *refs):
     send_ref, keep_ref = refs[-2:]
     group = lax.axis_index("row")
     half = lax.rem(lax.axis_index("col"), 2)
-    pieces = [ref[...] for ref in refs[:-2]]
-    aways = [2 * t + 3 - half for t in range(len(pieces))]
+    pieces = [jnp.where(half == 0, whole_ref[...], handed_ref[...])] + [ref[...] for ref in refs[:-2]]
+    aways = [1] + [2 * t + 1 - half for t in range(1, len(pieces))]
     coef = early_ref[...] + coef_of(clusters, exc, aways, lanes_ref, v_ref, pieces)
     coef = coef.astype(BF16).astype(F32)
     row_lane = lanes_ref[0:1, :]
@@ -187,7 +214,6 @@
     pairs = col_count // 2
     width = panels // col_count
     span = clusters * exc
-    batch = others if others <= 4 else 1
     place = lax.axis_index("col")
     x = charges.reshape(span, panels)
     u = far_u.reshape(entries * rank, panels)
@@ -223,35 +249,47 @@
             name="near",
         )(near_rows, near_cols, x_near, near_blocks).reshape(span, panels)
 
-    whole = swap(x, "row", row_count, 1)
-    got = []
-    for d in range(2, row_count, 2):
-        perm = [
-            (r * col_count + c, (r ^ (d + c % 2)) * col_count + c)
+    def rows_perm(distance):
+        return [
+            (r * col_count + c, (r ^ distance(c % 2)) * col_count + c)
             for r in range(row_count)
             for c in range(col_count)
         ]
-        got.append(lax.ppermute(x, ("row", "col"), perm))
+
+    whole = lax.ppermute(x, ("row", "col"), rows_perm(lambda core: 1 - core))
+    got = [lax.ppermute(x, ("row", "col"), rows_perm(lambda core: d + core)) for d in range(2, row_count, 2)]
 
     def local():
-        send, keep, lanes = pl.pallas_call(
+        send, mask, lanes = pl.pallas_call(
             lambda *refs: mirror_kernel(clusters, exc, rank, others, *refs),
             in_specs=[ANY] * 5,
             out_specs=[VMEM] * 3,
-            out_shape=shares(others) + [jax.ShapeDtypeStruct((8, entries * rank), jnp.int32)],
+            out_shape=[
+                shares(others)[0],
+                jax.ShapeDtypeStruct((others * span, entries * rank), BF16),
+                jax.ShapeDtypeStruct((8, entries * rank), jnp.int32),
+            ],
             scratch_shapes=[
                 pltpu.SMEM(far_rows.shape, jnp.int32),
                 pltpu.SMEM(far_cols.shape, jnp.int32),
                 pltpu.VMEM(x.shape, BF16),
                 pltpu.VMEM(u.shape, BF16),
                 pltpu.VMEM(v.shape, BF16),
-                pltpu.VMEM((batch * span, entries * rank), BF16),
                 pltpu.SemaphoreType.DMA((5,)),
             ],
             compiler_params=params(others),
             cost_estimate=pl.CostEstimate(flops=1024, bytes_accessed=1024, transcendentals=0),
             name="mirror",
         )(far_rows, far_cols, x, u, v)
+        keep = pl.pallas_call(
+            lambda *refs: kept_kernel(clusters, exc, others, *refs),
+            in_specs=[VMEM] * 2,
+            out_specs=VMEM,
+            out_shape=shares(others)[1],
+            compiler_params=params(others),
+            cost_estimate=pl.CostEstimate(flops=1024, bytes_accessed=1024, transcendentals=0),
+            name="kept",
+        )(mask, v)
         total = pair_sum(send, keep)
         held = []
 
@@ -265,13 +303,15 @@
 
     mirror, near, lanes = stage(local)
     from_rows = [swap(mirror[d - 1], "row", row_count, d) for d in range(2, row_count)]
-    whole, *got, lanes = lax.optimization_barrier((whole, *got, lanes))
+    *got, lanes = lax.optimization_barrier((*got, lanes))
+    whole, *got = lax.optimization_barrier((whole, *got))
 
     def forward():
+        handed = swap(whole, "col", col_count, 1)
         other = [swap(piece, "col", col_count, 1) for piece in got]
         early, *fetched = pl.pallas_call(
-            lambda *refs: early_kernel(clusters, exc, 1 + len(got), *refs),
-            in_specs=[VMEM] + [ANY] * (4 + len(got)),
+            lambda *refs: early_kernel(clusters, exc, len(got), *refs),
+            in_specs=[VMEM] + [ANY] * (3 + len(got)),
             out_specs=[VMEM] * 4,
             out_shape=[
                 jax.ShapeDtypeStruct((exc, entries * rank), F32),
@@ -280,22 +320,22 @@
                 jax.ShapeDtypeStruct(near.shape, F32),
             ],
             scratch_shapes=[
-                pltpu.VMEM(((1 + len(got)) * span, panels), BF16),
-                pltpu.SemaphoreType.DMA((4 + len(got),)),
+                pltpu.VMEM((len(got) * span, panels), BF16),
+                pltpu.SemaphoreType.DMA((3 + len(got),)),
             ],
             compiler_params=params(others),
             cost_estimate=pl.CostEstimate(flops=1024, bytes_accessed=1024, transcendentals=0),
             name="early",
-        )(lanes, v, u, near, whole, *got)
+        )(lanes, v, u, near, *got)
         send, keep = pl.pallas_call(
             lambda *refs: forward_kernel(clusters, exc, *refs),
-            in_specs=[VMEM] * (5 + len(other)),
+            in_specs=[VMEM] * (7 + len(other)),
             out_specs=[VMEM] * 2,
             out_shape=shares(1),
             compiler_params=params(others),
             cost_estimate=pl.CostEstimate(flops=1024, bytes_accessed=1024, transcendentals=0),
             name="forward",
-        )(lanes, early, *fetched, *other)
+        )(lanes, early, *fetched, whole, handed, *other)
         return col_sum(pair_sum(send, keep)) + swap(mirror[0], "row", row_count, 1).astype(F32)
 
     total = stage(forward)

time: 30.6 us -> 32 us (1.046)
  starting transfers between devices: 12.9 us -> 15.8 us
  waiting for transfers between devices: 6.42 us -> 5.63 us
  Pallas kernels: 9.95 us -> 9.22 us
    ppermute x1 -> x2, starting transfers between devices: 2.59 us -> 7.51 us  [the longest x1 4.04 us: body(): lax.ppermute(x, ('row', 'col'), rows_perm(lambda core: d + core))]
    ppermute x9, starting transfers between devices: 10.3 us -> 8.27 us  [swap(): return lax.ppermute(value, axis, [(i, i ^ step) for i in range(size)])]
    pallas_call x1, Pallas kernels: 3.14 us -> 2.12 us  [local(): pl.pallas_call(lambda *refs: mirror_kernel(clusters, exc, rank, others, *...]
    ppermute x9, waiting for transfers between devices: 6.42 us -> 5.63 us  [swap(): return lax.ppermute(value, axis, [(i, i ^ step) for i in range(size)])]
    pallas_call x1 -> x2, Pallas kernels: 1.65 us -> 1.92 us  [the longest x1 1.55 us: forward(): pl.pallas_call(lambda *refs: early_kernel(clusters, exc, len(got), *refs)...]
  transfers between devices with their start and end apart: 10 -> 11, of which waited for: 5 -> 4; matrix products, arithmetic and copies ran while one was open for 1% -> 1% of each run, Pallas kernels for 33% -> 29%
where the time goes in v8:
time: 32 us; the launch traced here: 31.8 us
  starting transfers between devices  15.8 us (49%)
  Pallas kernels  9.22 us (29%)
  waiting for transfers between devices  5.63 us (18%)
  other arithmetic  0.85 us (3%)
    ppermute x9, starting transfers between devices, swap(): return lax.ppermute(value, axis, [(i, i ^ step) for i in range(size)])  8.27 us
    ppermute x9, waiting for transfers between devices, swap(): return lax.ppermute(value, axis, [(i, i ^ step) for i in range(size)])  5.63 us
    ppermute x1, starting transfers between devices, body(): lax.ppermute(x, ('row', 'col'), rows_perm(lambda core: d + core))  4.04 us
    pallas_call x1, Pallas kernels, near_of(): pl.pallas_call(lambda *refs: near_kernel(clusters, exc, *refs), in_specs=...  3.89 us
    ppermute x1, starting transfers between devices, body(): whole = lax.ppermute(x, ('row', 'col'), rows_perm(lambda core: 1 - core))  3.47 us
    pallas_call x1, Pallas kernels, local(): pl.pallas_call(lambda *refs: mirror_kernel(clusters, exc, rank, others, *...  2.12 us
    pallas_call x1, Pallas kernels, forward(): pl.pallas_call(lambda *refs: early_kernel(clusters, exc, len(got), *refs)...  1.55 us
    pallas_call x1, Pallas kernels, forward(): pl.pallas_call(lambda *refs: forward_kernel(clusters, exc, *refs), in_spe...  1.29 us
  transfers between devices with their start and end apart: 11, of which 4 were waited for; matrix products, arithmetic and copies ran while one was open for 1% of the time, Pallas kernels for 29%

profile of v8, /device:TPU:0, one launch (start us, length us, event | category | flops | bytes accessed | tf_op | source)
XLA Modules:
  0.0 31.8 jit_solution(956237275375871981)
XLA Ops:
  0.0 4.0 %collective-permute-start.7 = (bf16[128,1024]{1,0:T(8,128)(2,1)}, bf16[128,1024]{1,0:T(8,128)(2,1)S(1)}, u32[]{:S(2)}, u32[]{:S(2)}) collective-permute-start(bf16[128,1024]{1,0:T(8,128)(2,1)} %bitcast.22), channel_id=1, source_target_pairs={{0,8},{1,13},{2,10},{3,15},{4,12},{5,9},{6,14},{7,11},{8,0},{9,5},... | collective-permute-start | bytes 786440 | tf_op jit(solution)/shard_map/ppermute | solution.py:260
  4.0 3.5 %collective-permute-start.8 = (bf16[128,1024]{1,0:T(8,128)(2,1)}, bf16[128,1024]{1,0:T(8,128)(2,1)S(1)}, u32[]{:S(2)}, u32[]{:S(2)}) collective-permute-start(bf16[128,1024]{1,0:T(8,128)(2,1)} %bitcast.23), channel_id=1, source_target_pairs={{0,4},{1,1},{2,6},{3,3},{4,0},{5,5},{6,2},{7,7},{8,12},{9,9},{10,1... | collective-permute-start | bytes 786440 | tf_op jit(solution)/shard_map/ppermute | solution.py:259
  7.5 11.1 %conditional.2 = (bf16[128,256]{1,0:T(8,128)(2,1)S(1)}, bf16[128,256]{1,0:T(8,128)(2,1)S(1)}, bf16[128,256]{1,0:T(8,128)(2,1)S(1)}, f32[128,1024]{1,0:T(8,128)S(1)}, s32[8,384]{1,0:T(8,128)S(1)}) conditional(s32[]{:T(128)} %convert_element_type.40, () %tuple.23, (s32[24]{0:T(128)}, s32[24]{0:T(128)}, bf16[128,1024]{1,0:T(8,128)(2,1)}, ...), branch_computations={%region_0.0_spmd, %region_1.2_spmd} | conditional | flops 691222 | bytes 10096030 | solution.py:205
  7.5 2.1 %mirror.1 = (bf16[2,384,256]{2,1,0:T(8,128)(2,1)S(1)}, bf16[384,384]{1,0:T(8,128)(2,1)S(1)}, s32[8,384]{1,0:T(8,128)S(1)}) custom-call(s32[24]{0:T(128)} %get-tuple-element.96.refs_0_, s32[24]{0:T(128)} %get-tuple-element.97.refs_1_, bf16[128,1024]{1,0:T(8,128)(2,1)} %bitcast.25, bf16[384,1024]{1,0:T(8,128)(2,1)} %get-tuple-element.47.refs_3_, ...), custom_call_target="tpu_custom_call" | custom-call | flops 1024 | bytes 1024 | tf_op jit(solution)/shard_map/cond/branch_1_fun/mirror/pallas_call | solution.py:263
  9.7 0.1 collective-permute-start.5
  9.8 0.4 %kept.1 = f32[2,384,256]{2,1,0:T(8,128)S(1)} custom-call(bf16[384,384]{1,0:T(8,128)(2,1)S(1)} %get-tuple-element.49.refs_0_, bf16[384,1024]{1,0:T(8,128)(2,1)S(1)} %copy-done), custom_call_target="tpu_custom_call" | custom-call | flops 1024 | bytes 1024 | tf_op jit(solution)/shard_map/cond/branch_1_fun/kept/pallas_call | solution.py:284
  10.2 1.3 %collective-permute-done.5 = bf16[2,384,256]{2,1,0:T(8,128)(2,1)S(1)} collective-permute-done((bf16[2,384,256]{2,1,0:T(8,128)(2,1)S(1)}, bf16[2,384,256]{2,1,0:T(8,128)(2,1)S(1)}, u32[]{:S(2)}, u32[]{:S(2)}) %collective-permute-start.5) | collective-permute-done | bytes 393248 | tf_op jit(solution)/shard_map/cond/branch_1_fun/ppermute | solution.py:199
  11.5 0.1 convert_add_fusion
  11.6 1.6 %collective-permute-start.6 = (bf16[384,256]{1,0:T(8,128)(2,1)S(1)}, bf16[384,256]{1,0:T(8,128)(2,1)S(1)}, u32[]{:S(2)}, u32[]{:S(2)}) collective-permute-start(bf16[384,256]{1,0:T(8,128)(2,1)S(1)} %fusion.1), channel_id=1, source_target_pairs={{0,2},{1,3},{2,0},{3,1},{4,6},{5,7},{6,4},{7,5},{8,10},{9,11},{10,... | collective-permute-start | bytes 589832 | tf_op jit(solution)/shard_map/cond/branch_1_fun/ppermute | solution.py:199
  13.1 3.9 %near.1 = f32[4,32,1024]{2,1,0:T(8,128)S(1)} custom-call(s32[1]{0:T(128)} %get-tuple-element.98.refs_0_, s32[1]{0:T(128)} %get-tuple-element.99.refs_1_, bf16[4,32,1024]{2,1,0:T(8,128)(2,1)S(1)} %copy-done.1, bf16[1,1024,1024]{2,1,0:T(8,128)(2,1)} %get-tuple-element.100.refs_3_), custom_call_target="tpu_custom_call" | custom-call | flops 1024 | bytes 1024 | tf_op jit(solution)/shard_map/cond/branch_1_fun/near/pallas_call | solution.py:242
  17.0 1.6 %collective-permute-done.6 = bf16[384,256]{1,0:T(8,128)(2,1)S(1)} collective-permute-done((bf16[384,256]{1,0:T(8,128)(2,1)S(1)}, bf16[384,256]{1,0:T(8,128)(2,1)S(1)}, u32[]{:S(2)}, u32[]{:S(2)}) %collective-permute-start.6) | collective-permute-done | bytes 196640 | tf_op jit(solution)/shard_map/cond/branch_1_fun/ppermute | solution.py:199
  18.6 0.1 fusion
  18.7 0.1 collective-permute-start.10
  18.7 1.9 %collective-permute-start.9 = (bf16[128,256]{1,0:T(8,128)(2,1)S(1)}, bf16[128,256]{1,0:T(8,128)(2,1)S(1)}, u32[]{:S(2)}, u32[]{:S(2)}) collective-permute-start(bf16[128,256]{1,0:T(8,128)(2,1)S(1)} %get-tuple-element.89), channel_id=1, source_target_pairs={{0,8},{4,12},{8,0},{12,4},{1,9},{5,13},{9,1},{13,5},{2,10},{6,14},... | collective-permute-start | bytes 196616 | tf_op jit(solution)/shard_map/ppermute | solution.py:199
  20.7 10.4 %conditional.3 = (f32[128,256]{1,0:T(8,128)S(1)}) conditional(s32[]{:T(128)} %convert_element_type.40, () %tuple.22, (s32[8,384]{1,0:T(8,128)S(1)}, bf16[384,1024]{1,0:T(8,128)(2,1)}, bf16[384,1024]{1,0:T(8,128)(2,1)}, f32[128,1024]{1,0:T(8,128)S(1)}, bf16[128,1024]{1,0:T(8,128)(2,1)S(1)}, /*index=5*/bf16[128,1024]{1,0:T(8,128)(2,1)S(1)}, s32[]{:T(128)}, ...), branch_computations={%region_2.3_spmd, %region_3.4_spmd} | conditional | flops 264214 | bytes 4327870 | solution.py:205
  20.7 0.5 %collective-permute-start.1 = (bf16[128,1024]{1,0:T(8,128)(2,1)S(1)}, bf16[128,1024]{1,0:T(8,128)(2,1)S(1)}, u32[]{:S(2)}, u32[]{:S(2)}) collective-permute-start(bf16[128,1024]{1,0:T(8,128)(2,1)S(1)} %get-tuple-element.63.refs_4_), channel_id=1, source_target_pairs={{0,1},{1,0},{2,3},{3,2},{4,5},{5,4},{6,7},{7,6},{8,9},{9,8},{10,11... | collective-permute-start | bytes 786440 | tf_op jit(solution)/shard_map/cond/branch_1_fun/ppermute | solution.py:199
  21.2 1.5 %early.1 = (f32[32,384]{1,0:T(8,128)S(1)}, bf16[384,1024]{1,0:T(8,128)(2,1)S(1)}, bf16[384,1024]{1,0:T(8,128)(2,1)S(1)}, f32[128,1024]{1,0:T(8,128)S(1)}) custom-call(s32[8,384]{1,0:T(8,128)S(1)} %get-tuple-element.59.refs_0_, bf16[384,1024]{1,0:T(8,128)(2,1)} %get-tuple-element.60.refs_1_, bf16[384,1024]{1,0:T(8,128)(2,1)} %get-tuple-element.61.refs_2_, ...), custom_call_target="tpu_custom_call" | custom-call | flops 1024 | bytes 1024 | tf_op jit(solution)/shard_map/cond/branch_1_fun/early/pallas_call | solution.py:312
  22.7 1.3 %forward.1 = (bf16[2,128,256]{2,1,0:T(8,128)(2,1)S(1)}, f32[2,128,256]{2,1,0:T(8,128)S(1)}) custom-call(s32[8,384]{1,0:T(8,128)S(1)} %get-tuple-element.59.refs_0_, f32[32,384]{1,0:T(8,128)S(1)} %get-tuple-element.64.refs_1_, bf16[384,1024]{1,0:T(8,128)(2,1)S(1)} %get-tuple-element.65.refs_2_, bf16[384,1024]{1,0:T(8,128)(2,1)S(1)} %get-tuple-element.66.refs_3_, ...), custom_call_target="tpu_custom_call" | custom-call | flops 1024 | bytes 1024 | tf_op jit(solution)/shard_map/cond/branch_1_fun/forward/pallas_call | solution.py:330
  24.0 0.1 collective-permute-start.2
  24.2 2.5 %collective-permute-start.4 = (bf16[128,256]{1,0:T(8,128)(2,1)S(1)}, bf16[128,256]{1,0:T(8,128)(2,1)S(1)}, u32[]{:S(2)}, u32[]{:S(2)}) collective-permute-start(bf16[128,256]{1,0:T(8,128)(2,1)S(1)} %get-tuple-element.72), channel_id=1, source_target_pairs={{0,4},{4,0},{8,12},{12,8},{1,5},{5,1},{9,13},{13,9},{2,6},{6,2},{1... | collective-permute-start | bytes 196616 | tf_op jit(solution)/shard_map/cond/branch_1_fun/ppermute | solution.py:199
  26.7 1.6 %collective-permute-start.3 = (bf16[128,256]{1,0:T(8,128)(2,1)S(1)}, bf16[128,256]{1,0:T(8,128)(2,1)S(1)}, u32[]{:S(2)}, u32[]{:S(2)}) collective-permute-start(bf16[128,256]{1,0:T(8,128)(2,1)S(1)} %fusion.3), channel_id=1, source_target_pairs={{0,2},{1,3},{2,0},{3,1},{4,6},{5,7},{6,4},{7,5},{8,10},{9,11},{10,... | collective-permute-start | bytes 196616 | tf_op jit(solution)/shard_map/cond/branch_1_fun/ppermute | solution.py:199
  28.3 1.1 %collective-permute-done.4 = bf16[128,256]{1,0:T(8,128)(2,1)S(1)} collective-permute-done((bf16[128,256]{1,0:T(8,128)(2,1)S(1)}, bf16[128,256]{1,0:T(8,128)(2,1)S(1)}, u32[]{:S(2)}, u32[]{:S(2)}) %collective-permute-start.4) | collective-permute-done | bytes 65568 | tf_op jit(solution)/shard_map/cond/branch_1_fun/ppermute | solution.py:199
  29.3 1.7 %collective-permute-done.3 = bf16[128,256]{1,0:T(8,128)(2,1)S(1)} collective-permute-done((bf16[128,256]{1,0:T(8,128)(2,1)S(1)}, bf16[128,256]{1,0:T(8,128)(2,1)S(1)}, u32[]{:S(2)}, u32[]{:S(2)}) %collective-permute-start.3) | collective-permute-done | bytes 65568 | tf_op jit(solution)/shard_map/cond/branch_1_fun/ppermute | solution.py:199
  31.1 0.7 %convert_add_fusion.2 = f32[128,256]{1,0:T(8,128)} fusion(bf16[128,256]{1,0:T(8,128)(2,1)S(1)} %collective-permute-done.10, f32[128,256]{1,0:T(8,128)S(1)} %get-tuple-element.114, bf16[128,256]{1,0:T(8,128)(2,1)S(1)} %collective-permute-done.9), kind=kLoop, calls=%fused_computation.10 | loop fusion | flops 131072 | bytes 393216 | tf_op jit(solution)/shard_map/add | solution.py:343
  (17 shorter events, 0.1 us)
Async XLA Ops:
  0.0 20.6 %collective-permute-start.7 = (bf16[128,1024]{1,0:T(8,128)(2,1)}, bf16[128,1024]{1,0:T(8,128)(2,1)S(1)}, u32[]{:S(2)}, u32[]{:S(2)}) collective-permute-start(bf16[128,1024]{1,0:T(8,128)(2,1)} %bitcast.22), channel_id=1, source_target_pairs={{0,8},{1,13},{2,10},{3,15},{4,12},{5,9},{6,14},{7,11},{8,0},{9,5},... | collective-permute-start | bytes 786440 | tf_op jit(solution)/shard_map/ppermute | solution.py:260
  4.0 16.6 %collective-permute-start.8 = (bf16[128,1024]{1,0:T(8,128)(2,1)}, bf16[128,1024]{1,0:T(8,128)(2,1)S(1)}, u32[]{:S(2)}, u32[]{:S(2)}) collective-permute-start(bf16[128,1024]{1,0:T(8,128)(2,1)} %bitcast.23), channel_id=1, source_target_pairs={{0,4},{1,1},{2,6},{3,3},{4,0},{5,5},{6,2},{7,7},{8,12},{9,9},{10,1... | collective-permute-start | bytes 786440 | tf_op jit(solution)/shard_map/ppermute | solution.py:259
  7.5 2.2 %copy-start = (bf16[384,1024]{1,0:T(8,128)(2,1)S(1)}, bf16[384,1024]{1,0:T(8,128)(2,1)}, u32[]{:S(2)}) copy-start(bf16[384,1024]{1,0:T(8,128)(2,1)} %get-tuple-element.48.refs_4_.refs_1_) | copy-start | bytes 2359300 | tf_op jit(solution)/shard_map/cond
  9.7 1.8 %collective-permute-start.5 = (bf16[2,384,256]{2,1,0:T(8,128)(2,1)S(1)}, bf16[2,384,256]{2,1,0:T(8,128)(2,1)S(1)}, u32[]{:S(2)}, u32[]{:S(2)}) collective-permute-start(bf16[2,384,256]{2,1,0:T(8,128)(2,1)S(1)} %get-tuple-element.50), channel_id=1, source_target_pairs={{0,1},{1,0},{2,3},{3,2},{4,5},{5,4},{6,7},{7,6},{8,9},{9,8},{10,11... | collective-permute-start | bytes 1179656 | tf_op jit(solution)/shard_map/cond/branch_1_fun/ppermute | solution.py:199
  9.8 3.4 %copy-start.1 = (bf16[4,32,1024]{2,1,0:T(8,128)(2,1)S(1)}, bf16[4,32,1024]{2,1,0:T(8,128)(2,1)}, u32[]{:S(2)}) copy-start(bf16[4,32,1024]{2,1,0:T(8,128)(2,1)} %get-tuple-element.56.refs_2_) | copy-start | bytes 786436 | tf_op jit(solution)/shard_map/cond
  11.6 7.0 %collective-permute-start.6 = (bf16[384,256]{1,0:T(8,128)(2,1)S(1)}, bf16[384,256]{1,0:T(8,128)(2,1)S(1)}, u32[]{:S(2)}, u32[]{:S(2)}) collective-permute-start(bf16[384,256]{1,0:T(8,128)(2,1)S(1)} %fusion.1), channel_id=1, source_target_pairs={{0,2},{1,3},{2,0},{3,1},{4,6},{5,7},{6,4},{7,5},{8,10},{9,11},{10,... | collective-permute-start | bytes 589832 | tf_op jit(solution)/shard_map/cond/branch_1_fun/ppermute | solution.py:199
  18.7 12.4 %collective-permute-start.10 = (bf16[128,256]{1,0:T(8,128)(2,1)S(1)}, bf16[128,256]{1,0:T(8,128)(2,1)S(1)}, u32[]{:S(2)}, u32[]{:S(2)}) collective-permute-start(bf16[128,256]{1,0:T(8,128)(2,1)S(1)} %get-tuple-element.90), channel_id=1, source_target_pairs={{0,12},{4,8},{8,4},{12,0},{1,13},{5,9},{9,5},{13,1},{2,14},{6,10},... | collective-permute-start | bytes 196616 | tf_op jit(solution)/shard_map/ppermute | solution.py:199
  18.7 12.3 %collective-permute-start.9 = (bf16[128,256]{1,0:T(8,128)(2,1)S(1)}, bf16[128,256]{1,0:T(8,128)(2,1)S(1)}, u32[]{:S(2)}, u32[]{:S(2)}) collective-permute-start(bf16[128,256]{1,0:T(8,128)(2,1)S(1)} %get-tuple-element.89), channel_id=1, source_target_pairs={{0,8},{4,12},{8,0},{12,4},{1,9},{5,13},{9,1},{13,5},{2,10},{6,14},... | collective-permute-start | bytes 196616 | tf_op jit(solution)/shard_map/ppermute | solution.py:199
  20.7 2.1 %collective-permute-start = (bf16[128,1024]{1,0:T(8,128)(2,1)S(1)}, bf16[128,1024]{1,0:T(8,128)(2,1)S(1)}, u32[]{:S(2)}, u32[]{:S(2)}) collective-permute-start(bf16[128,1024]{1,0:T(8,128)(2,1)S(1)} %get-tuple-element.68.refs_5_), channel_id=1, source_target_pairs={{0,1},{1,0},{2,3},{3,2},{4,5},{5,4},{6,7},{7,6},{8,9},{9,8},{10,11... | collective-permute-start | bytes 786440 | tf_op jit(solution)/shard_map/cond/branch_1_fun/ppermute | solution.py:199
  20.7 2.1 %collective-permute-start.1 = (bf16[128,1024]{1,0:T(8,128)(2,1)S(1)}, bf16[128,1024]{1,0:T(8,128)(2,1)S(1)}, u32[]{:S(2)}, u32[]{:S(2)}) collective-permute-start(bf16[128,1024]{1,0:T(8,128)(2,1)S(1)} %get-tuple-element.63.refs_4_), channel_id=1, source_target_pairs={{0,1},{1,0},{2,3},{3,2},{4,5},{5,4},{6,7},{7,6},{8,9},{9,8},{10,11... | collective-permute-start | bytes 786440 | tf_op jit(solution)/shard_map/cond/branch_1_fun/ppermute | solution.py:199
  24.0 2.6 %collective-permute-start.2 = (bf16[2,128,256]{2,1,0:T(8,128)(2,1)S(1)}, bf16[2,128,256]{2,1,0:T(8,128)(2,1)S(1)}, u32[]{:S(2)}, u32[]{:S(2)}) collective-permute-start(bf16[2,128,256]{2,1,0:T(8,128)(2,1)S(1)} %get-tuple-element.70), channel_id=1, source_target_pairs={{0,1},{1,0},{2,3},{3,2},{4,5},{5,4},{6,7},{7,6},{8,9},{9,8},{10,11... | collective-permute-start | bytes 393224 | tf_op jit(solution)/shard_map/cond/branch_1_fun/ppermute | solution.py:199
  24.2 5.2 %collective-permute-start.4 = (bf16[128,256]{1,0:T(8,128)(2,1)S(1)}, bf16[128,256]{1,0:T(8,128)(2,1)S(1)}, u32[]{:S(2)}, u32[]{:S(2)}) collective-permute-start(bf16[128,256]{1,0:T(8,128)(2,1)S(1)} %get-tuple-element.72), channel_id=1, source_target_pairs={{0,4},{4,0},{8,12},{12,8},{1,5},{5,1},{9,13},{13,9},{2,6},{6,2},{1... | collective-permute-start | bytes 196616 | tf_op jit(solution)/shard_map/cond/branch_1_fun/ppermute | solution.py:199
  26.7 4.3 %collective-permute-start.3 = (bf16[128,256]{1,0:T(8,128)(2,1)S(1)}, bf16[128,256]{1,0:T(8,128)(2,1)S(1)}, u32[]{:S(2)}, u32[]{:S(2)}) collective-permute-start(bf16[128,256]{1,0:T(8,128)(2,1)S(1)} %fusion.3), channel_id=1, source_target_pairs={{0,2},{1,3},{2,0},{3,1},{4,6},{5,7},{6,4},{7,5},{8,10},{9,11},{10,... | collective-permute-start | bytes 196616 | tf_op jit(solution)/shard_map/cond/branch_1_fun/ppermute | solution.py:199

commit v9 on v8

--- a/solution.py
+++ b/solution.py
@@ -171,18 +171,18 @@
     for copy in copies[: 1 + count]:
         copy.wait()
     pieces = [pieces_ref[i * span : (i + 1) * span] for i in range(count)]
-    aways = [2 * t + half for t in range(1, count + 1)]
+    aways = [1] + [2 * t + half for t in range(1, count)]
     coef_ref[...] = coef_of(clusters, exc, aways, lanes_ref, targets[0], pieces)
     for copy in copies[1 + count :]:
         copy.wait()
 
 
-def forward_kernel(clusters, exc, lanes_ref, early_ref, v_ref, u_ref, near_ref, whole_ref, handed_ref, *refs):
+def forward_kernel(clusters, exc, lanes_ref, early_ref, v_ref, u_ref, near_ref, *refs):
     send_ref, keep_ref = refs[-2:]
     group = lax.axis_index("row")
     half = lax.rem(lax.axis_index("col"), 2)
-    pieces = [jnp.where(half == 0, whole_ref[...], handed_ref[...])] + [ref[...] for ref in refs[:-2]]
-    aways = [1] + [2 * t + 1 - half for t in range(1, len(pieces))]
+    pieces = [ref[...] for ref in refs[:-2]]
+    aways = [2 * t + 3 - half for t in range(len(pieces))]
     coef = early_ref[...] + coef_of(clusters, exc, aways, lanes_ref, v_ref, pieces)
     coef = coef.astype(BF16).astype(F32)
     row_lane = lanes_ref[0:1, :]
@@ -251,13 +251,13 @@
 
     def rows_perm(distance):
         return [
-            (r * col_count + c, (r ^ distance(c % 2)) * col_count + c)
+            (r * col_count + c, (r ^ (distance + c % 2)) * col_count + c)
             for r in range(row_count)
             for c in range(col_count)
         ]
 
-    whole = lax.ppermute(x, ("row", "col"), rows_perm(lambda core: 1 - core))
-    got = [lax.ppermute(x, ("row", "col"), rows_perm(lambda core: d + core)) for d in range(2, row_count, 2)]
+    whole = swap(x, "row", row_count, 1)
+    got = [lax.ppermute(x, ("row", "col"), rows_perm(d)) for d in range(2, row_count, 2)]
 
     def local():
         send, mask, lanes = pl.pallas_call(
@@ -307,11 +307,10 @@
     whole, *got = lax.optimization_barrier((whole, *got))
 
     def forward():
-        handed = swap(whole, "col", col_count, 1)
         other = [swap(piece, "col", col_count, 1) for piece in got]
         early, *fetched = pl.pallas_call(
-            lambda *refs: early_kernel(clusters, exc, len(got), *refs),
-            in_specs=[VMEM] + [ANY] * (3 + len(got)),
+            lambda *refs: early_kernel(clusters, exc, 1 + len(got), *refs),
+            in_specs=[VMEM] + [ANY] * (4 + len(got)),
             out_specs=[VMEM] * 4,
             out_shape=[
                 jax.ShapeDtypeStruct((exc, entries * rank), F32),
@@ -320,22 +319,22 @@
                 jax.ShapeDtypeStruct(near.shape, F32),
             ],
             scratch_shapes=[
-                pltpu.VMEM((len(got) * span, panels), BF16),
-                pltpu.SemaphoreType.DMA((3 + len(got),)),
+                pltpu.VMEM(((1 + len(got)) * span, panels), BF16),
+                pltpu.SemaphoreType.DMA((4 + len(got),)),
             ],
             compiler_params=params(others),
             cost_estimate=pl.CostEstimate(flops=1024, bytes_accessed=1024, transcendentals=0),
             name="early",
-        )(lanes, v, u, near, *got)
+        )(lanes, v, u, near, whole, *got)
         send, keep = pl.pallas_call(
             lambda *refs: forward_kernel(clusters, exc, *refs),
-            in_specs=[VMEM] * (7 + len(other)),
+            in_specs=[VMEM] * (5 + len(other)),
             out_specs=[VMEM] * 2,
             out_shape=shares(1),
             compiler_params=params(others),
             cost_estimate=pl.CostEstimate(flops=1024, bytes_accessed=1024, transcendentals=0),
             name="forward",
-        )(lanes, early, *fetched, whole, handed, *other)
+        )(lanes, early, *fetched, *other)
         return col_sum(pair_sum(send, keep)) + swap(mirror[0], "row", row_count, 1).astype(F32)
 
     total = stage(forward)

time: 32 us -> 29.7 us (0.928)
  starting transfers between devices: 15.8 us -> 12.9 us
  waiting for transfers between devices: 5.63 us -> 6.17 us
    ppermute x2 -> x1, starting transfers between devices: 7.51 us -> 4.04 us  [body(): lax.ppermute(x, ('row', 'col'), rows_perm(d))]
    ppermute x9, starting transfers between devices: 8.27 us -> 8.89 us  [swap(): return lax.ppermute(value, axis, [(i, i ^ step) for i in range(size)])]
    ppermute x9, waiting for transfers between devices: 5.63 us -> 6.17 us  [swap(): return lax.ppermute(value, axis, [(i, i ^ step) for i in range(size)])]
  transfers between devices with their start and end apart: 11 -> 10, of which waited for: 4 -> 5; matrix products, arithmetic and copies ran while one was open for 1% -> 1% of each run, Pallas kernels for 29% -> 32%
where the time goes in v9:
time: 29.7 us; the launch traced here: 29.5 us
  starting transfers between devices  12.9 us (43%)
  Pallas kernels  9.3 us (31%)
  waiting for transfers between devices  6.17 us (21%)
  other arithmetic  0.85 us (3%)
    ppermute x9, starting transfers between devices, swap(): return lax.ppermute(value, axis, [(i, i ^ step) for i in range(size)])  8.89 us
    ppermute x9, waiting for transfers between devices, swap(): return lax.ppermute(value, axis, [(i, i ^ step) for i in range(size)])  6.17 us
    ppermute x1, starting transfers between devices, body(): lax.ppermute(x, ('row', 'col'), rows_perm(d))  4.04 us
    pallas_call x1, Pallas kernels, near_of(): pl.pallas_call(lambda *refs: near_kernel(clusters, exc, *refs), in_specs=...  3.89 us
    pallas_call x1, Pallas kernels, local(): pl.pallas_call(lambda *refs: mirror_kernel(clusters, exc, rank, others, *...  2.11 us
    pallas_call x1, Pallas kernels, forward(): pl.pallas_call(lambda *refs: early_kernel(clusters, exc, 1 + len(got), *r...  1.64 us
    pallas_call x1, Pallas kernels, forward(): pl.pallas_call(lambda *refs: forward_kernel(clusters, exc, *refs), in_spe...  1.27 us
    add x1, other arithmetic, body(): total = total + term.astype(F32)  0.68 us
  transfers between devices with their start and end apart: 10, of which 5 were waited for; matrix products, arithmetic and copies ran while one was open for 1% of the time, Pallas kernels for 32%

profile of v9, /device:TPU:0, one launch (start us, length us, event | category | flops | bytes accessed | tf_op | source)
XLA Modules:
  0.0 29.5 jit_solution(17547890790617097703)
XLA Ops:
  0.0 4.0 %collective-permute-start.6 = (bf16[128,1024]{1,0:T(8,128)(2,1)}, bf16[128,1024]{1,0:T(8,128)(2,1)S(1)}, u32[]{:S(2)}, u32[]{:S(2)}) collective-permute-start(bf16[128,1024]{1,0:T(8,128)(2,1)} %bitcast.22), channel_id=1, source_target_pairs={{0,8},{1,13},{2,10},{3,15},{4,12},{5,9},{6,14},{7,11},{8,0},{9,5},... | collective-permute-start | bytes 786440 | tf_op jit(solution)/shard_map/ppermute | solution.py:260
  4.0 1.6 %collective-permute-start.7 = (bf16[128,1024]{1,0:T(8,128)(2,1)}, bf16[128,1024]{1,0:T(8,128)(2,1)S(1)}, u32[]{:S(2)}, u32[]{:S(2)}) collective-permute-start(bf16[128,1024]{1,0:T(8,128)(2,1)} %bitcast.23), channel_id=1, source_target_pairs={{0,4},{4,0},{8,12},{12,8},{1,5},{5,1},{9,13},{13,9},{2,6},{6,2},{1... | collective-permute-start | bytes 786440 | tf_op jit(solution)/shard_map/ppermute | solution.py:199
  5.6 11.1 %conditional.2 = (bf16[128,256]{1,0:T(8,128)(2,1)S(1)}, bf16[128,256]{1,0:T(8,128)(2,1)S(1)}, bf16[128,256]{1,0:T(8,128)(2,1)S(1)}, f32[128,1024]{1,0:T(8,128)S(1)}, s32[8,384]{1,0:T(8,128)S(1)}) conditional(s32[]{:T(128)} %convert_element_type.40, () %tuple.23, (s32[24]{0:T(128)}, s32[24]{0:T(128)}, bf16[128,1024]{1,0:T(8,128)(2,1)}, ...), branch_computations={%region_0.0_spmd, %region_1.2_spmd} | conditional | flops 691222 | bytes 10096030 | solution.py:205
  5.6 2.1 %mirror.1 = (bf16[2,384,256]{2,1,0:T(8,128)(2,1)S(1)}, bf16[384,384]{1,0:T(8,128)(2,1)S(1)}, s32[8,384]{1,0:T(8,128)S(1)}) custom-call(s32[24]{0:T(128)} %get-tuple-element.96.refs_0_, s32[24]{0:T(128)} %get-tuple-element.97.refs_1_, bf16[128,1024]{1,0:T(8,128)(2,1)} %bitcast.25, bf16[384,1024]{1,0:T(8,128)(2,1)} %get-tuple-element.47.refs_3_, ...), custom_call_target="tpu_custom_call" | custom-call | flops 1024 | bytes 1024 | tf_op jit(solution)/shard_map/cond/branch_1_fun/mirror/pallas_call | solution.py:263
  7.7 0.1 collective-permute-start.4
  7.8 0.4 %kept.1 = f32[2,384,256]{2,1,0:T(8,128)S(1)} custom-call(bf16[384,384]{1,0:T(8,128)(2,1)S(1)} %get-tuple-element.49.refs_0_, bf16[384,1024]{1,0:T(8,128)(2,1)S(1)} %copy-done), custom_call_target="tpu_custom_call" | custom-call | flops 1024 | bytes 1024 | tf_op jit(solution)/shard_map/cond/branch_1_fun/kept/pallas_call | solution.py:284
  8.2 1.3 %collective-permute-done.4 = bf16[2,384,256]{2,1,0:T(8,128)(2,1)S(1)} collective-permute-done((bf16[2,384,256]{2,1,0:T(8,128)(2,1)S(1)}, bf16[2,384,256]{2,1,0:T(8,128)(2,1)S(1)}, u32[]{:S(2)}, u32[]{:S(2)}) %collective-permute-start.4) | collective-permute-done | bytes 393248 | tf_op jit(solution)/shard_map/cond/branch_1_fun/ppermute | solution.py:199
  9.5 0.1 convert_add_fusion
  9.6 1.5 %collective-permute-start.5 = (bf16[384,256]{1,0:T(8,128)(2,1)S(1)}, bf16[384,256]{1,0:T(8,128)(2,1)S(1)}, u32[]{:S(2)}, u32[]{:S(2)}) collective-permute-start(bf16[384,256]{1,0:T(8,128)(2,1)S(1)} %fusion.1), channel_id=1, source_target_pairs={{0,2},{1,3},{2,0},{3,1},{4,6},{5,7},{6,4},{7,5},{8,10},{9,11},{10,... | collective-permute-start | bytes 589832 | tf_op jit(solution)/shard_map/cond/branch_1_fun/ppermute | solution.py:199
  11.2 3.9 %near.1 = f32[4,32,1024]{2,1,0:T(8,128)S(1)} custom-call(s32[1]{0:T(128)} %get-tuple-element.98.refs_0_, s32[1]{0:T(128)} %get-tuple-element.99.refs_1_, bf16[4,32,1024]{2,1,0:T(8,128)(2,1)S(1)} %copy-done.1, bf16[1,1024,1024]{2,1,0:T(8,128)(2,1)} %get-tuple-element.100.refs_3_), custom_call_target="tpu_custom_call" | custom-call | flops 1024 | bytes 1024 | tf_op jit(solution)/shard_map/cond/branch_1_fun/near/pallas_call | solution.py:242
  15.1 1.6 %collective-permute-done.5 = bf16[384,256]{1,0:T(8,128)(2,1)S(1)} collective-permute-done((bf16[384,256]{1,0:T(8,128)(2,1)S(1)}, bf16[384,256]{1,0:T(8,128)(2,1)S(1)}, u32[]{:S(2)}, u32[]{:S(2)}) %collective-permute-start.5) | collective-permute-done | bytes 196640 | tf_op jit(solution)/shard_map/cond/branch_1_fun/ppermute | solution.py:199
  16.7 0.1 fusion
  16.7 0.4 %collective-permute-start.8 = (bf16[128,256]{1,0:T(8,128)(2,1)S(1)}, bf16[128,256]{1,0:T(8,128)(2,1)S(1)}, u32[]{:S(2)}, u32[]{:S(2)}) collective-permute-start(bf16[128,256]{1,0:T(8,128)(2,1)S(1)} %get-tuple-element.89), channel_id=1, source_target_pairs={{0,8},{4,12},{8,0},{12,4},{1,9},{5,13},{9,1},{13,5},{2,10},{6,14},... | collective-permute-start | bytes 196616 | tf_op jit(solution)/shard_map/ppermute | solution.py:199
  17.1 2.6 %collective-permute-start.9 = (bf16[128,256]{1,0:T(8,128)(2,1)S(1)}, bf16[128,256]{1,0:T(8,128)(2,1)S(1)}, u32[]{:S(2)}, u32[]{:S(2)}) collective-permute-start(bf16[128,256]{1,0:T(8,128)(2,1)S(1)} %get-tuple-element.90), channel_id=1, source_target_pairs={{0,12},{4,8},{8,4},{12,0},{1,13},{5,9},{9,5},{13,1},{2,14},{6,10},... | collective-permute-start | bytes 196616 | tf_op jit(solution)/shard_map/ppermute | solution.py:199
  19.8 9.0 %conditional.3 = (f32[128,256]{1,0:T(8,128)S(1)}) conditional(s32[]{:T(128)} %convert_element_type.40, () %tuple.22, (s32[8,384]{1,0:T(8,128)S(1)}, bf16[384,1024]{1,0:T(8,128)(2,1)}, bf16[384,1024]{1,0:T(8,128)(2,1)}, f32[128,1024]{1,0:T(8,128)S(1)}, bf16[128,1024]{1,0:T(8,128)(2,1)S(1)}, /*index=5*/bf16[128,1024]{1,0:T(8,128)(2,1)S(1)}, s32[]{:T(128)}, ...), branch_computations={%region_2.3_spmd, %region_3.4_spmd} | conditional | flops 264214 | bytes 3279254 | solution.py:205
  19.8 1.6 %early.1 = (f32[32,384]{1,0:T(8,128)S(1)}, bf16[384,1024]{1,0:T(8,128)(2,1)S(1)}, bf16[384,1024]{1,0:T(8,128)(2,1)S(1)}, f32[128,1024]{1,0:T(8,128)S(1)}) custom-call(s32[8,384]{1,0:T(8,128)S(1)} %get-tuple-element.59.refs_0_, bf16[384,1024]{1,0:T(8,128)(2,1)} %get-tuple-element.60.refs_1_, bf16[384,1024]{1,0:T(8,128)(2,1)} %get-tuple-element.61.refs_2_, ...), custom_call_target="tpu_custom_call" | custom-call | flops 1024 | bytes 1024 | tf_op jit(solution)/shard_map/cond/branch_1_fun/early/pallas_call | solution.py:311
  21.4 1.3 %forward.1 = (bf16[2,128,256]{2,1,0:T(8,128)(2,1)S(1)}, f32[2,128,256]{2,1,0:T(8,128)S(1)}) custom-call(s32[8,384]{1,0:T(8,128)S(1)} %get-tuple-element.59.refs_0_, f32[32,384]{1,0:T(8,128)S(1)} %get-tuple-element.65.refs_1_, bf16[384,1024]{1,0:T(8,128)(2,1)S(1)} %get-tuple-element.66.refs_2_, bf16[384,1024]{1,0:T(8,128)(2,1)S(1)} %get-tuple-element.67.refs_3_, ...), custom_call_target="tpu_custom_call" | custom-call | flops 1024 | bytes 1024 | tf_op jit(solution)/shard_map/cond/branch_1_fun/forward/pallas_call | solution.py:329
  22.7 0.6 %collective-permute-start.1 = (bf16[2,128,256]{2,1,0:T(8,128)(2,1)S(1)}, bf16[2,128,256]{2,1,0:T(8,128)(2,1)S(1)}, u32[]{:S(2)}, u32[]{:S(2)}) collective-permute-start(bf16[2,128,256]{2,1,0:T(8,128)(2,1)S(1)} %get-tuple-element.70), channel_id=1, source_target_pairs={{0,1},{1,0},{2,3},{3,2},{4,5},{5,4},{6,7},{7,6},{8,9},{9,8},{10,11... | collective-permute-start | bytes 393224 | tf_op jit(solution)/shard_map/cond/branch_1_fun/ppermute | solution.py:199
  23.3 0.5 %collective-permute-start.3 = (bf16[128,256]{1,0:T(8,128)(2,1)S(1)}, bf16[128,256]{1,0:T(8,128)(2,1)S(1)}, u32[]{:S(2)}, u32[]{:S(2)}) collective-permute-start(bf16[128,256]{1,0:T(8,128)(2,1)S(1)} %get-tuple-element.72), channel_id=1, source_target_pairs={{0,4},{4,0},{8,12},{12,8},{1,5},{5,1},{9,13},{13,9},{2,6},{6,2},{1... | collective-permute-start | bytes 196616 | tf_op jit(solution)/shard_map/cond/branch_1_fun/ppermute | solution.py:199
  23.8 0.5 %collective-permute-done.1 = bf16[2,128,256]{2,1,0:T(8,128)(2,1)S(1)} collective-permute-done((bf16[2,128,256]{2,1,0:T(8,128)(2,1)S(1)}, bf16[2,128,256]{2,1,0:T(8,128)(2,1)S(1)}, u32[]{:S(2)}, u32[]{:S(2)}) %collective-permute-start.1) | collective-permute-done | bytes 131104 | tf_op jit(solution)/shard_map/cond/branch_1_fun/ppermute | solution.py:199
  24.3 1.6 %collective-permute-start.2 = (bf16[128,256]{1,0:T(8,128)(2,1)S(1)}, bf16[128,256]{1,0:T(8,128)(2,1)S(1)}, u32[]{:S(2)}, u32[]{:S(2)}) collective-permute-start(bf16[128,256]{1,0:T(8,128)(2,1)S(1)} %fusion.3), channel_id=1, source_target_pairs={{0,2},{1,3},{2,0},{3,1},{4,6},{5,7},{6,4},{7,5},{8,10},{9,11},{10,... | collective-permute-start | bytes 196616 | tf_op jit(solution)/shard_map/cond/branch_1_fun/ppermute | solution.py:199
  25.9 1.7 %collective-permute-done.3 = bf16[128,256]{1,0:T(8,128)(2,1)S(1)} collective-permute-done((bf16[128,256]{1,0:T(8,128)(2,1)S(1)}, bf16[128,256]{1,0:T(8,128)(2,1)S(1)}, u32[]{:S(2)}, u32[]{:S(2)}) %collective-permute-start.3) | collective-permute-done | bytes 65568 | tf_op jit(solution)/shard_map/cond/branch_1_fun/ppermute | solution.py:199
  27.6 1.2 %collective-permute-done.2 = bf16[128,256]{1,0:T(8,128)(2,1)S(1)} collective-permute-done((bf16[128,256]{1,0:T(8,128)(2,1)S(1)}, bf16[128,256]{1,0:T(8,128)(2,1)S(1)}, u32[]{:S(2)}, u32[]{:S(2)}) %collective-permute-start.2) | collective-permute-done | bytes 65568 | tf_op jit(solution)/shard_map/cond/branch_1_fun/ppermute | solution.py:199
  28.8 0.7 %convert_add_fusion.2 = f32[128,256]{1,0:T(8,128)} fusion(bf16[128,256]{1,0:T(8,128)(2,1)S(1)} %collective-permute-done.9, f32[128,256]{1,0:T(8,128)S(1)} %get-tuple-element.114, bf16[128,256]{1,0:T(8,128)(2,1)S(1)} %collective-permute-done.8), kind=kLoop, calls=%fused_computation.10 | loop fusion | flops 131072 | bytes 393216 | tf_op jit(solution)/shard_map/add | solution.py:342
  (15 shorter events, 0.1 us)
Async XLA Ops:
  0.0 19.8 %collective-permute-start.6 = (bf16[128,1024]{1,0:T(8,128)(2,1)}, bf16[128,1024]{1,0:T(8,128)(2,1)S(1)}, u32[]{:S(2)}, u32[]{:S(2)}) collective-permute-start(bf16[128,1024]{1,0:T(8,128)(2,1)} %bitcast.22), channel_id=1, source_target_pairs={{0,8},{1,13},{2,10},{3,15},{4,12},{5,9},{6,14},{7,11},{8,0},{9,5},... | collective-permute-start | bytes 786440 | tf_op jit(solution)/shard_map/ppermute | solution.py:260
  4.0 15.7 %collective-permute-start.7 = (bf16[128,1024]{1,0:T(8,128)(2,1)}, bf16[128,1024]{1,0:T(8,128)(2,1)S(1)}, u32[]{:S(2)}, u32[]{:S(2)}) collective-permute-start(bf16[128,1024]{1,0:T(8,128)(2,1)} %bitcast.23), channel_id=1, source_target_pairs={{0,4},{4,0},{8,12},{12,8},{1,5},{5,1},{9,13},{13,9},{2,6},{6,2},{1... | collective-permute-start | bytes 786440 | tf_op jit(solution)/shard_map/ppermute | solution.py:199
  5.6 2.2 %copy-start = (bf16[384,1024]{1,0:T(8,128)(2,1)S(1)}, bf16[384,1024]{1,0:T(8,128)(2,1)}, u32[]{:S(2)}) copy-start(bf16[384,1024]{1,0:T(8,128)(2,1)} %get-tuple-element.48.refs_4_.refs_1_) | copy-start | bytes 2359300 | tf_op jit(solution)/shard_map/cond
  7.7 1.8 %collective-permute-start.4 = (bf16[2,384,256]{2,1,0:T(8,128)(2,1)S(1)}, bf16[2,384,256]{2,1,0:T(8,128)(2,1)S(1)}, u32[]{:S(2)}, u32[]{:S(2)}) collective-permute-start(bf16[2,384,256]{2,1,0:T(8,128)(2,1)S(1)} %get-tuple-element.50), channel_id=1, source_target_pairs={{0,1},{1,0},{2,3},{3,2},{4,5},{5,4},{6,7},{7,6},{8,9},{9,8},{10,11... | collective-permute-start | bytes 1179656 | tf_op jit(solution)/shard_map/cond/branch_1_fun/ppermute | solution.py:199
  7.8 3.4 %copy-start.1 = (bf16[4,32,1024]{2,1,0:T(8,128)(2,1)S(1)}, bf16[4,32,1024]{2,1,0:T(8,128)(2,1)}, u32[]{:S(2)}) copy-start(bf16[4,32,1024]{2,1,0:T(8,128)(2,1)} %get-tuple-element.56.refs_2_) | copy-start | bytes 786436 | tf_op jit(solution)/shard_map/cond
  9.6 7.0 %collective-permute-start.5 = (bf16[384,256]{1,0:T(8,128)(2,1)S(1)}, bf16[384,256]{1,0:T(8,128)(2,1)S(1)}, u32[]{:S(2)}, u32[]{:S(2)}) collective-permute-start(bf16[384,256]{1,0:T(8,128)(2,1)S(1)} %fusion.1), channel_id=1, source_target_pairs={{0,2},{1,3},{2,0},{3,1},{4,6},{5,7},{6,4},{7,5},{8,10},{9,11},{10,... | collective-permute-start | bytes 589832 | tf_op jit(solution)/shard_map/cond/branch_1_fun/ppermute | solution.py:199
  16.7 12.1 %collective-permute-start.8 = (bf16[128,256]{1,0:T(8,128)(2,1)S(1)}, bf16[128,256]{1,0:T(8,128)(2,1)S(1)}, u32[]{:S(2)}, u32[]{:S(2)}) collective-permute-start(bf16[128,256]{1,0:T(8,128)(2,1)S(1)} %get-tuple-element.89), channel_id=1, source_target_pairs={{0,8},{4,12},{8,0},{12,4},{1,9},{5,13},{9,1},{13,5},{2,10},{6,14},... | collective-permute-start | bytes 196616 | tf_op jit(solution)/shard_map/ppermute | solution.py:199
  17.1 11.7 %collective-permute-start.9 = (bf16[128,256]{1,0:T(8,128)(2,1)S(1)}, bf16[128,256]{1,0:T(8,128)(2,1)S(1)}, u32[]{:S(2)}, u32[]{:S(2)}) collective-permute-start(bf16[128,256]{1,0:T(8,128)(2,1)S(1)} %get-tuple-element.90), channel_id=1, source_target_pairs={{0,12},{4,8},{8,4},{12,0},{1,13},{5,9},{9,5},{13,1},{2,14},{6,10},... | collective-permute-start | bytes 196616 | tf_op jit(solution)/shard_map/ppermute | solution.py:199
  19.8 1.7 %collective-permute-start = (bf16[128,1024]{1,0:T(8,128)(2,1)S(1)}, bf16[128,1024]{1,0:T(8,128)(2,1)S(1)}, u32[]{:S(2)}, u32[]{:S(2)}) collective-permute-start(bf16[128,1024]{1,0:T(8,128)(2,1)S(1)} %get-tuple-element.64.refs_5_), channel_id=1, source_target_pairs={{0,1},{1,0},{2,3},{3,2},{4,5},{5,4},{6,7},{7,6},{8,9},{9,8},{10,11... | collective-permute-start | bytes 786440 | tf_op jit(solution)/shard_map/cond/branch_1_fun/ppermute | solution.py:199
  22.7 1.6 %collective-permute-start.1 = (bf16[2,128,256]{2,1,0:T(8,128)(2,1)S(1)}, bf16[2,128,256]{2,1,0:T(8,128)(2,1)S(1)}, u32[]{:S(2)}, u32[]{:S(2)}) collective-permute-start(bf16[2,128,256]{2,1,0:T(8,128)(2,1)S(1)} %get-tuple-element.70), channel_id=1, source_target_pairs={{0,1},{1,0},{2,3},{3,2},{4,5},{5,4},{6,7},{7,6},{8,9},{9,8},{10,11... | collective-permute-start | bytes 393224 | tf_op jit(solution)/shard_map/cond/branch_1_fun/ppermute | solution.py:199
  23.3 4.3 %collective-permute-start.3 = (bf16[128,256]{1,0:T(8,128)(2,1)S(1)}, bf16[128,256]{1,0:T(8,128)(2,1)S(1)}, u32[]{:S(2)}, u32[]{:S(2)}) collective-permute-start(bf16[128,256]{1,0:T(8,128)(2,1)S(1)} %get-tuple-element.72), channel_id=1, source_target_pairs={{0,4},{4,0},{8,12},{12,8},{1,5},{5,1},{9,13},{13,9},{2,6},{6,2},{1... | collective-permute-start | bytes 196616 | tf_op jit(solution)/shard_map/cond/branch_1_fun/ppermute | solution.py:199
  24.3 4.4 %collective-permute-start.2 = (bf16[128,256]{1,0:T(8,128)(2,1)S(1)}, bf16[128,256]{1,0:T(8,128)(2,1)S(1)}, u32[]{:S(2)}, u32[]{:S(2)}) collective-permute-start(bf16[128,256]{1,0:T(8,128)(2,1)S(1)} %fusion.3), channel_id=1, source_target_pairs={{0,2},{1,3},{2,0},{3,1},{4,6},{5,7},{6,4},{7,5},{8,10},{9,11},{10,... | collective-permute-start | bytes 196616 | tf_op jit(solution)/shard_map/cond/branch_1_fun/ppermute | solution.py:199

commit v10 on v9

--- a/solution.py
+++ b/solution.py
@@ -85,21 +85,21 @@
     copies = [
         pltpu.make_async_copy(src, dst, sems.at[i])
         for i, (src, dst) in enumerate(
-            [(rows_hbm, rows_ref), (cols_hbm, cols_ref), (x_hbm, x_ref), (u_hbm, u_ref), (v_hbm, v_ref)]
+            [(u_hbm, u_ref), (x_hbm, x_ref), (rows_hbm, rows_ref), (cols_hbm, cols_ref), (v_hbm, v_ref)]
         )
     ]
     for copy in copies:
         copy.start()
     group = lax.axis_index("row")
     half = lax.rem(lax.axis_index("col"), 2)
-    copies[0].wait()
-    copies[1].wait()
+    copies[2].wait()
+    copies[3].wait()
     row_lane = lane_ids(rows_ref, rank)
     col_lane = lane_ids(cols_ref, rank)
     lanes_ref[0:1, :] = row_lane
     lanes_ref[1:2, :] = col_lane
-    copies[2].wait()
-    copies[3].wait()
+    copies[0].wait()
+    copies[1].wait()
     every = dot_t(x_ref[...], u_ref[...])
     coef = jnp.zeros((exc, every.shape[1]), F32)
     for c in range(clusters):
@@ -228,12 +228,13 @@
     def pair_sum(send, keep):
         return keep + swap(send, "col", col_count, 1).astype(F32)
 
-    def col_sum(total, between=lambda leaving: leaving):
+    def chunks(total):
         def chunk(m):
             return lax.dynamic_index_in_dim(total, place // 2 ^ m, 0, keepdims=False)
 
-        leaving = between([chunk(m).astype(BF16) for m in range(1, pairs)])
-        out = chunk(0)
+        return chunk(0), [chunk(m).astype(BF16) for m in range(1, pairs)]
+
+    def col_sum(out, leaving):
         for m, part in enumerate(leaving):
             out = out + swap(part, "col", col_count, 2 * m + 2).astype(F32)
         return out
@@ -291,20 +292,15 @@
             name="kept",
         )(mask, v)
         total = pair_sum(send, keep)
-        held = []
-
-        def with_near(leaving):
-            *leaving, x_near = lax.optimization_barrier((*leaving, charges))
-            held.append(near_of(x_near))
-            return leaving
-
-        mirror = col_sum(total, with_near).astype(BF16)
-        return [mirror[i * span : (i + 1) * span] for i in range(others)], held[0], lanes
-
-    mirror, near, lanes = stage(local)
-    from_rows = [swap(mirror[d - 1], "row", row_count, d) for d in range(2, row_count)]
-    *got, lanes = lax.optimization_barrier((*got, lanes))
-    whole, *got = lax.optimization_barrier((whole, *got))
+        far, leaving = chunks(total[:, span:])
+        *leaving, x_near = lax.optimization_barrier((*leaving, charges))
+        near = near_of(x_near)
+        far = col_sum(far, leaving).astype(BF16)
+        return chunks(total[:, :span]), [far[i * span : (i + 1) * span] for i in range(others - 1)], near, lanes
+
+    (one, one_leaving), far, near, lanes = stage(local)
+    from_rows = [swap(part, "row", row_count, i + 2) for i, part in enumerate(far)]
+    whole, *got, lanes = lax.optimization_barrier((whole, *got, lanes))
 
     def forward():
         other = [swap(piece, "col", col_count, 1) for piece in got]
@@ -335,7 +331,8 @@
             cost_estimate=pl.CostEstimate(flops=1024, bytes_accessed=1024, transcendentals=0),
             name="forward",
         )(lanes, early, *fetched, *other)
-        return col_sum(pair_sum(send, keep)) + swap(mirror[0], "row", row_count, 1).astype(F32)
+        joined = col_sum(one, one_leaving).astype(BF16)
+        return col_sum(*chunks(pair_sum(send, keep))) + swap(joined, "row", row_count, 1).astype(F32)
 
     total = stage(forward)
     for term in from_rows:

time: 29.7 us -> 31.8 us (1.071)
  starting transfers between devices: 12.9 us -> 14.9 us
  waiting for transfers between devices: 6.17 us -> 4.49 us
  local copies, waits for them, and re-layouts: 0.07 us -> 1.41 us
  other arithmetic: 0.85 us -> 1.84 us
  Pallas kernels: 9.3 us -> 8.76 us
    ppermute x9 -> x10, starting transfers between devices: 8.89 us -> 12.3 us  [swap(): return lax.ppermute(value, axis, [(i, i ^ step) for i in range(size)])]
    ppermute x9 -> x10, waiting for transfers between devices: 6.17 us -> 4.49 us  [swap(): return lax.ppermute(value, axis, [(i, i ^ step) for i in range(size)])]
    ppermute x1, starting transfers between devices: 4.04 us -> 2.59 us  [body(): lax.ppermute(x, ('row', 'col'), rows_perm(d))]
    add x2, other arithmetic: 0.1 us -> 1.1 us  [pair_sum(): return keep + swap(send, 'col', col_count, 1).astype(F32)]
    slice x1 -> x3, local copies, waits for them, and re-layouts: 0.02 us -> 0.71 us  [the longest x1 0.65 us: local(): far[i * span:(i + 1) * span]]
    pallas_call x1, Pallas kernels: 3.89 us -> 3.25 us  [near_of(): pl.pallas_call(lambda *refs: near_kernel(clusters, exc, *refs), in_specs=...]
    convert_element_type x2 -> x3, local copies, waits for them, and re-layouts: 0.05 us -> 0.68 us  [chunks(): return (chunk(0), [chunk(m).astype(BF16) for m in range(1, pairs)])]
  transfers between devices with their start and end apart: 10 -> 11, of which waited for: 5 -> 4; matrix products, arithmetic and copies ran while one was open for 1% -> 8% of each run, Pallas kernels for 32% -> 28%
where the time goes in v10:
time: 31.8 us; the launch traced here: 31.6 us
  starting transfers between devices  14.9 us (47%)
  Pallas kernels  8.76 us (28%)
  waiting for transfers between devices  4.49 us (14%)
  other arithmetic  1.84 us (6%)
  local copies, waits for them, and re-layouts  1.41 us (4%)
    ppermute x10, starting transfers between devices, swap(): return lax.ppermute(value, axis, [(i, i ^ step) for i in range(size)])  12.3 us
    ppermute x10, waiting for transfers between devices, swap(): return lax.ppermute(value, axis, [(i, i ^ step) for i in range(size)])  4.49 us
    pallas_call x1, Pallas kernels, near_of(): pl.pallas_call(lambda *refs: near_kernel(clusters, exc, *refs), in_specs=...  3.25 us
    ppermute x1, starting transfers between devices, body(): lax.ppermute(x, ('row', 'col'), rows_perm(d))  2.59 us
    pallas_call x1, Pallas kernels, local(): pl.pallas_call(lambda *refs: mirror_kernel(clusters, exc, rank, others, *...  2.09 us
    pallas_call x1, Pallas kernels, forward(): pl.pallas_call(lambda *refs: early_kernel(clusters, exc, 1 + len(got), *r...  1.77 us
    pallas_call x1, Pallas kernels, forward(): pl.pallas_call(lambda *refs: forward_kernel(clusters, exc, *refs), in_spe...  1.27 us
    add x2, other arithmetic, pair_sum(): return keep + swap(send, 'col', col_count, 1).astype(F32)  1.1 us
  transfers between devices with their start and end apart: 11, of which 4 were waited for; matrix products, arithmetic and copies ran while one was open for 8% of the time, Pallas kernels for 28%

profile of v10, /device:TPU:0, one launch (start us, length us, event | category | flops | bytes accessed | tf_op | source)
XLA Modules:
  0.0 31.6 jit_solution(1619565145446683148)
XLA Ops:
  0.0 3.0 %collective-permute-start.7 = (bf16[128,1024]{1,0:T(8,128)(2,1)}, bf16[128,1024]{1,0:T(8,128)(2,1)}, u32[]{:S(2)}, u32[]{:S(2)}) collective-permute-start(bf16[128,1024]{1,0:T(8,128)(2,1)} %bitcast.26), channel_id=1, source_target_pairs={{0,4},{4,0},{8,12},{12,8},{1,5},{5,1},{9,13},{13,9},{2,6},{6,2},{1... | collective-permute-start | bytes 786440 | tf_op jit(solution)/shard_map/ppermute | solution.py:199
  3.0 2.6 %collective-permute-start.8 = (bf16[128,1024]{1,0:T(8,128)(2,1)}, bf16[128,1024]{1,0:T(8,128)(2,1)}, u32[]{:S(2)}, u32[]{:S(2)}) collective-permute-start(bf16[128,1024]{1,0:T(8,128)(2,1)} %bitcast.27), channel_id=1, source_target_pairs={{0,8},{1,13},{2,10},{3,15},{4,12},{5,9},{6,14},{7,11},{8,0},{9,5},... | collective-permute-start | bytes 786440 | tf_op jit(solution)/shard_map/ppermute | solution.py:261
  5.6 11.5 %conditional.2 = (f32[128,256]{1,0:T(8,128)S(1)}, bf16[128,256]{1,0:T(8,128)(2,1)}, bf16[128,256]{1,0:T(8,128)(2,1)}, bf16[128,256]{1,0:T(8,128)(2,1)}, f32[128,1024]{1,0:T(8,128)S(1)}, /*index=5*/s32[8,384]{1,0:T(8,128)S(1)}) conditional(s32[]{:T(128)} %convert_element_type.52, () %tuple.22, (s32[24]{0:T(128)}, s32[24]{0:T(128)}, ...), branch_computations={%region_0.0_spmd, %region_1.2_spmd} | conditional | flops 592918 | bytes 18615726 | solution.py:205
  5.6 2.1 %mirror.1 = (bf16[2,384,256]{2,1,0:T(8,128)(2,1)S(1)}, bf16[384,384]{1,0:T(8,128)(2,1)S(1)}, s32[8,384]{1,0:T(8,128)S(1)}) custom-call(s32[24]{0:T(128)} %get-tuple-element.99.refs_0_, s32[24]{0:T(128)} %get-tuple-element.100.refs_1_, bf16[128,1024]{1,0:T(8,128)(2,1)} %bitcast.29, bf16[384,1024]{1,0:T(8,128)(2,1)} %get-tuple-element.49.refs_3_, ...), custom_call_target="tpu_custom_call" | custom-call | flops 1024 | bytes 1024 | tf_op jit(solution)/shard_map/cond/branch_1_fun/mirror/pallas_call | solution.py:264
  7.8 0.4 %kept.1 = f32[2,384,256]{2,1,0:T(8,128)S(1)} custom-call(bf16[384,384]{1,0:T(8,128)(2,1)S(1)} %get-tuple-element.51.refs_0_, bf16[384,1024]{1,0:T(8,128)(2,1)S(1)} %copy-done), custom_call_target="tpu_custom_call" | custom-call | flops 1024 | bytes 1024 | tf_op jit(solution)/shard_map/cond/branch_1_fun/kept/pallas_call | solution.py:285
  8.2 1.4 %collective-permute-done.5 = bf16[2,384,256]{2,1,0:T(8,128)(2,1)} collective-permute-done((bf16[2,384,256]{2,1,0:T(8,128)(2,1)S(1)}, bf16[2,384,256]{2,1,0:T(8,128)(2,1)}, u32[]{:S(2)}, u32[]{:S(2)}) %collective-permute-start.5) | collective-permute-done | bytes 393248 | tf_op jit(solution)/shard_map/cond/branch_1_fun/ppermute | solution.py:199
  9.6 1.1 %convert_add_fusion = f32[2,384,256]{2,1,0:T(8,128)S(1)} fusion(f32[2,384,256]{2,1,0:T(8,128)S(1)} %kept.1, bf16[2,384,256]{2,1,0:T(8,128)(2,1)} %collective-permute-done.5), kind=kLoop, calls=%fused_computation | loop fusion | flops 393216 | bytes 1966080 | tf_op jit(solution)/shard_map/cond/branch_1_fun/add | solution.py:229
  10.8 1.6 %collective-permute-start.6 = (bf16[256,256]{1,0:T(8,128)(2,1)S(1)}, bf16[256,256]{1,0:T(8,128)(2,1)S(1)}, u32[]{:S(2)}, u32[]{:S(2)}) collective-permute-start(bf16[256,256]{1,0:T(8,128)(2,1)S(1)} %fusion.1), channel_id=1, source_target_pairs={{0,2},{1,3},{2,0},{3,1},{4,6},{5,7},{6,4},{7,5},{8,10},{9,11},{10,... | collective-permute-start | bytes 393224 | tf_op jit(solution)/shard_map/cond/branch_1_fun/ppermute | solution.py:199
  12.4 0.6 %fusion.2 = bf16[128,256]{1,0:T(8,128)(2,1)} fusion(f32[2,128,256]{2,1,0:T(8,128)S(1)} %slice.12, s32[]{:T(128)S(6)} %select_n.24), kind=kLoop, calls=%fused_computation.7 | loop fusion | bytes 131076 | tf_op jit(solution)/shard_map/cond/branch_1_fun/convert_element_type | solution.py:235
  13.0 3.3 %near.1 = f32[4,32,1024]{2,1,0:T(8,128)S(1)} custom-call(s32[1]{0:T(128)} %get-tuple-element.101.refs_0_, s32[1]{0:T(128)} %get-tuple-element.102.refs_1_, bf16[4,32,1024]{2,1,0:T(8,128)(2,1)} %get-tuple-element.58.refs_2_, bf16[1,1024,1024]{2,1,0:T(8,128)(2,1)S(1)} %copy-done.1), custom_call_target="tpu_custom_call" | custom-call | flops 1024 | bytes 1024 | tf_op jit(solution)/shard_map/cond/branch_1_fun/near/pallas_call | solution.py:243
  16.3 0.1 collective-permute-done.6
  16.5 0.7 %fusion.5 = (bf16[128,256]{1,0:T(8,128)(2,1)}, bf16[128,256]{1,0:T(8,128)(2,1)}) fusion(bf16[256,256]{1,0:T(8,128)(2,1)S(1)} %fusion), kind=kLoop, calls=%fused_computation.15 | loop fusion | bytes 262144 | tf_op jit(solution)/shard_map/cond/branch_1_fun/slice | solution.py:299
  17.1 0.4 %collective-permute-start.10 = (bf16[128,256]{1,0:T(8,128)(2,1)}, bf16[128,256]{1,0:T(8,128)(2,1)S(1)}, u32[]{:S(2)}, u32[]{:S(2)}) collective-permute-start(bf16[128,256]{1,0:T(8,128)(2,1)} %get-tuple-element.93), channel_id=1, source_target_pairs={{0,12},{4,8},{8,4},{12,0},{1,13},{5,9},{9,5},{13,1},{2,14},{6,10},... | collective-permute-start | bytes 196616 | tf_op jit(solution)/shard_map/ppermute | solution.py:199
  17.5 1.5 %collective-permute-start.9 = (bf16[128,256]{1,0:T(8,128)(2,1)}, bf16[128,256]{1,0:T(8,128)(2,1)S(1)}, u32[]{:S(2)}, u32[]{:S(2)}) collective-permute-start(bf16[128,256]{1,0:T(8,128)(2,1)} %get-tuple-element.92), channel_id=1, source_target_pairs={{0,8},{4,12},{8,0},{12,4},{1,9},{5,13},{9,1},{13,5},{2,10},{6,14},... | collective-permute-start | bytes 196616 | tf_op jit(solution)/shard_map/ppermute | solution.py:199
  19.0 11.9 %conditional.3 = (f32[128,256]{1,0:T(8,128)S(1)}) conditional(s32[]{:T(128)} %convert_element_type.52, () %tuple.21, (s32[8,384]{1,0:T(8,128)S(1)}, bf16[384,1024]{1,0:T(8,128)(2,1)}, bf16[384,1024]{1,0:T(8,128)(2,1)}, f32[128,1024]{1,0:T(8,128)S(1)}, bf16[128,1024]{1,0:T(8,128)(2,1)}, /*index=5*/bf16[128,1024]{1,0:T(8,128)(2,1)}, s32[]{:T(128)}, ...), branch_computations={%region_2.3_spmd, %region_3.4_spmd} | conditional | flops 362518 | bytes 3803582 | solution.py:205
  19.0 1.6 %collective-permute-start.3 = (bf16[128,256]{1,0:T(8,128)(2,1)}, bf16[128,256]{1,0:T(8,128)(2,1)S(1)}, u32[]{:S(2)}, u32[]{:S(2)}) collective-permute-start(bf16[128,256]{1,0:T(8,128)(2,1)} %get-tuple-element.75), channel_id=1, source_target_pairs={{0,2},{1,3},{2,0},{3,1},{4,6},{5,7},{6,4},{7,5},{8,10},{9,11},{10,... | collective-permute-start | bytes 196616 | tf_op jit(solution)/shard_map/cond/branch_1_fun/ppermute | solution.py:199
  20.6 1.8 %early.1 = (f32[32,384]{1,0:T(8,128)S(1)}, bf16[384,1024]{1,0:T(8,128)(2,1)S(1)}, bf16[384,1024]{1,0:T(8,128)(2,1)S(1)}, f32[128,1024]{1,0:T(8,128)S(1)}) custom-call(s32[8,384]{1,0:T(8,128)S(1)} %get-tuple-element.61.refs_0_, bf16[384,1024]{1,0:T(8,128)(2,1)} %get-tuple-element.62.refs_1_, bf16[384,1024]{1,0:T(8,128)(2,1)} %get-tuple-element.63.refs_2_, ...), custom_call_target="tpu_custom_call" | custom-call | flops 1024 | bytes 1024 | tf_op jit(solution)/shard_map/cond/branch_1_fun/early/pallas_call | solution.py:307
  22.4 1.3 %forward.1 = (bf16[2,128,256]{2,1,0:T(8,128)(2,1)S(1)}, f32[2,128,256]{2,1,0:T(8,128)S(1)}) custom-call(s32[8,384]{1,0:T(8,128)S(1)} %get-tuple-element.61.refs_0_, f32[32,384]{1,0:T(8,128)S(1)} %get-tuple-element.67.refs_1_, bf16[384,1024]{1,0:T(8,128)(2,1)S(1)} %get-tuple-element.68.refs_2_, bf16[384,1024]{1,0:T(8,128)(2,1)S(1)} %get-tuple-element.69.refs_3_, ...), custom_call_target="tpu_custom_call" | custom-call | flops 1024 | bytes 1024 | tf_op jit(solution)/shard_map/cond/branch_1_fun/forward/pallas_call | solution.py:325
  23.7 0.2 collective-permute-start.1
  23.9 2.5 %collective-permute-start.4 = (bf16[128,256]{1,0:T(8,128)(2,1)S(1)}, bf16[128,256]{1,0:T(8,128)(2,1)S(1)}, u32[]{:S(2)}, u32[]{:S(2)}) collective-permute-start(bf16[128,256]{1,0:T(8,128)(2,1)S(1)} %add_convert_fusion), channel_id=1, source_target_pairs={{0,4},{4,0},{8,12},{12,8},{1,5},{5,1},{9,13},{13,9},{2,6},{6,2},{1... | collective-permute-start | bytes 196616 | tf_op jit(solution)/shard_map/cond/branch_1_fun/ppermute | solution.py:199
  26.5 1.4 %collective-permute-start.2 = (bf16[128,256]{1,0:T(8,128)(2,1)S(1)}, bf16[128,256]{1,0:T(8,128)(2,1)S(1)}, u32[]{:S(2)}, u32[]{:S(2)}) collective-permute-start(bf16[128,256]{1,0:T(8,128)(2,1)S(1)} %fusion.4), channel_id=1, source_target_pairs={{0,2},{1,3},{2,0},{3,1},{4,6},{5,7},{6,4},{7,5},{8,10},{9,11},{10,... | collective-permute-start | bytes 196616 | tf_op jit(solution)/shard_map/cond/branch_1_fun/ppermute | solution.py:199
  27.9 1.2 %collective-permute-done.4 = bf16[128,256]{1,0:T(8,128)(2,1)S(1)} collective-permute-done((bf16[128,256]{1,0:T(8,128)(2,1)S(1)}, bf16[128,256]{1,0:T(8,128)(2,1)S(1)}, u32[]{:S(2)}, u32[]{:S(2)}) %collective-permute-start.4) | collective-permute-done | bytes 65568 | tf_op jit(solution)/shard_map/cond/branch_1_fun/ppermute | solution.py:199
  29.1 1.8 %collective-permute-done.2 = bf16[128,256]{1,0:T(8,128)(2,1)S(1)} collective-permute-done((bf16[128,256]{1,0:T(8,128)(2,1)S(1)}, bf16[128,256]{1,0:T(8,128)(2,1)S(1)}, u32[]{:S(2)}, u32[]{:S(2)}) %collective-permute-start.2) | collective-permute-done | bytes 65568 | tf_op jit(solution)/shard_map/cond/branch_1_fun/ppermute | solution.py:199
  30.9 0.7 %convert_add_fusion.2 = f32[128,256]{1,0:T(8,128)} fusion(bf16[128,256]{1,0:T(8,128)(2,1)S(1)} %collective-permute-done.10, f32[128,256]{1,0:T(8,128)S(1)} %get-tuple-element.118, bf16[128,256]{1,0:T(8,128)(2,1)S(1)} %collective-permute-done.9), kind=kLoop, calls=%fused_computation.14 | loop fusion | flops 131072 | bytes 393216 | tf_op jit(solution)/shard_map/add | solution.py:339
  (22 shorter events, 0.3 us)
Async XLA Ops:
  0.0 19.0 %collective-permute-start.7 = (bf16[128,1024]{1,0:T(8,128)(2,1)}, bf16[128,1024]{1,0:T(8,128)(2,1)}, u32[]{:S(2)}, u32[]{:S(2)}) collective-permute-start(bf16[128,1024]{1,0:T(8,128)(2,1)} %bitcast.26), channel_id=1, source_target_pairs={{0,4},{4,0},{8,12},{12,8},{1,5},{5,1},{9,13},{13,9},{2,6},{6,2},{1... | collective-permute-start | bytes 786440 | tf_op jit(solution)/shard_map/ppermute | solution.py:199
  3.0 16.0 %collective-permute-start.8 = (bf16[128,1024]{1,0:T(8,128)(2,1)}, bf16[128,1024]{1,0:T(8,128)(2,1)}, u32[]{:S(2)}, u32[]{:S(2)}) collective-permute-start(bf16[128,1024]{1,0:T(8,128)(2,1)} %bitcast.27), channel_id=1, source_target_pairs={{0,8},{1,13},{2,10},{3,15},{4,12},{5,9},{6,14},{7,11},{8,0},{9,5},... | collective-permute-start | bytes 786440 | tf_op jit(solution)/shard_map/ppermute | solution.py:261
  5.6 2.2 %copy-start = (bf16[384,1024]{1,0:T(8,128)(2,1)S(1)}, bf16[384,1024]{1,0:T(8,128)(2,1)}, u32[]{:S(2)}) copy-start(bf16[384,1024]{1,0:T(8,128)(2,1)} %get-tuple-element.50.refs_4_.refs_1_) | copy-start | bytes 2359300 | tf_op jit(solution)/shard_map/cond
  7.7 1.9 %collective-permute-start.5 = (bf16[2,384,256]{2,1,0:T(8,128)(2,1)S(1)}, bf16[2,384,256]{2,1,0:T(8,128)(2,1)}, u32[]{:S(2)}, u32[]{:S(2)}) collective-permute-start(bf16[2,384,256]{2,1,0:T(8,128)(2,1)S(1)} %get-tuple-element.52), channel_id=1, source_target_pairs={{0,1},{1,0},{2,3},{3,2},{4,5},{5,4},{6,7},{7,6},{8,9},{9,8},{10,11... | collective-permute-start | bytes 1179656 | tf_op jit(solution)/shard_map/cond/branch_1_fun/ppermute | solution.py:199
  8.2 4.8 %copy-start.1 = (bf16[1,1024,1024]{2,1,0:T(8,128)(2,1)S(1)}, bf16[1,1024,1024]{2,1,0:T(8,128)(2,1)}, u32[]{:S(2)}) copy-start(bf16[1,1024,1024]{2,1,0:T(8,128)(2,1)} %get-tuple-element.103.refs_3_) | copy-start | bytes 6291460 | tf_op jit(solution)/shard_map/cond
  10.8 5.6 %collective-permute-start.6 = (bf16[256,256]{1,0:T(8,128)(2,1)S(1)}, bf16[256,256]{1,0:T(8,128)(2,1)S(1)}, u32[]{:S(2)}, u32[]{:S(2)}) collective-permute-start(bf16[256,256]{1,0:T(8,128)(2,1)S(1)} %fusion.1), channel_id=1, source_target_pairs={{0,2},{1,3},{2,0},{3,1},{4,6},{5,7},{6,4},{7,5},{8,10},{9,11},{10,... | collective-permute-start | bytes 393224 | tf_op jit(solution)/shard_map/cond/branch_1_fun/ppermute | solution.py:199
  17.1 13.8 %collective-permute-start.10 = (bf16[128,256]{1,0:T(8,128)(2,1)}, bf16[128,256]{1,0:T(8,128)(2,1)S(1)}, u32[]{:S(2)}, u32[]{:S(2)}) collective-permute-start(bf16[128,256]{1,0:T(8,128)(2,1)} %get-tuple-element.93), channel_id=1, source_target_pairs={{0,12},{4,8},{8,4},{12,0},{1,13},{5,9},{9,5},{13,1},{2,14},{6,10},... | collective-permute-start | bytes 196616 | tf_op jit(solution)/shard_map/ppermute | solution.py:199
  17.5 13.4 %collective-permute-start.9 = (bf16[128,256]{1,0:T(8,128)(2,1)}, bf16[128,256]{1,0:T(8,128)(2,1)S(1)}, u32[]{:S(2)}, u32[]{:S(2)}) collective-permute-start(bf16[128,256]{1,0:T(8,128)(2,1)} %get-tuple-element.92), channel_id=1, source_target_pairs={{0,8},{4,12},{8,0},{12,4},{1,9},{5,13},{9,1},{13,5},{2,10},{6,14},... | collective-permute-start | bytes 196616 | tf_op jit(solution)/shard_map/ppermute | solution.py:199
  19.0 3.4 %collective-permute-start = (bf16[128,1024]{1,0:T(8,128)(2,1)}, bf16[128,1024]{1,0:T(8,128)(2,1)S(1)}, u32[]{:S(2)}, u32[]{:S(2)}) collective-permute-start(bf16[128,1024]{1,0:T(8,128)(2,1)} %get-tuple-element.66.refs_5_), channel_id=1, source_target_pairs={{0,1},{1,0},{2,3},{3,2},{4,5},{5,4},{6,7},{7,6},{8,9},{9,8},{10,11... | collective-permute-start | bytes 786440 | tf_op jit(solution)/shard_map/cond/branch_1_fun/ppermute | solution.py:199
  19.0 4.9 %collective-permute-start.3 = (bf16[128,256]{1,0:T(8,128)(2,1)}, bf16[128,256]{1,0:T(8,128)(2,1)S(1)}, u32[]{:S(2)}, u32[]{:S(2)}) collective-permute-start(bf16[128,256]{1,0:T(8,128)(2,1)} %get-tuple-element.75), channel_id=1, source_target_pairs={{0,2},{1,3},{2,0},{3,1},{4,6},{5,7},{6,4},{7,5},{8,10},{9,11},{10,... | collective-permute-start | bytes 196616 | tf_op jit(solution)/shard_map/cond/branch_1_fun/ppermute | solution.py:199
  23.7 2.8 %collective-permute-start.1 = (bf16[2,128,256]{2,1,0:T(8,128)(2,1)S(1)}, bf16[2,128,256]{2,1,0:T(8,128)(2,1)S(1)}, u32[]{:S(2)}, u32[]{:S(2)}) collective-permute-start(bf16[2,128,256]{2,1,0:T(8,128)(2,1)S(1)} %get-tuple-element.72), channel_id=1, source_target_pairs={{0,1},{1,0},{2,3},{3,2},{4,5},{5,4},{6,7},{7,6},{8,9},{9,8},{10,11... | collective-permute-start | bytes 393224 | tf_op jit(solution)/shard_map/cond/branch_1_fun/ppermute | solution.py:199
  23.9 5.2 %collective-permute-start.4 = (bf16[128,256]{1,0:T(8,128)(2,1)S(1)}, bf16[128,256]{1,0:T(8,128)(2,1)S(1)}, u32[]{:S(2)}, u32[]{:S(2)}) collective-permute-start(bf16[128,256]{1,0:T(8,128)(2,1)S(1)} %add_convert_fusion), channel_id=1, source_target_pairs={{0,4},{4,0},{8,12},{12,8},{1,5},{5,1},{9,13},{13,9},{2,6},{6,2},{1... | collective-permute-start | bytes 196616 | tf_op jit(solution)/shard_map/cond/branch_1_fun/ppermute | solution.py:199
  26.5 4.3 %collective-permute-start.2 = (bf16[128,256]{1,0:T(8,128)(2,1)S(1)}, bf16[128,256]{1,0:T(8,128)(2,1)S(1)}, u32[]{:S(2)}, u32[]{:S(2)}) collective-permute-start(bf16[128,256]{1,0:T(8,128)(2,1)S(1)} %fusion.4), channel_id=1, source_target_pairs={{0,2},{1,3},{2,0},{3,1},{4,6},{5,7},{6,4},{7,5},{8,10},{9,11},{10,... | collective-permute-start | bytes 196616 | tf_op jit(solution)/shard_map/cond/branch_1_fun/ppermute | solution.py:199

commit v11 on v10

--- a/solution.py
+++ b/solution.py
@@ -131,6 +131,14 @@
     each(steps, one)
 
 
+def pair_kernel(split, keep_ref, recv_ref, *out_refs):
+    mine = lax.axis_index("col") // 2
+    for m in range(keep_ref.shape[0]):
+        total = keep_ref[mine ^ m] + recv_ref[mine ^ m].astype(F32)
+        out_refs[2 * m][...] = total[:split].astype(out_refs[2 * m].dtype)
+        out_refs[2 * m + 1][...] = total[split:].astype(out_refs[2 * m + 1].dtype)
+
+
 def near_kernel(clusters, exc, rows_ref, cols_ref, x_ref, n_ref, out_ref):
     first = lax.axis_index("row") * clusters
     out_ref[...] = jnp.zeros_like(out_ref)
@@ -291,12 +299,23 @@
             cost_estimate=pl.CostEstimate(flops=1024, bytes_accessed=1024, transcendentals=0),
             name="kept",
         )(mask, v)
-        total = pair_sum(send, keep)
-        far, leaving = chunks(total[:, span:])
+        kinds = [F32] + [BF16] * (pairs - 1)
+        one, far, *leaving = pl.pallas_call(
+            lambda *refs: pair_kernel(span, *refs),
+            in_specs=[VMEM] * 2,
+            out_specs=[VMEM] * (2 * pairs),
+            out_shape=[
+                jax.ShapeDtypeStruct((rows * span, width), kind) for kind in kinds for rows in (1, others - 1)
+            ],
+            compiler_params=params(others),
+            cost_estimate=pl.CostEstimate(flops=1024, bytes_accessed=1024, transcendentals=0),
+            name="pair",
+        )(keep, swap(send, "col", col_count, 1))
+        one_leaving, leaving = leaving[::2], leaving[1::2]
         *leaving, x_near = lax.optimization_barrier((*leaving, charges))
         near = near_of(x_near)
         far = col_sum(far, leaving).astype(BF16)
-        return chunks(total[:, :span]), [far[i * span : (i + 1) * span] for i in range(others - 1)], near, lanes
+        return (one, one_leaving), [far[i * span : (i + 1) * span] for i in range(others - 1)], near, lanes
 
     (one, one_leaving), far, near, lanes = stage(local)
     from_rows = [swap(part, "row", row_count, i + 2) for i, part in enumerate(far)]

time: 31.8 us -> 31.7 us (level)
  local copies, waits for them, and re-layouts: 1.41 us -> 0.04 us
  waiting for transfers between devices: 4.49 us -> 5.83 us
  other arithmetic: 1.84 us -> 0.77 us
  starting transfers between devices: 14.9 us -> 15.9 us
    add x2 -> x1, other arithmetic: 1.1 us -> 0.03 us  [pair_sum(): return keep + swap(send, 'col', col_count, 1).astype(F32)]
    ppermute x10, starting transfers between devices: 12.3 us -> 13.3 us  [swap(): return lax.ppermute(value, axis, [(i, i ^ step) for i in range(size)])]
    ppermute x10, waiting for transfers between devices: 4.49 us -> 5.33 us  [swap(): return lax.ppermute(value, axis, [(i, i ^ step) for i in range(size)])]
    convert_element_type x3 -> x1, local copies, waits for them, and re-layouts: 0.68 us -> 0.02 us  [chunks(): return (chunk(0), [chunk(m).astype(BF16) for m in range(1, pairs)])]
    slice x1, local copies, waits for them, and re-layouts: 0.65 us -> 0.01 us  [local(): far[i * span:(i + 1) * span]]
    ppermute x1, waiting for transfers between devices: 0.01 us -> 0.49 us  [body(): lax.ppermute(x, ('row', 'col'), rows_perm(d))]
  transfers between devices with their start and end apart: 11 -> 11, of which waited for: 4 -> 5; matrix products, arithmetic and copies ran while one was open for 8% -> 0% of each run, Pallas kernels for 28% -> 28%
where the time goes in v11:
time: 31.7 us; the launch traced here: 31.5 us
  starting transfers between devices  15.9 us (50%)
  Pallas kernels  8.83 us (28%)
  waiting for transfers between devices  5.83 us (18%)
  other arithmetic  0.77 us (2%)
    ppermute x10, starting transfers between devices, swap(): return lax.ppermute(value, axis, [(i, i ^ step) for i in range(size)])  13.3 us
    ppermute x10, waiting for transfers between devices, swap(): return lax.ppermute(value, axis, [(i, i ^ step) for i in range(size)])  5.33 us
    pallas_call x1, Pallas kernels, near_of(): pl.pallas_call(lambda *refs: near_kernel(clusters, exc, *refs), in_specs=...  3.18 us
    ppermute x1, starting transfers between devices, body(): lax.ppermute(x, ('row', 'col'), rows_perm(d))  2.59 us
    pallas_call x1, Pallas kernels, local(): pl.pallas_call(lambda *refs: mirror_kernel(clusters, exc, rank, others, *...  2.16 us
    pallas_call x1, Pallas kernels, forward(): pl.pallas_call(lambda *refs: early_kernel(clusters, exc, 1 + len(got), *r...  1.77 us
    pallas_call x1, Pallas kernels, forward(): pl.pallas_call(lambda *refs: forward_kernel(clusters, exc, *refs), in_spe...  1.27 us
    add x1, other arithmetic, body(): total = total + term.astype(F32)  0.68 us
  transfers between devices with their start and end apart: 11, of which 5 were waited for; matrix products, arithmetic and copies ran while one was open for 0% of the time, Pallas kernels for 28%

profile of v11, /device:TPU:0, one launch (start us, length us, event | category | flops | bytes accessed | tf_op | source)
XLA Modules:
  0.0 31.5 jit_solution(10372025616382830708)
XLA Ops:
  0.0 3.0 %collective-permute-start.7 = (bf16[128,1024]{1,0:T(8,128)(2,1)}, bf16[128,1024]{1,0:T(8,128)(2,1)}, u32[]{:S(2)}, u32[]{:S(2)}) collective-permute-start(bf16[128,1024]{1,0:T(8,128)(2,1)} %bitcast.15), channel_id=1, source_target_pairs={{0,4},{4,0},{8,12},{12,8},{1,5},{5,1},{9,13},{13,9},{2,6},{6,2},{1... | collective-permute-start | bytes 786440 | tf_op jit(solution)/shard_map/ppermute | solution.py:207
  3.0 2.6 %collective-permute-start.8 = (bf16[128,1024]{1,0:T(8,128)(2,1)}, bf16[128,1024]{1,0:T(8,128)(2,1)}, u32[]{:S(2)}, u32[]{:S(2)}) collective-permute-start(bf16[128,1024]{1,0:T(8,128)(2,1)} %bitcast.16), channel_id=1, source_target_pairs={{0,8},{1,13},{2,10},{3,15},{4,12},{5,9},{6,14},{7,11},{8,0},{9,5},... | collective-permute-start | bytes 786440 | tf_op jit(solution)/shard_map/ppermute | solution.py:269
  5.6 9.7 %conditional.2 = (f32[128,256]{1,0:T(8,128)S(1)}, bf16[128,256]{1,0:T(8,128)(2,1)S(1)}, bf16[128,256]{1,0:T(8,128)(2,1)S(1)}, bf16[128,256]{1,0:T(8,128)(2,1)S(1...) conditional(s32[]{:T(128)} %convert_element_type.37, () %tuple.22, (s32[24]{0:T(128)}, s32[24]{0:T(128)}, ...), branch_computations={%region_0.0_spmd, %region_1.0_spmd} | conditional | flops 200704 | bytes 15470804 | solution.py:213
  5.6 2.2 %mirror.1 = (bf16[2,384,256]{2,1,0:T(8,128)(2,1)S(1)}, bf16[384,384]{1,0:T(8,128)(2,1)S(1)}, s32[8,384]{1,0:T(8,128)S(1)}) custom-call(s32[24]{0:T(128)} %get-tuple-element.100.refs_0_, s32[24]{0:T(128)} %get-tuple-element.101.refs_1_, bf16[128,1024]{1,0:T(8,128)(2,1)} %bitcast.18, bf16[384,1024]{1,0:T(8,128)(2,1)} %get-tuple-element.47.refs_3_, ...), custom_call_target="tpu_custom_call" | custom-call | flops 1024 | bytes 1024 | tf_op jit(solution)/shard_map/cond/branch_1_fun/mirror/pallas_call | solution.py:272
  7.8 0.1 collective-permute-start.5
  7.9 0.4 %kept.1.refs_0_ = f32[2,384,256]{2,1,0:T(8,128)S(1)} custom-call(bf16[384,384]{1,0:T(8,128)(2,1)S(1)} %get-tuple-element.49.refs_0_, bf16[384,1024]{1,0:T(8,128)(2,1)S(1)} %copy-done), custom_call_target="tpu_custom_call" | custom-call | flops 1024 | bytes 1024 | tf_op jit(solution)/shard_map/cond/branch_1_fun/kept/pallas_call | solution.py:293
  8.3 1.3 %collective-permute-done.5.refs_1_ = bf16[2,384,256]{2,1,0:T(8,128)(2,1)S(1)} collective-permute-done((bf16[2,384,256]{2,1,0:T(8,128)(2,1)S(1)}, bf16[2,384,256]{2,1,0:T(8,128)(2,1)S(1)}, u32[]{:S(2)}, u32[]{:S(2)}) %collective-permute-start.5) | collective-permute-done | bytes 393248 | tf_op jit(solution)/shard_map/cond/branch_1_fun/ppermute | solution.py:207
  9.6 0.1 pair.1
  9.6 1.6 %collective-permute-start.6 = (bf16[256,256]{1,0:T(8,128)(2,1)S(1)}, bf16[256,256]{1,0:T(8,128)(2,1)S(1)}, u32[]{:S(2)}, u32[]{:S(2)}) collective-permute-start(bf16[256,256]{1,0:T(8,128)(2,1)S(1)} %get-tuple-element.56), channel_id=1, source_target_pairs={{0,2},{1,3},{2,0},{3,1},{4,6},{5,7},{6,4},{7,5},{8,10},{9,11},{10,... | collective-permute-start | bytes 393224 | tf_op jit(solution)/shard_map/cond/branch_1_fun/ppermute | solution.py:207
  11.2 3.2 %near.1 = f32[4,32,1024]{2,1,0:T(8,128)} custom-call(s32[1]{0:T(128)} %get-tuple-element.102.refs_0_, s32[1]{0:T(128)} %get-tuple-element.103.refs_1_, bf16[4,32,1024]{2,1,0:T(8,128)(2,1)S(1)} %copy-done.2, bf16[1,1024,1024]{2,1,0:T(8,128)(2,1)S(1)} %copy-done.1), custom_call_target="tpu_custom_call" | custom-call | flops 1024 | bytes 1024 | tf_op jit(solution)/shard_map/cond/branch_1_fun/near/pallas_call | solution.py:251
  14.4 0.9 %collective-permute-done.6 = bf16[256,256]{1,0:T(8,128)(2,1)S(1)} collective-permute-done((bf16[256,256]{1,0:T(8,128)(2,1)S(1)}, bf16[256,256]{1,0:T(8,128)(2,1)S(1)}, u32[]{:S(2)}, u32[]{:S(2)}) %collective-permute-start.6) | collective-permute-done | bytes 131104 | tf_op jit(solution)/shard_map/cond/branch_1_fun/ppermute | solution.py:207
  15.3 0.4 %collective-permute-start.10 = (bf16[128,256]{1,0:T(8,128)(2,1)S(1)}, bf16[128,256]{1,0:T(8,128)(2,1)S(1)}, u32[]{:S(2)}, u32[]{:S(2)}) collective-permute-start(bf16[128,256]{1,0:T(8,128)(2,1)S(1)} %get-tuple-element.94), channel_id=1, source_target_pairs={{0,12},{4,8},{8,4},{12,0},{1,13},{5,9},{9,5},{13,1},{2,14},{6,10},... | collective-permute-start | bytes 196616 | tf_op jit(solution)/shard_map/ppermute | solution.py:207
  15.7 1.5 %collective-permute-start.9 = (bf16[128,256]{1,0:T(8,128)(2,1)S(1)}, bf16[128,256]{1,0:T(8,128)(2,1)S(1)}, u32[]{:S(2)}, u32[]{:S(2)}) collective-permute-start(bf16[128,256]{1,0:T(8,128)(2,1)S(1)} %get-tuple-element.93), channel_id=1, source_target_pairs={{0,8},{4,12},{8,0},{12,4},{1,9},{5,13},{9,1},{13,5},{2,10},{6,14},... | collective-permute-start | bytes 196616 | tf_op jit(solution)/shard_map/ppermute | solution.py:207
  17.3 0.5 %collective-permute-done.8 = bf16[128,1024]{1,0:T(8,128)(2,1)} collective-permute-done((bf16[128,1024]{1,0:T(8,128)(2,1)}, bf16[128,1024]{1,0:T(8,128)(2,1)}, u32[]{:S(2)}, u32[]{:S(2)}) %collective-permute-start.8) | collective-permute-done | bytes 262176 | tf_op jit(solution)/shard_map/ppermute | solution.py:269
  17.8 13.1 %conditional.3 = (f32[128,256]{1,0:T(8,128)S(1)}) conditional(s32[]{:T(128)} %convert_element_type.37, () %tuple.21, (s32[8,384]{1,0:T(8,128)S(1)}, bf16[384,1024]{1,0:T(8,128)(2,1)}, bf16[384,1024]{1,0:T(8,128)(2,1)}, f32[128,1024]{1,0:T(8,128)}, bf16[128,1024]{1,0:T(8,128)(2,1)}, /*index=5*/bf16[128,1024]{1,0:T(8,128)(2,1)}, s32[]{:T(128)}, ...), branch_computations={%region_2.0_spmd, %region_3.4_spmd} | conditional | flops 362518 | bytes 3803582 | solution.py:213
  17.8 1.5 %collective-permute-start.3 = (bf16[128,256]{1,0:T(8,128)(2,1)S(1)}, bf16[128,256]{1,0:T(8,128)(2,1)S(1)}, u32[]{:S(2)}, u32[]{:S(2)}) collective-permute-start(bf16[128,256]{1,0:T(8,128)(2,1)S(1)} %get-tuple-element.76), channel_id=1, source_target_pairs={{0,2},{1,3},{2,0},{3,1},{4,6},{5,7},{6,4},{7,5},{8,10},{9,11},{10,... | collective-permute-start | bytes 196616 | tf_op jit(solution)/shard_map/cond/branch_1_fun/ppermute | solution.py:207
  19.3 1.8 %early.1 = (f32[32,384]{1,0:T(8,128)S(1)}, bf16[384,1024]{1,0:T(8,128)(2,1)S(1)}, bf16[384,1024]{1,0:T(8,128)(2,1)S(1)}, f32[128,1024]{1,0:T(8,128)S(1)}) custom-call(s32[8,384]{1,0:T(8,128)S(1)} %get-tuple-element.62.refs_0_, bf16[384,1024]{1,0:T(8,128)(2,1)} %get-tuple-element.63.refs_1_, bf16[384,1024]{1,0:T(8,128)(2,1)} %get-tuple-element.64.refs_2_, ...), custom_call_target="tpu_custom_call" | custom-call | flops 1024 | bytes 1024 | tf_op jit(solution)/shard_map/cond/branch_1_fun/early/pallas_call | solution.py:326
  21.1 1.3 %forward.1 = (bf16[2,128,256]{2,1,0:T(8,128)(2,1)S(1)}, f32[2,128,256]{2,1,0:T(8,128)S(1)}) custom-call(s32[8,384]{1,0:T(8,128)S(1)} %get-tuple-element.62.refs_0_, f32[32,384]{1,0:T(8,128)S(1)} %get-tuple-element.68.refs_1_, bf16[384,1024]{1,0:T(8,128)(2,1)S(1)} %get-tuple-element.69.refs_2_, bf16[384,1024]{1,0:T(8,128)(2,1)S(1)} %get-tuple-element.70.refs_3_, ...), custom_call_target="tpu_custom_call" | custom-call | flops 1024 | bytes 1024 | tf_op jit(solution)/shard_map/cond/branch_1_fun/forward/pallas_call | solution.py:344
  22.4 0.3 collective-permute-start.1
  22.7 3.7 %collective-permute-start.4 = (bf16[128,256]{1,0:T(8,128)(2,1)S(1)}, bf16[128,256]{1,0:T(8,128)(2,1)S(1)}, u32[]{:S(2)}, u32[]{:S(2)}) collective-permute-start(bf16[128,256]{1,0:T(8,128)(2,1)S(1)} %add_convert_fusion.1), channel_id=1, source_target_pairs={{0,4},{4,0},{8,12},{12,8},{1,5},{5,1},{9,13},{13,9},{2,6},{6,2},{1... | collective-permute-start | bytes 196616 | tf_op jit(solution)/shard_map/cond/branch_1_fun/ppermute | solution.py:207
  26.5 1.2 %collective-permute-start.2 = (bf16[128,256]{1,0:T(8,128)(2,1)S(1)}, bf16[128,256]{1,0:T(8,128)(2,1)S(1)}, u32[]{:S(2)}, u32[]{:S(2)}) collective-permute-start(bf16[128,256]{1,0:T(8,128)(2,1)S(1)} %fusion.1), channel_id=1, source_target_pairs={{0,2},{1,3},{2,0},{3,1},{4,6},{5,7},{6,4},{7,5},{8,10},{9,11},{10,... | collective-permute-start | bytes 196616 | tf_op jit(solution)/shard_map/cond/branch_1_fun/ppermute | solution.py:207
  27.7 1.3 %collective-permute-done.4 = bf16[128,256]{1,0:T(8,128)(2,1)S(1)} collective-permute-done((bf16[128,256]{1,0:T(8,128)(2,1)S(1)}, bf16[128,256]{1,0:T(8,128)(2,1)S(1)}, u32[]{:S(2)}, u32[]{:S(2)}) %collective-permute-start.4) | collective-permute-done | bytes 65568 | tf_op jit(solution)/shard_map/cond/branch_1_fun/ppermute | solution.py:207
  28.9 1.9 %collective-permute-done.2 = bf16[128,256]{1,0:T(8,128)(2,1)S(1)} collective-permute-done((bf16[128,256]{1,0:T(8,128)(2,1)S(1)}, bf16[128,256]{1,0:T(8,128)(2,1)S(1)}, u32[]{:S(2)}, u32[]{:S(2)}) %collective-permute-start.2) | collective-permute-done | bytes 65568 | tf_op jit(solution)/shard_map/cond/branch_1_fun/ppermute | solution.py:207
  30.9 0.7 %convert_add_fusion.1 = f32[128,256]{1,0:T(8,128)} fusion(bf16[128,256]{1,0:T(8,128)(2,1)S(1)} %collective-permute-done.10, f32[128,256]{1,0:T(8,128)S(1)} %get-tuple-element.119, bf16[128,256]{1,0:T(8,128)(2,1)S(1)} %collective-permute-done.9), kind=kLoop, calls=%fused_computation.7 | loop fusion | flops 131072 | bytes 393216 | tf_op jit(solution)/shard_map/add | solution.py:358
  (19 shorter events, 0.1 us)
Async XLA Ops:
  0.0 17.3 %collective-permute-start.7 = (bf16[128,1024]{1,0:T(8,128)(2,1)}, bf16[128,1024]{1,0:T(8,128)(2,1)}, u32[]{:S(2)}, u32[]{:S(2)}) collective-permute-start(bf16[128,1024]{1,0:T(8,128)(2,1)} %bitcast.15), channel_id=1, source_target_pairs={{0,4},{4,0},{8,12},{12,8},{1,5},{5,1},{9,13},{13,9},{2,6},{6,2},{1... | collective-permute-start | bytes 786440 | tf_op jit(solution)/shard_map/ppermute | solution.py:207
  3.0 14.7 %collective-permute-start.8 = (bf16[128,1024]{1,0:T(8,128)(2,1)}, bf16[128,1024]{1,0:T(8,128)(2,1)}, u32[]{:S(2)}, u32[]{:S(2)}) collective-permute-start(bf16[128,1024]{1,0:T(8,128)(2,1)} %bitcast.16), channel_id=1, source_target_pairs={{0,8},{1,13},{2,10},{3,15},{4,12},{5,9},{6,14},{7,11},{8,0},{9,5},... | collective-permute-start | bytes 786440 | tf_op jit(solution)/shard_map/ppermute | solution.py:269
  5.6 2.3 %copy-start = (bf16[384,1024]{1,0:T(8,128)(2,1)S(1)}, bf16[384,1024]{1,0:T(8,128)(2,1)}, u32[]{:S(2)}) copy-start(bf16[384,1024]{1,0:T(8,128)(2,1)} %get-tuple-element.48.refs_4_.refs_1_) | copy-start | bytes 2359300 | tf_op jit(solution)/shard_map/cond
  5.6 5.6 %copy-start.1 = (bf16[1,1024,1024]{2,1,0:T(8,128)(2,1)S(1)}, bf16[1,1024,1024]{2,1,0:T(8,128)(2,1)}, u32[]{:S(2)}) copy-start(bf16[1,1024,1024]{2,1,0:T(8,128)(2,1)} %get-tuple-element.104.refs_3_) | copy-start | bytes 6291460 | tf_op jit(solution)/shard_map/cond
  5.6 5.6 %copy-start.2 = (bf16[4,32,1024]{2,1,0:T(8,128)(2,1)S(1)}, bf16[4,32,1024]{2,1,0:T(8,128)(2,1)}, u32[]{:S(2)}) copy-start(bf16[4,32,1024]{2,1,0:T(8,128)(2,1)} %get-tuple-element.59.refs_2_) | copy-start | bytes 786436 | tf_op jit(solution)/shard_map/cond
  7.8 1.8 %collective-permute-start.5 = (bf16[2,384,256]{2,1,0:T(8,128)(2,1)S(1)}, bf16[2,384,256]{2,1,0:T(8,128)(2,1)S(1)}, u32[]{:S(2)}, u32[]{:S(2)}) collective-permute-start(bf16[2,384,256]{2,1,0:T(8,128)(2,1)S(1)} %get-tuple-element.50), channel_id=1, source_target_pairs={{0,1},{1,0},{2,3},{3,2},{4,5},{5,4},{6,7},{7,6},{8,9},{9,8},{10,11... | collective-permute-start | bytes 1179656 | tf_op jit(solution)/shard_map/cond/branch_1_fun/ppermute | solution.py:207
  9.6 5.6 %collective-permute-start.6 = (bf16[256,256]{1,0:T(8,128)(2,1)S(1)}, bf16[256,256]{1,0:T(8,128)(2,1)S(1)}, u32[]{:S(2)}, u32[]{:S(2)}) collective-permute-start(bf16[256,256]{1,0:T(8,128)(2,1)S(1)} %get-tuple-element.56), channel_id=1, source_target_pairs={{0,2},{1,3},{2,0},{3,1},{4,6},{5,7},{6,4},{7,5},{8,10},{9,11},{10,... | collective-permute-start | bytes 393224 | tf_op jit(solution)/shard_map/cond/branch_1_fun/ppermute | solution.py:207
  15.3 15.5 %collective-permute-start.10 = (bf16[128,256]{1,0:T(8,128)(2,1)S(1)}, bf16[128,256]{1,0:T(8,128)(2,1)S(1)}, u32[]{:S(2)}, u32[]{:S(2)}) collective-permute-start(bf16[128,256]{1,0:T(8,128)(2,1)S(1)} %get-tuple-element.94), channel_id=1, source_target_pairs={{0,12},{4,8},{8,4},{12,0},{1,13},{5,9},{9,5},{13,1},{2,14},{6,10},... | collective-permute-start | bytes 196616 | tf_op jit(solution)/shard_map/ppermute | solution.py:207
  15.7 15.1 %collective-permute-start.9 = (bf16[128,256]{1,0:T(8,128)(2,1)S(1)}, bf16[128,256]{1,0:T(8,128)(2,1)S(1)}, u32[]{:S(2)}, u32[]{:S(2)}) collective-permute-start(bf16[128,256]{1,0:T(8,128)(2,1)S(1)} %get-tuple-element.93), channel_id=1, source_target_pairs={{0,8},{4,12},{8,0},{12,4},{1,9},{5,13},{9,1},{13,5},{2,10},{6,14},... | collective-permute-start | bytes 196616 | tf_op jit(solution)/shard_map/ppermute | solution.py:207
  17.8 3.3 %collective-permute-start = (bf16[128,1024]{1,0:T(8,128)(2,1)}, bf16[128,1024]{1,0:T(8,128)(2,1)S(1)}, u32[]{:S(2)}, u32[]{:S(2)}) collective-permute-start(bf16[128,1024]{1,0:T(8,128)(2,1)} %get-tuple-element.67.refs_5_), channel_id=1, source_target_pairs={{0,1},{1,0},{2,3},{3,2},{4,5},{5,4},{6,7},{7,6},{8,9},{9,8},{10,11... | collective-permute-start | bytes 786440 | tf_op jit(solution)/shard_map/cond/branch_1_fun/ppermute | solution.py:207
  17.8 4.9 %collective-permute-start.3 = (bf16[128,256]{1,0:T(8,128)(2,1)S(1)}, bf16[128,256]{1,0:T(8,128)(2,1)S(1)}, u32[]{:S(2)}, u32[]{:S(2)}) collective-permute-start(bf16[128,256]{1,0:T(8,128)(2,1)S(1)} %get-tuple-element.76), channel_id=1, source_target_pairs={{0,2},{1,3},{2,0},{3,1},{4,6},{5,7},{6,4},{7,5},{8,10},{9,11},{10,... | collective-permute-start | bytes 196616 | tf_op jit(solution)/shard_map/cond/branch_1_fun/ppermute | solution.py:207
  22.4 4.1 %collective-permute-start.1 = (bf16[2,128,256]{2,1,0:T(8,128)(2,1)S(1)}, bf16[2,128,256]{2,1,0:T(8,128)(2,1)S(1)}, u32[]{:S(2)}, u32[]{:S(2)}) collective-permute-start(bf16[2,128,256]{2,1,0:T(8,128)(2,1)S(1)} %get-tuple-element.73), channel_id=1, source_target_pairs={{0,1},{1,0},{2,3},{3,2},{4,5},{5,4},{6,7},{7,6},{8,9},{9,8},{10,11... | collective-permute-start | bytes 393224 | tf_op jit(solution)/shard_map/cond/branch_1_fun/ppermute | solution.py:207
  22.7 6.3 %collective-permute-start.4 = (bf16[128,256]{1,0:T(8,128)(2,1)S(1)}, bf16[128,256]{1,0:T(8,128)(2,1)S(1)}, u32[]{:S(2)}, u32[]{:S(2)}) collective-permute-start(bf16[128,256]{1,0:T(8,128)(2,1)S(1)} %add_convert_fusion.1), channel_id=1, source_target_pairs={{0,4},{4,0},{8,12},{12,8},{1,5},{5,1},{9,13},{13,9},{2,6},{6,2},{1... | collective-permute-start | bytes 196616 | tf_op jit(solution)/shard_map/cond/branch_1_fun/ppermute | solution.py:207
  26.5 4.3 %collective-permute-start.2 = (bf16[128,256]{1,0:T(8,128)(2,1)S(1)}, bf16[128,256]{1,0:T(8,128)(2,1)S(1)}, u32[]{:S(2)}, u32[]{:S(2)}) collective-permute-start(bf16[128,256]{1,0:T(8,128)(2,1)S(1)} %fusion.1), channel_id=1, source_target_pairs={{0,2},{1,3},{2,0},{3,1},{4,6},{5,7},{6,4},{7,5},{8,10},{9,11},{10,... | collective-permute-start | bytes 196616 | tf_op jit(solution)/shard_map/cond/branch_1_fun/ppermute | solution.py:207

commit v12 on v11

--- a/solution.py
+++ b/solution.py
@@ -319,7 +319,9 @@
 
     (one, one_leaving), far, near, lanes = stage(local)
     from_rows = [swap(part, "row", row_count, i + 2) for i, part in enumerate(far)]
-    whole, *got, lanes = lax.optimization_barrier((whole, *got, lanes))
+    *got, lanes = lax.optimization_barrier((*got, lanes))
+    one_parts = [swap(part, "col", col_count, 2 * m + 2) for m, part in enumerate(one_leaving)]
+    got, one_parts, whole = lax.optimization_barrier((got, one_parts, whole))
 
     def forward():
         other = [swap(piece, "col", col_count, 1) for piece in got]
@@ -350,7 +352,7 @@
             cost_estimate=pl.CostEstimate(flops=1024, bytes_accessed=1024, transcendentals=0),
             name="forward",
         )(lanes, early, *fetched, *other)
-        joined = col_sum(one, one_leaving).astype(BF16)
+        joined = sum([part.astype(F32) for part in one_parts], one).astype(BF16)
         return col_sum(*chunks(pair_sum(send, keep))) + swap(joined, "row", row_count, 1).astype(F32)
 
     total = stage(forward)

time: 31.7 us -> 31.3 us (0.987)
  starting transfers between devices: 15.9 us -> 13.8 us
  waiting for transfers between devices: 5.83 us -> 7.26 us
  local copies, waits for them, and re-layouts: 0.04 us -> 0.69 us
  Pallas kernels: 8.83 us -> 8.51 us
    ppermute x10, starting transfers between devices: 13.3 us -> 9.8 us  [swap(): return lax.ppermute(value, axis, [(i, i ^ step) for i in range(size)])]
    ppermute x10, waiting for transfers between devices: 5.33 us -> 7.26 us  [swap(): return lax.ppermute(value, axis, [(i, i ^ step) for i in range(size)])]
    ppermute x1, starting transfers between devices: 2.59 us -> 4.04 us  [body(): lax.ppermute(x, ('row', 'col'), rows_perm(d))]
    pallas_call x1, Pallas kernels: 3.18 us -> 2.37 us  [near_of(): pl.pallas_call(lambda *refs: near_kernel(clusters, exc, *refs), in_specs=...]
    slice x1, local copies, waits for them, and re-layouts: 0.01 us -> 0.66 us  [local(): far[i * span:(i + 1) * span]]
    pallas_call x1, Pallas kernels: 0.07 us -> 0.68 us  [local(): pl.pallas_call(lambda *refs: pair_kernel(span, *refs), in_specs=[VMEM] *...]
    ppermute x1, waiting for transfers between devices: 0.49 us -> 0.01 us  [body(): lax.ppermute(x, ('row', 'col'), rows_perm(d))]
  transfers between devices with their start and end apart: 11 -> 11, of which waited for: 5 -> 5; matrix products, arithmetic and copies ran while one was open for 0% -> 2% of each run, Pallas kernels for 28% -> 27%
where the time goes in v12:
time: 31.3 us; the launch traced here: 31.2 us
  starting transfers between devices  13.8 us (44%)
  Pallas kernels  8.51 us (27%)
  waiting for transfers between devices  7.26 us (23%)
  other arithmetic  0.76 us (2%)
  local copies, waits for them, and re-layouts  0.69 us (2%)
    ppermute x10, starting transfers between devices, swap(): return lax.ppermute(value, axis, [(i, i ^ step) for i in range(size)])  9.8 us
    ppermute x10, waiting for transfers between devices, swap(): return lax.ppermute(value, axis, [(i, i ^ step) for i in range(size)])  7.26 us
    ppermute x1, starting transfers between devices, body(): lax.ppermute(x, ('row', 'col'), rows_perm(d))  4.04 us
    pallas_call x1, Pallas kernels, near_of(): pl.pallas_call(lambda *refs: near_kernel(clusters, exc, *refs), in_specs=...  2.37 us
    pallas_call x1, Pallas kernels, local(): pl.pallas_call(lambda *refs: mirror_kernel(clusters, exc, rank, others, *...  2.16 us
    pallas_call x1, Pallas kernels, forward(): pl.pallas_call(lambda *refs: early_kernel(clusters, exc, 1 + len(got), *r...  1.65 us
    pallas_call x1, Pallas kernels, forward(): pl.pallas_call(lambda *refs: forward_kernel(clusters, exc, *refs), in_spe...  1.27 us
    pallas_call x1, Pallas kernels, local(): pl.pallas_call(lambda *refs: pair_kernel(span, *refs), in_specs=[VMEM] *...  0.68 us
  transfers between devices with their start and end apart: 11, of which 5 were waited for; matrix products, arithmetic and copies ran while one was open for 2% of the time, Pallas kernels for 27%

profile of v12, /device:TPU:0, one launch (start us, length us, event | category | flops | bytes accessed | tf_op | source)
XLA Modules:
  0.0 31.2 jit_solution(9563889536156991321)
XLA Ops:
  0.0 4.0 %collective-permute-start.6 = (bf16[128,1024]{1,0:T(8,128)(2,1)}, bf16[128,1024]{1,0:T(8,128)(2,1)S(1)}, u32[]{:S(2)}, u32[]{:S(2)}) collective-permute-start(bf16[128,1024]{1,0:T(8,128)(2,1)} %bitcast.16), channel_id=1, source_target_pairs={{0,8},{1,13},{2,10},{3,15},{4,12},{5,9},{6,14},{7,11},{8,0},{9,5},... | collective-permute-start | bytes 786440 | tf_op jit(solution)/shard_map/ppermute | solution.py:269
  4.0 1.6 %collective-permute-start.8 = (bf16[128,1024]{1,0:T(8,128)(2,1)}, bf16[128,1024]{1,0:T(8,128)(2,1)S(1)}, u32[]{:S(2)}, u32[]{:S(2)}) collective-permute-start(bf16[128,1024]{1,0:T(8,128)(2,1)} %bitcast.17), channel_id=1, source_target_pairs={{0,4},{4,0},{8,12},{12,8},{1,5},{5,1},{9,13},{13,9},{2,6},{6,2},{1... | collective-permute-start | bytes 786440 | tf_op jit(solution)/shard_map/ppermute | solution.py:207
  5.6 10.9 %conditional.2 = (f32[128,256]{1,0:T(8,128)S(1)}, bf16[128,256]{1,0:T(8,128)(2,1)}, bf16[128,256]{1,0:T(8,128)(2,1)}, bf16[128,256]{1,0:T(8,128)(2,1)}, f32[128,1024]{1,0:T(8,128)S(1)}, /*index=5*/s32[8,384]{1,0:T(8,128)S(1)}) conditional(s32[]{:T(128)} %convert_element_type.37, () %tuple.23, (s32[24]{0:T(128)}, s32[24]{0:T(128)}, ...), branch_computations={%region_0.0_spmd, %region_1.0_spmd} | conditional | flops 200704 | bytes 15470804 | solution.py:213
  5.6 2.2 %mirror.1 = (bf16[2,384,256]{2,1,0:T(8,128)(2,1)S(1)}, bf16[384,384]{1,0:T(8,128)(2,1)S(1)}, s32[8,384]{1,0:T(8,128)S(1)}) custom-call(s32[24]{0:T(128)} %get-tuple-element.104.refs_0_, s32[24]{0:T(128)} %get-tuple-element.105.refs_1_, bf16[128,1024]{1,0:T(8,128)(2,1)} %bitcast.19, bf16[384,1024]{1,0:T(8,128)(2,1)} %get-tuple-element.47.refs_3_, ...), custom_call_target="tpu_custom_call" | custom-call | flops 1024 | bytes 1024 | tf_op jit(solution)/shard_map/cond/branch_1_fun/mirror/pallas_call | solution.py:272
  7.9 0.4 %kept.1.refs_0_ = f32[2,384,256]{2,1,0:T(8,128)S(1)} custom-call(bf16[384,384]{1,0:T(8,128)(2,1)S(1)} %get-tuple-element.49.refs_0_, bf16[384,1024]{1,0:T(8,128)(2,1)S(1)} %copy-done), custom_call_target="tpu_custom_call" | custom-call | flops 1024 | bytes 1024 | tf_op jit(solution)/shard_map/cond/branch_1_fun/kept/pallas_call | solution.py:293
  8.3 1.3 %collective-permute-done.4.refs_1_ = bf16[2,384,256]{2,1,0:T(8,128)(2,1)S(1)} collective-permute-done((bf16[2,384,256]{2,1,0:T(8,128)(2,1)S(1)}, bf16[2,384,256]{2,1,0:T(8,128)(2,1)S(1)}, u32[]{:S(2)}, u32[]{:S(2)}) %collective-permute-start.4) | collective-permute-done | bytes 393248 | tf_op jit(solution)/shard_map/cond/branch_1_fun/ppermute | solution.py:207
  9.6 0.7 %pair.1 = (f32[128,256]{1,0:T(8,128)S(1)}, f32[256,256]{1,0:T(8,128)S(1)}, bf16[128,256]{1,0:T(8,128)(2,1)}, bf16[256,256]{1,0:T(8,128)(2,1)S(1)}) custom-call(f32[2,384,256]{2,1,0:T(8,128)S(1)} %kept.1.refs_0_, bf16[2,384,256]{2,1,0:T(8,128)(2,1)S(1)} %collective-permute-done.4.refs_1_), custom_call_target="tpu_custom_call" | custom-call | flops 1024 | bytes 1024 | tf_op jit(solution)/shard_map/cond/branch_1_fun/pair/pallas_call | solution.py:303
  10.3 1.5 %collective-permute-start.5 = (bf16[256,256]{1,0:T(8,128)(2,1)S(1)}, bf16[256,256]{1,0:T(8,128)(2,1)S(1)}, u32[]{:S(2)}, u32[]{:S(2)}) collective-permute-start(bf16[256,256]{1,0:T(8,128)(2,1)S(1)} %get-tuple-element.56), channel_id=1, source_target_pairs={{0,2},{1,3},{2,0},{3,1},{4,6},{5,7},{6,4},{7,5},{8,10},{9,11},{10,... | collective-permute-start | bytes 393224 | tf_op jit(solution)/shard_map/cond/branch_1_fun/ppermute | solution.py:207
  11.8 2.4 %near.1 = f32[4,32,1024]{2,1,0:T(8,128)S(1)} custom-call(s32[1]{0:T(128)} %get-tuple-element.106.refs_0_, s32[1]{0:T(128)} %get-tuple-element.107.refs_1_, bf16[4,32,1024]{2,1,0:T(8,128)(2,1)S(1)} %copy-done.2, bf16[1,1024,1024]{2,1,0:T(8,128)(2,1)S(1)} %copy-done.1), custom_call_target="tpu_custom_call" | custom-call | flops 1024 | bytes 1024 | tf_op jit(solution)/shard_map/cond/branch_1_fun/near/pallas_call | solution.py:251
  14.1 1.7 %collective-permute-done.5 = bf16[256,256]{1,0:T(8,128)(2,1)S(1)} collective-permute-done((bf16[256,256]{1,0:T(8,128)(2,1)S(1)}, bf16[256,256]{1,0:T(8,128)(2,1)S(1)}, u32[]{:S(2)}, u32[]{:S(2)}) %collective-permute-start.5) | collective-permute-done | bytes 131104 | tf_op jit(solution)/shard_map/cond/branch_1_fun/ppermute | solution.py:207
  15.8 0.7 %fusion.2 = (bf16[128,256]{1,0:T(8,128)(2,1)}, bf16[128,256]{1,0:T(8,128)(2,1)}) fusion(bf16[256,256]{1,0:T(8,128)(2,1)S(1)} %add_convert_fusion), kind=kLoop, calls=%fused_computation.8 | loop fusion | bytes 262144 | tf_op jit(solution)/shard_map/cond/branch_1_fun/slice | solution.py:318
  16.5 1.5 %collective-permute-start.7 = (bf16[128,256]{1,0:T(8,128)(2,1)}, bf16[128,256]{1,0:T(8,128)(2,1)S(1)}, u32[]{:S(2)}, u32[]{:S(2)}) collective-permute-start(bf16[128,256]{1,0:T(8,128)(2,1)} %get-tuple-element.92), channel_id=1, source_target_pairs={{0,2},{1,3},{2,0},{3,1},{4,6},{5,7},{6,4},{7,5},{8,10},{9,11},{10,... | collective-permute-start | bytes 196616 | tf_op jit(solution)/shard_map/ppermute | solution.py:207
  18.0 0.2 collective-permute-start.10
  18.2 1.8 %collective-permute-start.9 = (bf16[128,256]{1,0:T(8,128)(2,1)}, bf16[128,256]{1,0:T(8,128)(2,1)S(1)}, u32[]{:S(2)}, u32[]{:S(2)}) collective-permute-start(bf16[128,256]{1,0:T(8,128)(2,1)} %get-tuple-element.97), channel_id=1, source_target_pairs={{0,8},{4,12},{8,0},{12,4},{1,9},{5,13},{9,1},{13,5},{2,10},{6,14},... | collective-permute-start | bytes 196616 | tf_op jit(solution)/shard_map/ppermute | solution.py:207
  20.0 0.9 %collective-permute-done.7 = bf16[128,256]{1,0:T(8,128)(2,1)S(1)} collective-permute-done((bf16[128,256]{1,0:T(8,128)(2,1)}, bf16[128,256]{1,0:T(8,128)(2,1)S(1)}, u32[]{:S(2)}, u32[]{:S(2)}) %collective-permute-start.7) | collective-permute-done | bytes 65568 | tf_op jit(solution)/shard_map/ppermute | solution.py:207
  21.0 9.5 %conditional.3 = (f32[128,256]{1,0:T(8,128)S(1)}) conditional(s32[]{:T(128)} %convert_element_type.37, () %tuple.22, (s32[8,384]{1,0:T(8,128)S(1)}, bf16[384,1024]{1,0:T(8,128)(2,1)}, bf16[384,1024]{1,0:T(8,128)(2,1)}, f32[128,1024]{1,0:T(8,128)S(1)}, bf16[128,1024]{1,0:T(8,128)(2,1)S(1)}, /*index=5*/bf16[128,1024]{1,0:T(8,128)(2,1)S(1)}, s32[]{:T(128)}, ...), branch_computations={%region_2.0_spmd, %region_3.4_spmd} | conditional | flops 362518 | bytes 3541398 | solution.py:213
  21.0 1.6 %early.1 = (f32[32,384]{1,0:T(8,128)S(1)}, bf16[384,1024]{1,0:T(8,128)(2,1)S(1)}, bf16[384,1024]{1,0:T(8,128)(2,1)S(1)}, f32[128,1024]{1,0:T(8,128)S(1)}) custom-call(s32[8,384]{1,0:T(8,128)S(1)} %get-tuple-element.62.refs_0_, bf16[384,1024]{1,0:T(8,128)(2,1)} %get-tuple-element.63.refs_1_, bf16[384,1024]{1,0:T(8,128)(2,1)} %get-tuple-element.64.refs_2_, ...), custom_call_target="tpu_custom_call" | custom-call | flops 1024 | bytes 1024 | tf_op jit(solution)/shard_map/cond/branch_1_fun/early/pallas_call | solution.py:328
  22.6 1.3 %forward.1 = (bf16[2,128,256]{2,1,0:T(8,128)(2,1)S(1)}, f32[2,128,256]{2,1,0:T(8,128)S(1)}) custom-call(s32[8,384]{1,0:T(8,128)S(1)} %get-tuple-element.62.refs_0_, f32[32,384]{1,0:T(8,128)S(1)} %get-tuple-element.68.refs_1_, bf16[384,1024]{1,0:T(8,128)(2,1)S(1)} %get-tuple-element.69.refs_2_, bf16[384,1024]{1,0:T(8,128)(2,1)S(1)} %get-tuple-element.70.refs_3_, ...), custom_call_target="tpu_custom_call" | custom-call | flops 1024 | bytes 1024 | tf_op jit(solution)/shard_map/cond/branch_1_fun/forward/pallas_call | solution.py:346
  23.9 0.6 %collective-permute-start.1 = (bf16[2,128,256]{2,1,0:T(8,128)(2,1)S(1)}, bf16[2,128,256]{2,1,0:T(8,128)(2,1)S(1)}, u32[]{:S(2)}, u32[]{:S(2)}) collective-permute-start(bf16[2,128,256]{2,1,0:T(8,128)(2,1)S(1)} %get-tuple-element.73), channel_id=1, source_target_pairs={{0,1},{1,0},{2,3},{3,2},{4,5},{5,4},{6,7},{7,6},{8,9},{9,8},{10,11... | collective-permute-start | bytes 393224 | tf_op jit(solution)/shard_map/cond/branch_1_fun/ppermute | solution.py:207
  24.5 1.6 %collective-permute-start.3 = (bf16[128,256]{1,0:T(8,128)(2,1)S(1)}, bf16[128,256]{1,0:T(8,128)(2,1)S(1)}, u32[]{:S(2)}, u32[]{:S(2)}) collective-permute-start(bf16[128,256]{1,0:T(8,128)(2,1)S(1)} %add_convert_fusion.1), channel_id=1, source_target_pairs={{0,4},{4,0},{8,12},{12,8},{1,5},{5,1},{9,13},{13,9},{2,6},{6,2},{1... | collective-permute-start | bytes 196616 | tf_op jit(solution)/shard_map/cond/branch_1_fun/ppermute | solution.py:207
  26.1 1.0 %collective-permute-start.2 = (bf16[128,256]{1,0:T(8,128)(2,1)S(1)}, bf16[128,256]{1,0:T(8,128)(2,1)S(1)}, u32[]{:S(2)}, u32[]{:S(2)}) collective-permute-start(bf16[128,256]{1,0:T(8,128)(2,1)S(1)} %fusion.1), channel_id=1, source_target_pairs={{0,2},{1,3},{2,0},{3,1},{4,6},{5,7},{6,4},{7,5},{8,10},{9,11},{10,... | collective-permute-start | bytes 196616 | tf_op jit(solution)/shard_map/cond/branch_1_fun/ppermute | solution.py:207
  27.1 1.7 %collective-permute-done.3 = bf16[128,256]{1,0:T(8,128)(2,1)S(1)} collective-permute-done((bf16[128,256]{1,0:T(8,128)(2,1)S(1)}, bf16[128,256]{1,0:T(8,128)(2,1)S(1)}, u32[]{:S(2)}, u32[]{:S(2)}) %collective-permute-start.3) | collective-permute-done | bytes 65568 | tf_op jit(solution)/shard_map/cond/branch_1_fun/ppermute | solution.py:207
  28.8 1.6 %collective-permute-done.2 = bf16[128,256]{1,0:T(8,128)(2,1)S(1)} collective-permute-done((bf16[128,256]{1,0:T(8,128)(2,1)S(1)}, bf16[128,256]{1,0:T(8,128)(2,1)S(1)}, u32[]{:S(2)}, u32[]{:S(2)}) %collective-permute-start.2) | collective-permute-done | bytes 65568 | tf_op jit(solution)/shard_map/cond/branch_1_fun/ppermute | solution.py:207
  30.5 0.7 %convert_add_fusion.1 = f32[128,256]{1,0:T(8,128)} fusion(bf16[128,256]{1,0:T(8,128)(2,1)S(1)} %collective-permute-done.10, f32[128,256]{1,0:T(8,128)S(1)} %get-tuple-element.123, bf16[128,256]{1,0:T(8,128)(2,1)S(1)} %collective-permute-done.9), kind=kLoop, calls=%fused_computation.7 | loop fusion | flops 131072 | bytes 393216 | tf_op jit(solution)/shard_map/add | solution.py:360
  (19 shorter events, 0.2 us)
Async XLA Ops:
  0.0 20.0 %collective-permute-start.6 = (bf16[128,1024]{1,0:T(8,128)(2,1)}, bf16[128,1024]{1,0:T(8,128)(2,1)S(1)}, u32[]{:S(2)}, u32[]{:S(2)}) collective-permute-start(bf16[128,1024]{1,0:T(8,128)(2,1)} %bitcast.16), channel_id=1, source_target_pairs={{0,8},{1,13},{2,10},{3,15},{4,12},{5,9},{6,14},{7,11},{8,0},{9,5},... | collective-permute-start | bytes 786440 | tf_op jit(solution)/shard_map/ppermute | solution.py:269
  4.0 16.9 %collective-permute-start.8 = (bf16[128,1024]{1,0:T(8,128)(2,1)}, bf16[128,1024]{1,0:T(8,128)(2,1)S(1)}, u32[]{:S(2)}, u32[]{:S(2)}) collective-permute-start(bf16[128,1024]{1,0:T(8,128)(2,1)} %bitcast.17), channel_id=1, source_target_pairs={{0,4},{4,0},{8,12},{12,8},{1,5},{5,1},{9,13},{13,9},{2,6},{6,2},{1... | collective-permute-start | bytes 786440 | tf_op jit(solution)/shard_map/ppermute | solution.py:207
  5.6 2.3 %copy-start = (bf16[384,1024]{1,0:T(8,128)(2,1)S(1)}, bf16[384,1024]{1,0:T(8,128)(2,1)}, u32[]{:S(2)}) copy-start(bf16[384,1024]{1,0:T(8,128)(2,1)} %get-tuple-element.48.refs_4_.refs_1_) | copy-start | bytes 2359300 | tf_op jit(solution)/shard_map/cond
  5.6 6.1 %copy-start.1 = (bf16[1,1024,1024]{2,1,0:T(8,128)(2,1)S(1)}, bf16[1,1024,1024]{2,1,0:T(8,128)(2,1)}, u32[]{:S(2)}) copy-start(bf16[1,1024,1024]{2,1,0:T(8,128)(2,1)} %get-tuple-element.108.refs_3_) | copy-start | bytes 6291460 | tf_op jit(solution)/shard_map/cond
  5.6 6.1 %copy-start.2 = (bf16[4,32,1024]{2,1,0:T(8,128)(2,1)S(1)}, bf16[4,32,1024]{2,1,0:T(8,128)(2,1)}, u32[]{:S(2)}) copy-start(bf16[4,32,1024]{2,1,0:T(8,128)(2,1)} %get-tuple-element.59.refs_2_) | copy-start | bytes 786436 | tf_op jit(solution)/shard_map/cond
  7.8 1.8 %collective-permute-start.4 = (bf16[2,384,256]{2,1,0:T(8,128)(2,1)S(1)}, bf16[2,384,256]{2,1,0:T(8,128)(2,1)S(1)}, u32[]{:S(2)}, u32[]{:S(2)}) collective-permute-start(bf16[2,384,256]{2,1,0:T(8,128)(2,1)S(1)} %get-tuple-element.50), channel_id=1, source_target_pairs={{0,1},{1,0},{2,3},{3,2},{4,5},{5,4},{6,7},{7,6},{8,9},{9,8},{10,11... | collective-permute-start | bytes 1179656 | tf_op jit(solution)/shard_map/cond/branch_1_fun/ppermute | solution.py:207
  10.3 5.5 %collective-permute-start.5 = (bf16[256,256]{1,0:T(8,128)(2,1)S(1)}, bf16[256,256]{1,0:T(8,128)(2,1)S(1)}, u32[]{:S(2)}, u32[]{:S(2)}) collective-permute-start(bf16[256,256]{1,0:T(8,128)(2,1)S(1)} %get-tuple-element.56), channel_id=1, source_target_pairs={{0,2},{1,3},{2,0},{3,1},{4,6},{5,7},{6,4},{7,5},{8,10},{9,11},{10,... | collective-permute-start | bytes 393224 | tf_op jit(solution)/shard_map/cond/branch_1_fun/ppermute | solution.py:207
  16.5 4.5 %collective-permute-start.7 = (bf16[128,256]{1,0:T(8,128)(2,1)}, bf16[128,256]{1,0:T(8,128)(2,1)S(1)}, u32[]{:S(2)}, u32[]{:S(2)}) collective-permute-start(bf16[128,256]{1,0:T(8,128)(2,1)} %get-tuple-element.92), channel_id=1, source_target_pairs={{0,2},{1,3},{2,0},{3,1},{4,6},{5,7},{6,4},{7,5},{8,10},{9,11},{10,... | collective-permute-start | bytes 196616 | tf_op jit(solution)/shard_map/ppermute | solution.py:207
  18.0 12.5 %collective-permute-start.10 = (bf16[128,256]{1,0:T(8,128)(2,1)}, bf16[128,256]{1,0:T(8,128)(2,1)S(1)}, u32[]{:S(2)}, u32[]{:S(2)}) collective-permute-start(bf16[128,256]{1,0:T(8,128)(2,1)} %get-tuple-element.98), channel_id=1, source_target_pairs={{0,12},{4,8},{8,4},{12,0},{1,13},{5,9},{9,5},{13,1},{2,14},{6,10},... | collective-permute-start | bytes 196616 | tf_op jit(solution)/shard_map/ppermute | solution.py:207
  18.2 12.3 %collective-permute-start.9 = (bf16[128,256]{1,0:T(8,128)(2,1)}, bf16[128,256]{1,0:T(8,128)(2,1)S(1)}, u32[]{:S(2)}, u32[]{:S(2)}) collective-permute-start(bf16[128,256]{1,0:T(8,128)(2,1)} %get-tuple-element.97), channel_id=1, source_target_pairs={{0,8},{4,12},{8,0},{12,4},{1,9},{5,13},{9,1},{13,5},{2,10},{6,14},... | collective-permute-start | bytes 196616 | tf_op jit(solution)/shard_map/ppermute | solution.py:207
  21.0 1.7 %collective-permute-start = (bf16[128,1024]{1,0:T(8,128)(2,1)S(1)}, bf16[128,1024]{1,0:T(8,128)(2,1)S(1)}, u32[]{:S(2)}, u32[]{:S(2)}) collective-permute-start(bf16[128,1024]{1,0:T(8,128)(2,1)S(1)} %get-tuple-element.67.refs_5_), channel_id=1, source_target_pairs={{0,1},{1,0},{2,3},{3,2},{4,5},{5,4},{6,7},{7,6},{8,9},{9,8},{10,11... | collective-permute-start | bytes 786440 | tf_op jit(solution)/shard_map/cond/branch_1_fun/ppermute | solution.py:207
  23.9 2.1 %collective-permute-start.1 = (bf16[2,128,256]{2,1,0:T(8,128)(2,1)S(1)}, bf16[2,128,256]{2,1,0:T(8,128)(2,1)S(1)}, u32[]{:S(2)}, u32[]{:S(2)}) collective-permute-start(bf16[2,128,256]{2,1,0:T(8,128)(2,1)S(1)} %get-tuple-element.73), channel_id=1, source_target_pairs={{0,1},{1,0},{2,3},{3,2},{4,5},{5,4},{6,7},{7,6},{8,9},{9,8},{10,11... | collective-permute-start | bytes 393224 | tf_op jit(solution)/shard_map/cond/branch_1_fun/ppermute | solution.py:207
  24.5 4.3 %collective-permute-start.3 = (bf16[128,256]{1,0:T(8,128)(2,1)S(1)}, bf16[128,256]{1,0:T(8,128)(2,1)S(1)}, u32[]{:S(2)}, u32[]{:S(2)}) collective-permute-start(bf16[128,256]{1,0:T(8,128)(2,1)S(1)} %add_convert_fusion.1), channel_id=1, source_target_pairs={{0,4},{4,0},{8,12},{12,8},{1,5},{5,1},{9,13},{13,9},{2,6},{6,2},{1... | collective-permute-start | bytes 196616 | tf_op jit(solution)/shard_map/cond/branch_1_fun/ppermute | solution.py:207
  26.1 4.3 %collective-permute-start.2 = (bf16[128,256]{1,0:T(8,128)(2,1)S(1)}, bf16[128,256]{1,0:T(8,128)(2,1)S(1)}, u32[]{:S(2)}, u32[]{:S(2)}) collective-permute-start(bf16[128,256]{1,0:T(8,128)(2,1)S(1)} %fusion.1), channel_id=1, source_target_pairs={{0,2},{1,3},{2,0},{3,1},{4,6},{5,7},{6,4},{7,5},{8,10},{9,11},{10,... | collective-permute-start | bytes 196616 | tf_op jit(solution)/shard_map/cond/branch_1_fun/ppermute | solution.py:207

commit v13 on v11

--- a/solution.py
+++ b/solution.py
@@ -319,7 +319,8 @@
 
     (one, one_leaving), far, near, lanes = stage(local)
     from_rows = [swap(part, "row", row_count, i + 2) for i, part in enumerate(far)]
-    whole, *got, lanes = lax.optimization_barrier((whole, *got, lanes))
+    *got, lanes = lax.optimization_barrier((*got, lanes))
+    whole, *got = lax.optimization_barrier((whole, *got))
 
     def forward():
         other = [swap(piece, "col", col_count, 1) for piece in got]

time: 31.7 us -> 30 us (0.946)
  starting transfers between devices: 15.9 us -> 14.7 us
  waiting for transfers between devices: 5.83 us -> 5.33 us
    ppermute x10, starting transfers between devices: 13.3 us -> 10.7 us  [swap(): return lax.ppermute(value, axis, [(i, i ^ step) for i in range(size)])]
    ppermute x1, starting transfers between devices: 2.59 us -> 4.04 us  [body(): lax.ppermute(x, ('row', 'col'), rows_perm(d))]
    ppermute x1, waiting for transfers between devices: 0.49 us -> 0.01 us  [body(): lax.ppermute(x, ('row', 'col'), rows_perm(d))]
  transfers between devices with their start and end apart: 11 -> 11, of which waited for: 5 -> 4; matrix products, arithmetic and copies ran while one was open for 0% -> 0% of each run, Pallas kernels for 28% -> 30%
where the time goes in v13:
time: 30 us; the launch traced here: 29.8 us
  starting transfers between devices  14.7 us (49%)
  Pallas kernels  8.83 us (29%)
  waiting for transfers between devices  5.33 us (18%)
  other arithmetic  0.77 us (3%)
    ppermute x10, starting transfers between devices, swap(): return lax.ppermute(value, axis, [(i, i ^ step) for i in range(size)])  10.7 us
    ppermute x10, waiting for transfers between devices, swap(): return lax.ppermute(value, axis, [(i, i ^ step) for i in range(size)])  5.33 us
    ppermute x1, starting transfers between devices, body(): lax.ppermute(x, ('row', 'col'), rows_perm(d))  4.04 us
    pallas_call x1, Pallas kernels, near_of(): pl.pallas_call(lambda *refs: near_kernel(clusters, exc, *refs), in_specs=...  3.18 us
    pallas_call x1, Pallas kernels, local(): pl.pallas_call(lambda *refs: mirror_kernel(clusters, exc, rank, others, *...  2.16 us
    pallas_call x1, Pallas kernels, forward(): pl.pallas_call(lambda *refs: early_kernel(clusters, exc, 1 + len(got), *r...  1.77 us
    pallas_call x1, Pallas kernels, forward(): pl.pallas_call(lambda *refs: forward_kernel(clusters, exc, *refs), in_spe...  1.27 us
    add x1, other arithmetic, body(): total = total + term.astype(F32)  0.68 us
  transfers between devices with their start and end apart: 11, of which 4 were waited for; matrix products, arithmetic and copies ran while one was open for 0% of the time, Pallas kernels for 30%

profile of v13, /device:TPU:0, one launch (start us, length us, event | category | flops | bytes accessed | tf_op | source)
XLA Modules:
  0.0 29.8 jit_solution(8926229077145411217)
XLA Ops:
  0.0 4.0 %collective-permute-start.7 = (bf16[128,1024]{1,0:T(8,128)(2,1)}, bf16[128,1024]{1,0:T(8,128)(2,1)}, u32[]{:S(2)}, u32[]{:S(2)}) collective-permute-start(bf16[128,1024]{1,0:T(8,128)(2,1)} %bitcast.15), channel_id=1, source_target_pairs={{0,8},{1,13},{2,10},{3,15},{4,12},{5,9},{6,14},{7,11},{8,0},{9,5},... | collective-permute-start | bytes 786440 | tf_op jit(solution)/shard_map/ppermute | solution.py:269
  4.0 1.6 %collective-permute-start.8 = (bf16[128,1024]{1,0:T(8,128)(2,1)}, bf16[128,1024]{1,0:T(8,128)(2,1)}, u32[]{:S(2)}, u32[]{:S(2)}) collective-permute-start(bf16[128,1024]{1,0:T(8,128)(2,1)} %bitcast.16), channel_id=1, source_target_pairs={{0,4},{4,0},{8,12},{12,8},{1,5},{5,1},{9,13},{13,9},{2,6},{6,2},{1... | collective-permute-start | bytes 786440 | tf_op jit(solution)/shard_map/ppermute | solution.py:207
  5.6 9.7 %conditional.2 = (f32[128,256]{1,0:T(8,128)S(1)}, bf16[128,256]{1,0:T(8,128)(2,1)S(1)}, bf16[128,256]{1,0:T(8,128)(2,1)S(1)}, bf16[128,256]{1,0:T(8,128)(2,1)S(1...) conditional(s32[]{:T(128)} %convert_element_type.37, () %tuple.23, (s32[24]{0:T(128)}, s32[24]{0:T(128)}, ...), branch_computations={%region_0.0_spmd, %region_1.0_spmd} | conditional | flops 200704 | bytes 15470804 | solution.py:213
  5.6 2.2 %mirror.1 = (bf16[2,384,256]{2,1,0:T(8,128)(2,1)S(1)}, bf16[384,384]{1,0:T(8,128)(2,1)S(1)}, s32[8,384]{1,0:T(8,128)S(1)}) custom-call(s32[24]{0:T(128)} %get-tuple-element.102.refs_0_, s32[24]{0:T(128)} %get-tuple-element.103.refs_1_, bf16[128,1024]{1,0:T(8,128)(2,1)} %bitcast.18, bf16[384,1024]{1,0:T(8,128)(2,1)} %get-tuple-element.47.refs_3_, ...), custom_call_target="tpu_custom_call" | custom-call | flops 1024 | bytes 1024 | tf_op jit(solution)/shard_map/cond/branch_1_fun/mirror/pallas_call | solution.py:272
  7.8 0.1 collective-permute-start.5
  7.9 0.4 %kept.1.refs_0_ = f32[2,384,256]{2,1,0:T(8,128)S(1)} custom-call(bf16[384,384]{1,0:T(8,128)(2,1)S(1)} %get-tuple-element.49.refs_0_, bf16[384,1024]{1,0:T(8,128)(2,1)S(1)} %copy-done), custom_call_target="tpu_custom_call" | custom-call | flops 1024 | bytes 1024 | tf_op jit(solution)/shard_map/cond/branch_1_fun/kept/pallas_call | solution.py:293
  8.3 1.3 %collective-permute-done.5.refs_1_ = bf16[2,384,256]{2,1,0:T(8,128)(2,1)S(1)} collective-permute-done((bf16[2,384,256]{2,1,0:T(8,128)(2,1)S(1)}, bf16[2,384,256]{2,1,0:T(8,128)(2,1)S(1)}, u32[]{:S(2)}, u32[]{:S(2)}) %collective-permute-start.5) | collective-permute-done | bytes 393248 | tf_op jit(solution)/shard_map/cond/branch_1_fun/ppermute | solution.py:207
  9.6 0.1 pair.1
  9.6 1.6 %collective-permute-start.6 = (bf16[256,256]{1,0:T(8,128)(2,1)S(1)}, bf16[256,256]{1,0:T(8,128)(2,1)S(1)}, u32[]{:S(2)}, u32[]{:S(2)}) collective-permute-start(bf16[256,256]{1,0:T(8,128)(2,1)S(1)} %get-tuple-element.56), channel_id=1, source_target_pairs={{0,2},{1,3},{2,0},{3,1},{4,6},{5,7},{6,4},{7,5},{8,10},{9,11},{10,... | collective-permute-start | bytes 393224 | tf_op jit(solution)/shard_map/cond/branch_1_fun/ppermute | solution.py:207
  11.2 3.2 %near.1 = f32[4,32,1024]{2,1,0:T(8,128)} custom-call(s32[1]{0:T(128)} %get-tuple-element.104.refs_0_, s32[1]{0:T(128)} %get-tuple-element.105.refs_1_, bf16[4,32,1024]{2,1,0:T(8,128)(2,1)S(1)} %copy-done.2, bf16[1,1024,1024]{2,1,0:T(8,128)(2,1)S(1)} %copy-done.1), custom_call_target="tpu_custom_call" | custom-call | flops 1024 | bytes 1024 | tf_op jit(solution)/shard_map/cond/branch_1_fun/near/pallas_call | solution.py:251
  14.4 0.9 %collective-permute-done.6 = bf16[256,256]{1,0:T(8,128)(2,1)S(1)} collective-permute-done((bf16[256,256]{1,0:T(8,128)(2,1)S(1)}, bf16[256,256]{1,0:T(8,128)(2,1)S(1)}, u32[]{:S(2)}, u32[]{:S(2)}) %collective-permute-start.6) | collective-permute-done | bytes 131104 | tf_op jit(solution)/shard_map/cond/branch_1_fun/ppermute | solution.py:207
  15.3 0.1 collective-permute-start.10
  15.4 2.1 %collective-permute-start.9 = (bf16[128,256]{1,0:T(8,128)(2,1)S(1)}, bf16[128,256]{1,0:T(8,128)(2,1)S(1)}, u32[]{:S(2)}, u32[]{:S(2)}) collective-permute-start(bf16[128,256]{1,0:T(8,128)(2,1)S(1)} %get-tuple-element.95), channel_id=1, source_target_pairs={{0,8},{4,12},{8,0},{12,4},{1,9},{5,13},{9,1},{13,5},{2,10},{6,14},... | collective-permute-start | bytes 196616 | tf_op jit(solution)/shard_map/ppermute | solution.py:207
  17.4 0.0 collective-permute-done.7
  17.4 11.7 %conditional.3 = (f32[128,256]{1,0:T(8,128)S(1)}) conditional(s32[]{:T(128)} %convert_element_type.37, () %tuple.22, (s32[8,384]{1,0:T(8,128)S(1)}, bf16[384,1024]{1,0:T(8,128)(2,1)}, bf16[384,1024]{1,0:T(8,128)(2,1)}, f32[128,1024]{1,0:T(8,128)}, bf16[128,1024]{1,0:T(8,128)(2,1)}, /*index=5*/bf16[128,1024]{1,0:T(8,128)(2,1)}, s32[]{:T(128)}, ...), branch_computations={%region_2.0_spmd, %region_3.4_spmd} | conditional | flops 362518 | bytes 3803582 | solution.py:213
  17.4 1.6 %collective-permute-start.3 = (bf16[128,256]{1,0:T(8,128)(2,1)S(1)}, bf16[128,256]{1,0:T(8,128)(2,1)S(1)}, u32[]{:S(2)}, u32[]{:S(2)}) collective-permute-start(bf16[128,256]{1,0:T(8,128)(2,1)S(1)} %get-tuple-element.76), channel_id=1, source_target_pairs={{0,2},{1,3},{2,0},{3,1},{4,6},{5,7},{6,4},{7,5},{8,10},{9,11},{10,... | collective-permute-start | bytes 196616 | tf_op jit(solution)/shard_map/cond/branch_1_fun/ppermute | solution.py:207
  19.0 1.8 %early.1 = (f32[32,384]{1,0:T(8,128)S(1)}, bf16[384,1024]{1,0:T(8,128)(2,1)S(1)}, bf16[384,1024]{1,0:T(8,128)(2,1)S(1)}, f32[128,1024]{1,0:T(8,128)S(1)}) custom-call(s32[8,384]{1,0:T(8,128)S(1)} %get-tuple-element.62.refs_0_, bf16[384,1024]{1,0:T(8,128)(2,1)} %get-tuple-element.63.refs_1_, bf16[384,1024]{1,0:T(8,128)(2,1)} %get-tuple-element.64.refs_2_, ...), custom_call_target="tpu_custom_call" | custom-call | flops 1024 | bytes 1024 | tf_op jit(solution)/shard_map/cond/branch_1_fun/early/pallas_call | solution.py:327
  20.8 1.3 %forward.1 = (bf16[2,128,256]{2,1,0:T(8,128)(2,1)S(1)}, f32[2,128,256]{2,1,0:T(8,128)S(1)}) custom-call(s32[8,384]{1,0:T(8,128)S(1)} %get-tuple-element.62.refs_0_, f32[32,384]{1,0:T(8,128)S(1)} %get-tuple-element.68.refs_1_, bf16[384,1024]{1,0:T(8,128)(2,1)S(1)} %get-tuple-element.69.refs_2_, bf16[384,1024]{1,0:T(8,128)(2,1)S(1)} %get-tuple-element.70.refs_3_, ...), custom_call_target="tpu_custom_call" | custom-call | flops 1024 | bytes 1024 | tf_op jit(solution)/shard_map/cond/branch_1_fun/forward/pallas_call | solution.py:345
  22.1 0.3 collective-permute-start.1
  22.4 2.3 %collective-permute-start.4 = (bf16[128,256]{1,0:T(8,128)(2,1)S(1)}, bf16[128,256]{1,0:T(8,128)(2,1)S(1)}, u32[]{:S(2)}, u32[]{:S(2)}) collective-permute-start(bf16[128,256]{1,0:T(8,128)(2,1)S(1)} %add_convert_fusion.1), channel_id=1, source_target_pairs={{0,4},{4,0},{8,12},{12,8},{1,5},{5,1},{9,13},{13,9},{2,6},{6,2},{1... | collective-permute-start | bytes 196616 | tf_op jit(solution)/shard_map/cond/branch_1_fun/ppermute | solution.py:207
  24.8 1.2 %collective-permute-start.2 = (bf16[128,256]{1,0:T(8,128)(2,1)S(1)}, bf16[128,256]{1,0:T(8,128)(2,1)S(1)}, u32[]{:S(2)}, u32[]{:S(2)}) collective-permute-start(bf16[128,256]{1,0:T(8,128)(2,1)S(1)} %fusion.1), channel_id=1, source_target_pairs={{0,2},{1,3},{2,0},{3,1},{4,6},{5,7},{6,4},{7,5},{8,10},{9,11},{10,... | collective-permute-start | bytes 196616 | tf_op jit(solution)/shard_map/cond/branch_1_fun/ppermute | solution.py:207
  26.0 1.4 %collective-permute-done.4 = bf16[128,256]{1,0:T(8,128)(2,1)S(1)} collective-permute-done((bf16[128,256]{1,0:T(8,128)(2,1)S(1)}, bf16[128,256]{1,0:T(8,128)(2,1)S(1)}, u32[]{:S(2)}, u32[]{:S(2)}) %collective-permute-start.4) | collective-permute-done | bytes 65568 | tf_op jit(solution)/shard_map/cond/branch_1_fun/ppermute | solution.py:207
  27.3 1.8 %collective-permute-done.2 = bf16[128,256]{1,0:T(8,128)(2,1)S(1)} collective-permute-done((bf16[128,256]{1,0:T(8,128)(2,1)S(1)}, bf16[128,256]{1,0:T(8,128)(2,1)S(1)}, u32[]{:S(2)}, u32[]{:S(2)}) %collective-permute-start.2) | collective-permute-done | bytes 65568 | tf_op jit(solution)/shard_map/cond/branch_1_fun/ppermute | solution.py:207
  29.2 0.7 %convert_add_fusion.1 = f32[128,256]{1,0:T(8,128)} fusion(bf16[128,256]{1,0:T(8,128)(2,1)S(1)} %collective-permute-done.10, f32[128,256]{1,0:T(8,128)S(1)} %get-tuple-element.121, bf16[128,256]{1,0:T(8,128)(2,1)S(1)} %collective-permute-done.9), kind=kLoop, calls=%fused_computation.7 | loop fusion | flops 131072 | bytes 393216 | tf_op jit(solution)/shard_map/add | solution.py:359
  (19 shorter events, 0.1 us)
Async XLA Ops:
  0.0 17.4 %collective-permute-start.7 = (bf16[128,1024]{1,0:T(8,128)(2,1)}, bf16[128,1024]{1,0:T(8,128)(2,1)}, u32[]{:S(2)}, u32[]{:S(2)}) collective-permute-start(bf16[128,1024]{1,0:T(8,128)(2,1)} %bitcast.15), channel_id=1, source_target_pairs={{0,8},{1,13},{2,10},{3,15},{4,12},{5,9},{6,14},{7,11},{8,0},{9,5},... | collective-permute-start | bytes 786440 | tf_op jit(solution)/shard_map/ppermute | solution.py:269
  4.0 13.4 %collective-permute-start.8 = (bf16[128,1024]{1,0:T(8,128)(2,1)}, bf16[128,1024]{1,0:T(8,128)(2,1)}, u32[]{:S(2)}, u32[]{:S(2)}) collective-permute-start(bf16[128,1024]{1,0:T(8,128)(2,1)} %bitcast.16), channel_id=1, source_target_pairs={{0,4},{4,0},{8,12},{12,8},{1,5},{5,1},{9,13},{13,9},{2,6},{6,2},{1... | collective-permute-start | bytes 786440 | tf_op jit(solution)/shard_map/ppermute | solution.py:207
  5.6 2.3 %copy-start = (bf16[384,1024]{1,0:T(8,128)(2,1)S(1)}, bf16[384,1024]{1,0:T(8,128)(2,1)}, u32[]{:S(2)}) copy-start(bf16[384,1024]{1,0:T(8,128)(2,1)} %get-tuple-element.48.refs_4_.refs_1_) | copy-start | bytes 2359300 | tf_op jit(solution)/shard_map/cond
  5.6 5.6 %copy-start.1 = (bf16[1,1024,1024]{2,1,0:T(8,128)(2,1)S(1)}, bf16[1,1024,1024]{2,1,0:T(8,128)(2,1)}, u32[]{:S(2)}) copy-start(bf16[1,1024,1024]{2,1,0:T(8,128)(2,1)} %get-tuple-element.106.refs_3_) | copy-start | bytes 6291460 | tf_op jit(solution)/shard_map/cond
  5.6 5.6 %copy-start.2 = (bf16[4,32,1024]{2,1,0:T(8,128)(2,1)S(1)}, bf16[4,32,1024]{2,1,0:T(8,128)(2,1)}, u32[]{:S(2)}) copy-start(bf16[4,32,1024]{2,1,0:T(8,128)(2,1)} %get-tuple-element.59.refs_2_) | copy-start | bytes 786436 | tf_op jit(solution)/shard_map/cond
  7.8 1.8 %collective-permute-start.5 = (bf16[2,384,256]{2,1,0:T(8,128)(2,1)S(1)}, bf16[2,384,256]{2,1,0:T(8,128)(2,1)S(1)}, u32[]{:S(2)}, u32[]{:S(2)}) collective-permute-start(bf16[2,384,256]{2,1,0:T(8,128)(2,1)S(1)} %get-tuple-element.50), channel_id=1, source_target_pairs={{0,1},{1,0},{2,3},{3,2},{4,5},{5,4},{6,7},{7,6},{8,9},{9,8},{10,11... | collective-permute-start | bytes 1179656 | tf_op jit(solution)/shard_map/cond/branch_1_fun/ppermute | solution.py:207
  9.6 5.6 %collective-permute-start.6 = (bf16[256,256]{1,0:T(8,128)(2,1)S(1)}, bf16[256,256]{1,0:T(8,128)(2,1)S(1)}, u32[]{:S(2)}, u32[]{:S(2)}) collective-permute-start(bf16[256,256]{1,0:T(8,128)(2,1)S(1)} %get-tuple-element.56), channel_id=1, source_target_pairs={{0,2},{1,3},{2,0},{3,1},{4,6},{5,7},{6,4},{7,5},{8,10},{9,11},{10,... | collective-permute-start | bytes 393224 | tf_op jit(solution)/shard_map/cond/branch_1_fun/ppermute | solution.py:207
  15.3 13.8 %collective-permute-start.10 = (bf16[128,256]{1,0:T(8,128)(2,1)S(1)}, bf16[128,256]{1,0:T(8,128)(2,1)S(1)}, u32[]{:S(2)}, u32[]{:S(2)}) collective-permute-start(bf16[128,256]{1,0:T(8,128)(2,1)S(1)} %get-tuple-element.96), channel_id=1, source_target_pairs={{0,12},{4,8},{8,4},{12,0},{1,13},{5,9},{9,5},{13,1},{2,14},{6,10},... | collective-permute-start | bytes 196616 | tf_op jit(solution)/shard_map/ppermute | solution.py:207
  15.4 13.8 %collective-permute-start.9 = (bf16[128,256]{1,0:T(8,128)(2,1)S(1)}, bf16[128,256]{1,0:T(8,128)(2,1)S(1)}, u32[]{:S(2)}, u32[]{:S(2)}) collective-permute-start(bf16[128,256]{1,0:T(8,128)(2,1)S(1)} %get-tuple-element.95), channel_id=1, source_target_pairs={{0,8},{4,12},{8,0},{12,4},{1,9},{5,13},{9,1},{13,5},{2,10},{6,14},... | collective-permute-start | bytes 196616 | tf_op jit(solution)/shard_map/ppermute | solution.py:207
  17.4 3.4 %collective-permute-start = (bf16[128,1024]{1,0:T(8,128)(2,1)}, bf16[128,1024]{1,0:T(8,128)(2,1)S(1)}, u32[]{:S(2)}, u32[]{:S(2)}) collective-permute-start(bf16[128,1024]{1,0:T(8,128)(2,1)} %get-tuple-element.67.refs_5_), channel_id=1, source_target_pairs={{0,1},{1,0},{2,3},{3,2},{4,5},{5,4},{6,7},{7,6},{8,9},{9,8},{10,11... | collective-permute-start | bytes 786440 | tf_op jit(solution)/shard_map/cond/branch_1_fun/ppermute | solution.py:207
  17.4 4.9 %collective-permute-start.3 = (bf16[128,256]{1,0:T(8,128)(2,1)S(1)}, bf16[128,256]{1,0:T(8,128)(2,1)S(1)}, u32[]{:S(2)}, u32[]{:S(2)}) collective-permute-start(bf16[128,256]{1,0:T(8,128)(2,1)S(1)} %get-tuple-element.76), channel_id=1, source_target_pairs={{0,2},{1,3},{2,0},{3,1},{4,6},{5,7},{6,4},{7,5},{8,10},{9,11},{10,... | collective-permute-start | bytes 196616 | tf_op jit(solution)/shard_map/cond/branch_1_fun/ppermute | solution.py:207
  22.1 2.6 %collective-permute-start.1 = (bf16[2,128,256]{2,1,0:T(8,128)(2,1)S(1)}, bf16[2,128,256]{2,1,0:T(8,128)(2,1)S(1)}, u32[]{:S(2)}, u32[]{:S(2)}) collective-permute-start(bf16[2,128,256]{2,1,0:T(8,128)(2,1)S(1)} %get-tuple-element.73), channel_id=1, source_target_pairs={{0,1},{1,0},{2,3},{3,2},{4,5},{5,4},{6,7},{7,6},{8,9},{9,8},{10,11... | collective-permute-start | bytes 393224 | tf_op jit(solution)/shard_map/cond/branch_1_fun/ppermute | solution.py:207
  22.4 4.9 %collective-permute-start.4 = (bf16[128,256]{1,0:T(8,128)(2,1)S(1)}, bf16[128,256]{1,0:T(8,128)(2,1)S(1)}, u32[]{:S(2)}, u32[]{:S(2)}) collective-permute-start(bf16[128,256]{1,0:T(8,128)(2,1)S(1)} %add_convert_fusion.1), channel_id=1, source_target_pairs={{0,4},{4,0},{8,12},{12,8},{1,5},{5,1},{9,13},{13,9},{2,6},{6,2},{1... | collective-permute-start | bytes 196616 | tf_op jit(solution)/shard_map/cond/branch_1_fun/ppermute | solution.py:207
  24.8 4.3 %collective-permute-start.2 = (bf16[128,256]{1,0:T(8,128)(2,1)S(1)}, bf16[128,256]{1,0:T(8,128)(2,1)S(1)}, u32[]{:S(2)}, u32[]{:S(2)}) collective-permute-start(bf16[128,256]{1,0:T(8,128)(2,1)S(1)} %fusion.1), channel_id=1, source_target_pairs={{0,2},{1,3},{2,0},{3,1},{4,6},{5,7},{6,4},{7,5},{8,10},{9,11},{10,... | collective-permute-start | bytes 196616 | tf_op jit(solution)/shard_map/cond/branch_1_fun/ppermute | solution.py:207

commit v14 on v13

--- a/solution.py
+++ b/solution.py
@@ -351,8 +351,11 @@
             cost_estimate=pl.CostEstimate(flops=1024, bytes_accessed=1024, transcendentals=0),
             name="forward",
         )(lanes, early, *fetched, *other)
-        joined = col_sum(one, one_leaving).astype(BF16)
-        return col_sum(*chunks(pair_sum(send, keep))) + swap(joined, "row", row_count, 1).astype(F32)
+        send, mine = lax.optimization_barrier((send, one))
+        joined = col_sum(mine, one_leaving).astype(BF16)
+        send, joined = lax.optimization_barrier((send, joined))
+        summed = lax.optimization_barrier(col_sum(*chunks(pair_sum(send, keep))))
+        return summed + swap(joined, "row", row_count, 1).astype(F32)
 
     total = stage(forward)
     for term in from_rows:

time: 30 us -> 31.8 us (1.060)
  waiting for transfers between devices: 5.33 us -> 6.75 us
  local copies, waits for them, and re-layouts: 0.04 us -> 0.69 us
  Pallas kernels: 8.83 us -> 8.5 us
    ppermute x10, waiting for transfers between devices: 5.33 us -> 6.74 us  [swap(): return lax.ppermute(value, axis, [(i, i ^ step) for i in range(size)])]
    pallas_call x1, Pallas kernels: 3.18 us -> 2.37 us  [near_of(): pl.pallas_call(lambda *refs: near_kernel(clusters, exc, *refs), in_specs=...]
    slice x1, local copies, waits for them, and re-layouts: 0.01 us -> 0.66 us  [local(): far[i * span:(i + 1) * span]]
    pallas_call x1, Pallas kernels: 0.07 us -> 0.68 us  [local(): pl.pallas_call(lambda *refs: pair_kernel(span, *refs), in_specs=[VMEM] *...]
  transfers between devices with their start and end apart: 11 -> 11, of which waited for: 4 -> 6; matrix products, arithmetic and copies ran while one was open for 0% -> 2% of each run, Pallas kernels for 30% -> 27%
where the time goes in v14:
time: 31.8 us; the launch traced here: 31.6 us
  starting transfers between devices  14.7 us (46%)
  Pallas kernels  8.5 us (27%)
  waiting for transfers between devices  6.75 us (21%)
  other arithmetic  0.77 us (2%)
  local copies, waits for them, and re-layouts  0.69 us (2%)
    ppermute x10, starting transfers between devices, swap(): return lax.ppermute(value, axis, [(i, i ^ step) for i in range(size)])  10.7 us
    ppermute x10, waiting for transfers between devices, swap(): return lax.ppermute(value, axis, [(i, i ^ step) for i in range(size)])  6.74 us
    ppermute x1, starting transfers between devices, body(): lax.ppermute(x, ('row', 'col'), rows_perm(d))  4.04 us
    pallas_call x1, Pallas kernels, near_of(): pl.pallas_call(lambda *refs: near_kernel(clusters, exc, *refs), in_specs=...  2.37 us
    pallas_call x1, Pallas kernels, local(): pl.pallas_call(lambda *refs: mirror_kernel(clusters, exc, rank, others, *...  2.16 us
    pallas_call x1, Pallas kernels, forward(): pl.pallas_call(lambda *refs: early_kernel(clusters, exc, 1 + len(got), *r...  1.64 us
    pallas_call x1, Pallas kernels, forward(): pl.pallas_call(lambda *refs: forward_kernel(clusters, exc, *refs), in_spe...  1.27 us
    pallas_call x1, Pallas kernels, local(): pl.pallas_call(lambda *refs: pair_kernel(span, *refs), in_specs=[VMEM] *...  0.68 us
  transfers between devices with their start and end apart: 11, of which 6 were waited for; matrix products, arithmetic and copies ran while one was open for 2% of the time, Pallas kernels for 27%

profile of v14, /device:TPU:0, one launch (start us, length us, event | category | flops | bytes accessed | tf_op | source)
XLA Modules:
  0.0 31.6 jit_solution(6307185717438056634)
XLA Ops:
  0.0 4.0 %collective-permute-start.7 = (bf16[128,1024]{1,0:T(8,128)(2,1)}, bf16[128,1024]{1,0:T(8,128)(2,1)S(1)}, u32[]{:S(2)}, u32[]{:S(2)}) collective-permute-start(bf16[128,1024]{1,0:T(8,128)(2,1)} %bitcast.14), channel_id=1, source_target_pairs={{0,8},{1,13},{2,10},{3,15},{4,12},{5,9},{6,14},{7,11},{8,0},{9,5},... | collective-permute-start | bytes 786440 | tf_op jit(solution)/shard_map/ppermute | solution.py:269
  4.0 1.6 %collective-permute-start.8 = (bf16[128,1024]{1,0:T(8,128)(2,1)}, bf16[128,1024]{1,0:T(8,128)(2,1)S(1)}, u32[]{:S(2)}, u32[]{:S(2)}) collective-permute-start(bf16[128,1024]{1,0:T(8,128)(2,1)} %bitcast.15), channel_id=1, source_target_pairs={{0,4},{4,0},{8,12},{12,8},{1,5},{5,1},{9,13},{13,9},{2,6},{6,2},{1... | collective-permute-start | bytes 786440 | tf_op jit(solution)/shard_map/ppermute | solution.py:207
  5.6 10.9 %conditional.2 = (f32[128,256]{1,0:T(8,128)S(1)}, bf16[128,256]{1,0:T(8,128)(2,1)}, bf16[128,256]{1,0:T(8,128)(2,1)}, bf16[128,256]{1,0:T(8,128)(2,1)}, f32[128,1024]{1,0:T(8,128)S(1)}, /*index=5*/s32[8,384]{1,0:T(8,128)S(1)}) conditional(s32[]{:T(128)} %convert_element_type.37, () %tuple.25, (s32[24]{0:T(128)}, s32[24]{0:T(128)}, ...), branch_computations={%region_0.0_spmd, %region_1.0_spmd} | conditional | flops 200704 | bytes 15470804 | solution.py:213
  5.6 2.2 %mirror.1 = (bf16[2,384,256]{2,1,0:T(8,128)(2,1)S(1)}, bf16[384,384]{1,0:T(8,128)(2,1)S(1)}, s32[8,384]{1,0:T(8,128)S(1)}) custom-call(s32[24]{0:T(128)} %get-tuple-element.106.refs_0_, s32[24]{0:T(128)} %get-tuple-element.107.refs_1_, bf16[128,1024]{1,0:T(8,128)(2,1)} %bitcast.17, bf16[384,1024]{1,0:T(8,128)(2,1)} %get-tuple-element.47.refs_3_, ...), custom_call_target="tpu_custom_call" | custom-call | flops 1024 | bytes 1024 | tf_op jit(solution)/shard_map/cond/branch_1_fun/mirror/pallas_call | solution.py:272
  7.8 0.1 collective-permute-start.5
  7.9 0.4 %kept.1.refs_0_ = f32[2,384,256]{2,1,0:T(8,128)S(1)} custom-call(bf16[384,384]{1,0:T(8,128)(2,1)S(1)} %get-tuple-element.49.refs_0_, bf16[384,1024]{1,0:T(8,128)(2,1)S(1)} %copy-done), custom_call_target="tpu_custom_call" | custom-call | flops 1024 | bytes 1024 | tf_op jit(solution)/shard_map/cond/branch_1_fun/kept/pallas_call | solution.py:293
  8.3 1.3 %collective-permute-done.5.refs_1_ = bf16[2,384,256]{2,1,0:T(8,128)(2,1)S(1)} collective-permute-done((bf16[2,384,256]{2,1,0:T(8,128)(2,1)S(1)}, bf16[2,384,256]{2,1,0:T(8,128)(2,1)S(1)}, u32[]{:S(2)}, u32[]{:S(2)}) %collective-permute-start.5) | collective-permute-done | bytes 393248 | tf_op jit(solution)/shard_map/cond/branch_1_fun/ppermute | solution.py:207
  9.6 0.7 %pair.1 = (f32[128,256]{1,0:T(8,128)S(1)}, f32[256,256]{1,0:T(8,128)S(1)}, bf16[128,256]{1,0:T(8,128)(2,1)}, bf16[256,256]{1,0:T(8,128)(2,1)S(1)}) custom-call(f32[2,384,256]{2,1,0:T(8,128)S(1)} %kept.1.refs_0_, bf16[2,384,256]{2,1,0:T(8,128)(2,1)S(1)} %collective-permute-done.5.refs_1_), custom_call_target="tpu_custom_call" | custom-call | flops 1024 | bytes 1024 | tf_op jit(solution)/shard_map/cond/branch_1_fun/pair/pallas_call | solution.py:303
  10.3 1.5 %collective-permute-start.6 = (bf16[256,256]{1,0:T(8,128)(2,1)S(1)}, bf16[256,256]{1,0:T(8,128)(2,1)S(1)}, u32[]{:S(2)}, u32[]{:S(2)}) collective-permute-start(bf16[256,256]{1,0:T(8,128)(2,1)S(1)} %get-tuple-element.56), channel_id=1, source_target_pairs={{0,2},{1,3},{2,0},{3,1},{4,6},{5,7},{6,4},{7,5},{8,10},{9,11},{10,... | collective-permute-start | bytes 393224 | tf_op jit(solution)/shard_map/cond/branch_1_fun/ppermute | solution.py:207
  11.8 2.4 %near.1 = f32[4,32,1024]{2,1,0:T(8,128)S(1)} custom-call(s32[1]{0:T(128)} %get-tuple-element.108.refs_0_, s32[1]{0:T(128)} %get-tuple-element.109.refs_1_, bf16[4,32,1024]{2,1,0:T(8,128)(2,1)S(1)} %copy-done.2, bf16[1,1024,1024]{2,1,0:T(8,128)(2,1)S(1)} %copy-done.1), custom_call_target="tpu_custom_call" | custom-call | flops 1024 | bytes 1024 | tf_op jit(solution)/shard_map/cond/branch_1_fun/near/pallas_call | solution.py:251
  14.1 1.7 %collective-permute-done.6 = bf16[256,256]{1,0:T(8,128)(2,1)S(1)} collective-permute-done((bf16[256,256]{1,0:T(8,128)(2,1)S(1)}, bf16[256,256]{1,0:T(8,128)(2,1)S(1)}, u32[]{:S(2)}, u32[]{:S(2)}) %collective-permute-start.6) | collective-permute-done | bytes 131104 | tf_op jit(solution)/shard_map/cond/branch_1_fun/ppermute | solution.py:207
  15.8 0.7 %fusion.1 = (bf16[128,256]{1,0:T(8,128)(2,1)}, bf16[128,256]{1,0:T(8,128)(2,1)}) fusion(bf16[256,256]{1,0:T(8,128)(2,1)S(1)} %add_convert_fusion), kind=kLoop, calls=%fused_computation.8 | loop fusion | bytes 262144 | tf_op jit(solution)/shard_map/cond/branch_1_fun/slice | solution.py:318
  16.5 2.1 %collective-permute-start.9 = (bf16[128,256]{1,0:T(8,128)(2,1)}, bf16[128,256]{1,0:T(8,128)(2,1)S(1)}, u32[]{:S(2)}, u32[]{:S(2)}) collective-permute-start(bf16[128,256]{1,0:T(8,128)(2,1)} %get-tuple-element.99), channel_id=1, source_target_pairs={{0,8},{4,12},{8,0},{12,4},{1,9},{5,13},{9,1},{13,5},{2,10},{6,14},... | collective-permute-start | bytes 196616 | tf_op jit(solution)/shard_map/ppermute | solution.py:207
  18.6 12.3 %conditional.3 = (f32[128,256]{1,0:T(8,128)S(1)}) conditional(s32[]{:T(128)} %convert_element_type.37, () %tuple.24, (s32[8,384]{1,0:T(8,128)S(1)}, bf16[384,1024]{1,0:T(8,128)(2,1)}, bf16[384,1024]{1,0:T(8,128)(2,1)}, f32[128,1024]{1,0:T(8,128)S(1)}, bf16[128,1024]{1,0:T(8,128)(2,1)S(1)}, /*index=5*/bf16[128,1024]{1,0:T(8,128)(2,1)S(1)}, ...), branch_computations={%region_2.0_spmd, %region_3.4_spmd} | conditional | flops 362518 | bytes 4065726 | solution.py:213
  18.6 1.6 %collective-permute-start.1 = (bf16[128,256]{1,0:T(8,128)(2,1)}, bf16[128,256]{1,0:T(8,128)(2,1)S(1)}, u32[]{:S(2)}, u32[]{:S(2)}) collective-permute-start(bf16[128,256]{1,0:T(8,128)(2,1)} %get-tuple-element.77), channel_id=1, source_target_pairs={{0,2},{1,3},{2,0},{3,1},{4,6},{5,7},{6,4},{7,5},{8,10},{9,11},{10,... | collective-permute-start | bytes 196616 | tf_op jit(solution)/shard_map/cond/branch_1_fun/ppermute | solution.py:207
  20.1 1.6 %early.1 = (f32[32,384]{1,0:T(8,128)S(1)}, bf16[384,1024]{1,0:T(8,128)(2,1)S(1)}, bf16[384,1024]{1,0:T(8,128)(2,1)S(1)}, f32[128,1024]{1,0:T(8,128)S(1)}) custom-call(s32[8,384]{1,0:T(8,128)S(1)} %get-tuple-element.62.refs_0_, bf16[384,1024]{1,0:T(8,128)(2,1)} %get-tuple-element.63.refs_1_, bf16[384,1024]{1,0:T(8,128)(2,1)} %get-tuple-element.64.refs_2_, ...), custom_call_target="tpu_custom_call" | custom-call | flops 1024 | bytes 1024 | tf_op jit(solution)/shard_map/cond/branch_1_fun/early/pallas_call | solution.py:327
  21.8 1.3 %forward.1 = (bf16[2,128,256]{2,1,0:T(8,128)(2,1)S(1)}, f32[2,128,256]{2,1,0:T(8,128)S(1)}) custom-call(s32[8,384]{1,0:T(8,128)S(1)} %get-tuple-element.62.refs_0_, f32[32,384]{1,0:T(8,128)S(1)} %get-tuple-element.68.refs_1_, bf16[384,1024]{1,0:T(8,128)(2,1)S(1)} %get-tuple-element.69.refs_2_, bf16[384,1024]{1,0:T(8,128)(2,1)S(1)} %get-tuple-element.70.refs_3_, ...), custom_call_target="tpu_custom_call" | custom-call | flops 1024 | bytes 1024 | tf_op jit(solution)/shard_map/cond/branch_1_fun/forward/pallas_call | solution.py:345
  23.1 0.2 collective-permute-done.1
  23.4 1.3 %collective-permute-done.2 = bf16[2,128,256]{2,1,0:T(8,128)(2,1)S(1)} collective-permute-done((bf16[2,128,256]{2,1,0:T(8,128)(2,1)S(1)}, bf16[2,128,256]{2,1,0:T(8,128)(2,1)S(1)}, u32[]{:S(2)}, u32[]{:S(2)}) %collective-permute-start.2) | collective-permute-done | bytes 131104 | tf_op jit(solution)/shard_map/cond/branch_1_fun/ppermute | solution.py:207
  24.8 1.6 %collective-permute-start.3 = (bf16[128,256]{1,0:T(8,128)(2,1)S(1)}, bf16[128,256]{1,0:T(8,128)(2,1)S(1)}, u32[]{:S(2)}, u32[]{:S(2)}) collective-permute-start(bf16[128,256]{1,0:T(8,128)(2,1)S(1)} %fusion), channel_id=1, source_target_pairs={{0,2},{1,3},{2,0},{3,1},{4,6},{5,7},{6,4},{7,5},{8,10},{9,11},{10,... | collective-permute-start | bytes 196616 | tf_op jit(solution)/shard_map/cond/branch_1_fun/ppermute | solution.py:207
  26.3 2.3 %collective-permute-start.4 = (bf16[128,256]{1,0:T(8,128)(2,1)S(1)}, bf16[128,256]{1,0:T(8,128)(2,1)S(1)}, u32[]{:S(2)}, u32[]{:S(2)}) collective-permute-start(bf16[128,256]{1,0:T(8,128)(2,1)S(1)} %add_convert_fusion.1), channel_id=1, source_target_pairs={{0,4},{4,0},{8,12},{12,8},{1,5},{5,1},{9,13},{13,9},{2,6},{6,2},{1... | collective-permute-start | bytes 196616 | tf_op jit(solution)/shard_map/cond/branch_1_fun/ppermute | solution.py:207
  28.6 0.5 %collective-permute-done.3 = bf16[128,256]{1,0:T(8,128)(2,1)S(1)} collective-permute-done((bf16[128,256]{1,0:T(8,128)(2,1)S(1)}, bf16[128,256]{1,0:T(8,128)(2,1)S(1)}, u32[]{:S(2)}, u32[]{:S(2)}) %collective-permute-start.3) | collective-permute-done | bytes 65568 | tf_op jit(solution)/shard_map/cond/branch_1_fun/ppermute | solution.py:207
  29.1 1.8 %collective-permute-done.4 = bf16[128,256]{1,0:T(8,128)(2,1)S(1)} collective-permute-done((bf16[128,256]{1,0:T(8,128)(2,1)S(1)}, bf16[128,256]{1,0:T(8,128)(2,1)S(1)}, u32[]{:S(2)}, u32[]{:S(2)}) %collective-permute-start.4) | collective-permute-done | bytes 65568 | tf_op jit(solution)/shard_map/cond/branch_1_fun/ppermute | solution.py:207
  30.9 0.7 %convert_add_fusion.2 = f32[128,256]{1,0:T(8,128)} fusion(bf16[128,256]{1,0:T(8,128)(2,1)S(1)} %collective-permute-done.10, f32[128,256]{1,0:T(8,128)S(1)} %get-tuple-element.125, bf16[128,256]{1,0:T(8,128)(2,1)S(1)} %collective-permute-done.9), kind=kLoop, calls=%fused_computation.7 | loop fusion | flops 131072 | bytes 393216 | tf_op jit(solution)/shard_map/add | solution.py:362
  (20 shorter events, 0.2 us)
Async XLA Ops:
  0.0 18.6 %collective-permute-start.7 = (bf16[128,1024]{1,0:T(8,128)(2,1)}, bf16[128,1024]{1,0:T(8,128)(2,1)S(1)}, u32[]{:S(2)}, u32[]{:S(2)}) collective-permute-start(bf16[128,1024]{1,0:T(8,128)(2,1)} %bitcast.14), channel_id=1, source_target_pairs={{0,8},{1,13},{2,10},{3,15},{4,12},{5,9},{6,14},{7,11},{8,0},{9,5},... | collective-permute-start | bytes 786440 | tf_op jit(solution)/shard_map/ppermute | solution.py:269
  4.0 14.5 %collective-permute-start.8 = (bf16[128,1024]{1,0:T(8,128)(2,1)}, bf16[128,1024]{1,0:T(8,128)(2,1)S(1)}, u32[]{:S(2)}, u32[]{:S(2)}) collective-permute-start(bf16[128,1024]{1,0:T(8,128)(2,1)} %bitcast.15), channel_id=1, source_target_pairs={{0,4},{4,0},{8,12},{12,8},{1,5},{5,1},{9,13},{13,9},{2,6},{6,2},{1... | collective-permute-start | bytes 786440 | tf_op jit(solution)/shard_map/ppermute | solution.py:207
  5.6 2.3 %copy-start = (bf16[384,1024]{1,0:T(8,128)(2,1)S(1)}, bf16[384,1024]{1,0:T(8,128)(2,1)}, u32[]{:S(2)}) copy-start(bf16[384,1024]{1,0:T(8,128)(2,1)} %get-tuple-element.48.refs_4_.refs_1_) | copy-start | bytes 2359300 | tf_op jit(solution)/shard_map/cond
  5.6 6.1 %copy-start.1 = (bf16[1,1024,1024]{2,1,0:T(8,128)(2,1)S(1)}, bf16[1,1024,1024]{2,1,0:T(8,128)(2,1)}, u32[]{:S(2)}) copy-start(bf16[1,1024,1024]{2,1,0:T(8,128)(2,1)} %get-tuple-element.110.refs_3_) | copy-start | bytes 6291460 | tf_op jit(solution)/shard_map/cond
  5.6 6.1 %copy-start.2 = (bf16[4,32,1024]{2,1,0:T(8,128)(2,1)S(1)}, bf16[4,32,1024]{2,1,0:T(8,128)(2,1)}, u32[]{:S(2)}) copy-start(bf16[4,32,1024]{2,1,0:T(8,128)(2,1)} %get-tuple-element.59.refs_2_) | copy-start | bytes 786436 | tf_op jit(solution)/shard_map/cond
  7.8 1.8 %collective-permute-start.5 = (bf16[2,384,256]{2,1,0:T(8,128)(2,1)S(1)}, bf16[2,384,256]{2,1,0:T(8,128)(2,1)S(1)}, u32[]{:S(2)}, u32[]{:S(2)}) collective-permute-start(bf16[2,384,256]{2,1,0:T(8,128)(2,1)S(1)} %get-tuple-element.50), channel_id=1, source_target_pairs={{0,1},{1,0},{2,3},{3,2},{4,5},{5,4},{6,7},{7,6},{8,9},{9,8},{10,11... | collective-permute-start | bytes 1179656 | tf_op jit(solution)/shard_map/cond/branch_1_fun/ppermute | solution.py:207
  10.3 5.5 %collective-permute-start.6 = (bf16[256,256]{1,0:T(8,128)(2,1)S(1)}, bf16[256,256]{1,0:T(8,128)(2,1)S(1)}, u32[]{:S(2)}, u32[]{:S(2)}) collective-permute-start(bf16[256,256]{1,0:T(8,128)(2,1)S(1)} %get-tuple-element.56), channel_id=1, source_target_pairs={{0,2},{1,3},{2,0},{3,1},{4,6},{5,7},{6,4},{7,5},{8,10},{9,11},{10,... | collective-permute-start | bytes 393224 | tf_op jit(solution)/shard_map/cond/branch_1_fun/ppermute | solution.py:207
  16.5 14.4 %collective-permute-start.10 = (bf16[128,256]{1,0:T(8,128)(2,1)}, bf16[128,256]{1,0:T(8,128)(2,1)S(1)}, u32[]{:S(2)}, u32[]{:S(2)}) collective-permute-start(bf16[128,256]{1,0:T(8,128)(2,1)} %get-tuple-element.100), channel_id=1, source_target_pairs={{0,12},{4,8},{8,4},{12,0},{1,13},{5,9},{9,5},{13,1},{2,14},{6,10},... | collective-permute-start | bytes 196616 | tf_op jit(solution)/shard_map/ppermute | solution.py:207
  16.5 14.4 %collective-permute-start.9 = (bf16[128,256]{1,0:T(8,128)(2,1)}, bf16[128,256]{1,0:T(8,128)(2,1)S(1)}, u32[]{:S(2)}, u32[]{:S(2)}) collective-permute-start(bf16[128,256]{1,0:T(8,128)(2,1)} %get-tuple-element.99), channel_id=1, source_target_pairs={{0,8},{4,12},{8,0},{12,4},{1,9},{5,13},{9,1},{13,5},{2,10},{6,14},... | collective-permute-start | bytes 196616 | tf_op jit(solution)/shard_map/ppermute | solution.py:207
  18.6 3.2 %collective-permute-start = (bf16[128,1024]{1,0:T(8,128)(2,1)S(1)}, bf16[128,1024]{1,0:T(8,128)(2,1)S(1)}, u32[]{:S(2)}, u32[]{:S(2)}) collective-permute-start(bf16[128,1024]{1,0:T(8,128)(2,1)S(1)} %get-tuple-element.67.refs_5_), channel_id=1, source_target_pairs={{0,1},{1,0},{2,3},{3,2},{4,5},{5,4},{6,7},{7,6},{8,9},{9,8},{10,11... | collective-permute-start | bytes 786440 | tf_op jit(solution)/shard_map/cond/branch_1_fun/ppermute | solution.py:207
  18.6 4.7 %collective-permute-start.1 = (bf16[128,256]{1,0:T(8,128)(2,1)}, bf16[128,256]{1,0:T(8,128)(2,1)S(1)}, u32[]{:S(2)}, u32[]{:S(2)}) collective-permute-start(bf16[128,256]{1,0:T(8,128)(2,1)} %get-tuple-element.77), channel_id=1, source_target_pairs={{0,2},{1,3},{2,0},{3,1},{4,6},{5,7},{6,4},{7,5},{8,10},{9,11},{10,... | collective-permute-start | bytes 196616 | tf_op jit(solution)/shard_map/cond/branch_1_fun/ppermute | solution.py:207
  23.3 1.4 %collective-permute-start.2 = (bf16[2,128,256]{2,1,0:T(8,128)(2,1)S(1)}, bf16[2,128,256]{2,1,0:T(8,128)(2,1)S(1)}, u32[]{:S(2)}, u32[]{:S(2)}) collective-permute-start(bf16[2,128,256]{2,1,0:T(8,128)(2,1)S(1)} %get-tuple-element.78), channel_id=1, source_target_pairs={{0,1},{1,0},{2,3},{3,2},{4,5},{5,4},{6,7},{7,6},{8,9},{9,8},{10,11... | collective-permute-start | bytes 393224 | tf_op jit(solution)/shard_map/cond/branch_1_fun/ppermute | solution.py:207
  24.8 4.3 %collective-permute-start.3 = (bf16[128,256]{1,0:T(8,128)(2,1)S(1)}, bf16[128,256]{1,0:T(8,128)(2,1)S(1)}, u32[]{:S(2)}, u32[]{:S(2)}) collective-permute-start(bf16[128,256]{1,0:T(8,128)(2,1)S(1)} %fusion), channel_id=1, source_target_pairs={{0,2},{1,3},{2,0},{3,1},{4,6},{5,7},{6,4},{7,5},{8,10},{9,11},{10,... | collective-permute-start | bytes 196616 | tf_op jit(solution)/shard_map/cond/branch_1_fun/ppermute | solution.py:207
  26.3 4.6 %collective-permute-start.4 = (bf16[128,256]{1,0:T(8,128)(2,1)S(1)}, bf16[128,256]{1,0:T(8,128)(2,1)S(1)}, u32[]{:S(2)}, u32[]{:S(2)}) collective-permute-start(bf16[128,256]{1,0:T(8,128)(2,1)S(1)} %add_convert_fusion.1), channel_id=1, source_target_pairs={{0,4},{4,0},{8,12},{12,8},{1,5},{5,1},{9,13},{13,9},{2,6},{6,2},{1... | collective-permute-start | bytes 196616 | tf_op jit(solution)/shard_map/cond/branch_1_fun/ppermute | solution.py:207

commit v15 on v13

--- a/solution.py
+++ b/solution.py
@@ -355,8 +355,9 @@
         return col_sum(*chunks(pair_sum(send, keep))) + swap(joined, "row", row_count, 1).astype(F32)
 
     total = stage(forward)
-    for term in from_rows:
+    for term in from_rows[:-1]:
         total = total + term.astype(F32)
+    total = lax.optimization_barrier(total) + from_rows[-1].astype(F32)
     return total.reshape(clusters, exc, width)
 
 

time: 30 us -> 29.7 us (0.990)
  starting transfers between devices: 14.7 us -> 13.9 us
  waiting for transfers between devices: 5.33 us -> 5.81 us
    ppermute x10, starting transfers between devices: 10.7 us -> 9.88 us  [swap(): return lax.ppermute(value, axis, [(i, i ^ step) for i in range(size)])]
    add x0 -> x1, other arithmetic: none -> 0.67 us  [body(): total = lax.optimization_barrier(total) + from_rows[-1].astype(F32)]
    add x1, other arithmetic: 0.68 us -> 0.01 us  [body(): total = total + term.astype(F32)]
    ppermute x10, waiting for transfers between devices: 5.33 us -> 5.81 us  [swap(): return lax.ppermute(value, axis, [(i, i ^ step) for i in range(size)])]
  transfers between devices with their start and end apart: 11 -> 11, of which waited for: 4 -> 5; matrix products, arithmetic and copies ran while one was open for 0% -> 0% of each run, Pallas kernels for 30% -> 30%
where the time goes in v15:
time: 29.7 us; the launch traced here: 29.5 us
  starting transfers between devices  13.9 us (47%)
  Pallas kernels  8.83 us (30%)
  waiting for transfers between devices  5.81 us (20%)
  other arithmetic  0.78 us (3%)
    ppermute x10, starting transfers between devices, swap(): return lax.ppermute(value, axis, [(i, i ^ step) for i in range(size)])  9.88 us
    ppermute x10, waiting for transfers between devices, swap(): return lax.ppermute(value, axis, [(i, i ^ step) for i in range(size)])  5.81 us
    ppermute x1, starting transfers between devices, body(): lax.ppermute(x, ('row', 'col'), rows_perm(d))  4.04 us
    pallas_call x1, Pallas kernels, near_of(): pl.pallas_call(lambda *refs: near_kernel(clusters, exc, *refs), in_specs=...  3.18 us
    pallas_call x1, Pallas kernels, local(): pl.pallas_call(lambda *refs: mirror_kernel(clusters, exc, rank, others, *...  2.16 us
    pallas_call x1, Pallas kernels, forward(): pl.pallas_call(lambda *refs: early_kernel(clusters, exc, 1 + len(got), *r...  1.77 us
    pallas_call x1, Pallas kernels, forward(): pl.pallas_call(lambda *refs: forward_kernel(clusters, exc, *refs), in_spe...  1.27 us
    add x1, other arithmetic, body(): total = lax.optimization_barrier(total) + from_rows[-1].astype(F32)  0.67 us
  transfers between devices with their start and end apart: 11, of which 5 were waited for; matrix products, arithmetic and copies ran while one was open for 0% of the time, Pallas kernels for 30%

profile of v15, /device:TPU:0, one launch (start us, length us, event | category | flops | bytes accessed | tf_op | source)
XLA Modules:
  0.0 29.5 jit_solution(17732641501651744517)
XLA Ops:
  0.0 4.0 %collective-permute-start.7 = (bf16[128,1024]{1,0:T(8,128)(2,1)}, bf16[128,1024]{1,0:T(8,128)(2,1)}, u32[]{:S(2)}, u32[]{:S(2)}) collective-permute-start(bf16[128,1024]{1,0:T(8,128)(2,1)} %bitcast.15), channel_id=1, source_target_pairs={{0,8},{1,13},{2,10},{3,15},{4,12},{5,9},{6,14},{7,11},{8,0},{9,5},... | collective-permute-start | bytes 786440 | tf_op jit(solution)/shard_map/ppermute | solution.py:269
  4.0 1.6 %collective-permute-start.8 = (bf16[128,1024]{1,0:T(8,128)(2,1)}, bf16[128,1024]{1,0:T(8,128)(2,1)}, u32[]{:S(2)}, u32[]{:S(2)}) collective-permute-start(bf16[128,1024]{1,0:T(8,128)(2,1)} %bitcast.16), channel_id=1, source_target_pairs={{0,4},{4,0},{8,12},{12,8},{1,5},{5,1},{9,13},{13,9},{2,6},{6,2},{1... | collective-permute-start | bytes 786440 | tf_op jit(solution)/shard_map/ppermute | solution.py:207
  5.6 9.7 %conditional.2 = (f32[128,256]{1,0:T(8,128)S(1)}, bf16[128,256]{1,0:T(8,128)(2,1)S(1)}, bf16[128,256]{1,0:T(8,128)(2,1)S(1)}, bf16[128,256]{1,0:T(8,128)(2,1)S(1...) conditional(s32[]{:T(128)} %convert_element_type.37, () %tuple.23, (s32[24]{0:T(128)}, s32[24]{0:T(128)}, ...), branch_computations={%region_0.0_spmd, %region_1.0_spmd} | conditional | flops 200704 | bytes 15470804 | solution.py:213
  5.6 2.2 %mirror.1 = (bf16[2,384,256]{2,1,0:T(8,128)(2,1)S(1)}, bf16[384,384]{1,0:T(8,128)(2,1)S(1)}, s32[8,384]{1,0:T(8,128)S(1)}) custom-call(s32[24]{0:T(128)} %get-tuple-element.102.refs_0_, s32[24]{0:T(128)} %get-tuple-element.103.refs_1_, bf16[128,1024]{1,0:T(8,128)(2,1)} %bitcast.18, bf16[384,1024]{1,0:T(8,128)(2,1)} %get-tuple-element.47.refs_3_, ...), custom_call_target="tpu_custom_call" | custom-call | flops 1024 | bytes 1024 | tf_op jit(solution)/shard_map/cond/branch_1_fun/mirror/pallas_call | solution.py:272
  7.8 0.1 collective-permute-start.5
  7.9 0.4 %kept.1.refs_0_ = f32[2,384,256]{2,1,0:T(8,128)S(1)} custom-call(bf16[384,384]{1,0:T(8,128)(2,1)S(1)} %get-tuple-element.49.refs_0_, bf16[384,1024]{1,0:T(8,128)(2,1)S(1)} %copy-done), custom_call_target="tpu_custom_call" | custom-call | flops 1024 | bytes 1024 | tf_op jit(solution)/shard_map/cond/branch_1_fun/kept/pallas_call | solution.py:293
  8.3 1.3 %collective-permute-done.5.refs_1_ = bf16[2,384,256]{2,1,0:T(8,128)(2,1)S(1)} collective-permute-done((bf16[2,384,256]{2,1,0:T(8,128)(2,1)S(1)}, bf16[2,384,256]{2,1,0:T(8,128)(2,1)S(1)}, u32[]{:S(2)}, u32[]{:S(2)}) %collective-permute-start.5) | collective-permute-done | bytes 393248 | tf_op jit(solution)/shard_map/cond/branch_1_fun/ppermute | solution.py:207
  9.6 0.1 pair.1
  9.6 1.6 %collective-permute-start.6 = (bf16[256,256]{1,0:T(8,128)(2,1)S(1)}, bf16[256,256]{1,0:T(8,128)(2,1)S(1)}, u32[]{:S(2)}, u32[]{:S(2)}) collective-permute-start(bf16[256,256]{1,0:T(8,128)(2,1)S(1)} %get-tuple-element.56), channel_id=1, source_target_pairs={{0,2},{1,3},{2,0},{3,1},{4,6},{5,7},{6,4},{7,5},{8,10},{9,11},{10,... | collective-permute-start | bytes 393224 | tf_op jit(solution)/shard_map/cond/branch_1_fun/ppermute | solution.py:207
  11.2 3.2 %near.1 = f32[4,32,1024]{2,1,0:T(8,128)} custom-call(s32[1]{0:T(128)} %get-tuple-element.104.refs_0_, s32[1]{0:T(128)} %get-tuple-element.105.refs_1_, bf16[4,32,1024]{2,1,0:T(8,128)(2,1)S(1)} %copy-done.2, bf16[1,1024,1024]{2,1,0:T(8,128)(2,1)S(1)} %copy-done.1), custom_call_target="tpu_custom_call" | custom-call | flops 1024 | bytes 1024 | tf_op jit(solution)/shard_map/cond/branch_1_fun/near/pallas_call | solution.py:251
  14.4 0.9 %collective-permute-done.6 = bf16[256,256]{1,0:T(8,128)(2,1)S(1)} collective-permute-done((bf16[256,256]{1,0:T(8,128)(2,1)S(1)}, bf16[256,256]{1,0:T(8,128)(2,1)S(1)}, u32[]{:S(2)}, u32[]{:S(2)}) %collective-permute-start.6) | collective-permute-done | bytes 131104 | tf_op jit(solution)/shard_map/cond/branch_1_fun/ppermute | solution.py:207
  15.3 0.4 %collective-permute-start.9 = (bf16[128,256]{1,0:T(8,128)(2,1)S(1)}, bf16[128,256]{1,0:T(8,128)(2,1)S(1)}, u32[]{:S(2)}, u32[]{:S(2)}) collective-permute-start(bf16[128,256]{1,0:T(8,128)(2,1)S(1)} %get-tuple-element.95), channel_id=1, source_target_pairs={{0,8},{4,12},{8,0},{12,4},{1,9},{5,13},{9,1},{13,5},{2,10},{6,14},... | collective-permute-start | bytes 196616 | tf_op jit(solution)/shard_map/ppermute | solution.py:207
  15.7 2.6 %collective-permute-start.10 = (bf16[128,256]{1,0:T(8,128)(2,1)S(1)}, bf16[128,256]{1,0:T(8,128)(2,1)S(1)}, u32[]{:S(2)}, u32[]{:S(2)}) collective-permute-start(bf16[128,256]{1,0:T(8,128)(2,1)S(1)} %get-tuple-element.96), channel_id=1, source_target_pairs={{0,12},{4,8},{8,4},{12,0},{1,13},{5,9},{9,5},{13,1},{2,14},{6,10},... | collective-permute-start | bytes 196616 | tf_op jit(solution)/shard_map/ppermute | solution.py:207
  18.3 10.5 %conditional.3 = (f32[128,256]{1,0:T(8,128)S(1)}) conditional(s32[]{:T(128)} %convert_element_type.37, () %tuple.22, (s32[8,384]{1,0:T(8,128)S(1)}, bf16[384,1024]{1,0:T(8,128)(2,1)}, bf16[384,1024]{1,0:T(8,128)(2,1)}, f32[128,1024]{1,0:T(8,128)}, bf16[128,1024]{1,0:T(8,128)(2,1)}, /*index=5*/bf16[128,1024]{1,0:T(8,128)(2,1)}, s32[]{:T(128)}, ...), branch_computations={%region_2.0_spmd, %region_3.4_spmd} | conditional | flops 362518 | bytes 3803582 | solution.py:213
  18.3 1.6 %collective-permute-start.3 = (bf16[128,256]{1,0:T(8,128)(2,1)S(1)}, bf16[128,256]{1,0:T(8,128)(2,1)S(1)}, u32[]{:S(2)}, u32[]{:S(2)}) collective-permute-start(bf16[128,256]{1,0:T(8,128)(2,1)S(1)} %get-tuple-element.76), channel_id=1, source_target_pairs={{0,2},{1,3},{2,0},{3,1},{4,6},{5,7},{6,4},{7,5},{8,10},{9,11},{10,... | collective-permute-start | bytes 196616 | tf_op jit(solution)/shard_map/cond/branch_1_fun/ppermute | solution.py:207
  19.9 1.8 %early.1 = (f32[32,384]{1,0:T(8,128)S(1)}, bf16[384,1024]{1,0:T(8,128)(2,1)S(1)}, bf16[384,1024]{1,0:T(8,128)(2,1)S(1)}, f32[128,1024]{1,0:T(8,128)S(1)}) custom-call(s32[8,384]{1,0:T(8,128)S(1)} %get-tuple-element.62.refs_0_, bf16[384,1024]{1,0:T(8,128)(2,1)} %get-tuple-element.63.refs_1_, bf16[384,1024]{1,0:T(8,128)(2,1)} %get-tuple-element.64.refs_2_, ...), custom_call_target="tpu_custom_call" | custom-call | flops 1024 | bytes 1024 | tf_op jit(solution)/shard_map/cond/branch_1_fun/early/pallas_call | solution.py:327
  21.7 1.3 %forward.1 = (bf16[2,128,256]{2,1,0:T(8,128)(2,1)S(1)}, f32[2,128,256]{2,1,0:T(8,128)S(1)}) custom-call(s32[8,384]{1,0:T(8,128)S(1)} %get-tuple-element.62.refs_0_, f32[32,384]{1,0:T(8,128)S(1)} %get-tuple-element.68.refs_1_, bf16[384,1024]{1,0:T(8,128)(2,1)S(1)} %get-tuple-element.69.refs_2_, bf16[384,1024]{1,0:T(8,128)(2,1)S(1)} %get-tuple-element.70.refs_3_, ...), custom_call_target="tpu_custom_call" | custom-call | flops 1024 | bytes 1024 | tf_op jit(solution)/shard_map/cond/branch_1_fun/forward/pallas_call | solution.py:345
  23.0 0.2 collective-permute-start.1
  23.2 0.9 %collective-permute-start.4 = (bf16[128,256]{1,0:T(8,128)(2,1)S(1)}, bf16[128,256]{1,0:T(8,128)(2,1)S(1)}, u32[]{:S(2)}, u32[]{:S(2)}) collective-permute-start(bf16[128,256]{1,0:T(8,128)(2,1)S(1)} %add_convert_fusion.1), channel_id=1, source_target_pairs={{0,4},{4,0},{8,12},{12,8},{1,5},{5,1},{9,13},{13,9},{2,6},{6,2},{1... | collective-permute-start | bytes 196616 | tf_op jit(solution)/shard_map/cond/branch_1_fun/ppermute | solution.py:207
  24.2 0.2 collective-permute-done.1
  24.5 0.9 %collective-permute-start.2 = (bf16[128,256]{1,0:T(8,128)(2,1)S(1)}, bf16[128,256]{1,0:T(8,128)(2,1)S(1)}, u32[]{:S(2)}, u32[]{:S(2)}) collective-permute-start(bf16[128,256]{1,0:T(8,128)(2,1)S(1)} %fusion.1), channel_id=1, source_target_pairs={{0,2},{1,3},{2,0},{3,1},{4,6},{5,7},{6,4},{7,5},{8,10},{9,11},{10,... | collective-permute-start | bytes 196616 | tf_op jit(solution)/shard_map/cond/branch_1_fun/ppermute | solution.py:207
  25.4 2.2 %collective-permute-done.4 = bf16[128,256]{1,0:T(8,128)(2,1)S(1)} collective-permute-done((bf16[128,256]{1,0:T(8,128)(2,1)S(1)}, bf16[128,256]{1,0:T(8,128)(2,1)S(1)}, u32[]{:S(2)}, u32[]{:S(2)}) %collective-permute-start.4) | collective-permute-done | bytes 65568 | tf_op jit(solution)/shard_map/cond/branch_1_fun/ppermute | solution.py:207
  27.6 1.1 %collective-permute-done.2 = bf16[128,256]{1,0:T(8,128)(2,1)S(1)} collective-permute-done((bf16[128,256]{1,0:T(8,128)(2,1)S(1)}, bf16[128,256]{1,0:T(8,128)(2,1)S(1)}, u32[]{:S(2)}, u32[]{:S(2)}) %collective-permute-start.2) | collective-permute-done | bytes 65568 | tf_op jit(solution)/shard_map/cond/branch_1_fun/ppermute | solution.py:207
  28.9 0.7 %convert_add_fusion.1 = f32[128,256]{1,0:T(8,128)} fusion(f32[128,256]{1,0:T(8,128)S(1)} %convert_add_fusion.2, bf16[128,256]{1,0:T(8,128)(2,1)S(1)} %collective-permute-done.10), kind=kLoop, calls=%fused_computation.7 | loop fusion | flops 65536 | bytes 327680 | tf_op jit(solution)/shard_map/add | solution.py:360
  (20 shorter events, 0.2 us)
Async XLA Ops:
  0.0 18.3 %collective-permute-start.7 = (bf16[128,1024]{1,0:T(8,128)(2,1)}, bf16[128,1024]{1,0:T(8,128)(2,1)}, u32[]{:S(2)}, u32[]{:S(2)}) collective-permute-start(bf16[128,1024]{1,0:T(8,128)(2,1)} %bitcast.15), channel_id=1, source_target_pairs={{0,8},{1,13},{2,10},{3,15},{4,12},{5,9},{6,14},{7,11},{8,0},{9,5},... | collective-permute-start | bytes 786440 | tf_op jit(solution)/shard_map/ppermute | solution.py:269
  4.0 14.3 %collective-permute-start.8 = (bf16[128,1024]{1,0:T(8,128)(2,1)}, bf16[128,1024]{1,0:T(8,128)(2,1)}, u32[]{:S(2)}, u32[]{:S(2)}) collective-permute-start(bf16[128,1024]{1,0:T(8,128)(2,1)} %bitcast.16), channel_id=1, source_target_pairs={{0,4},{4,0},{8,12},{12,8},{1,5},{5,1},{9,13},{13,9},{2,6},{6,2},{1... | collective-permute-start | bytes 786440 | tf_op jit(solution)/shard_map/ppermute | solution.py:207
  5.6 2.3 %copy-start = (bf16[384,1024]{1,0:T(8,128)(2,1)S(1)}, bf16[384,1024]{1,0:T(8,128)(2,1)}, u32[]{:S(2)}) copy-start(bf16[384,1024]{1,0:T(8,128)(2,1)} %get-tuple-element.48.refs_4_.refs_1_) | copy-start | bytes 2359300 | tf_op jit(solution)/shard_map/cond
  5.6 5.6 %copy-start.1 = (bf16[1,1024,1024]{2,1,0:T(8,128)(2,1)S(1)}, bf16[1,1024,1024]{2,1,0:T(8,128)(2,1)}, u32[]{:S(2)}) copy-start(bf16[1,1024,1024]{2,1,0:T(8,128)(2,1)} %get-tuple-element.106.refs_3_) | copy-start | bytes 6291460 | tf_op jit(solution)/shard_map/cond
  5.6 5.6 %copy-start.2 = (bf16[4,32,1024]{2,1,0:T(8,128)(2,1)S(1)}, bf16[4,32,1024]{2,1,0:T(8,128)(2,1)}, u32[]{:S(2)}) copy-start(bf16[4,32,1024]{2,1,0:T(8,128)(2,1)} %get-tuple-element.59.refs_2_) | copy-start | bytes 786436 | tf_op jit(solution)/shard_map/cond
  7.8 1.8 %collective-permute-start.5 = (bf16[2,384,256]{2,1,0:T(8,128)(2,1)S(1)}, bf16[2,384,256]{2,1,0:T(8,128)(2,1)S(1)}, u32[]{:S(2)}, u32[]{:S(2)}) collective-permute-start(bf16[2,384,256]{2,1,0:T(8,128)(2,1)S(1)} %get-tuple-element.50), channel_id=1, source_target_pairs={{0,1},{1,0},{2,3},{3,2},{4,5},{5,4},{6,7},{7,6},{8,9},{9,8},{10,11... | collective-permute-start | bytes 1179656 | tf_op jit(solution)/shard_map/cond/branch_1_fun/ppermute | solution.py:207
  9.6 5.6 %collective-permute-start.6 = (bf16[256,256]{1,0:T(8,128)(2,1)S(1)}, bf16[256,256]{1,0:T(8,128)(2,1)S(1)}, u32[]{:S(2)}, u32[]{:S(2)}) collective-permute-start(bf16[256,256]{1,0:T(8,128)(2,1)S(1)} %get-tuple-element.56), channel_id=1, source_target_pairs={{0,2},{1,3},{2,0},{3,1},{4,6},{5,7},{6,4},{7,5},{8,10},{9,11},{10,... | collective-permute-start | bytes 393224 | tf_op jit(solution)/shard_map/cond/branch_1_fun/ppermute | solution.py:207
  15.3 13.5 %collective-permute-start.9 = (bf16[128,256]{1,0:T(8,128)(2,1)S(1)}, bf16[128,256]{1,0:T(8,128)(2,1)S(1)}, u32[]{:S(2)}, u32[]{:S(2)}) collective-permute-start(bf16[128,256]{1,0:T(8,128)(2,1)S(1)} %get-tuple-element.95), channel_id=1, source_target_pairs={{0,8},{4,12},{8,0},{12,4},{1,9},{5,13},{9,1},{13,5},{2,10},{6,14},... | collective-permute-start | bytes 196616 | tf_op jit(solution)/shard_map/ppermute | solution.py:207
  15.7 13.2 %collective-permute-start.10 = (bf16[128,256]{1,0:T(8,128)(2,1)S(1)}, bf16[128,256]{1,0:T(8,128)(2,1)S(1)}, u32[]{:S(2)}, u32[]{:S(2)}) collective-permute-start(bf16[128,256]{1,0:T(8,128)(2,1)S(1)} %get-tuple-element.96), channel_id=1, source_target_pairs={{0,12},{4,8},{8,4},{12,0},{1,13},{5,9},{9,5},{13,1},{2,14},{6,10},... | collective-permute-start | bytes 196616 | tf_op jit(solution)/shard_map/ppermute | solution.py:207
  18.3 3.4 %collective-permute-start = (bf16[128,1024]{1,0:T(8,128)(2,1)}, bf16[128,1024]{1,0:T(8,128)(2,1)S(1)}, u32[]{:S(2)}, u32[]{:S(2)}) collective-permute-start(bf16[128,1024]{1,0:T(8,128)(2,1)} %get-tuple-element.67.refs_5_), channel_id=1, source_target_pairs={{0,1},{1,0},{2,3},{3,2},{4,5},{5,4},{6,7},{7,6},{8,9},{9,8},{10,11... | collective-permute-start | bytes 786440 | tf_op jit(solution)/shard_map/cond/branch_1_fun/ppermute | solution.py:207
  18.3 4.9 %collective-permute-start.3 = (bf16[128,256]{1,0:T(8,128)(2,1)S(1)}, bf16[128,256]{1,0:T(8,128)(2,1)S(1)}, u32[]{:S(2)}, u32[]{:S(2)}) collective-permute-start(bf16[128,256]{1,0:T(8,128)(2,1)S(1)} %get-tuple-element.76), channel_id=1, source_target_pairs={{0,2},{1,3},{2,0},{3,1},{4,6},{5,7},{6,4},{7,5},{8,10},{9,11},{10,... | collective-permute-start | bytes 196616 | tf_op jit(solution)/shard_map/cond/branch_1_fun/ppermute | solution.py:207
  23.0 1.4 %collective-permute-start.1 = (bf16[2,128,256]{2,1,0:T(8,128)(2,1)S(1)}, bf16[2,128,256]{2,1,0:T(8,128)(2,1)S(1)}, u32[]{:S(2)}, u32[]{:S(2)}) collective-permute-start(bf16[2,128,256]{2,1,0:T(8,128)(2,1)S(1)} %get-tuple-element.73), channel_id=1, source_target_pairs={{0,1},{1,0},{2,3},{3,2},{4,5},{5,4},{6,7},{7,6},{8,9},{9,8},{10,11... | collective-permute-start | bytes 393224 | tf_op jit(solution)/shard_map/cond/branch_1_fun/ppermute | solution.py:207
  23.2 4.4 %collective-permute-start.4 = (bf16[128,256]{1,0:T(8,128)(2,1)S(1)}, bf16[128,256]{1,0:T(8,128)(2,1)S(1)}, u32[]{:S(2)}, u32[]{:S(2)}) collective-permute-start(bf16[128,256]{1,0:T(8,128)(2,1)S(1)} %add_convert_fusion.1), channel_id=1, source_target_pairs={{0,4},{4,0},{8,12},{12,8},{1,5},{5,1},{9,13},{13,9},{2,6},{6,2},{1... | collective-permute-start | bytes 196616 | tf_op jit(solution)/shard_map/cond/branch_1_fun/ppermute | solution.py:207
  24.5 4.3 %collective-permute-start.2 = (bf16[128,256]{1,0:T(8,128)(2,1)S(1)}, bf16[128,256]{1,0:T(8,128)(2,1)S(1)}, u32[]{:S(2)}, u32[]{:S(2)}) collective-permute-start(bf16[128,256]{1,0:T(8,128)(2,1)S(1)} %fusion.1), channel_id=1, source_target_pairs={{0,2},{1,3},{2,0},{3,1},{4,6},{5,7},{6,4},{7,5},{8,10},{9,11},{10,... | collective-permute-start | bytes 196616 | tf_op jit(solution)/shard_map/cond/branch_1_fun/ppermute | solution.py:207

commit v16 on v15

--- a/solution.py
+++ b/solution.py
@@ -166,12 +166,12 @@
 
 
 def early_kernel(clusters, exc, count, lanes_ref, *refs):
-    sources, (coef_ref, *targets) = refs[: 3 + count], refs[3 + count : 7 + count]
-    pieces_ref, sems = refs[7 + count :]
+    sources, (coef_ref, *targets) = refs[: 4 + count], refs[4 + count : 9 + count]
+    pieces_ref, sems = refs[9 + count :]
     span = clusters * exc
     moves = [(sources[0], targets[0])]
-    moves += [(src, pieces_ref.at[i * span : (i + 1) * span]) for i, src in enumerate(sources[3:])]
-    moves += list(zip(sources[1:3], targets[1:]))
+    moves += [(src, pieces_ref.at[i * span : (i + 1) * span]) for i, src in enumerate(sources[4:])]
+    moves += list(zip(sources[1:4], targets[1:]))
     copies = [pltpu.make_async_copy(src, dst, sems.at[i]) for i, (src, dst) in enumerate(moves)]
     for copy in copies:
         copy.start()
@@ -179,7 +179,7 @@
     for copy in copies[: 1 + count]:
         copy.wait()
     pieces = [pieces_ref[i * span : (i + 1) * span] for i in range(count)]
-    aways = [1] + [2 * t + half for t in range(1, count)]
+    aways = [2 * t + half for t in range(1, count + 1)]
     coef_ref[...] = coef_of(clusters, exc, aways, lanes_ref, targets[0], pieces)
     for copy in copies[1 + count :]:
         copy.wait()
@@ -190,7 +190,7 @@
     group = lax.axis_index("row")
     half = lax.rem(lax.axis_index("col"), 2)
     pieces = [ref[...] for ref in refs[:-2]]
-    aways = [2 * t + 3 - half for t in range(len(pieces))]
+    aways = [1] + [2 * t + 1 - half for t in range(1, len(pieces))]
     coef = early_ref[...] + coef_of(clusters, exc, aways, lanes_ref, v_ref, pieces)
     coef = coef.astype(BF16).astype(F32)
     row_lane = lanes_ref[0:1, :]
@@ -325,17 +325,18 @@
     def forward():
         other = [swap(piece, "col", col_count, 1) for piece in got]
         early, *fetched = pl.pallas_call(
-            lambda *refs: early_kernel(clusters, exc, 1 + len(got), *refs),
+            lambda *refs: early_kernel(clusters, exc, len(got), *refs),
             in_specs=[VMEM] + [ANY] * (4 + len(got)),
-            out_specs=[VMEM] * 4,
+            out_specs=[VMEM] * 5,
             out_shape=[
                 jax.ShapeDtypeStruct((exc, entries * rank), F32),
                 jax.ShapeDtypeStruct(v.shape, BF16),
                 jax.ShapeDtypeStruct(u.shape, BF16),
                 jax.ShapeDtypeStruct(near.shape, F32),
+                jax.ShapeDtypeStruct(x.shape, BF16),
             ],
             scratch_shapes=[
-                pltpu.VMEM(((1 + len(got)) * span, panels), BF16),
+                pltpu.VMEM((len(got) * span, panels), BF16),
                 pltpu.SemaphoreType.DMA((4 + len(got),)),
             ],
             compiler_params=params(others),
@@ -344,7 +345,7 @@
         )(lanes, v, u, near, whole, *got)
         send, keep = pl.pallas_call(
             lambda *refs: forward_kernel(clusters, exc, *refs),
-            in_specs=[VMEM] * (5 + len(other)),
+            in_specs=[VMEM] * (6 + len(other)),
             out_specs=[VMEM] * 2,
             out_shape=shares(1),
             compiler_params=params(others),

time: 29.7 us -> 30.5 us (1.027)
  other arithmetic: 0.78 us -> 1.69 us
  waiting for transfers between devices: 5.81 us -> 5.22 us
  Pallas kernels: 8.83 us -> 9.36 us
    convert_element_type x1, other arithmetic: 0.01 us -> 0.92 us  [forward(): joined = col_sum(one, one_leaving).astype(BF16)]
    pallas_call x1, Pallas kernels: 0.07 us -> 0.71 us  [local(): pl.pallas_call(lambda *refs: pair_kernel(span, *refs), in_specs=[VMEM] *...]
    ppermute x10, waiting for transfers between devices: 5.81 us -> 5.22 us  [swap(): return lax.ppermute(value, axis, [(i, i ^ step) for i in range(size)])]
  transfers between devices with their start and end apart: 11 -> 11, of which waited for: 5 -> 4; matrix products, arithmetic and copies ran while one was open for 0% -> 3% of each run, Pallas kernels for 30% -> 31%
where the time goes in v16:
time: 30.5 us; the launch traced here: 30.3 us
  starting transfers between devices  13.9 us (46%)
  Pallas kernels  9.36 us (31%)
  waiting for transfers between devices  5.22 us (17%)
  other arithmetic  1.69 us (6%)
    ppermute x10, starting transfers between devices, swap(): return lax.ppermute(value, axis, [(i, i ^ step) for i in range(size)])  9.84 us
    ppermute x10, waiting for transfers between devices, swap(): return lax.ppermute(value, axis, [(i, i ^ step) for i in range(size)])  5.22 us
    ppermute x1, starting transfers between devices, body(): lax.ppermute(x, ('row', 'col'), rows_perm(d))  4.04 us
    pallas_call x1, Pallas kernels, near_of(): pl.pallas_call(lambda *refs: near_kernel(clusters, exc, *refs), in_specs=...  3.19 us
    pallas_call x1, Pallas kernels, local(): pl.pallas_call(lambda *refs: mirror_kernel(clusters, exc, rank, others, *...  2.16 us
    pallas_call x1, Pallas kernels, forward(): pl.pallas_call(lambda *refs: early_kernel(clusters, exc, len(got), *refs)...  1.64 us
    pallas_call x1, Pallas kernels, forward(): pl.pallas_call(lambda *refs: forward_kernel(clusters, exc, *refs), in_spe...  1.29 us
    convert_element_type x1, other arithmetic, forward(): joined = col_sum(one, one_leaving).astype(BF16)  0.92 us
  transfers between devices with their start and end apart: 11, of which 4 were waited for; matrix products, arithmetic and copies ran while one was open for 3% of the time, Pallas kernels for 31%

profile of v16, /device:TPU:0, one launch (start us, length us, event | category | flops | bytes accessed | tf_op | source)
XLA Modules:
  0.0 30.3 jit_solution(5234745064568752782)
XLA Ops:
  0.0 4.0 %collective-permute-start.7 = (bf16[128,1024]{1,0:T(8,128)(2,1)}, bf16[128,1024]{1,0:T(8,128)(2,1)}, u32[]{:S(2)}, u32[]{:S(2)}) collective-permute-start(bf16[128,1024]{1,0:T(8,128)(2,1)} %bitcast.15), channel_id=1, source_target_pairs={{0,8},{1,13},{2,10},{3,15},{4,12},{5,9},{6,14},{7,11},{8,0},{9,5},... | collective-permute-start | bytes 786440 | tf_op jit(solution)/shard_map/ppermute | solution.py:269
  4.0 1.6 %collective-permute-start.8 = (bf16[128,1024]{1,0:T(8,128)(2,1)}, bf16[128,1024]{1,0:T(8,128)(2,1)S(1)}, u32[]{:S(2)}, u32[]{:S(2)}) collective-permute-start(bf16[128,1024]{1,0:T(8,128)(2,1)} %bitcast.16), channel_id=1, source_target_pairs={{0,4},{4,0},{8,12},{12,8},{1,5},{5,1},{9,13},{13,9},{2,6},{6,2},{1... | collective-permute-start | bytes 786440 | tf_op jit(solution)/shard_map/ppermute | solution.py:207
  5.6 10.3 %conditional.2 = (f32[128,256]{1,0:T(8,128)}, bf16[128,256]{1,0:T(8,128)(2,1)S(1)}, bf16[128,256]{1,0:T(8,128)(2,1)S(1)}, bf16[128,256]{1,0:T(8,128)(2,1)S(1)}, ...) conditional(s32[]{:T(128)} %convert_element_type.37, () %tuple.23, (s32[24]{0:T(128)}, s32[24]{0:T(128)}, ...), branch_computations={%region_0.0_spmd, %region_1.0_spmd} | conditional | flops 200704 | bytes 15470804 | solution.py:213
  5.6 2.2 %mirror.1 = (bf16[2,384,256]{2,1,0:T(8,128)(2,1)S(1)}, bf16[384,384]{1,0:T(8,128)(2,1)S(1)}, s32[8,384]{1,0:T(8,128)S(1)}) custom-call(s32[24]{0:T(128)} %get-tuple-element.103.refs_0_, s32[24]{0:T(128)} %get-tuple-element.104.refs_1_, bf16[128,1024]{1,0:T(8,128)(2,1)} %bitcast.18, bf16[384,1024]{1,0:T(8,128)(2,1)} %get-tuple-element.47.refs_3_, ...), custom_call_target="tpu_custom_call" | custom-call | flops 1024 | bytes 1024 | tf_op jit(solution)/shard_map/cond/branch_1_fun/mirror/pallas_call | solution.py:272
  7.8 0.1 collective-permute-start.5
  7.9 0.4 %kept.1.refs_0_ = f32[2,384,256]{2,1,0:T(8,128)S(1)} custom-call(bf16[384,384]{1,0:T(8,128)(2,1)S(1)} %get-tuple-element.49.refs_0_, bf16[384,1024]{1,0:T(8,128)(2,1)S(1)} %copy-done), custom_call_target="tpu_custom_call" | custom-call | flops 1024 | bytes 1024 | tf_op jit(solution)/shard_map/cond/branch_1_fun/kept/pallas_call | solution.py:293
  8.3 1.3 %collective-permute-done.5.refs_1_ = bf16[2,384,256]{2,1,0:T(8,128)(2,1)S(1)} collective-permute-done((bf16[2,384,256]{2,1,0:T(8,128)(2,1)S(1)}, bf16[2,384,256]{2,1,0:T(8,128)(2,1)S(1)}, u32[]{:S(2)}, u32[]{:S(2)}) %collective-permute-start.5) | collective-permute-done | bytes 393248 | tf_op jit(solution)/shard_map/cond/branch_1_fun/ppermute | solution.py:207
  9.6 0.7 %pair.1 = (f32[128,256]{1,0:T(8,128)}, f32[256,256]{1,0:T(8,128)S(1)}, bf16[128,256]{1,0:T(8,128)(2,1)S(1)}, bf16[256,256]{1,0:T(8,128)(2,1)S(1)}) custom-call(f32[2,384,256]{2,1,0:T(8,128)S(1)} %kept.1.refs_0_, bf16[2,384,256]{2,1,0:T(8,128)(2,1)S(1)} %collective-permute-done.5.refs_1_), custom_call_target="tpu_custom_call" | custom-call | flops 1024 | bytes 1024 | tf_op jit(solution)/shard_map/cond/branch_1_fun/pair/pallas_call | solution.py:303
  10.3 1.5 %collective-permute-start.6 = (bf16[256,256]{1,0:T(8,128)(2,1)S(1)}, bf16[256,256]{1,0:T(8,128)(2,1)S(1)}, u32[]{:S(2)}, u32[]{:S(2)}) collective-permute-start(bf16[256,256]{1,0:T(8,128)(2,1)S(1)} %get-tuple-element.56), channel_id=1, source_target_pairs={{0,2},{1,3},{2,0},{3,1},{4,6},{5,7},{6,4},{7,5},{8,10},{9,11},{10,... | collective-permute-start | bytes 393224 | tf_op jit(solution)/shard_map/cond/branch_1_fun/ppermute | solution.py:207
  11.8 3.2 %near.1 = f32[4,32,1024]{2,1,0:T(8,128)} custom-call(s32[1]{0:T(128)} %get-tuple-element.105.refs_0_, s32[1]{0:T(128)} %get-tuple-element.106.refs_1_, bf16[4,32,1024]{2,1,0:T(8,128)(2,1)S(1)} %copy-done.2, bf16[1,1024,1024]{2,1,0:T(8,128)(2,1)S(1)} %copy-done.1), custom_call_target="tpu_custom_call" | custom-call | flops 1024 | bytes 1024 | tf_op jit(solution)/shard_map/cond/branch_1_fun/near/pallas_call | solution.py:251
  15.0 0.9 %collective-permute-done.6 = bf16[256,256]{1,0:T(8,128)(2,1)S(1)} collective-permute-done((bf16[256,256]{1,0:T(8,128)(2,1)S(1)}, bf16[256,256]{1,0:T(8,128)(2,1)S(1)}, u32[]{:S(2)}, u32[]{:S(2)}) %collective-permute-start.6) | collective-permute-done | bytes 131104 | tf_op jit(solution)/shard_map/cond/branch_1_fun/ppermute | solution.py:207
  15.9 0.4 %collective-permute-start.9 = (bf16[128,256]{1,0:T(8,128)(2,1)S(1)}, bf16[128,256]{1,0:T(8,128)(2,1)S(1)}, u32[]{:S(2)}, u32[]{:S(2)}) collective-permute-start(bf16[128,256]{1,0:T(8,128)(2,1)S(1)} %get-tuple-element.96), channel_id=1, source_target_pairs={{0,8},{4,12},{8,0},{12,4},{1,9},{5,13},{9,1},{13,5},{2,10},{6,14},... | collective-permute-start | bytes 196616 | tf_op jit(solution)/shard_map/ppermute | solution.py:207
  16.3 2.6 %collective-permute-start.10 = (bf16[128,256]{1,0:T(8,128)(2,1)S(1)}, bf16[128,256]{1,0:T(8,128)(2,1)S(1)}, u32[]{:S(2)}, u32[]{:S(2)}) collective-permute-start(bf16[128,256]{1,0:T(8,128)(2,1)S(1)} %get-tuple-element.97), channel_id=1, source_target_pairs={{0,12},{4,8},{8,4},{12,0},{1,13},{5,9},{9,5},{13,1},{2,14},{6,10},... | collective-permute-start | bytes 196616 | tf_op jit(solution)/shard_map/ppermute | solution.py:207
  18.9 10.7 %conditional.3 = (f32[128,256]{1,0:T(8,128)S(1)}) conditional(s32[]{:T(128)} %convert_element_type.37, () %tuple.22, (s32[8,384]{1,0:T(8,128)S(1)}, bf16[384,1024]{1,0:T(8,128)(2,1)}, bf16[384,1024]{1,0:T(8,128)(2,1)}, f32[128,1024]{1,0:T(8,128)}, bf16[128,1024]{1,0:T(8,128)(2,1)S(1)}, /*index=5*/bf16[128,1024]{1,0:T(8,128)(2,1)}, s32[]{:T(128)}, ...), branch_computations={%region_2.0_spmd, %region_3.4_spmd} | conditional | flops 362518 | bytes 3803582 | solution.py:213
  18.9 1.6 %collective-permute-start.3 = (bf16[128,256]{1,0:T(8,128)(2,1)S(1)}, bf16[128,256]{1,0:T(8,128)(2,1)S(1)}, u32[]{:S(2)}, u32[]{:S(2)}) collective-permute-start(bf16[128,256]{1,0:T(8,128)(2,1)S(1)} %get-tuple-element.77), channel_id=1, source_target_pairs={{0,2},{1,3},{2,0},{3,1},{4,6},{5,7},{6,4},{7,5},{8,10},{9,11},{10,... | collective-permute-start | bytes 196616 | tf_op jit(solution)/shard_map/cond/branch_1_fun/ppermute | solution.py:207
  20.5 1.6 %early.1 = (f32[32,384]{1,0:T(8,128)S(1)}, bf16[384,1024]{1,0:T(8,128)(2,1)S(1)}, bf16[384,1024]{1,0:T(8,128)(2,1)S(1)}, f32[128,1024]{1,0:T(8,128)S(1)}, bf16[128,1024]{1,0:T(8,128)(2,1)S(1)}) custom-call(s32[8,384]{1,0:T(8,128)S(1)} %get-tuple-element.62.refs_0_, bf16[384,1024]{1,0:T(8,128)(2,1)} %get-tuple-element.63.refs_1_, ...), custom_call_target="tpu_custom_call" | custom-call | flops 1024 | bytes 1024 | tf_op jit(solution)/shard_map/cond/branch_1_fun/early/pallas_call | solution.py:327
  22.1 1.3 %forward.1 = (bf16[2,128,256]{2,1,0:T(8,128)(2,1)S(1)}, f32[2,128,256]{2,1,0:T(8,128)S(1)}) custom-call(s32[8,384]{1,0:T(8,128)S(1)} %get-tuple-element.62.refs_0_, f32[32,384]{1,0:T(8,128)S(1)} %get-tuple-element.68.refs_1_, bf16[384,1024]{1,0:T(8,128)(2,1)S(1)} %get-tuple-element.69.refs_2_, bf16[384,1024]{1,0:T(8,128)(2,1)S(1)} %get-tuple-element.70.refs_3_, ...), custom_call_target="tpu_custom_call" | custom-call | flops 1024 | bytes 1024 | tf_op jit(solution)/shard_map/cond/branch_1_fun/forward/pallas_call | solution.py:346
  23.4 0.2 collective-permute-start.1
  23.7 0.9 %add_convert_fusion.1 = bf16[128,256]{1,0:T(8,128)(2,1)S(1)} fusion(f32[128,256]{1,0:T(8,128)} %get-tuple-element.76, bf16[128,256]{1,0:T(8,128)(2,1)S(1)} %collective-permute-done.3), kind=kLoop, calls=%fused_computation.4 | loop fusion | flops 98304 | bytes 262144 | tf_op jit(solution)/shard_map/cond/branch_1_fun/convert_element_type | solution.py:355
  24.6 0.6 %collective-permute-start.4 = (bf16[128,256]{1,0:T(8,128)(2,1)S(1)}, bf16[128,256]{1,0:T(8,128)(2,1)S(1)}, u32[]{:S(2)}, u32[]{:S(2)}) collective-permute-start(bf16[128,256]{1,0:T(8,128)(2,1)S(1)} %add_convert_fusion.1), channel_id=1, source_target_pairs={{0,4},{4,0},{8,12},{12,8},{1,5},{5,1},{9,13},{13,9},{2,6},{6,2},{1... | collective-permute-start | bytes 196616 | tf_op jit(solution)/shard_map/cond/branch_1_fun/ppermute | solution.py:207
  25.3 1.3 %collective-permute-start.2 = (bf16[128,256]{1,0:T(8,128)(2,1)S(1)}, bf16[128,256]{1,0:T(8,128)(2,1)S(1)}, u32[]{:S(2)}, u32[]{:S(2)}) collective-permute-start(bf16[128,256]{1,0:T(8,128)(2,1)S(1)} %fusion.1), channel_id=1, source_target_pairs={{0,2},{1,3},{2,0},{3,1},{4,6},{5,7},{6,4},{7,5},{8,10},{9,11},{10,... | collective-permute-start | bytes 196616 | tf_op jit(solution)/shard_map/cond/branch_1_fun/ppermute | solution.py:207
  26.6 2.5 %collective-permute-done.4 = bf16[128,256]{1,0:T(8,128)(2,1)S(1)} collective-permute-done((bf16[128,256]{1,0:T(8,128)(2,1)S(1)}, bf16[128,256]{1,0:T(8,128)(2,1)S(1)}, u32[]{:S(2)}, u32[]{:S(2)}) %collective-permute-start.4) | collective-permute-done | bytes 65568 | tf_op jit(solution)/shard_map/cond/branch_1_fun/ppermute | solution.py:207
  29.0 0.6 %collective-permute-done.2 = bf16[128,256]{1,0:T(8,128)(2,1)S(1)} collective-permute-done((bf16[128,256]{1,0:T(8,128)(2,1)S(1)}, bf16[128,256]{1,0:T(8,128)(2,1)S(1)}, u32[]{:S(2)}, u32[]{:S(2)}) %collective-permute-start.2) | collective-permute-done | bytes 65568 | tf_op jit(solution)/shard_map/cond/branch_1_fun/ppermute | solution.py:207
  29.7 0.7 %convert_add_fusion.1 = f32[128,256]{1,0:T(8,128)} fusion(f32[128,256]{1,0:T(8,128)S(1)} %convert_add_fusion.2, bf16[128,256]{1,0:T(8,128)(2,1)S(1)} %collective-permute-done.10), kind=kLoop, calls=%fused_computation.7 | loop fusion | flops 65536 | bytes 327680 | tf_op jit(solution)/shard_map/add | solution.py:361
  (20 shorter events, 0.2 us)
Async XLA Ops:
  0.0 18.9 %collective-permute-start.7 = (bf16[128,1024]{1,0:T(8,128)(2,1)}, bf16[128,1024]{1,0:T(8,128)(2,1)}, u32[]{:S(2)}, u32[]{:S(2)}) collective-permute-start(bf16[128,1024]{1,0:T(8,128)(2,1)} %bitcast.15), channel_id=1, source_target_pairs={{0,8},{1,13},{2,10},{3,15},{4,12},{5,9},{6,14},{7,11},{8,0},{9,5},... | collective-permute-start | bytes 786440 | tf_op jit(solution)/shard_map/ppermute | solution.py:269
  4.0 14.9 %collective-permute-start.8 = (bf16[128,1024]{1,0:T(8,128)(2,1)}, bf16[128,1024]{1,0:T(8,128)(2,1)S(1)}, u32[]{:S(2)}, u32[]{:S(2)}) collective-permute-start(bf16[128,1024]{1,0:T(8,128)(2,1)} %bitcast.16), channel_id=1, source_target_pairs={{0,4},{4,0},{8,12},{12,8},{1,5},{5,1},{9,13},{13,9},{2,6},{6,2},{1... | collective-permute-start | bytes 786440 | tf_op jit(solution)/shard_map/ppermute | solution.py:207
  5.6 2.3 %copy-start = (bf16[384,1024]{1,0:T(8,128)(2,1)S(1)}, bf16[384,1024]{1,0:T(8,128)(2,1)}, u32[]{:S(2)}) copy-start(bf16[384,1024]{1,0:T(8,128)(2,1)} %get-tuple-element.48.refs_4_.refs_1_) | copy-start | bytes 2359300 | tf_op jit(solution)/shard_map/cond
  5.6 6.2 %copy-start.1 = (bf16[1,1024,1024]{2,1,0:T(8,128)(2,1)S(1)}, bf16[1,1024,1024]{2,1,0:T(8,128)(2,1)}, u32[]{:S(2)}) copy-start(bf16[1,1024,1024]{2,1,0:T(8,128)(2,1)} %get-tuple-element.107.refs_3_) | copy-start | bytes 6291460 | tf_op jit(solution)/shard_map/cond
  5.6 6.2 %copy-start.2 = (bf16[4,32,1024]{2,1,0:T(8,128)(2,1)S(1)}, bf16[4,32,1024]{2,1,0:T(8,128)(2,1)}, u32[]{:S(2)}) copy-start(bf16[4,32,1024]{2,1,0:T(8,128)(2,1)} %get-tuple-element.59.refs_2_) | copy-start | bytes 786436 | tf_op jit(solution)/shard_map/cond
  7.8 1.8 %collective-permute-start.5 = (bf16[2,384,256]{2,1,0:T(8,128)(2,1)S(1)}, bf16[2,384,256]{2,1,0:T(8,128)(2,1)S(1)}, u32[]{:S(2)}, u32[]{:S(2)}) collective-permute-start(bf16[2,384,256]{2,1,0:T(8,128)(2,1)S(1)} %get-tuple-element.50), channel_id=1, source_target_pairs={{0,1},{1,0},{2,3},{3,2},{4,5},{5,4},{6,7},{7,6},{8,9},{9,8},{10,11... | collective-permute-start | bytes 1179656 | tf_op jit(solution)/shard_map/cond/branch_1_fun/ppermute | solution.py:207
  10.3 5.5 %collective-permute-start.6 = (bf16[256,256]{1,0:T(8,128)(2,1)S(1)}, bf16[256,256]{1,0:T(8,128)(2,1)S(1)}, u32[]{:S(2)}, u32[]{:S(2)}) collective-permute-start(bf16[256,256]{1,0:T(8,128)(2,1)S(1)} %get-tuple-element.56), channel_id=1, source_target_pairs={{0,2},{1,3},{2,0},{3,1},{4,6},{5,7},{6,4},{7,5},{8,10},{9,11},{10,... | collective-permute-start | bytes 393224 | tf_op jit(solution)/shard_map/cond/branch_1_fun/ppermute | solution.py:207
  15.9 13.7 %collective-permute-start.9 = (bf16[128,256]{1,0:T(8,128)(2,1)S(1)}, bf16[128,256]{1,0:T(8,128)(2,1)S(1)}, u32[]{:S(2)}, u32[]{:S(2)}) collective-permute-start(bf16[128,256]{1,0:T(8,128)(2,1)S(1)} %get-tuple-element.96), channel_id=1, source_target_pairs={{0,8},{4,12},{8,0},{12,4},{1,9},{5,13},{9,1},{13,5},{2,10},{6,14},... | collective-permute-start | bytes 196616 | tf_op jit(solution)/shard_map/ppermute | solution.py:207
  16.3 13.4 %collective-permute-start.10 = (bf16[128,256]{1,0:T(8,128)(2,1)S(1)}, bf16[128,256]{1,0:T(8,128)(2,1)S(1)}, u32[]{:S(2)}, u32[]{:S(2)}) collective-permute-start(bf16[128,256]{1,0:T(8,128)(2,1)S(1)} %get-tuple-element.97), channel_id=1, source_target_pairs={{0,12},{4,8},{8,4},{12,0},{1,13},{5,9},{9,5},{13,1},{2,14},{6,10},... | collective-permute-start | bytes 196616 | tf_op jit(solution)/shard_map/ppermute | solution.py:207
  18.9 3.2 %collective-permute-start = (bf16[128,1024]{1,0:T(8,128)(2,1)}, bf16[128,1024]{1,0:T(8,128)(2,1)S(1)}, u32[]{:S(2)}, u32[]{:S(2)}) collective-permute-start(bf16[128,1024]{1,0:T(8,128)(2,1)} %get-tuple-element.67.refs_5_), channel_id=1, source_target_pairs={{0,1},{1,0},{2,3},{3,2},{4,5},{5,4},{6,7},{7,6},{8,9},{9,8},{10,11... | collective-permute-start | bytes 786440 | tf_op jit(solution)/shard_map/cond/branch_1_fun/ppermute | solution.py:207
  18.9 4.8 %collective-permute-start.3 = (bf16[128,256]{1,0:T(8,128)(2,1)S(1)}, bf16[128,256]{1,0:T(8,128)(2,1)S(1)}, u32[]{:S(2)}, u32[]{:S(2)}) collective-permute-start(bf16[128,256]{1,0:T(8,128)(2,1)S(1)} %get-tuple-element.77), channel_id=1, source_target_pairs={{0,2},{1,3},{2,0},{3,1},{4,6},{5,7},{6,4},{7,5},{8,10},{9,11},{10,... | collective-permute-start | bytes 196616 | tf_op jit(solution)/shard_map/cond/branch_1_fun/ppermute | solution.py:207
  23.4 1.8 %collective-permute-start.1 = (bf16[2,128,256]{2,1,0:T(8,128)(2,1)S(1)}, bf16[2,128,256]{2,1,0:T(8,128)(2,1)S(1)}, u32[]{:S(2)}, u32[]{:S(2)}) collective-permute-start(bf16[2,128,256]{2,1,0:T(8,128)(2,1)S(1)} %get-tuple-element.74), channel_id=1, source_target_pairs={{0,1},{1,0},{2,3},{3,2},{4,5},{5,4},{6,7},{7,6},{8,9},{9,8},{10,11... | collective-permute-start | bytes 393224 | tf_op jit(solution)/shard_map/cond/branch_1_fun/ppermute | solution.py:207
  24.6 4.4 %collective-permute-start.4 = (bf16[128,256]{1,0:T(8,128)(2,1)S(1)}, bf16[128,256]{1,0:T(8,128)(2,1)S(1)}, u32[]{:S(2)}, u32[]{:S(2)}) collective-permute-start(bf16[128,256]{1,0:T(8,128)(2,1)S(1)} %add_convert_fusion.1), channel_id=1, source_target_pairs={{0,4},{4,0},{8,12},{12,8},{1,5},{5,1},{9,13},{13,9},{2,6},{6,2},{1... | collective-permute-start | bytes 196616 | tf_op jit(solution)/shard_map/cond/branch_1_fun/ppermute | solution.py:207
  25.3 4.3 %collective-permute-start.2 = (bf16[128,256]{1,0:T(8,128)(2,1)S(1)}, bf16[128,256]{1,0:T(8,128)(2,1)S(1)}, u32[]{:S(2)}, u32[]{:S(2)}) collective-permute-start(bf16[128,256]{1,0:T(8,128)(2,1)S(1)} %fusion.1), channel_id=1, source_target_pairs={{0,2},{1,3},{2,0},{3,1},{4,6},{5,7},{6,4},{7,5},{8,10},{9,11},{10,... | collective-permute-start | bytes 196616 | tf_op jit(solution)/shard_map/cond/branch_1_fun/ppermute | solution.py:207
